TPU v7x, 32 devices: a whole 2x2x4 slice. The times are simulated.
32 devices in a mesh: groups: 2 (over y), row: 4 (over z), col: 4 (over x, core).
Axes of the slice: x: 2, y: 2, z: 4, core: 2. Of those that a mesh axis runs over, the one named last changes fastest.
Arguments:
- vectors: float32 [4, 256, 16384], P('groups', 'col', 'row'), parts along dimension 0, may hold values from -0.046875 to 0.046875
- factors: float32 [4, 256, 256], P('groups'), parts along dimension 0, as said below
- eigvecs: float32 [32768, 2048], P(('groups', 'row'), 'col'), parts along dimension 0, may hold values from -6 to 6
Outputs:
- transformed: float32 [32768, 2048], P(('groups', 'row'), 'col'), parts along dimension 0
There are 2 independent parts, one for each index of `groups`. A program takes and returns all parts, laid end to end along the dimension named above; each array names one. Nothing has to cross between parts.
Inputs may be any that keep to these rules, and one draw needn't show every extreme that they name: factors[k] is upper triangular with a positive diagonal.
All inputs are finite; a program needn't handle non-finite values.
Results may differ from a plain program's by a relative error of at most 0.0001.
Values sent between devices are 32-bit elements; how exact they have to be, the bound alone decides.
No kernel may reach another device: no remote copies, remote signals or barrier semaphores. Data moves between devices by JAX's collectives and lax.ppermute only.
A program may use at most 128 MiB of HBM per device.

v0:
```python
import jax
import jax.numpy as jnp
from jax import lax
from jax.sharding import PartitionSpec as P

HIGH = lax.Precision.HIGHEST


def local(vectors, factors, eigvecs):
    rows_here = eigvecs.shape[0]
    first = lax.axis_index("row") * rows_here
    full = lax.all_gather(vectors, "col", axis=1, tiled=True)
    width = full.shape[1]
    along = lax.broadcasted_iota(jnp.int32, (width, rows_here), 0)
    across = lax.broadcasted_iota(jnp.int32, (width, rows_here), 1) + first
    block_zero = jnp.where(across >= along, full[0], 0.0)
    block_one = jnp.where(across >= along + width, full[1], 0.0)
    current = eigvecs
    for index, reflector in ((1, block_one), (0, block_zero)):
        partial_value = jnp.dot(reflector, current, precision=HIGH)
        summed = lax.psum(partial_value, "row")
        scaled = jnp.dot(factors[index], summed, precision=HIGH)
        current = current - jnp.dot(reflector.T, scaled, precision=HIGH)
    return current


def solution(mesh):
    placed = (P("groups", "col", "row"), P("groups", None, None), P(("groups", "row"), "col"))
    return jax.shard_map(
        local, mesh=mesh, in_specs=placed, out_specs=P(("groups", "row"), "col"), check_vma=False
    )
```

profile of v0, /device:TPU:0, one launch (start us, length us, event | category | flops | bytes accessed | tf_op | source)
XLA Modules:
  0.0 218.0 jit_solution(8895059077144726701)
XLA Ops:
  6.5 0.0 all-gather.2.cloned.1.call-start
  6.5 0.7 all-gather.2.cloned.1.call-update
  7.3 0.0 all-reduce.3.cloned.1.call-start
  7.3 0.0 copy-start.1
  7.3 62.6 %all-gather.2.cloned.1.call-done = f32[2,256,4096]{2,1,0:T(8,128)} async-done(((f32[2,64,4096]{2,1,0:T(8,128)}), f32[2,256,4096]{2,1,0:T(8,128)}) %all-gather.2.cloned.1.call-update) | async-done | bytes 8388624 | tf_op jit(solution)/shard_map/all_gather | solution.py:12
  69.9 11.9 %fusion.3 = f32[256,512]{1,0:T(8,128)} fusion(f32[4096,512]{1,0:T(8,128)} %param.5, f32[2,256,4096]{2,1,0:T(8,128)} %all-gather.2.cloned.1.call-done, s32[4096]{0:T(1024)S(1)} %iota_add_fusion, s32[256]{0:T(256)S(1)} %iota_add_fusion.1), kind=kOutput, calls=%fused_computation.7 | convolution fusion | flops 6444548096 | bytes 13124608 | tf_op jit(solution)/shard_map/dot_general | solution.py:20
  81.9 0.0 all-reduce.3.cloned.1.call-update
  81.9 0.2 all-reduce.5.cloned.1.call-start
  82.1 38.2 %all-reduce.3.cloned.1.call-done = f32[256,512]{1,0:T(8,128)} async-done(((f32[256,512]{1,0:T(8,128)}), f32[256,512]{1,0:T(8,128)}) %all-reduce.3.cloned.1.call-update) | async-done | bytes 524304 | tf_op jit(solution)/shard_map/psum | solution.py:21
  120.3 0.0 copy-done.1
  120.3 0.0 slice-start
  120.3 2.2 %fusion.20 = f32[512,256]{1,0:T(8,128)S(1)} fusion(f32[256,512]{1,0:T(8,128)} %all-reduce.3.cloned.1.call-done, f32[2,256,256]{2,1,0:T(8,128)S(1)} %copy-done.1), kind=kOutput, calls=%fused_computation.21 | convolution fusion | flops 402653184 | bytes 1310720 | tf_op jit(solution)/shard_map/dot_general | solution.py:22
  122.5 0.0 slice-start.1
  122.6 17.5 %convolution_subtract_fusion.1 = f32[4096,512]{1,0:T(8,128)S(1)} fusion(f32[4096,512]{1,0:T(8,128)} %param.5, f32[512,256]{1,0:T(8,128)S(1)} %fusion.20, f32[2,256,4096]{2,1,0:T(8,128)} %all-gather.2.cloned.1.call-done, s32[4096]{0:T(1024)S(1)} %iota_add_fusion, s32[256]{0:T(256)S(1)} %iota_add_fusion.1), kind=kOutput, calls=%fused_computation.1 | convolution fusion | flops 6446645248 | bytes 21513216 | tf_op jit(solution)/shard_map/dot_general | solution.py:23
  140.1 0.0 copy-start
  140.1 3.4 %copy-done = f32[4096,512]{1,0:T(8,128)} copy-done((f32[4096,512]{1,0:T(8,128)}, f32[4096,512]{1,0:T(8,128)S(1)}, u32[]{:S(2)}) %copy-start) | copy-done | bytes 8388632
  143.5 0.0 slice-done
  143.5 0.0 slice-done.1
  143.5 8.3 %fusion.6 = f32[256,512]{1,0:T(8,128)} fusion(f32[4096,512]{1,0:T(8,128)S(1)} %convolution_subtract_fusion.1, f32[2,256,4096]{2,1,0:T(8,128)S(1)} %bitcast.25, s32[4096]{0:T(1024)S(1)} %iota_add_fusion), kind=kOutput, calls=%fused_computation.8 | convolution fusion | flops 6444548096 | bytes 13123584 | tf_op jit(solution)/shard_map/dot_general | solution.py:20
  151.8 0.0 all-reduce.5.cloned.1.call-update
  151.9 38.4 %all-reduce.5.cloned.1.call-done = f32[256,512]{1,0:T(8,128)} async-done(((f32[256,512]{1,0:T(8,128)}), f32[256,512]{1,0:T(8,128)}) %all-reduce.5.cloned.1.call-update) | async-done | bytes 524304 | tf_op jit(solution)/shard_map/psum | solution.py:21
  190.3 2.0 fusion.18
  192.3 19.2 %convolution_subtract_fusion = f32[4096,512]{1,0:T(8,128)} fusion(f32[4096,512]{1,0:T(8,128)} %copy-done, f32[512,256]{1,0:T(8,128)S(1)} %fusion.18, f32[2,256,4096]{2,1,0:T(8,128)} %all-gather.2.cloned.1.call-done, s32[4096]{0:T(1024)S(1)} %iota_add_fusion), kind=kOutput, calls=%fused_computation | convolution fusion | flops 6446645248 | bytes 21512192 | tf_op jit(solution)/shard_map/dot_general | solution.py:23
  (3 shorter events, 0.0 us)
Async XLA Ops:
  6.5 63.4 %all-gather.2.cloned.1.call-start = ((), (), s32[]{:S(2)}) async-start(), calls=%async_computation | async-start | bytes 10485760 | tf_op jit(solution)/shard_map/all_gather | solution.py:12
  7.3 113.1 %all-reduce.3.cloned.1.call-start = ((), (), s32[]{:S(2)}) async-start(), calls=%async_computation.1 | async-start | bytes 1048576 | tf_op jit(solution)/shard_map/psum | solution.py:21
  7.3 113.0 %copy-start.1 = (f32[2,256,256]{2,1,0:T(8,128)S(1)}, f32[2,256,256]{2,1,0:T(8,128)}, u32[]{:S(2)}) copy-start(f32[2,256,256]{2,1,0:T(8,128)} %param.4) | copy-start | bytes 1572868
  81.9 108.4 %all-reduce.5.cloned.1.call-start = ((), (), s32[]{:S(2)}) async-start(), calls=%async_computation.2 | async-start | bytes 1048576 | tf_op jit(solution)/shard_map/psum | solution.py:21
  120.3 23.1 %slice-start = ((s8[8388608]{0:T(1024)(128)(4,1)}), s8[4194304]{0:T(1024)(128)(4,1)S(1)}, s32[]{:S(2)}) async-start(s8[8388608]{0:T(1024)(128)(4,1)} %bitcast.24), calls=%async_computation.3 | async-start | bytes 8388608
  122.5 20.9 %slice-start.1 = ((s8[8388608]{0:T(1024)(128)(4,1)}), s8[4194304]{0:T(1024)(128)(4,1)S(1)}, s32[]{:S(2)}) async-start(s8[8388608]{0:T(1024)(128)(4,1)} %bitcast.24), calls=%async_computation.4 | async-start | bytes 8388608
  140.1 3.4 %copy-start = (f32[4096,512]{1,0:T(8,128)}, f32[4096,512]{1,0:T(8,128)S(1)}, u32[]{:S(2)}) copy-start(f32[4096,512]{1,0:T(8,128)S(1)} %convolution_subtract_fusion.1) | copy-start | bytes 25165828
Sparse Core Ops, SparseCore 0:
  8.9 60.9 all-gather.1
  82.0 38.2 all-reduce.2
  152.0 38.2 all-reduce.4
where the time goes:
time: 218 us
  waiting for transfers between devices  140 us (64%)
  matrix products  61.2 us (28%)
  between operations  13.2 us (6%)
  local copies, waits for them, and re-layouts  3.41 us (2%)
    psum x2, waiting for transfers between devices, local(): summed = lax.psum(partial_value, 'row')  76.6 us
    all_gather x1, waiting for transfers between devices, local(): full = lax.all_gather(vectors, 'col', axis=1, tiled=True)  62.6 us
    dot_general x2, matrix products, local(): current = current - jnp.dot(reflector.T, scaled, precision=HIGH)  36.7 us
    dot_general x2, matrix products, local(): partial_value = jnp.dot(reflector, current, precision=HIGH)  20.3 us
  transfers between devices with their start and end apart: 3, of which 3 were waited for; matrix products, arithmetic and copies ran while one was open for 0% of the time, Pallas kernels for 0%

commit v1 on v0

v1 whole, which is shorter than its diff:
```python
import functools

import jax
import jax.numpy as jnp
from jax import lax
from jax.experimental import pallas as pl
from jax.experimental.pallas import tpu as pltpu
from jax.sharding import PartitionSpec as P

F32, BF16 = jnp.float32, jnp.bfloat16
PIECES = ((1, 0, 32), (1, 32, 64), (0, 0, 40), (0, 40, 64))
NN = (((1,), (0,)), ((), ()))
NT = (((1,), (1,)), ((), ()))
TN = (((0,), (0,)), ((), ()))


def params(mib):
    return pltpu.CompilerParams(
        dimension_semantics=("arbitrary",), vmem_limit_bytes=mib * 1024 * 1024
    )


def whole(shape):
    return pl.BlockSpec(shape, lambda i: (0,) * len(shape))


def cost(flops, moved):
    return pl.CostEstimate(flops=flops, bytes_accessed=moved, transcendentals=0)


SCALARS = pl.BlockSpec(memory_space=pltpu.SMEM)


def split(value):
    high = value.astype(BF16)
    return high, (value - high.astype(F32)).astype(BF16)


def full_dot(a, b, dims=NN):
    return lax.dot_general(a, b, dims, precision=lax.Precision.HIGHEST, preferred_element_type=F32)


def three(vh, vl, b, dims):
    rows = vh.shape[0]
    bh, bl = split(b)
    first = lax.dot_general(jnp.concatenate([vh, vl]), bh, dims, preferred_element_type=F32)
    second = lax.dot_general(vh, bl, dims, preferred_element_type=F32)
    return first[:rows] + first[rows:] + second


def cut(where, vectors, pieces):
    _, share, here = vectors.shape
    step = min(here, 1024)

    def body(where_ref, in_ref, *outs):
        for (block, low, high), out in zip(pieces, outs):
            shape = (high - low, step)
            along = lax.broadcasted_iota(jnp.int32, shape, 0) + (where_ref[0] + low)
            across = lax.broadcasted_iota(jnp.int32, shape, 1) + (where_ref[1] + pl.program_id(0) * step)
            out[...] = jnp.where(across >= along + block * where_ref[2], in_ref[block, low:high], 0.0)

    return pl.pallas_call(
        body,
        grid=(here // step,),
        in_specs=[SCALARS, pl.BlockSpec((2, share, step), lambda i: (0, 0, i))],
        out_specs=[pl.BlockSpec((b - a, step), lambda i: (0, i)) for _, a, b in pieces],
        out_shape=[jax.ShapeDtypeStruct((b - a, here), F32) for _, a, b in pieces],
        compiler_params=params(16),
        cost_estimate=cost(0, 4 * vectors.size * 2),
        name="cut",
    )(where, vectors)


def project(rows, partners, eigvecs, bit=None):
    here, nc = eigvecs.shape
    step = min(here, 512)
    height = sum(r.shape[0] for r in rows)
    extra = sum(r.shape[0] for r in partners)
    steps = here // step

    def body(*refs):
        refs = list(refs)
        bit_ref = refs.pop(0) if bit is not None else None
        row_refs, partner_refs = refs[: len(rows)], refs[len(rows) : len(rows) + len(partners)]
        eig_ref = refs[len(rows) + len(partners)]
        outs, acc = refs[len(rows) + len(partners) + 1 : -1], refs[-1]
        k = pl.program_id(0)

        @pl.when(k == 0)
        def _():
            acc[...] = jnp.zeros_like(acc)

        vh, vl = split(jnp.concatenate([r[...] for r in row_refs]))
        acc[:, :nc] += three(vh, vl, eig_ref[...], NN)
        if partners:
            acc[:, nc:] += three(vh, vl, jnp.concatenate([r[...] for r in partner_refs]), NT)

        @pl.when(k == steps - 1)
        def _():
            if bit is None:
                outs[0][...] = acc[...]
            else:
                half = height // 2
                zero = bit_ref[0] == 0
                outs[0][...] = jnp.where(zero, acc[:half], acc[half:])
                outs[1][...] = jnp.where(zero, acc[half:], acc[:half])

    count = 1 if bit is None else 2
    shape = (height // count, nc + extra)
    return pl.pallas_call(
        body,
        grid=(steps,),
        in_specs=([] if bit is None else [SCALARS])
        + [pl.BlockSpec((r.shape[0], step), lambda i: (0, i)) for r in rows + partners]
        + [pl.BlockSpec((step, nc), lambda i: (i, 0))],
        out_specs=[whole(shape)] * count,
        out_shape=[jax.ShapeDtypeStruct(shape, F32)] * count,
        scratch_shapes=[pltpu.VMEM((height, nc + extra), F32)],
        compiler_params=params(32),
        cost_estimate=cost(6 * height * here * (nc + extra), 4 * (eigvecs.size + height * here)),
        name="project",
    )(*([] if bit is None else [bit]), *rows, *partners, eigvecs)


def turn(pieces):
    here = pieces[0].shape[1]
    step = min(here, 512)
    height = sum(r.shape[0] for r in pieces)

    def body(*refs):
        turned = jnp.concatenate([r[...] for r in refs[:-2]]).T
        high, low = split(turned)
        refs[-2][...] = high
        refs[-1][...] = low

    return pl.pallas_call(
        body,
        grid=(here // step,),
        in_specs=[pl.BlockSpec((r.shape[0], step), lambda i: (0, i)) for r in pieces],
        out_specs=[pl.BlockSpec((step, height), lambda i: (i, 0))] * 2,
        out_shape=[jax.ShapeDtypeStruct((here, height), BF16)] * 2,
        compiler_params=params(16),
        cost_estimate=cost(0, 8 * height * here),
        name="turn",
    )(*pieces)


def reorder(where, factors, share, chips, segments):
    width = factors.shape[1]

    def body(where_ref, in_ref, *outs):
        chip, core = where_ref[3], where_ref[4]
        for block, out in enumerate(outs):
            picks = []
            for step, other, low, high in segments[block]:
                at = (lax.rem(chip + step, chips) * 2 + (core + other) % 2) * share + low
                shape = (high - low, width)
                same = lax.broadcasted_iota(jnp.int32, shape, 1) == lax.broadcasted_iota(jnp.int32, shape, 0) + at
                picks.append(jnp.where(same, 1.0, 0.0))
            pick = jnp.concatenate(picks)
            out[...] = full_dot(full_dot(pick, in_ref[block]), pick, NT)

    return pl.pallas_call(
        body,
        grid=(1,),
        in_specs=[SCALARS, whole(factors.shape)],
        out_specs=[whole((width, width))] * 2,
        out_shape=[jax.ShapeDtypeStruct((width, width), F32)] * 2,
        compiler_params=params(16),
        cost_estimate=cost(48 * width**3, 8 * factors.size),
        name="reorder",
    )(where, factors)


def update(make, ins, factor, turned, current, with_scaled):
    here, nc = current.shape
    width = factor.shape[0]
    step = min(here, 512)

    def body(*refs):
        in_refs, rest = refs[: len(ins)], refs[len(ins) :]
        factor_ref, high_ref, low_ref, cur_ref = rest[:4]
        outs, (sh_ref, sl_ref) = rest[4:-2], rest[-2:]

        @pl.when(pl.program_id(0) == 0)
        def _():
            scaled = full_dot(factor_ref[...], make(*in_refs))
            sh_ref[...], sl_ref[...] = split(scaled)
            if with_scaled:
                outs[1][...] = scaled

        high, low = high_ref[...], low_ref[...]
        sh, sl = sh_ref[...], sl_ref[...]
        dot = functools.partial(jnp.dot, preferred_element_type=F32)
        outs[0][...] = cur_ref[...] - (dot(high, sh) + dot(high, sl) + dot(low, sh))

    def spec(value):
        return SCALARS if value.dtype == jnp.int32 else whole(value.shape)

    tall = pl.BlockSpec((step, width), lambda i: (i, 0))
    wide = pl.BlockSpec((step, nc), lambda i: (i, 0))
    out_specs, out_shape = [wide], [jax.ShapeDtypeStruct((here, nc), F32)]
    if with_scaled:
        out_specs.append(whole((width, nc)))
        out_shape.append(jax.ShapeDtypeStruct((width, nc), F32))
    return pl.pallas_call(
        body,
        grid=(here // step,),
        in_specs=[spec(v) for v in ins] + [whole(factor.shape), tall, tall, wide],
        out_specs=out_specs,
        out_shape=out_shape,
        scratch_shapes=[pltpu.VMEM((width, nc), BF16)] * 2,
        compiler_params=params(32),
        cost_estimate=cost(6 * here * width * nc, 4 * here * (2 * nc + width)),
        name="update",
    )(*ins, factor, *turned, current)


def make_local(chips, rows):
    cols = 2 * chips

    def core_swap(value):
        return lax.ppermute(value, "col", [(i, i ^ 1) for i in range(cols)])

    def from_chip(value, step):
        return lax.ppermute(value, "col", [((i + 2 * step) % cols, i) for i in range(cols)])

    def row_swap(value, step):
        return lax.ppermute(value, "row", [(i, i ^ step) for i in range(rows)])

    def row_sum(value, step=1):
        while step < rows:
            value = value + row_swap(value, step)
            step *= 2
        return value

    def halves_sum(keep, send):
        mine = row_sum(keep + row_swap(send, 1), 2)
        return mine, row_swap(mine, 1)

    def local(vectors, factors, eigvecs):
        share, here = vectors.shape[1:]
        nc = eigvecs.shape[1]
        width = share * cols
        half = 2 * share
        col, row = lax.axis_index("col"), lax.axis_index("row")
        where = jnp.stack([col * share, row * here, jnp.int32(width), col // 2, col % 2]).astype(jnp.int32)
        bit = (row % 2).astype(jnp.int32)[None]
        pieces = []
        for block, low, high in PIECES:
            low, high = low * share // 64 // 8 * 8, high * share // 64 // 8 * 8
            pieces.append((block, low, high))

        mine = cut(where, vectors, pieces)
        far = [(step, p, from_chip(m, step)) for p, m in zip(pieces, mine) for step in range(1, chips)]
        own, segments = {0: [], 1: []}, {0: [], 1: []}
        for (block, low, high), m in zip(pieces, mine):
            own[block] += [m, core_swap(m)]
            segments[block] += [(0, 0, low, high), (0, 1, low, high)]
        all_ones, all_zeros = list(own[1]), list(own[0])
        ones = [halves_sum(*project(own[1], own[0], eigvecs, bit))]
        own_zero = lax.psum(project(own[0], [], eigvecs)[0], "row")
        zeros = []
        for step, (block, low, high), value in far:
            pair = [value, core_swap(value)]
            segments[block] += [(step, 0, low, high), (step, 1, low, high)]
            if block == 1:
                all_ones += pair
                ones.append(halves_sum(*project(pair, own[0], eigvecs, bit)))
            else:
                all_zeros += pair
                zeros.append(row_sum(project(pair, all_ones, eigvecs)[0]))
        t0, t1 = reorder(where, factors, share, chips, segments)

        def joined(bit_ref, refs, columns):
            parts = []
            zero = bit_ref[0] == 0
            for a, b in zip(refs[::2], refs[1::2]):
                a, b = a[:, columns], b[:, columns]
                parts += [jnp.where(zero, a, b), jnp.where(zero, b, a)]
            return jnp.concatenate(parts)

        flat = [v for pair in ones for v in pair]

        def make_one(bit_ref, *refs):
            return joined(bit_ref, refs, slice(0, nc))

        def make_zero(bit_ref, scaled_ref, own_ref, *refs):
            ones_refs, zero_refs = refs[: len(flat)], refs[len(flat) :]
            scaled = scaled_ref[...]
            turned_gram = joined(bit_ref, ones_refs, slice(nc, nc + half))
            parts = [own_ref[...] - full_dot(turned_gram, scaled, TN)]
            later = jnp.concatenate([r[...] for r in zero_refs])
            parts.append(later[:, :nc] - full_dot(later[:, nc:], scaled))
            return jnp.concatenate(parts)

        current, scaled = update(make_one, [bit, *flat], t1, turn(all_ones), eigvecs, True)
        (out,) = update(make_zero, [bit, scaled, own_zero, *flat, *zeros], t0, turn(all_zeros), current, False)
        return out

    return local


def solution(mesh):
    placed = (P("groups", "col", "row"), P("groups", None, None), P(("groups", "row"), "col"))
    local = make_local(mesh.shape["col"] // 2, mesh.shape["row"])
    return jax.shard_map(
        local, mesh=mesh, in_specs=placed, out_specs=P(("groups", "row"), "col"), check_vma=False
    )
```

time: 218 us -> 187 us (0.86); the launches traced: 218 us -> 185 us
  waiting for transfers between devices: 140 us -> 46.3 us
  Pallas kernels: 0 us -> 63.1 us
  matrix products: 61.2 us -> 0 us
  local copies, waits for them, and re-layouts: 3.41 us -> 31.3 us
  starting transfers between devices: 0.26 us -> 26 us
  other arithmetic: 0.01 us -> 4.22 us
    psum x2 -> x1, waiting for transfers between devices: 76.6 us -> 6.68 us  [local(): own_zero = lax.psum(project(own[0], [], eigvecs)[0], 'row')]
    pallas_call x0 -> x12, Pallas kernels: none -> 63.1 us  [the longest x6 34 us: project(): pl.pallas_call(body, grid=(steps,), in_specs=([] if bit is None else [SCA...]
    all_gather x1 -> x0, waiting for transfers between devices: 62.6 us -> none  [local(): full = lax.all_gather(vectors, 'col', axis=1, tiled=True)]
    dot_general x6 -> x0, matrix products: 61.2 us -> none  [the longest x2 36.7 us: local(): current = current - jnp.dot(reflector.T, scaled, precision=HIGH)]
    ppermute x0 -> x25, waiting for transfers between devices: none -> 39.6 us  [the longest x4 34.8 us: from_chip(): lax.ppermute(value, 'col', [((i + 2 * step) % cols, i) for i in range(col...]
    unnamed x8 -> x56, local copies, waits for them, and re-layouts: 3.41 us -> 31.2 us
    ppermute x0 -> x25, starting transfers between devices: none -> 26 us  [the longest x13 18.2 us: row_swap(): return lax.ppermute(value, 'row', [(i, i ^ step) for i in range(rows)])]
    add x2 -> x10, other arithmetic: 0.01 us -> 4.22 us  [the longest x7 4.18 us: row_sum(): value = value + row_swap(value, step)]
  transfers between devices with their start and end apart: 3 -> 26, of which waited for: 3 -> 4; matrix products, arithmetic and copies ran while one was open for 0% -> 2% of each run, Pallas kernels for 0% -> 29%
where the time goes in v1:
time: 187 us; the launch traced here: 185 us
  Pallas kernels  63.1 us (34%)
  waiting for transfers between devices  46.3 us (25%)
  local copies, waits for them, and re-layouts  31.3 us (17%)
  starting transfers between devices  26 us (14%)
  between operations  13.7 us (7%)
  other arithmetic  4.22 us (2%)
    ppermute x4, waiting for transfers between devices, from_chip(): lax.ppermute(value, 'col', [((i + 2 * step) % cols, i) for i in range(col...  34.8 us
    pallas_call x6, Pallas kernels, project(): pl.pallas_call(body, grid=(steps,), in_specs=([] if bit is None else [SCA...  34 us
    unnamed x56, local copies, waits for them, and re-layouts  31.2 us
    ppermute x13, starting transfers between devices, row_swap(): return lax.ppermute(value, 'row', [(i, i ^ step) for i in range(rows)])  18.2 us
    pallas_call x2, Pallas kernels, update(): pl.pallas_call(body, grid=(here // step,), in_specs=[spec(v) for v in ins...  15.8 us
    pallas_call x2, Pallas kernels, turn(): pl.pallas_call(body, grid=(here // step,), in_specs=[pl.BlockSpec((r.shap...  10.2 us
    ppermute x4, starting transfers between devices, from_chip(): lax.ppermute(value, 'col', [((i + 2 * step) % cols, i) for i in range(col...  6.77 us
    psum x1, waiting for transfers between devices, local(): own_zero = lax.psum(project(own[0], [], eigvecs)[0], 'row')  6.68 us
  transfers between devices with their start and end apart: 26, of which 4 were waited for; matrix products, arithmetic and copies ran while one was open for 2% of the time, Pallas kernels for 29%

profile of v1, /device:TPU:0, one launch (start us, length us, event | category | flops | bytes accessed | tf_op | source)
XLA Modules:
  0.0 184.6 jit_solution(7550362582018323756)
XLA Ops:
  6.6 1.6 copy-done.16
  9.3 3.0 %collective-permute-start.7 = (f32[32,4096]{1,0:T(8,128)S(1)}, f32[32,4096]{1,0:T(8,128)}, u32[]{:S(2)}, u32[]{:S(2)}) collective-permute-start(f32[32,4096]{1,0:T(8,128)S(1)} %get-tuple-element.23.refs_1_.refs_0_.refs_2_), channel_id=1, source_target_pairs={{2,0},{3,1},{0,2},{1,3},{6,4},{7,5},{4,6},{5,7},{10,8},{11,9},{8,1... | collective-permute-start | bytes 1572872 | tf_op jit(solution)/shard_map/ppermute | solution.py:226
  12.5 1.9 %collective-permute-start.12 = (f32[32,4096]{1,0:T(8,128)S(1)}, f32[32,4096]{1,0:T(8,128)}, u32[]{:S(2)}, u32[]{:S(2)}) collective-permute-start(f32[32,4096]{1,0:T(8,128)S(1)} %get-tuple-element.24.refs_3_.refs_2_.refs_4_), channel_id=1, source_target_pairs={{2,0},{3,1},{0,2},{1,3},{6,4},{7,5},{4,6},{5,7},{10,8},{11,9},{8,1... | collective-permute-start | bytes 1572872 | tf_op jit(solution)/shard_map/ppermute | solution.py:226
  14.8 10.3 %collective-permute-done.7.refs_1_.refs_4_.refs_6_ = f32[32,4096]{1,0:T(8,128)} collective-permute-done((f32[32,4096]{1,0:T(8,128)S(1)}, f32[32,4096]{1,0:T(8,128)}, u32[]{:S(2)}, u32[]{:S(2)}) %collective-permute-start.7) | collective-permute-done | bytes 524320 | tf_op jit(solution)/shard_map/ppermute | solution.py:226
  25.2 24.4 %collective-permute-done.12.refs_1_.refs_6_.refs_8_ = f32[32,4096]{1,0:T(8,128)} collective-permute-done((f32[32,4096]{1,0:T(8,128)S(1)}, f32[32,4096]{1,0:T(8,128)}, u32[]{:S(2)}, u32[]{:S(2)}) %collective-permute-start.12) | collective-permute-done | bytes 524320 | tf_op jit(solution)/shard_map/ppermute | solution.py:226
  51.7 1.7 collective-permute-start.21
  53.5 3.4 %copy-done = f32[4096,512]{1,0:T(8,128)S(1)} copy-done((f32[4096,512]{1,0:T(8,128)S(1)}, f32[4096,512]{1,0:T(8,128)}, u32[]{:S(2)}) %copy-start) | copy-done | bytes 8388632
  58.9 4.5 %project.6 = (f32[64,640]{1,0:T(8,128)S(1)}, f32[64,640]{1,0:T(8,128)S(1)}) custom-call(s32[1]{0:T(128)} %bitcast.refs_0_, f32[32,4096]{1,0:T(8,128)S(1)} %get-tuple-element.23.refs_1_.refs_0_.refs_2_, f32[32,4096]{1,0:T(8,128)S(1)} %copy-done.6, f32[32,4096]{1,0:T(8,128)S(1)} %get-tuple-element.24.refs_3_.refs_2_.refs_4_, f32[32,4096]{1,0:T(8,128)S(1)} %copy-done.9, ...), custom_call_target="tpu_custom_call" | custom-call | flops 2013265920 | bytes 10485760 | tf_op jit(solution)/shard_map/project/pallas_call | solution.py:110
  63.4 1.6 collective-permute-start.4
  65.1 4.7 %collective-permute-done.4 = f32[64,640]{1,0:T(8,128)S(1)} collective-permute-done((f32[64,640]{1,0:T(8,128)S(1)}, f32[64,640]{1,0:T(8,128)S(1)}, u32[]{:S(2)}, u32[]{:S(2)}) %collective-permute-start.4) | collective-permute-done | bytes 163872 | tf_op jit(solution)/shard_map/ppermute | solution.py:229
  69.8 2.7 %collective-permute-start.5 = (f32[64,640]{1,0:T(8,128)S(1)}, f32[64,640]{1,0:T(8,128)S(1)}, u32[]{:S(2)}, u32[]{:S(2)}) collective-permute-start(f32[64,640]{1,0:T(8,128)S(1)} %add.42), channel_id=1, source_target_pairs={{0,8},{4,12},{8,0},{12,4},{1,9},{5,13},{9,1},{13,5},{2,10},{6,14},... | collective-permute-start | bytes 491528 | tf_op jit(solution)/shard_map/ppermute | solution.py:229
  72.5 5.7 %project.8 = (f32[32,640]{1,0:T(8,128)S(1)}, f32[32,640]{1,0:T(8,128)S(1)}) custom-call(s32[1]{0:T(128)} %bitcast.refs_0_, f32[32,4096]{1,0:T(8,128)} %collective-permute-done.12.refs_1_.refs_6_.refs_8_, f32[32,4096]{1,0:T(8,128)} %collective-permute-done.13.refs_2_.refs_7_.refs_9_, f32[40,4096]{1,0:T(8,128)S(1)} %get-tuple-element.25.refs_5_.refs_3_.refs_0_, ...), custom_call_target="tpu_custom_call" | custom-call | flops 1006632960 | bytes 9437184 | tf_op jit(solution)/shard_map/project/pallas_call | solution.py:110
  78.2 1.6 collective-permute-start.14
  79.9 5.7 %project.7 = (f32[32,640]{1,0:T(8,128)S(1)}, f32[32,640]{1,0:T(8,128)S(1)}) custom-call(s32[1]{0:T(128)} %bitcast.refs_0_, f32[32,4096]{1,0:T(8,128)} %collective-permute-done.7.refs_1_.refs_4_.refs_6_, f32[32,4096]{1,0:T(8,128)} %collective-permute-done.8.refs_2_.refs_5_.refs_7_, f32[40,4096]{1,0:T(8,128)S(1)} %get-tuple-element.25.refs_5_.refs_3_.refs_0_, ...), custom_call_target="tpu_custom_call" | custom-call | flops 1006632960 | bytes 9437184 | tf_op jit(solution)/shard_map/project/pallas_call | solution.py:110
  86.1 7.4 %project.10 = f32[80,768]{1,0:T(8,128)} custom-call(f32[40,4096]{1,0:T(8,128)} %collective-permute-done.17.refs_0_.refs_4_, f32[40,4096]{1,0:T(8,128)} %collective-permute-done.18.refs_1_.refs_5_, f32[32,4096]{1,0:T(8,128)S(1)} %get-tuple-element.23.refs_1_.refs_0_.refs_2_, f32[32,4096]{1,0:T(8,128)S(1)} %copy-done.6, ...), custom_call_target="tpu_custom_call" | custom-call | flops 1509949440 | bytes 9699328 | tf_op jit(solution)/shard_map/project/pallas_call | solution.py:110
  93.5 1.6 collective-permute-start.19
  95.1 2.0 %reorder.1 = (f32[256,256]{1,0:T(8,128)S(1)}, f32[256,256]{1,0:T(8,128)S(1)}) custom-call(s32[5]{0:T(128)S(1)} %stack.19.where_ref, f32[2,256,256]{2,1,0:T(8,128)S(1)} %copy-done.27), custom_call_target="tpu_custom_call" | custom-call | flops 805306368 | bytes 1048576 | tf_op jit(solution)/shard_map/reorder/pallas_call | solution.py:163
  98.7 2.6 %collective-permute-start.10 = (f32[32,640]{1,0:T(8,128)S(1)}, f32[32,640]{1,0:T(8,128)S(1)}, u32[]{:S(2)}, u32[]{:S(2)}) collective-permute-start(f32[32,640]{1,0:T(8,128)S(1)} %add.44), channel_id=1, source_target_pairs={{0,8},{4,12},{8,0},{12,4},{1,9},{5,13},{9,1},{13,5},{2,10},{6,14},... | collective-permute-start | bytes 245768 | tf_op jit(solution)/shard_map/ppermute | solution.py:229
  101.4 7.3 %project.11 = f32[48,768]{1,0:T(8,128)} custom-call(f32[24,4096]{1,0:T(8,128)S(1)} %collective-permute-done.21.refs_0_.refs_6_, f32[24,4096]{1,0:T(8,128)S(1)} %collective-permute-done.22.refs_1_.refs_7_, f32[32,4096]{1,0:T(8,128)S(1)} %get-tuple-element.23.refs_1_.refs_0_.refs_2_, f32[32,4096]{1,0:T(8,128)S(1)} %copy-done.6, ...), custom_call_target="tpu_custom_call" | custom-call | flops 905969664 | bytes 9175040 | tf_op jit(solution)/shard_map/project/pallas_call | solution.py:110
  108.6 1.6 collective-permute-start.23
  111.9 1.6 collective-permute-start.11
  113.5 3.5 %project.9 = f32[128,512]{1,0:T(8,128)S(1)} custom-call(f32[40,4096]{1,0:T(8,128)S(1)} %get-tuple-element.25.refs_5_.refs_3_.refs_0_, f32[40,4096]{1,0:T(8,128)S(1)} %collective-permute-done.2.refs_6_.refs_4_.refs_1_, f32[24,4096]{1,0:T(8,128)S(1)} %get-tuple-element.26.refs_7_.refs_5_.refs_2_, ...), custom_call_target="tpu_custom_call" | custom-call | flops 1610612736 | bytes 10485760 | tf_op jit(solution)/shard_map/project/pallas_call | solution.py:110
  119.9 5.2 %turn.2 = (bf16[4096,256]{1,0:T(8,128)(2,1)S(1)}, bf16[4096,256]{1,0:T(8,128)(2,1)S(1)}) custom-call(f32[32,4096]{1,0:T(8,128)S(1)} %get-tuple-element.23.refs_1_.refs_0_.refs_2_, f32[32,4096]{1,0:T(8,128)S(1)} %copy-done.7, f32[32,4096]{1,0:T(8,128)S(1)} %get-tuple-element.24.refs_3_.refs_2_.refs_4_, f32[32,4096]{1,0:T(8,128)S(1)} %copy-done.11, ...), custom_call_target="tpu_custom_call" | custom-call | bytes 8388608 | tf_op jit(solution)/shard_map/turn/pallas_call | solution.py:136
  127.5 2.7 %collective-permute-start.20 = (f32[80,768]{1,0:T(8,128)S(1)}, f32[80,768]{1,0:T(8,128)S(1)}, u32[]{:S(2)}, u32[]{:S(2)}) collective-permute-start(f32[80,768]{1,0:T(8,128)S(1)} %add.48), channel_id=1, source_target_pairs={{0,8},{4,12},{8,0},{12,4},{1,9},{5,13},{9,1},{13,5},{2,10},{6,14},... | collective-permute-start | bytes 737288 | tf_op jit(solution)/shard_map/ppermute | solution.py:229
  130.2 3.4 %copy-done.2 = f32[4096,512]{1,0:T(8,128)S(1)} copy-done((f32[4096,512]{1,0:T(8,128)S(1)}, f32[4096,512]{1,0:T(8,128)}, u32[]{:S(2)}) %copy-start.2) | copy-done | bytes 8388632
  133.6 6.6 %update.2 = (f32[4096,512]{1,0:T(8,128)S(1)}, f32[256,512]{1,0:T(8,128)S(1)}) custom-call(s32[1]{0:T(128)} %bitcast.refs_0_, f32[64,640]{1,0:T(8,128)} %add.43.refs_1_.refs_3_, f32[64,640]{1,0:T(8,128)} %collective-permute-done.6.refs_2_.refs_4_, f32[32,640]{1,0:T(8,128)} %add.45.refs_3_.refs_5_, f32[32,640]{1,0:T(8,128)} %collective-permute-done.11.refs_4_.refs_6_, ...), custom_call_target="tpu_custom_call" | custom-call | flops 3221225472 | bytes 20971520 | tf_op jit(solution)/shard_map/update/pallas_call | solution.py:206
  140.3 3.4 %copy-done.3 = f32[4096,512]{1,0:T(8,128)} copy-done((f32[4096,512]{1,0:T(8,128)}, f32[4096,512]{1,0:T(8,128)S(1)}, u32[]{:S(2)}) %copy-start.3) | copy-done | bytes 8388632
  144.4 5.1 %turn.3 = (bf16[4096,256]{1,0:T(8,128)(2,1)S(1)}, bf16[4096,256]{1,0:T(8,128)(2,1)S(1)}) custom-call(f32[40,4096]{1,0:T(8,128)S(1)} %get-tuple-element.25.refs_5_.refs_3_.refs_0_, f32[40,4096]{1,0:T(8,128)S(1)} %collective-permute-done.2.refs_6_.refs_4_.refs_1_, f32[24,4096]{1,0:T(8,128)S(1)} %get-tuple-element.26.refs_7_.refs_5_.refs_2_, ...), custom_call_target="tpu_custom_call" | custom-call | bytes 8388608 | tf_op jit(solution)/shard_map/turn/pallas_call | solution.py:136
  152.3 6.7 %all-reduce.2.cloned.1.call-done.refs_2_ = f32[128,512]{1,0:T(8,128)} async-done(((f32[128,512]{1,0:T(8,128)}), f32[128,512]{1,0:T(8,128)}) %all-reduce.2.cloned.1.call-update) | async-done | bytes 262160 | tf_op jit(solution)/shard_map/psum | solution.py:262
  159.0 3.4 %copy-done.4 = f32[4096,512]{1,0:T(8,128)S(1)} copy-done((f32[4096,512]{1,0:T(8,128)S(1)}, f32[4096,512]{1,0:T(8,128)}, u32[]{:S(2)}) %copy-start.4) | copy-done | bytes 8388632
  162.4 1.6 copy-done.13
  168.5 9.2 %update.3 = f32[4096,512]{1,0:T(8,128)} custom-call(s32[1]{0:T(128)} %bitcast.refs_0_, f32[256,512]{1,0:T(8,128)S(1)} %copy-done.21, f32[128,512]{1,0:T(8,128)S(1)} %copy-done.24, f32[64,640]{1,0:T(8,128)} %add.43.refs_1_.refs_3_, f32[64,640]{1,0:T(8,128)} %collective-permute-done.6.refs_2_.refs_4_, f32[32,640]{1,0:T(8,128)} %add.45.refs_3_.refs_5_, ...), custom_call_target="tpu_custom_call" | custom-call | flops 3221225472 | bytes 20971520 | tf_op jit(solution)/shard_map/update/pallas_call | solution.py:206
  (100 shorter events, 23.4 us)
Async XLA Ops:
  6.5 152.5 %all-reduce.2.cloned.1.call-start = ((), (), s32[]{:S(2)}) async-start(), calls=%async_computation | async-start | bytes 524288 | tf_op jit(solution)/shard_map/psum | solution.py:262
  9.3 15.9 %collective-permute-start.7 = (f32[32,4096]{1,0:T(8,128)S(1)}, f32[32,4096]{1,0:T(8,128)}, u32[]{:S(2)}, u32[]{:S(2)}) collective-permute-start(f32[32,4096]{1,0:T(8,128)S(1)} %get-tuple-element.23.refs_1_.refs_0_.refs_2_), channel_id=1, source_target_pairs={{2,0},{3,1},{0,2},{1,3},{6,4},{7,5},{4,6},{5,7},{10,8},{11,9},{8,1... | collective-permute-start | bytes 1572872 | tf_op jit(solution)/shard_map/ppermute | solution.py:226
  12.3 2.0 %collective-permute-start.3 = (f32[24,4096]{1,0:T(8,128)S(1)}, f32[24,4096]{1,0:T(8,128)S(1)}, u32[]{:S(2)}, u32[]{:S(2)}) collective-permute-start(f32[24,4096]{1,0:T(8,128)S(1)} %get-tuple-element.26.refs_7_.refs_5_.refs_2_), channel_id=1, source_target_pairs={{0,1},{1,0},{2,3},{3,2},{4,5},{5,4},{6,7},{7,6},{8,9},{9,8},{10,11... | collective-permute-start | bytes 1179656 | tf_op jit(solution)/shard_map/ppermute | solution.py:223
  12.3 37.3 %collective-permute-start.17 = (f32[40,4096]{1,0:T(8,128)S(1)}, f32[40,4096]{1,0:T(8,128)}, u32[]{:S(2)}, u32[]{:S(2)}) collective-permute-start(f32[40,4096]{1,0:T(8,128)S(1)} %get-tuple-element.25.refs_5_.refs_3_.refs_0_), channel_id=1, source_target_pairs={{2,0},{3,1},{0,2},{1,3},{6,4},{7,5},{4,6},{5,7},{10,8},{11,9},{8,1... | collective-permute-start | bytes 1966088 | tf_op jit(solution)/shard_map/ppermute | solution.py:226
  12.5 37.1 %collective-permute-start.12 = (f32[32,4096]{1,0:T(8,128)S(1)}, f32[32,4096]{1,0:T(8,128)}, u32[]{:S(2)}, u32[]{:S(2)}) collective-permute-start(f32[32,4096]{1,0:T(8,128)S(1)} %get-tuple-element.24.refs_3_.refs_2_.refs_4_), channel_id=1, source_target_pairs={{2,0},{3,1},{0,2},{1,3},{6,4},{7,5},{4,6},{5,7},{10,8},{11,9},{8,1... | collective-permute-start | bytes 1572872 | tf_op jit(solution)/shard_map/ppermute | solution.py:226
  14.3 39.1 %collective-permute-start.2 = (f32[40,4096]{1,0:T(8,128)S(1)}, f32[40,4096]{1,0:T(8,128)S(1)}, u32[]{:S(2)}, u32[]{:S(2)}) collective-permute-start(f32[40,4096]{1,0:T(8,128)S(1)} %get-tuple-element.25.refs_5_.refs_3_.refs_0_), channel_id=1, source_target_pairs={{0,1},{1,0},{2,3},{3,2},{4,5},{5,4},{6,7},{7,6},{8,9},{9,8},{10,11... | collective-permute-start | bytes 1966088 | tf_op jit(solution)/shard_map/ppermute | solution.py:223
  14.3 35.8 %collective-permute-start = (f32[32,4096]{1,0:T(8,128)S(1)}, f32[32,4096]{1,0:T(8,128)S(1)}, u32[]{:S(2)}, u32[]{:S(2)}) collective-permute-start(f32[32,4096]{1,0:T(8,128)S(1)} %get-tuple-element.23.refs_1_.refs_0_.refs_2_), channel_id=1, source_target_pairs={{0,1},{1,0},{2,3},{3,2},{4,5},{5,4},{6,7},{7,6},{8,9},{9,8},{10,11... | collective-permute-start | bytes 1572872 | tf_op jit(solution)/shard_map/ppermute | solution.py:223
  25.2 25.8 %collective-permute-start.1 = (f32[32,4096]{1,0:T(8,128)S(1)}, f32[32,4096]{1,0:T(8,128)S(1)}, u32[]{:S(2)}, u32[]{:S(2)}) collective-permute-start(f32[32,4096]{1,0:T(8,128)S(1)} %get-tuple-element.24.refs_3_.refs_2_.refs_4_), channel_id=1, source_target_pairs={{0,1},{1,0},{2,3},{3,2},{4,5},{5,4},{6,7},{7,6},{8,9},{9,8},{10,11... | collective-permute-start | bytes 1572872 | tf_op jit(solution)/shard_map/ppermute | solution.py:223
  49.6 22.9 %collective-permute-start.13 = (f32[32,4096]{1,0:T(8,128)}, f32[32,4096]{1,0:T(8,128)}, u32[]{:S(2)}, u32[]{:S(2)}) collective-permute-start(f32[32,4096]{1,0:T(8,128)} %collective-permute-done.12.refs_1_.refs_6_.refs_8_), channel_id=1, source_target_pairs={{0,1},{1,0},{2,3},{3,2},{4,5},{5,4},{6,7},{7,6},{8,9},{9,8},{10,11... | collective-permute-start | bytes 1572872 | tf_op jit(solution)/shard_map/ppermute | solution.py:223
  49.6 36.4 %collective-permute-start.18 = (f32[40,4096]{1,0:T(8,128)}, f32[40,4096]{1,0:T(8,128)}, u32[]{:S(2)}, u32[]{:S(2)}) collective-permute-start(f32[40,4096]{1,0:T(8,128)} %collective-permute-done.17.refs_0_.refs_4_), channel_id=1, source_target_pairs={{0,1},{1,0},{2,3},{3,2},{4,5},{5,4},{6,7},{7,6},{8,9},{9,8},{10,11... | collective-permute-start | bytes 1966088 | tf_op jit(solution)/shard_map/ppermute | solution.py:223
  50.9 28.9 %collective-permute-start.8 = (f32[32,4096]{1,0:T(8,128)}, f32[32,4096]{1,0:T(8,128)}, u32[]{:S(2)}, u32[]{:S(2)}) collective-permute-start(f32[32,4096]{1,0:T(8,128)} %collective-permute-done.7.refs_1_.refs_4_.refs_6_), channel_id=1, source_target_pairs={{0,1},{1,0},{2,3},{3,2},{4,5},{5,4},{6,7},{7,6},{8,9},{9,8},{10,11... | collective-permute-start | bytes 1572872 | tf_op jit(solution)/shard_map/ppermute | solution.py:223
  51.7 13.4 %collective-permute-start.21 = (f32[24,4096]{1,0:T(8,128)S(1)}, f32[24,4096]{1,0:T(8,128)S(1)}, u32[]{:S(2)}, u32[]{:S(2)}) collective-permute-start(f32[24,4096]{1,0:T(8,128)S(1)} %get-tuple-element.26.refs_7_.refs_5_.refs_2_), channel_id=1, source_target_pairs={{2,0},{3,1},{0,2},{1,3},{6,4},{7,5},{4,6},{5,7},{10,8},{11,9},{8,1... | collective-permute-start | bytes 1179656 | tf_op jit(solution)/shard_map/ppermute | solution.py:226
  58.9 13.6 %copy-start.1 = (f32[4096,512]{1,0:T(8,128)S(1)}, f32[4096,512]{1,0:T(8,128)}, u32[]{:S(2)}) copy-start(f32[4096,512]{1,0:T(8,128)} %refs_10_.5) | copy-start | bytes 25165828
  63.4 6.4 %collective-permute-start.4 = (f32[64,640]{1,0:T(8,128)S(1)}, f32[64,640]{1,0:T(8,128)S(1)}, u32[]{:S(2)}, u32[]{:S(2)}) collective-permute-start(f32[64,640]{1,0:T(8,128)S(1)} %get-tuple-element.28), channel_id=1, source_target_pairs={{0,4},{4,0},{8,12},{12,8},{1,5},{5,1},{9,13},{13,9},{2,6},{6,2},{1... | collective-permute-start | bytes 491528 | tf_op jit(solution)/shard_map/ppermute | solution.py:229
  65.1 36.3 %collective-permute-start.22 = (f32[24,4096]{1,0:T(8,128)S(1)}, f32[24,4096]{1,0:T(8,128)S(1)}, u32[]{:S(2)}, u32[]{:S(2)}) collective-permute-start(f32[24,4096]{1,0:T(8,128)S(1)} %collective-permute-done.21.refs_0_.refs_6_), channel_id=1, source_target_pairs={{0,1},{1,0},{2,3},{3,2},{4,5},{5,4},{6,7},{7,6},{8,9},{9,8},{10,11... | collective-permute-start | bytes 1179656 | tf_op jit(solution)/shard_map/ppermute | solution.py:223
  69.8 27.2 %collective-permute-start.5 = (f32[64,640]{1,0:T(8,128)S(1)}, f32[64,640]{1,0:T(8,128)S(1)}, u32[]{:S(2)}, u32[]{:S(2)}) collective-permute-start(f32[64,640]{1,0:T(8,128)S(1)} %add.42), channel_id=1, source_target_pairs={{0,8},{4,12},{8,0},{12,4},{1,9},{5,13},{9,1},{13,5},{2,10},{6,14},... | collective-permute-start | bytes 491528 | tf_op jit(solution)/shard_map/ppermute | solution.py:229
  78.2 7.9 %copy-start.10 = (f32[32,4096]{1,0:T(8,128)S(1)}, f32[32,4096]{1,0:T(8,128)}, u32[]{:S(2)}) copy-start(f32[32,4096]{1,0:T(8,128)} %copy-done.8) | copy-start | bytes 1572868
  78.2 20.1 %collective-permute-start.14 = (f32[32,640]{1,0:T(8,128)S(1)}, f32[32,640]{1,0:T(8,128)S(1)}, u32[]{:S(2)}, u32[]{:S(2)}) collective-permute-start(f32[32,640]{1,0:T(8,128)S(1)} %get-tuple-element.32), channel_id=1, source_target_pairs={{0,4},{4,0},{8,12},{12,8},{1,5},{5,1},{9,13},{13,9},{2,6},{6,2},{1... | collective-permute-start | bytes 245768 | tf_op jit(solution)/shard_map/ppermute | solution.py:229
  85.5 9.5 %copy-start.27 = (f32[2,256,256]{2,1,0:T(8,128)S(1)}, f32[2,256,256]{2,1,0:T(8,128)}, u32[]{:S(2)}) copy-start(f32[2,256,256]{2,1,0:T(8,128)} %in_ref.3) | copy-start | bytes 1572868
  85.5 13.1 %collective-permute-start.9 = (f32[32,640]{1,0:T(8,128)S(1)}, f32[32,640]{1,0:T(8,128)S(1)}, u32[]{:S(2)}, u32[]{:S(2)}) collective-permute-start(f32[32,640]{1,0:T(8,128)S(1)} %get-tuple-element.30), channel_id=1, source_target_pairs={{0,4},{4,0},{8,12},{12,8},{1,5},{5,1},{9,13},{13,9},{2,6},{6,2},{1... | collective-permute-start | bytes 245768 | tf_op jit(solution)/shard_map/ppermute | solution.py:229
  93.5 33.0 %collective-permute-start.19 = (f32[80,768]{1,0:T(8,128)}, f32[80,768]{1,0:T(8,128)}, u32[]{:S(2)}, u32[]{:S(2)}) collective-permute-start(f32[80,768]{1,0:T(8,128)} %project.10), channel_id=1, source_target_pairs={{0,4},{4,0},{8,12},{12,8},{1,5},{5,1},{9,13},{13,9},{2,6},{6,2},{1... | collective-permute-start | bytes 737288 | tf_op jit(solution)/shard_map/ppermute | solution.py:229
  97.8 32.4 %collective-permute-start.6 = (f32[64,640]{1,0:T(8,128)}, f32[64,640]{1,0:T(8,128)}, u32[]{:S(2)}, u32[]{:S(2)}) collective-permute-start(f32[64,640]{1,0:T(8,128)} %add.43.refs_1_.refs_3_), channel_id=1, source_target_pairs={{0,4},{4,0},{8,12},{12,8},{1,5},{5,1},{9,13},{13,9},{2,6},{6,2},{1... | collective-permute-start | bytes 491528 | tf_op jit(solution)/shard_map/ppermute | solution.py:229
  98.3 12.0 %collective-permute-start.15 = (f32[32,640]{1,0:T(8,128)S(1)}, f32[32,640]{1,0:T(8,128)S(1)}, u32[]{:S(2)}, u32[]{:S(2)}) collective-permute-start(f32[32,640]{1,0:T(8,128)S(1)} %add.46), channel_id=1, source_target_pairs={{0,8},{4,12},{8,0},{12,4},{1,9},{5,13},{9,1},{13,5},{2,10},{6,14},... | collective-permute-start | bytes 245768 | tf_op jit(solution)/shard_map/ppermute | solution.py:229
  98.7 12.6 %collective-permute-start.10 = (f32[32,640]{1,0:T(8,128)S(1)}, f32[32,640]{1,0:T(8,128)S(1)}, u32[]{:S(2)}, u32[]{:S(2)}) collective-permute-start(f32[32,640]{1,0:T(8,128)S(1)} %add.44), channel_id=1, source_target_pairs={{0,8},{4,12},{8,0},{12,4},{1,9},{5,13},{9,1},{13,5},{2,10},{6,14},... | collective-permute-start | bytes 245768 | tf_op jit(solution)/shard_map/ppermute | solution.py:229
  101.4 7.3 %copy-start.17 = (f32[24,4096]{1,0:T(8,128)}, f32[24,4096]{1,0:T(8,128)S(1)}, u32[]{:S(2)}) copy-start(f32[24,4096]{1,0:T(8,128)S(1)} %collective-permute-done.22.refs_1_.refs_7_) | copy-start | bytes 1179652
  108.6 16.4 %collective-permute-start.23 = (f32[48,768]{1,0:T(8,128)}, f32[48,768]{1,0:T(8,128)}, u32[]{:S(2)}, u32[]{:S(2)}) collective-permute-start(f32[48,768]{1,0:T(8,128)} %project.11), channel_id=1, source_target_pairs={{0,4},{4,0},{8,12},{12,8},{1,5},{5,1},{9,13},{13,9},{2,6},{6,2},{1... | collective-permute-start | bytes 442376 | tf_op jit(solution)/shard_map/ppermute | solution.py:229
  110.9 19.3 %collective-permute-start.16 = (f32[32,640]{1,0:T(8,128)}, f32[32,640]{1,0:T(8,128)}, u32[]{:S(2)}, u32[]{:S(2)}) collective-permute-start(f32[32,640]{1,0:T(8,128)} %add.47.refs_5_.refs_7_), channel_id=1, source_target_pairs={{0,4},{4,0},{8,12},{12,8},{1,5},{5,1},{9,13},{13,9},{2,6},{6,2},{1... | collective-permute-start | bytes 245768 | tf_op jit(solution)/shard_map/ppermute | solution.py:229
  111.9 18.3 %collective-permute-start.11 = (f32[32,640]{1,0:T(8,128)}, f32[32,640]{1,0:T(8,128)}, u32[]{:S(2)}, u32[]{:S(2)}) collective-permute-start(f32[32,640]{1,0:T(8,128)} %add.45.refs_3_.refs_5_), channel_id=1, source_target_pairs={{0,4},{4,0},{8,12},{12,8},{1,5},{5,1},{9,13},{13,9},{2,6},{6,2},{1... | collective-permute-start | bytes 245768 | tf_op jit(solution)/shard_map/ppermute | solution.py:229
  119.9 10.4 %copy-start.26 = (f32[256,256]{1,0:T(8,128)S(1)}, f32[256,256]{1,0:T(8,128)}, u32[]{:S(2)}) copy-start(f32[256,256]{1,0:T(8,128)} %copy-done.25) | copy-start | bytes 786436
  126.0 26.2 %collective-permute-start.24 = (f32[48,768]{1,0:T(8,128)S(1)}, f32[48,768]{1,0:T(8,128)S(1)}, u32[]{:S(2)}, u32[]{:S(2)}) collective-permute-start(f32[48,768]{1,0:T(8,128)S(1)} %add.50), channel_id=1, source_target_pairs={{0,8},{4,12},{8,0},{12,4},{1,9},{5,13},{9,1},{13,5},{2,10},{6,14},... | collective-permute-start | bytes 442376 | tf_op jit(solution)/shard_map/ppermute | solution.py:229
  127.5 24.7 %collective-permute-start.20 = (f32[80,768]{1,0:T(8,128)S(1)}, f32[80,768]{1,0:T(8,128)S(1)}, u32[]{:S(2)}, u32[]{:S(2)}) collective-permute-start(f32[80,768]{1,0:T(8,128)S(1)} %add.48), channel_id=1, source_target_pairs={{0,8},{4,12},{8,0},{12,4},{1,9},{5,13},{9,1},{13,5},{2,10},{6,14},... | collective-permute-start | bytes 737288 | tf_op jit(solution)/shard_map/ppermute | solution.py:229
  133.6 10.8 %copy-start.18 = (f32[24,4096]{1,0:T(8,128)S(1)}, f32[24,4096]{1,0:T(8,128)}, u32[]{:S(2)}) copy-start(f32[24,4096]{1,0:T(8,128)} %copy-done.17) | copy-start | bytes 1179652
  (22 other events, 37.3 us)
Sparse Core Ops, SparseCore 0:
  117.9 41.0 all-reduce.1

commit v2 on v1

--- a/solution.py
+++ b/solution.py
@@ -28,12 +28,17 @@
     return pl.CostEstimate(flops=flops, bytes_accessed=moved, transcendentals=0)
 
 
+ROOM = 56
 SCALARS = pl.BlockSpec(memory_space=pltpu.SMEM)
 
 
 def split(value):
     high = value.astype(BF16)
     return high, (value - high.astype(F32)).astype(BF16)
+
+
+def strips(pieces, step):
+    return [pl.BlockSpec((count, step), lambda i, at=at: (at, i)) for _, count, at in pieces]
 
 
 def full_dot(a, b, dims=NN):
@@ -48,34 +53,40 @@
     return first[:rows] + first[rows:] + second
 
 
-def cut(where, vectors, pieces):
+def cut(where, vectors, after, rows, name):
     _, share, here = vectors.shape
     step = min(here, 1024)
-
-    def body(where_ref, in_ref, *outs):
-        for (block, low, high), out in zip(pieces, outs):
+    height = sum(high - low for _, low, high in rows)
+
+    def body(where_ref, in_ref, *refs):
+        at = 0
+        for block, low, high in rows:
             shape = (high - low, step)
             along = lax.broadcasted_iota(jnp.int32, shape, 0) + (where_ref[0] + low)
             across = lax.broadcasted_iota(jnp.int32, shape, 1) + (where_ref[1] + pl.program_id(0) * step)
-            out[...] = jnp.where(across >= along + block * where_ref[2], in_ref[block, low:high], 0.0)
+            refs[-1][at : at + high - low] = jnp.where(
+                across >= along + block * where_ref[2], in_ref[block, low:high], 0.0
+            )
+            at += high - low
 
     return pl.pallas_call(
         body,
         grid=(here // step,),
-        in_specs=[SCALARS, pl.BlockSpec((2, share, step), lambda i: (0, 0, i))],
-        out_specs=[pl.BlockSpec((b - a, step), lambda i: (0, i)) for _, a, b in pieces],
-        out_shape=[jax.ShapeDtypeStruct((b - a, here), F32) for _, a, b in pieces],
-        compiler_params=params(16),
+        in_specs=[SCALARS, pl.BlockSpec((2, share, step), lambda i: (0, 0, i))]
+        + [pl.BlockSpec(memory_space=pl.ANY)] * len(after),
+        out_specs=pl.BlockSpec((height, step), lambda i: (0, i)),
+        out_shape=jax.ShapeDtypeStruct((height, here), F32),
+        compiler_params=params(8),
         cost_estimate=cost(0, 4 * vectors.size * 2),
-        name="cut",
-    )(where, vectors)
-
-
-def project(rows, partners, eigvecs, bit=None):
+        name=name,
+    )(where, vectors, *after)
+
+
+def project(name, rows, partners, eigvecs, bit=None):
     here, nc = eigvecs.shape
     step = min(here, 512)
-    height = sum(r.shape[0] for r in rows)
-    extra = sum(r.shape[0] for r in partners)
+    height = sum(count for _, count, _ in rows)
+    extra = sum(count for _, count, _ in partners)
     steps = here // step
 
     def body(*refs):
@@ -105,27 +116,27 @@
                 outs[0][...] = jnp.where(zero, acc[:half], acc[half:])
                 outs[1][...] = jnp.where(zero, acc[half:], acc[:half])
 
-    count = 1 if bit is None else 2
-    shape = (height // count, nc + extra)
+    outputs = 1 if bit is None else 2
+    shape = (height // outputs, nc + extra)
     return pl.pallas_call(
         body,
         grid=(steps,),
         in_specs=([] if bit is None else [SCALARS])
-        + [pl.BlockSpec((r.shape[0], step), lambda i: (0, i)) for r in rows + partners]
+        + strips(rows + partners, step)
         + [pl.BlockSpec((step, nc), lambda i: (i, 0))],
-        out_specs=[whole(shape)] * count,
-        out_shape=[jax.ShapeDtypeStruct(shape, F32)] * count,
+        out_specs=[whole(shape)] * outputs,
+        out_shape=[jax.ShapeDtypeStruct(shape, F32)] * outputs,
         scratch_shapes=[pltpu.VMEM((height, nc + extra), F32)],
-        compiler_params=params(32),
+        compiler_params=params(ROOM),
         cost_estimate=cost(6 * height * here * (nc + extra), 4 * (eigvecs.size + height * here)),
-        name="project",
-    )(*([] if bit is None else [bit]), *rows, *partners, eigvecs)
-
-
-def turn(pieces):
-    here = pieces[0].shape[1]
+        name=name,
+    )(*([] if bit is None else [bit]), *[r[0] for r in rows + partners], eigvecs)
+
+
+def turn(name, pieces):
+    here = pieces[0][0].shape[1]
     step = min(here, 512)
-    height = sum(r.shape[0] for r in pieces)
+    height = sum(count for _, count, _ in pieces)
 
     def body(*refs):
         turned = jnp.concatenate([r[...] for r in refs[:-2]]).T
@@ -136,13 +147,13 @@
     return pl.pallas_call(
         body,
         grid=(here // step,),
-        in_specs=[pl.BlockSpec((r.shape[0], step), lambda i: (0, i)) for r in pieces],
+        in_specs=strips(pieces, step),
         out_specs=[pl.BlockSpec((step, height), lambda i: (i, 0))] * 2,
         out_shape=[jax.ShapeDtypeStruct((here, height), BF16)] * 2,
-        compiler_params=params(16),
+        compiler_params=params(ROOM),
         cost_estimate=cost(0, 8 * height * here),
-        name="turn",
-    )(*pieces)
+        name=name,
+    )(*[r[0] for r in pieces])
 
 
 def reorder(where, factors, share, chips, segments):
@@ -166,13 +177,13 @@
         in_specs=[SCALARS, whole(factors.shape)],
         out_specs=[whole((width, width))] * 2,
         out_shape=[jax.ShapeDtypeStruct((width, width), F32)] * 2,
-        compiler_params=params(16),
+        compiler_params=params(ROOM),
         cost_estimate=cost(48 * width**3, 8 * factors.size),
         name="reorder",
     )(where, factors)
 
 
-def update(make, ins, factor, turned, current, with_scaled):
+def update(name, make, ins, factor, turned, current, with_scaled):
     here, nc = current.shape
     width = factor.shape[0]
     step = min(here, 512)
@@ -210,9 +221,9 @@
         out_specs=out_specs,
         out_shape=out_shape,
         scratch_shapes=[pltpu.VMEM((width, nc), BF16)] * 2,
-        compiler_params=params(32),
+        compiler_params=params(ROOM),
         cost_estimate=cost(6 * here * width * nc, 4 * here * (2 * nc + width)),
-        name="update",
+        name=name,
     )(*ins, factor, *turned, current)
 
 
@@ -228,15 +239,21 @@
     def row_swap(value, step):
         return lax.ppermute(value, "row", [(i, i ^ step) for i in range(rows)])
 
-    def row_sum(value, step=1):
+    def sums(value, send=None):
+        step = 1
+        if send is not None:
+            got = row_swap(send, 1)
+            yield got
+            value, step = value + got, 2
         while step < rows:
-            value = value + row_swap(value, step)
-            step *= 2
+            got = row_swap(value, step)
+            yield got
+            value, step = value + got, 2 * step
+        if send is not None:
+            other = row_swap(value, 1)
+            yield other
+            value = (value, other)
         return value
-
-    def halves_sum(keep, send):
-        mine = row_sum(keep + row_swap(send, 1), 2)
-        return mine, row_swap(mine, 1)
 
     def local(vectors, factors, eigvecs):
         share, here = vectors.shape[1:]
@@ -251,51 +268,77 @@
             low, high = low * share // 64 // 8 * 8, high * share // 64 // 8 * 8
             pieces.append((block, low, high))
 
-        mine = cut(where, vectors, pieces)
-        far = [(step, p, from_chip(m, step)) for p, m in zip(pieces, mine) for step in range(1, chips)]
-        own, segments = {0: [], 1: []}, {0: [], 1: []}
-        for (block, low, high), m in zip(pieces, mine):
-            own[block] += [m, core_swap(m)]
-            segments[block] += [(0, 0, low, high), (0, 1, low, high)]
+        def after(value, *others):
+            return lax.optimization_barrier((value, *others))[0]
+
+        far, last = [], ()
+        for n, (block, low, high) in enumerate(pieces):
+            sent = cut(where, vectors, last, [(block, low, high)], f"cut_{n}")
+            far += [(step, (block, low, high), from_chip(sent, step)) for step in range(1, chips)]
+            last = (sent,)
+        mine = cut(where, vectors, last, [(1, 0, share), (0, 0, share)], "cut_own")
+        sib = core_swap(mine)
+        own = {1: [(mine, share, 0), (sib, share, 0)], 0: [(mine, share, 1), (sib, share, 1)]}
+        segments = {k: [(0, 0, 0, share), (0, 1, 0, share)] for k in (0, 1)}
         all_ones, all_zeros = list(own[1]), list(own[0])
-        ones = [halves_sum(*project(own[1], own[0], eigvecs, bit))]
-        own_zero = lax.psum(project(own[0], [], eigvecs)[0], "row")
-        zeros = []
-        for step, (block, low, high), value in far:
-            pair = [value, core_swap(value)]
+        running, done, waits = [], {}, ()
+
+        def advance():
+            got = []
+            for key, chain in list(running):
+                try:
+                    got.append(next(chain))
+                except StopIteration as end:
+                    done[key] = end.value
+                    running.remove((key, chain))
+            return got
+
+        first = project("project_own", own[1] + own[0], own[0], eigvecs, bit)
+        running.append(("own", sums(*first)))
+        front = first
+        for n, (step, (block, low, high), value) in enumerate(far):
+            value = after(value, *front, *waits)
+            waits = advance()
+            pair = [(v, high - low, 0) for v in (value, core_swap(value))]
             segments[block] += [(step, 0, low, high), (step, 1, low, high)]
             if block == 1:
                 all_ones += pair
-                ones.append(halves_sum(*project(pair, own[0], eigvecs, bit)))
+                front = project(f"project_one_{n}", pair, own[0], eigvecs, bit)
             else:
                 all_zeros += pair
-                zeros.append(row_sum(project(pair, all_ones, eigvecs)[0]))
+                front = project(f"project_zero_{n}", pair, all_ones, eigvecs)
+            running.append((n, sums(*front)))
+        while running:
+            advance()
+        ones = [done["own"]] + [done[n] for n, f in enumerate(far) if f[1][0] == 1]
+        zeros = [done[n] for n, f in enumerate(far) if f[1][0] == 0]
         t0, t1 = reorder(where, factors, share, chips, segments)
+
+        flat = [v for pair in ones for v in pair]
 
         def joined(bit_ref, refs, columns):
             parts = []
             zero = bit_ref[0] == 0
             for a, b in zip(refs[::2], refs[1::2]):
                 a, b = a[:, columns], b[:, columns]
-                parts += [jnp.where(zero, a, b), jnp.where(zero, b, a)]
-            return jnp.concatenate(parts)
-
-        flat = [v for pair in ones for v in pair]
+                parts.append((jnp.where(zero, a, b), jnp.where(zero, b, a)))
+            ones = [parts[0][0]] + [p for pair in parts[1:] for p in pair]
+            return jnp.concatenate(ones), parts[0][1]
 
         def make_one(bit_ref, *refs):
-            return joined(bit_ref, refs, slice(0, nc))
-
-        def make_zero(bit_ref, scaled_ref, own_ref, *refs):
+            return joined(bit_ref, refs, slice(0, nc))[0]
+
+        def make_zero(bit_ref, scaled_ref, *refs):
             ones_refs, zero_refs = refs[: len(flat)], refs[len(flat) :]
             scaled = scaled_ref[...]
-            turned_gram = joined(bit_ref, ones_refs, slice(nc, nc + half))
-            parts = [own_ref[...] - full_dot(turned_gram, scaled, TN)]
+            turned_gram = joined(bit_ref, ones_refs, slice(nc, nc + half))[0]
+            parts = [joined(bit_ref, ones_refs[:2], slice(0, nc))[1] - full_dot(turned_gram, scaled, TN)]
             later = jnp.concatenate([r[...] for r in zero_refs])
             parts.append(later[:, :nc] - full_dot(later[:, nc:], scaled))
             return jnp.concatenate(parts)
 
-        current, scaled = update(make_one, [bit, *flat], t1, turn(all_ones), eigvecs, True)
-        (out,) = update(make_zero, [bit, scaled, own_zero, *flat, *zeros], t0, turn(all_zeros), current, False)
+        current, scaled = update("update_one", make_one, [bit, *flat], t1, turn("turn_one", all_ones), eigvecs, True)
+        (out,) = update("update_zero", make_zero, [bit, scaled, *flat, *zeros], t0, turn("turn_zero", all_zeros), current, False)
         return out
 
     return local

time: 187 us -> 141 us (0.75)
  waiting for transfers between devices: 46.3 us -> 7.22 us
  Pallas kernels: 63.1 us -> 97.2 us
  local copies, waits for them, and re-layouts: 31.3 us -> 5.64 us
  between operations: 13.7 us -> 0.3 us
  other arithmetic: 4.22 us -> 1.55 us
    ppermute x4, waiting for transfers between devices: 34.8 us -> 1.42 us  [from_chip(): lax.ppermute(value, 'col', [((i + 2 * step) % cols, i) for i in range(col...]
    unnamed x56 -> x46, local copies, waits for them, and re-layouts: 31.2 us -> 5.55 us
    pallas_call x6 -> x5, Pallas kernels: 34 us -> 47.3 us  [project(): pl.pallas_call(body, grid=(steps,), in_specs=([] if bit is None else [SCA...]
    pallas_call x2, Pallas kernels: 15.8 us -> 26.6 us  [update(): pl.pallas_call(body, grid=(here // step,), in_specs=[spec(v) for v in ins...]
    psum x1 -> x0, waiting for transfers between devices: 6.68 us -> none  [local(): own_zero = lax.psum(project(own[0], [], eigvecs)[0], 'row')]
    pallas_call x1 -> x5, Pallas kernels: 1.07 us -> 5.68 us  [cut(): pl.pallas_call(body, grid=(here // step,), in_specs=[SCALARS, pl.BlockSpe...]
    pallas_call x2, Pallas kernels: 10.2 us -> 14.5 us  [turn(): pl.pallas_call(body, grid=(here // step,), in_specs=strips(pieces, step),...]
    add x10, other arithmetic: 4.22 us -> 1.55 us  [the longest x7 1.5 us: sums(): value, step = (value + got, 2 * step)]
  transfers between devices with their start and end apart: 26 -> 22, of which waited for: 4 -> 4; matrix products, arithmetic and copies ran while one was open for 2% -> 1% of each run, Pallas kernels for 29% -> 56%
where the time goes in v2:
time: 141 us; the launch traced here: 140 us
  Pallas kernels  97.2 us (69%)
  starting transfers between devices  27.7 us (20%)
  waiting for transfers between devices  7.22 us (5%)
  local copies, waits for them, and re-layouts  5.64 us (4%)
  other arithmetic  1.55 us (1%)
    pallas_call x5, Pallas kernels, project(): pl.pallas_call(body, grid=(steps,), in_specs=([] if bit is None else [SCA...  47.3 us
    pallas_call x2, Pallas kernels, update(): pl.pallas_call(body, grid=(here // step,), in_specs=[spec(v) for v in ins...  26.6 us
    ppermute x13, starting transfers between devices, row_swap(): return lax.ppermute(value, 'row', [(i, i ^ step) for i in range(rows)])  19.6 us
    pallas_call x2, Pallas kernels, turn(): pl.pallas_call(body, grid=(here // step,), in_specs=strips(pieces, step),...  14.5 us
    ppermute x4, starting transfers between devices, from_chip(): lax.ppermute(value, 'col', [((i + 2 * step) % cols, i) for i in range(col...  7.21 us
    pallas_call x5, Pallas kernels, cut(): pl.pallas_call(body, grid=(here // step,), in_specs=[SCALARS, pl.BlockSpe...  5.68 us
    unnamed x46, local copies, waits for them, and re-layouts  5.55 us
    ppermute x13, waiting for transfers between devices, row_swap(): return lax.ppermute(value, 'row', [(i, i ^ step) for i in range(rows)])  4.44 us
  transfers between devices with their start and end apart: 22, of which 4 were waited for; matrix products, arithmetic and copies ran while one was open for 1% of the time, Pallas kernels for 56%

profile of v2, /device:TPU:0, one launch (start us, length us, event | category | flops | bytes accessed | tf_op | source)
XLA Modules:
  0.0 139.6 jit_solution(13591114801803080961)
XLA Ops:
  0.1 1.6 %copy-done.1 = f32[2,64,4096]{2,1,0:T(8,128)S(1)} copy-done((f32[2,64,4096]{2,1,0:T(8,128)S(1)}, f32[2,64,4096]{2,1,0:T(8,128)}, u32[]{:S(2)}) %copy-start.1) | copy-done | bytes 2097176
  1.7 2.0 %cut_0.1.refs_0_ = f32[32,4096]{1,0:T(8,128)} custom-call(s32[5]{0:T(128)S(1)} %stack.19.where_ref, f32[2,64,4096]{2,1,0:T(8,128)S(1)} %copy-done.1), custom_call_target="tpu_custom_call" | custom-call | bytes 4194304 | tf_op jit(solution)/shard_map/cut_0/pallas_call | solution.py:72
  3.7 0.9 cut_1.1.refs_0_
  4.6 0.9 cut_2.1.refs_0_
  6.3 1.1 cut_own.1.refs_1_.refs_3_.refs_5_.refs_0_.refs_2_
  8.0 2.6 %collective-permute-start.4 = (f32[32,4096]{1,0:T(8,128)}, f32[32,4096]{1,0:T(8,128)}, u32[]{:S(2)}, u32[]{:S(2)}) collective-permute-start(f32[32,4096]{1,0:T(8,128)} %cut_0.1.refs_0_), channel_id=1, source_target_pairs={{2,0},{3,1},{0,2},{1,3},{6,4},{7,5},{4,6},{5,7},{10,8},{11,9},{8,1... | collective-permute-start | bytes 1572872 | tf_op jit(solution)/shard_map/ppermute | solution.py:237
  10.5 1.4 collective-permute-done.refs_2_.refs_4_.refs_6_.refs_1_.refs_3_
  11.9 11.3 %project_own.1 = (f32[128,640]{1,0:T(8,128)}, f32[128,640]{1,0:T(8,128)}) custom-call(s32[1]{0:T(128)} %bitcast.refs_0_, f32[128,4096]{1,0:T(8,128)} %copy-done, f32[128,4096]{1,0:T(8,128)} %collective-permute-done.refs_2_.refs_4_.refs_6_.refs_1_.refs_3_, f32[128,4096]{1,0:T(8,128)} %copy-done, ...), custom_call_target="tpu_custom_call" | custom-call | flops 4026531840 | bytes 12582912 | tf_op jit(solution)/shard_map/project_own/pallas_call | solution.py:121
  23.7 2.6 %collective-permute-start.9 = (f32[32,4096]{1,0:T(8,128)S(1)}, f32[32,4096]{1,0:T(8,128)S(1)}, u32[]{:S(2)}, u32[]{:S(2)}) collective-permute-start(f32[32,4096]{1,0:T(8,128)S(1)} %cut_1.1.refs_0_), channel_id=1, source_target_pairs={{2,0},{3,1},{0,2},{1,3},{6,4},{7,5},{4,6},{5,7},{10,8},{11,9},{8,1... | collective-permute-start | bytes 1572872 | tf_op jit(solution)/shard_map/ppermute | solution.py:237
  26.3 1.6 %collective-permute-start.1 = (f32[128,640]{1,0:T(8,128)}, f32[128,640]{1,0:T(8,128)S(1)}, u32[]{:S(2)}, u32[]{:S(2)}) collective-permute-start(f32[128,640]{1,0:T(8,128)} %get-tuple-element.24), channel_id=1, source_target_pairs={{0,4},{4,0},{8,12},{12,8},{1,5},{5,1},{9,13},{13,9},{2,6},{6,2},{1... | collective-permute-start | bytes 983048 | tf_op jit(solution)/shard_map/ppermute | solution.py:240
  29.2 8.6 %project_one_0.1 = (f32[32,640]{1,0:T(8,128)}, f32[32,640]{1,0:T(8,128)}) custom-call(s32[1]{0:T(128)} %bitcast.refs_0_, f32[32,4096]{1,0:T(8,128)} %collective-permute-done.4.refs_1_.refs_2_.refs_4_, f32[32,4096]{1,0:T(8,128)} %copy-done.5, f32[128,4096]{1,0:T(8,128)} %copy-done, f32[128,4096]{1,0:T(8,128)} %collective-permute-done.refs_2_.refs_4_.refs_6_.refs_1_.refs_3_, ...), custom_call_target="tpu_custom_call" | custom-call | flops 1006632960 | bytes 9437184 | tf_op jit(solution)/shard_map/project_one_0/pallas_call | solution.py:121
  37.8 1.3 collective-permute-done.9.refs_1_.refs_4_.refs_6_
  39.1 3.2 %collective-permute-start.2 = (f32[128,640]{1,0:T(8,128)S(1)}, f32[128,640]{1,0:T(8,128)S(1)}, u32[]{:S(2)}, u32[]{:S(2)}) collective-permute-start(f32[128,640]{1,0:T(8,128)S(1)} %add.40), channel_id=1, source_target_pairs={{0,8},{4,12},{8,0},{12,4},{1,9},{5,13},{9,1},{13,5},{2,10},{6,14},... | collective-permute-start | bytes 983048 | tf_op jit(solution)/shard_map/ppermute | solution.py:240
  42.3 1.6 %collective-permute-start.6 = (f32[32,640]{1,0:T(8,128)}, f32[32,640]{1,0:T(8,128)S(1)}, u32[]{:S(2)}, u32[]{:S(2)}) collective-permute-start(f32[32,640]{1,0:T(8,128)} %get-tuple-element.27), channel_id=1, source_target_pairs={{0,4},{4,0},{8,12},{12,8},{1,5},{5,1},{9,13},{13,9},{2,6},{6,2},{1... | collective-permute-start | bytes 245768 | tf_op jit(solution)/shard_map/ppermute | solution.py:240
  44.7 8.6 %project_one_1.1 = (f32[32,640]{1,0:T(8,128)}, f32[32,640]{1,0:T(8,128)}) custom-call(s32[1]{0:T(128)} %bitcast.refs_0_, f32[32,4096]{1,0:T(8,128)} %copy-done.6, f32[32,4096]{1,0:T(8,128)} %copy-done.7, f32[128,4096]{1,0:T(8,128)} %copy-done, f32[128,4096]{1,0:T(8,128)} %collective-permute-done.refs_2_.refs_4_.refs_6_.refs_1_.refs_3_, f32[4096,512]{1,0:T(8,128)} %refs_8_.3), custom_call_target="tpu_custom_call" | custom-call | flops 1006632960 | bytes 9437184 | tf_op jit(solution)/shard_map/project_one_1/pallas_call | solution.py:121
  53.3 4.4 %collective-permute-done.2 = f32[128,640]{1,0:T(8,128)S(1)} collective-permute-done((f32[128,640]{1,0:T(8,128)S(1)}, f32[128,640]{1,0:T(8,128)S(1)}, u32[]{:S(2)}, u32[]{:S(2)}) %collective-permute-start.2) | collective-permute-done | bytes 327712 | tf_op jit(solution)/shard_map/ppermute | solution.py:240
  57.7 1.5 %collective-permute-start.18 = (f32[24,4096]{1,0:T(8,128)S(1)}, f32[24,4096]{1,0:T(8,128)S(1)}, u32[]{:S(2)}, u32[]{:S(2)}) collective-permute-start(f32[24,4096]{1,0:T(8,128)S(1)} %copy-done.3), channel_id=1, source_target_pairs={{2,0},{3,1},{0,2},{1,3},{6,4},{7,5},{4,6},{5,7},{10,8},{11,9},{8,1... | collective-permute-start | bytes 1179656 | tf_op jit(solution)/shard_map/ppermute | solution.py:237
  60.1 3.4 %collective-permute-start.7 = (f32[32,640]{1,0:T(8,128)S(1)}, f32[32,640]{1,0:T(8,128)S(1)}, u32[]{:S(2)}, u32[]{:S(2)}) collective-permute-start(f32[32,640]{1,0:T(8,128)S(1)} %add.42), channel_id=1, source_target_pairs={{0,8},{4,12},{8,0},{12,4},{1,9},{5,13},{9,1},{13,5},{2,10},{6,14},... | collective-permute-start | bytes 245768 | tf_op jit(solution)/shard_map/ppermute | solution.py:240
  63.6 0.9 copy-done.10
  64.4 9.5 %project_zero_2.1 = f32[80,768]{1,0:T(8,128)} custom-call(f32[40,4096]{1,0:T(8,128)} %copy-done.9, f32[40,4096]{1,0:T(8,128)} %copy-done.10, f32[128,4096]{1,0:T(8,128)} %copy-done, f32[128,4096]{1,0:T(8,128)} %collective-permute-done.refs_2_.refs_4_.refs_6_.refs_1_.refs_3_, f32[32,4096]{1,0:T(8,128)} %collective-permute-done.4.refs_1_.refs_2_.refs_4_, ...), custom_call_target="tpu_custom_call" | custom-call | flops 1509949440 | bytes 9699328 | tf_op jit(solution)/shard_map/project_zero_2/pallas_call | solution.py:121
  74.1 2.1 %collective-permute-start.16 = (f32[80,768]{1,0:T(8,128)}, f32[80,768]{1,0:T(8,128)S(1)}, u32[]{:S(2)}, u32[]{:S(2)}) collective-permute-start(f32[80,768]{1,0:T(8,128)} %project_zero_2.1), channel_id=1, source_target_pairs={{0,4},{4,0},{8,12},{12,8},{1,5},{5,1},{9,13},{13,9},{2,6},{6,2},{1... | collective-permute-start | bytes 737288 | tf_op jit(solution)/shard_map/ppermute | solution.py:240
  77.6 9.3 %project_zero_3.1 = f32[48,768]{1,0:T(8,128)} custom-call(f32[24,4096]{1,0:T(8,128)} %copy-done.11, f32[24,4096]{1,0:T(8,128)} %copy-done.12, f32[128,4096]{1,0:T(8,128)} %copy-done, f32[128,4096]{1,0:T(8,128)} %collective-permute-done.refs_2_.refs_4_.refs_6_.refs_1_.refs_3_, f32[32,4096]{1,0:T(8,128)} %collective-permute-done.4.refs_1_.refs_2_.refs_4_, ...), custom_call_target="tpu_custom_call" | custom-call | flops 905969664 | bytes 9175040 | tf_op jit(solution)/shard_map/project_zero_3/pallas_call | solution.py:121
  86.9 1.0 collective-permute-start.20
  87.9 1.1 collective-permute-start.8
  89.1 1.1 collective-permute-start.13
  90.1 3.2 %reorder.1 = (f32[256,256]{1,0:T(8,128)}, f32[256,256]{1,0:T(8,128)}) custom-call(s32[5]{0:T(128)} %copy-done.4, f32[2,256,256]{2,1,0:T(8,128)} %in_ref.11), custom_call_target="tpu_custom_call" | custom-call | flops 805306368 | bytes 1048576 | tf_op jit(solution)/shard_map/reorder/pallas_call | solution.py:174
  93.3 7.2 %turn_one.1 = (bf16[4096,256]{1,0:T(8,128)(2,1)}, bf16[4096,256]{1,0:T(8,128)(2,1)}) custom-call(f32[128,4096]{1,0:T(8,128)} %copy-done, f32[128,4096]{1,0:T(8,128)} %collective-permute-done.refs_2_.refs_4_.refs_6_.refs_1_.refs_3_, f32[32,4096]{1,0:T(8,128)} %collective-permute-done.4.refs_1_.refs_2_.refs_4_, f32[32,4096]{1,0:T(8,128)} %copy-done.5, ...), custom_call_target="tpu_custom_call" | custom-call | bytes 8388608 | tf_op jit(solution)/shard_map/turn_one/pallas_call | solution.py:147
  100.6 1.5 %collective-permute-start.17 = (f32[80,768]{1,0:T(8,128)S(1)}, f32[80,768]{1,0:T(8,128)S(1)}, u32[]{:S(2)}, u32[]{:S(2)}) collective-permute-start(f32[80,768]{1,0:T(8,128)S(1)} %add.46), channel_id=1, source_target_pairs={{0,8},{4,12},{8,0},{12,4},{1,9},{5,13},{9,1},{13,5},{2,10},{6,14},... | collective-permute-start | bytes 737288 | tf_op jit(solution)/shard_map/ppermute | solution.py:240
  102.1 1.6 %collective-permute-start.21 = (f32[48,768]{1,0:T(8,128)S(1)}, f32[48,768]{1,0:T(8,128)S(1)}, u32[]{:S(2)}, u32[]{:S(2)}) collective-permute-start(f32[48,768]{1,0:T(8,128)S(1)} %add.48), channel_id=1, source_target_pairs={{0,8},{4,12},{8,0},{12,4},{1,9},{5,13},{9,1},{13,5},{2,10},{6,14},... | collective-permute-start | bytes 442376 | tf_op jit(solution)/shard_map/ppermute | solution.py:240
  104.4 12.9 %update_one.1 = (f32[4096,512]{1,0:T(8,128)}, f32[256,512]{1,0:T(8,128)}) custom-call(s32[1]{0:T(128)} %bitcast.refs_0_, f32[128,640]{1,0:T(8,128)} %copy-done.8, f32[128,640]{1,0:T(8,128)} %copy-done.13, f32[32,640]{1,0:T(8,128)} %copy-done.15, f32[32,640]{1,0:T(8,128)} %copy-done.18, f32[32,640]{1,0:T(8,128)} %copy-done.16, f32[32,640]{1,0:T(8,128)} %copy-done.19, ...), custom_call_target="tpu_custom_call" | custom-call | flops 3221225472 | bytes 20971520 | tf_op jit(solution)/shard_map/update_one/pallas_call | solution.py:217
  117.3 7.2 %turn_zero.1 = (bf16[4096,256]{1,0:T(8,128)(2,1)}, bf16[4096,256]{1,0:T(8,128)(2,1)}) custom-call(f32[128,4096]{1,0:T(8,128)} %copy-done, f32[128,4096]{1,0:T(8,128)} %collective-permute-done.refs_2_.refs_4_.refs_6_.refs_1_.refs_3_, f32[40,4096]{1,0:T(8,128)} %copy-done.9, f32[40,4096]{1,0:T(8,128)} %copy-done.10, f32[24,4096]{1,0:T(8,128)} %copy-done.11, ...), custom_call_target="tpu_custom_call" | custom-call | bytes 8388608 | tf_op jit(solution)/shard_map/turn_zero/pallas_call | solution.py:147
  125.9 13.7 %update_zero.1 = f32[4096,512]{1,0:T(8,128)} custom-call(s32[1]{0:T(128)} %bitcast.refs_0_, f32[256,512]{1,0:T(8,128)} %get-tuple-element.34.refs_1_, f32[128,640]{1,0:T(8,128)} %copy-done.8, f32[128,640]{1,0:T(8,128)} %copy-done.13, f32[32,640]{1,0:T(8,128)} %copy-done.15, f32[32,640]{1,0:T(8,128)} %copy-done.18, f32[32,640]{1,0:T(8,128)} %copy-done.16, ...), custom_call_target="tpu_custom_call" | custom-call | flops 3221225472 | bytes 20971520 | tf_op jit(solution)/shard_map/update_zero/pallas_call | solution.py:217
  (84 shorter events, 8.7 us)
Async XLA Ops:
  7.4 4.4 %collective-permute-start = (f32[128,4096]{1,0:T(8,128)S(1)}, f32[128,4096]{1,0:T(8,128)}, u32[]{:S(2)}, u32[]{:S(2)}) collective-permute-start(f32[128,4096]{1,0:T(8,128)S(1)} %cut_own.1.refs_1_.refs_3_.refs_5_.refs_0_.refs_2_), channel_id=1, source_target_pairs={{0,1},{1,0},{2,3},{3,2},{4,5},{5,4},{6,7},{7,6},{8,9},{9,8},{10,11... | collective-permute-start | bytes 6291464 | tf_op jit(solution)/shard_map/ppermute | solution.py:234
  8.0 15.4 %collective-permute-start.4 = (f32[32,4096]{1,0:T(8,128)}, f32[32,4096]{1,0:T(8,128)}, u32[]{:S(2)}, u32[]{:S(2)}) collective-permute-start(f32[32,4096]{1,0:T(8,128)} %cut_0.1.refs_0_), channel_id=1, source_target_pairs={{2,0},{3,1},{0,2},{1,3},{6,4},{7,5},{4,6},{5,7},{10,8},{11,9},{8,1... | collective-permute-start | bytes 1572872 | tf_op jit(solution)/shard_map/ppermute | solution.py:237
  23.4 15.7 %copy-start.20 = (f32[128,640]{1,0:T(8,128)S(1)}, f32[128,640]{1,0:T(8,128)}, u32[]{:S(2)}) copy-start(f32[128,640]{1,0:T(8,128)} %get-tuple-element.23) | copy-start | bytes 983044
  23.4 5.1 %collective-permute-start.5 = (f32[32,4096]{1,0:T(8,128)}, f32[32,4096]{1,0:T(8,128)S(1)}, u32[]{:S(2)}, u32[]{:S(2)}) collective-permute-start(f32[32,4096]{1,0:T(8,128)} %collective-permute-done.4.refs_1_.refs_2_.refs_4_), channel_id=1, source_target_pairs={{0,1},{1,0},{2,3},{3,2},{4,5},{5,4},{6,7},{7,6},{8,9},{9,8},{10,11... | collective-permute-start | bytes 1572872 | tf_op jit(solution)/shard_map/ppermute | solution.py:234
  23.7 15.4 %collective-permute-start.9 = (f32[32,4096]{1,0:T(8,128)S(1)}, f32[32,4096]{1,0:T(8,128)S(1)}, u32[]{:S(2)}, u32[]{:S(2)}) collective-permute-start(f32[32,4096]{1,0:T(8,128)S(1)} %cut_1.1.refs_0_), channel_id=1, source_target_pairs={{2,0},{3,1},{0,2},{1,3},{6,4},{7,5},{4,6},{5,7},{10,8},{11,9},{8,1... | collective-permute-start | bytes 1572872 | tf_op jit(solution)/shard_map/ppermute | solution.py:237
  26.3 12.8 %collective-permute-start.1 = (f32[128,640]{1,0:T(8,128)}, f32[128,640]{1,0:T(8,128)S(1)}, u32[]{:S(2)}, u32[]{:S(2)}) collective-permute-start(f32[128,640]{1,0:T(8,128)} %get-tuple-element.24), channel_id=1, source_target_pairs={{0,4},{4,0},{8,12},{12,8},{1,5},{5,1},{9,13},{13,9},{2,6},{6,2},{1... | collective-permute-start | bytes 983048 | tf_op jit(solution)/shard_map/ppermute | solution.py:240
  27.9 25.4 %collective-permute-start.14 = (f32[40,4096]{1,0:T(8,128)S(1)}, f32[40,4096]{1,0:T(8,128)S(1)}, u32[]{:S(2)}, u32[]{:S(2)}) collective-permute-start(f32[40,4096]{1,0:T(8,128)S(1)} %cut_2.1.refs_0_), channel_id=1, source_target_pairs={{2,0},{3,1},{0,2},{1,3},{6,4},{7,5},{4,6},{5,7},{10,8},{11,9},{8,1... | collective-permute-start | bytes 1966088 | tf_op jit(solution)/shard_map/ppermute | solution.py:237
  39.0 4.8 %collective-permute-start.10 = (f32[32,4096]{1,0:T(8,128)S(1)}, f32[32,4096]{1,0:T(8,128)S(1)}, u32[]{:S(2)}, u32[]{:S(2)}) collective-permute-start(f32[32,4096]{1,0:T(8,128)S(1)} %collective-permute-done.9.refs_1_.refs_4_.refs_6_), channel_id=1, source_target_pairs={{0,1},{1,0},{2,3},{3,2},{4,5},{5,4},{6,7},{7,6},{8,9},{9,8},{10,11... | collective-permute-start | bytes 1572872 | tf_op jit(solution)/shard_map/ppermute | solution.py:234
  39.1 18.6 %copy-start.3 = (f32[24,4096]{1,0:T(8,128)S(1)}, f32[24,4096]{1,0:T(8,128)}, u32[]{:S(2)}) copy-start(f32[24,4096]{1,0:T(8,128)} %copy-done.2) | copy-start | bytes 1179652
  39.1 21.0 %copy-start.22 = (f32[32,640]{1,0:T(8,128)S(1)}, f32[32,640]{1,0:T(8,128)}, u32[]{:S(2)}) copy-start(f32[32,640]{1,0:T(8,128)} %get-tuple-element.26) | copy-start | bytes 245764
  39.1 18.6 %collective-permute-start.2 = (f32[128,640]{1,0:T(8,128)S(1)}, f32[128,640]{1,0:T(8,128)S(1)}, u32[]{:S(2)}, u32[]{:S(2)}) collective-permute-start(f32[128,640]{1,0:T(8,128)S(1)} %add.40), channel_id=1, source_target_pairs={{0,8},{4,12},{8,0},{12,4},{1,9},{5,13},{9,1},{13,5},{2,10},{6,14},... | collective-permute-start | bytes 983048 | tf_op jit(solution)/shard_map/ppermute | solution.py:240
  42.3 11.0 %collective-permute-start.6 = (f32[32,640]{1,0:T(8,128)}, f32[32,640]{1,0:T(8,128)S(1)}, u32[]{:S(2)}, u32[]{:S(2)}) collective-permute-start(f32[32,640]{1,0:T(8,128)} %get-tuple-element.27), channel_id=1, source_target_pairs={{0,4},{4,0},{8,12},{12,8},{1,5},{5,1},{9,13},{13,9},{2,6},{6,2},{1... | collective-permute-start | bytes 245768 | tf_op jit(solution)/shard_map/ppermute | solution.py:240
  53.2 10.3 %copy-start.9 = (f32[40,4096]{1,0:T(8,128)}, f32[40,4096]{1,0:T(8,128)S(1)}, u32[]{:S(2)}) copy-start(f32[40,4096]{1,0:T(8,128)S(1)} %collective-permute-done.14.refs_0_.refs_2_) | copy-start | bytes 1966084
  57.7 5.9 %collective-permute-start.15 = (f32[40,4096]{1,0:T(8,128)S(1)}, f32[40,4096]{1,0:T(8,128)S(1)}, u32[]{:S(2)}, u32[]{:S(2)}) collective-permute-start(f32[40,4096]{1,0:T(8,128)S(1)} %collective-permute-done.14.refs_0_.refs_2_), channel_id=1, source_target_pairs={{0,1},{1,0},{2,3},{3,2},{4,5},{5,4},{6,7},{7,6},{8,9},{9,8},{10,11... | collective-permute-start | bytes 1966088 | tf_op jit(solution)/shard_map/ppermute | solution.py:234
  57.7 16.3 %collective-permute-start.18 = (f32[24,4096]{1,0:T(8,128)S(1)}, f32[24,4096]{1,0:T(8,128)S(1)}, u32[]{:S(2)}, u32[]{:S(2)}) collective-permute-start(f32[24,4096]{1,0:T(8,128)S(1)} %copy-done.3), channel_id=1, source_target_pairs={{2,0},{3,1},{0,2},{1,3},{6,4},{7,5},{4,6},{5,7},{10,8},{11,9},{8,1... | collective-permute-start | bytes 1179656 | tf_op jit(solution)/shard_map/ppermute | solution.py:237
  59.2 14.7 %copy-start.8 = (f32[128,640]{1,0:T(8,128)}, f32[128,640]{1,0:T(8,128)S(1)}, u32[]{:S(2)}) copy-start(f32[128,640]{1,0:T(8,128)S(1)} %add.41.refs_1_.refs_2_) | copy-start | bytes 983044
  59.2 14.8 %collective-permute-start.3 = (f32[128,640]{1,0:T(8,128)S(1)}, f32[128,640]{1,0:T(8,128)S(1)}, u32[]{:S(2)}, u32[]{:S(2)}) collective-permute-start(f32[128,640]{1,0:T(8,128)S(1)} %add.41.refs_1_.refs_2_), channel_id=1, source_target_pairs={{0,4},{4,0},{8,12},{12,8},{1,5},{5,1},{9,13},{13,9},{2,6},{6,2},{1... | collective-permute-start | bytes 983048 | tf_op jit(solution)/shard_map/ppermute | solution.py:240
  60.1 16.1 %copy-start.21 = (f32[32,640]{1,0:T(8,128)S(1)}, f32[32,640]{1,0:T(8,128)}, u32[]{:S(2)}) copy-start(f32[32,640]{1,0:T(8,128)} %get-tuple-element.29) | copy-start | bytes 245764
  60.1 13.9 %collective-permute-start.7 = (f32[32,640]{1,0:T(8,128)S(1)}, f32[32,640]{1,0:T(8,128)S(1)}, u32[]{:S(2)}, u32[]{:S(2)}) collective-permute-start(f32[32,640]{1,0:T(8,128)S(1)} %add.42), channel_id=1, source_target_pairs={{0,8},{4,12},{8,0},{12,4},{1,9},{5,13},{9,1},{13,5},{2,10},{6,14},... | collective-permute-start | bytes 245768 | tf_op jit(solution)/shard_map/ppermute | solution.py:240
  63.5 10.5 %collective-permute-start.11 = (f32[32,640]{1,0:T(8,128)}, f32[32,640]{1,0:T(8,128)S(1)}, u32[]{:S(2)}, u32[]{:S(2)}) collective-permute-start(f32[32,640]{1,0:T(8,128)} %get-tuple-element.30), channel_id=1, source_target_pairs={{0,4},{4,0},{8,12},{12,8},{1,5},{5,1},{9,13},{13,9},{2,6},{6,2},{1... | collective-permute-start | bytes 245768 | tf_op jit(solution)/shard_map/ppermute | solution.py:240
  74.0 12.9 %copy-start.13 = (f32[128,640]{1,0:T(8,128)}, f32[128,640]{1,0:T(8,128)S(1)}, u32[]{:S(2)}) copy-start(f32[128,640]{1,0:T(8,128)S(1)} %collective-permute-done.3.refs_2_.refs_3_) | copy-start | bytes 983044
  74.0 2.8 %collective-permute-start.19 = (f32[24,4096]{1,0:T(8,128)S(1)}, f32[24,4096]{1,0:T(8,128)S(1)}, u32[]{:S(2)}, u32[]{:S(2)}) collective-permute-start(f32[24,4096]{1,0:T(8,128)S(1)} %collective-permute-done.18.refs_0_.refs_4_), channel_id=1, source_target_pairs={{0,1},{1,0},{2,3},{3,2},{4,5},{5,4},{6,7},{7,6},{8,9},{9,8},{10,11... | collective-permute-start | bytes 1179656 | tf_op jit(solution)/shard_map/ppermute | solution.py:234
  74.1 26.5 %collective-permute-start.16 = (f32[80,768]{1,0:T(8,128)}, f32[80,768]{1,0:T(8,128)S(1)}, u32[]{:S(2)}, u32[]{:S(2)}) collective-permute-start(f32[80,768]{1,0:T(8,128)} %project_zero_2.1), channel_id=1, source_target_pairs={{0,4},{4,0},{8,12},{12,8},{1,5},{5,1},{9,13},{13,9},{2,6},{6,2},{1... | collective-permute-start | bytes 737288 | tf_op jit(solution)/shard_map/ppermute | solution.py:240
  76.2 12.9 %collective-permute-start.12 = (f32[32,640]{1,0:T(8,128)S(1)}, f32[32,640]{1,0:T(8,128)S(1)}, u32[]{:S(2)}, u32[]{:S(2)}) collective-permute-start(f32[32,640]{1,0:T(8,128)S(1)} %add.44), channel_id=1, source_target_pairs={{0,8},{4,12},{8,0},{12,4},{1,9},{5,13},{9,1},{13,5},{2,10},{6,14},... | collective-permute-start | bytes 245768 | tf_op jit(solution)/shard_map/ppermute | solution.py:240
  86.9 15.2 %collective-permute-start.20 = (f32[48,768]{1,0:T(8,128)}, f32[48,768]{1,0:T(8,128)S(1)}, u32[]{:S(2)}, u32[]{:S(2)}) collective-permute-start(f32[48,768]{1,0:T(8,128)} %project_zero_3.1), channel_id=1, source_target_pairs={{0,4},{4,0},{8,12},{12,8},{1,5},{5,1},{9,13},{13,9},{2,6},{6,2},{1... | collective-permute-start | bytes 442376 | tf_op jit(solution)/shard_map/ppermute | solution.py:240
  87.9 12.6 %copy-start.15 = (f32[32,640]{1,0:T(8,128)}, f32[32,640]{1,0:T(8,128)S(1)}, u32[]{:S(2)}) copy-start(f32[32,640]{1,0:T(8,128)S(1)} %add.43.refs_3_.refs_4_) | copy-start | bytes 245764
  87.9 15.8 %collective-permute-start.8 = (f32[32,640]{1,0:T(8,128)S(1)}, f32[32,640]{1,0:T(8,128)S(1)}, u32[]{:S(2)}, u32[]{:S(2)}) collective-permute-start(f32[32,640]{1,0:T(8,128)S(1)} %add.43.refs_3_.refs_4_), channel_id=1, source_target_pairs={{0,4},{4,0},{8,12},{12,8},{1,5},{5,1},{9,13},{13,9},{2,6},{6,2},{1... | collective-permute-start | bytes 245768 | tf_op jit(solution)/shard_map/ppermute | solution.py:240
  89.1 11.5 %copy-start.16 = (f32[32,640]{1,0:T(8,128)}, f32[32,640]{1,0:T(8,128)S(1)}, u32[]{:S(2)}) copy-start(f32[32,640]{1,0:T(8,128)S(1)} %add.45.refs_5_.refs_6_) | copy-start | bytes 245764
  89.1 14.7 %collective-permute-start.13 = (f32[32,640]{1,0:T(8,128)S(1)}, f32[32,640]{1,0:T(8,128)S(1)}, u32[]{:S(2)}, u32[]{:S(2)}) collective-permute-start(f32[32,640]{1,0:T(8,128)S(1)} %add.45.refs_5_.refs_6_), channel_id=1, source_target_pairs={{0,4},{4,0},{8,12},{12,8},{1,5},{5,1},{9,13},{13,9},{2,6},{6,2},{1... | collective-permute-start | bytes 245768 | tf_op jit(solution)/shard_map/ppermute | solution.py:240
  93.3 8.8 %copy-start.17 = (f32[48,768]{1,0:T(8,128)S(1)}, f32[48,768]{1,0:T(8,128)}, u32[]{:S(2)}) copy-start(f32[48,768]{1,0:T(8,128)} %project_zero_3.1) | copy-start | bytes 442372
  100.6 23.9 %collective-permute-start.17 = (f32[80,768]{1,0:T(8,128)S(1)}, f32[80,768]{1,0:T(8,128)S(1)}, u32[]{:S(2)}, u32[]{:S(2)}) collective-permute-start(f32[80,768]{1,0:T(8,128)S(1)} %add.46), channel_id=1, source_target_pairs={{0,8},{4,12},{8,0},{12,4},{1,9},{5,13},{9,1},{13,5},{2,10},{6,14},... | collective-permute-start | bytes 737288 | tf_op jit(solution)/shard_map/ppermute | solution.py:240
  102.1 23.1 %collective-permute-start.21 = (f32[48,768]{1,0:T(8,128)S(1)}, f32[48,768]{1,0:T(8,128)S(1)}, u32[]{:S(2)}, u32[]{:S(2)}) collective-permute-start(f32[48,768]{1,0:T(8,128)S(1)} %add.48), channel_id=1, source_target_pairs={{0,8},{4,12},{8,0},{12,4},{1,9},{5,13},{9,1},{13,5},{2,10},{6,14},... | collective-permute-start | bytes 442376 | tf_op jit(solution)/shard_map/ppermute | solution.py:240
  (13 other events, 31.3 us)

commit v3 on v0

v3 whole, which is shorter than its diff:
```python
import jax
import jax.numpy as jnp
from jax import lax
from jax.experimental import pallas as pl
from jax.experimental.pallas import tpu as pltpu
from jax.sharding import PartitionSpec as P

F32, BF16 = jnp.float32, jnp.bfloat16
PIECES = ((1, 0, 32), (1, 32, 64), (0, 0, 40), (0, 40, 64))
SWAP_PARTS = 2
NN = (((1,), (0,)), ((), ()))
NT = (((1,), (1,)), ((), ()))
TN = (((0,), (0,)), ((), ()))
SCALARS = pl.BlockSpec(memory_space=pltpu.SMEM)
VMEM = pl.BlockSpec(memory_space=pltpu.VMEM)
HBM = pl.BlockSpec(memory_space=pltpu.HBM)
ANY = pl.BlockSpec(memory_space=pl.ANY)


def call(body, name, ins, specs, outs, out_specs, scratch=(), mib=16):
    return pl.pallas_call(
        body,
        in_specs=specs,
        out_specs=out_specs,
        out_shape=outs,
        scratch_shapes=list(scratch),
        compiler_params=pltpu.CompilerParams(vmem_limit_bytes=mib * 1024 * 1024),
        cost_estimate=pl.CostEstimate(flops=1, bytes_accessed=1, transcendentals=0),
        name=name,
    )(*ins)


def array(*shape, dtype=F32):
    return jax.ShapeDtypeStruct(shape, dtype)


def split(value):
    high = value.astype(BF16)
    return high, (value - high.astype(F32)).astype(BF16)


def dot(a, b, dims=NN):
    return lax.dot_general(a, b, dims, preferred_element_type=F32)


def full_dot(a, b, dims=NN):
    return lax.dot_general(a, b, dims, precision=lax.Precision.HIGHEST, preferred_element_type=F32)


def three(vh, vl, bh, bl, dims):
    rows = vh.shape[0]
    first = dot(jnp.concatenate([vh, vl]), bh, dims)
    return first[:rows] + first[rows:] + dot(vh, bl, dims)


def steps_of(here, step):
    step = min(here, step)
    return [pl.ds(at, step) for at in range(0, here, step)]


def cut(name, where, vectors, after, rows):
    here = vectors.shape[2]
    places, height = [], 0
    for block, low, high in rows:
        places.append((block, low, high, height))
        height += high - low

    def body(where_ref, in_ref, *refs):
        out, sems = refs[-2:]
        copies = [
            pltpu.make_async_copy(in_ref.at[block, low:high], out.at[at : at + high - low], sems.at[n])
            for n, (block, low, high, at) in enumerate(places)
        ]
        for copy in copies:
            copy.start()
        for copy, (block, low, high, at) in zip(copies, places):
            copy.wait()
            shape = (high - low, here)
            along = lax.broadcasted_iota(jnp.int32, shape, 0) + (where_ref[0] + low + block * where_ref[2])
            across = lax.broadcasted_iota(jnp.int32, shape, 1) + where_ref[1]
            out[at : at + high - low] = jnp.where(across >= along, out[at : at + high - low], 0.0)

    return call(
        body,
        name,
        (where, vectors, *after),
        [SCALARS, HBM] + [ANY] * len(after),
        array(height, here),
        VMEM,
        [pltpu.SemaphoreType.DMA((len(rows),))],
    )


def load(eigvecs):
    here, nc = eigvecs.shape
    steps = steps_of(here, 512)

    def body(in_ref, out, high, low, sems):
        copies = [pltpu.make_async_copy(in_ref.at[ds], out.at[ds], sems.at[n]) for n, ds in enumerate(steps)]
        for copy in copies:
            copy.start()
        for copy, ds in zip(copies, steps):
            copy.wait()
            high[ds, :], low[ds, :] = split(out[ds, :])

    outs = [array(here, nc), array(here, nc, dtype=BF16), array(here, nc, dtype=BF16)]
    sems = [pltpu.SemaphoreType.DMA((len(steps),))]
    return call(body, "load", (eigvecs,), [HBM], outs, [VMEM] * 3, sems)


def rows_of(refs, pieces, ds):
    return jnp.concatenate([ref[at : at + count, ds] for ref, (_, count, at) in zip(refs, pieces)])


def project(name, rows, partners, high, low, bit=None):
    here, nc = high.shape
    height = sum(count for _, count, _ in rows)
    extra = sum(count for _, count, _ in partners)
    steps = steps_of(here, 512)

    def body(*refs):
        refs = list(refs)
        acc = refs.pop()
        bit_ref = refs.pop(0) if bit is not None else None
        row_refs, refs = refs[: len(rows)], refs[len(rows) :]
        partner_refs, refs = refs[: len(partners)], refs[len(partners) :]
        high_ref, low_ref = refs[:2]
        outs = refs[2:]
        for n, ds in enumerate(steps):
            vh, vl = split(rows_of(row_refs, rows, ds))
            main = three(vh, vl, high_ref[ds, :], low_ref[ds, :], NN)
            gram = three(vh, vl, *split(rows_of(partner_refs, partners, ds)), NT)
            if n == 0:
                acc[:, :nc], acc[:, nc:] = main, gram
            else:
                acc[:, :nc] += main
                acc[:, nc:] += gram
        if bit is None:
            outs[0][...] = acc[...]
        else:
            half = height // 2
            zero = bit_ref[0] == 0
            outs[0][...] = jnp.where(zero, acc[:half], acc[half:])
            outs[1][...] = jnp.where(zero, acc[half:], acc[:half])

    outputs = 1 if bit is None else 2
    arrays = [r[0] for r in rows + partners] + [high, low]
    return call(
        body,
        name,
        ([] if bit is None else [bit]) + arrays,
        ([] if bit is None else [SCALARS]) + [VMEM] * len(arrays),
        [array(height // outputs, nc + extra)] * outputs,
        [VMEM] * outputs,
        [pltpu.VMEM((height, nc + extra), F32)],
    )


def reorder(where, factors, after, share, chips, segments):
    width = factors.shape[1]

    def body(where_ref, in_ref, *refs):
        chip, core = where_ref[3], where_ref[4]
        for block, out in enumerate(refs[-2:]):
            picks = []
            for step, other, low, high in segments[block]:
                at = (lax.rem(chip + step, chips) * 2 + (core + other) % 2) * share + low
                shape = (high - low, width)
                same = lax.broadcasted_iota(jnp.int32, shape, 1) == lax.broadcasted_iota(jnp.int32, shape, 0) + at
                picks.append(jnp.where(same, 1.0, 0.0))
            pick = jnp.concatenate(picks)
            out[...] = full_dot(full_dot(pick, in_ref[block]), pick, NT)

    specs = [SCALARS, VMEM] + [ANY] * len(after)
    return call(body, "reorder", (where, factors, *after), specs, [array(width, width)] * 2, [VMEM] * 2)


def update(name, make, ins, factor, pieces, current, last):
    here, nc = current.shape
    width = factor.shape[0]
    steps = steps_of(here, 256)

    def body(*refs):
        in_refs, refs = refs[: len(ins)], refs[len(ins) :]
        factor_ref, refs = refs[0], refs[1:]
        piece_refs, refs = refs[: len(pieces)], refs[len(pieces) :]
        cur_ref, out = refs[:2]
        scaled = full_dot(factor_ref[...], make(*in_refs))
        sh, sl = split(scaled)
        if not last:
            refs[2][...] = scaled
        copies = []
        for n, ds in enumerate(steps):
            vh, vl = split(rows_of(piece_refs, pieces, ds))
            new = cur_ref[ds, :] - (dot(vh, sh, TN) + dot(vh, sl, TN) + dot(vl, sh, TN))
            if last:
                held, sems = refs[2:]
                held[ds, :] = new
                copies.append(pltpu.make_async_copy(held.at[ds], out.at[ds], sems.at[n]))
                copies[-1].start()
            else:
                out[ds, :] = new
        for copy in copies:
            copy.wait()

    specs = [SCALARS if v.dtype == jnp.int32 else VMEM for v in ins] + [VMEM] * (len(pieces) + 2)
    args = [*ins, factor, *[p[0] for p in pieces], current]
    if last:
        scratch = [pltpu.VMEM((here, nc), F32), pltpu.SemaphoreType.DMA((len(steps),))]
        return call(body, name, args, specs, array(here, nc), HBM, scratch, 24)
    return call(body, name, args, specs, [array(here, nc), array(width, nc)], [VMEM] * 2)


def make_local(chips, rows):
    cols = 2 * chips

    def core_swap(value):
        return lax.ppermute(value, "col", [(i, i ^ 1) for i in range(cols)])

    def from_chip(value, step):
        return lax.ppermute(value, "col", [((i + 2 * step) % cols, i) for i in range(cols)])

    def row_swap(value, step):
        return lax.ppermute(value, "row", [(i, i ^ step) for i in range(rows)])

    def sums(value, send=None):
        step, got = 1, None
        if send is not None:
            got = row_swap(send, 1)
            yield got
            step = 2
        while step < rows:
            value = value if got is None else value + got
            got = row_swap(value, step)
            yield got
            step *= 2
        if send is not None:
            value = value + got
            got = row_swap(value, 1)
            yield got
        return value, got

    def local(vectors, factors, eigvecs):
        share, here = vectors.shape[1:]
        nc = eigvecs.shape[1]
        width = share * cols
        half = 2 * share
        col, row = lax.axis_index("col"), lax.axis_index("row")
        where = jnp.stack([col * share, row * here, jnp.int32(width), col // 2, col % 2]).astype(jnp.int32)
        bit = (row % 2).astype(jnp.int32)[None]
        pieces = []
        for block, low, high in PIECES:
            low, high = low * share // 64 // 8 * 8, high * share // 64 // 8 * 8
            pieces.append((block, low, high))

        def after(value, *others):
            return lax.optimization_barrier((value, *others))[0]

        far, last = [], ()
        for n, piece in enumerate(pieces):
            sent = cut(f"cut_{n}", where, vectors, last, [piece])
            far += [(step, piece, from_chip(sent, step)) for step in range(1, chips)]
            if n == 0:
                mine = cut("cut_own", where, vectors, (sent,), [(1, 0, share), (0, 0, share)])
                sib = core_swap(mine)
                current, high, low = load(after(eigvecs, mine))
                last = (high,)
        own = {1: [(mine, share, 0), (sib, share, 0)], 0: [(mine, share, share), (sib, share, share)]}
        segments = {k: [(0, 0, 0, share), (0, 1, 0, share)] for k in (0, 1)}
        all_ones, all_zeros = list(own[1]), list(own[0])
        running, done, waits = [], {}, ()

        def advance():
            got = []
            for key, chain in list(running):
                try:
                    got.append(next(chain))
                except StopIteration as end:
                    done[key] = end.value
                    running.remove((key, chain))
            return got

        front = project("project_own", own[1] + own[0], own[0], high, low, bit)
        running.append(("own", sums(*front)))
        for n, (step, (block, first, final), value) in enumerate(far):
            value = after(value, *front, *waits)
            waits = advance()
            pair = [(value, final - first, 0)]
            parts = SWAP_PARTS if (final - first) % (8 * SWAP_PARTS) == 0 else 1
            each = (final - first) // parts
            for part in range(parts):
                pair.append((core_swap(value[part * each : (part + 1) * each]), each, 0))
            segments[block] += [(step, 0, first, final), (step, 1, first, final)]
            if block == 1:
                all_ones += pair
                front = project(f"project_one_{n}", pair, own[0], high, low, bit)
            else:
                all_zeros += pair
                front = project(f"project_zero_{n}", pair, all_ones, high, low)
            running.append((n, sums(*front)))
        while running:
            advance()
        ones = [done["own"]] + [done[n] for n, f in enumerate(far) if f[1][0] == 1]
        zeros = [v for n, f in enumerate(far) if f[1][0] == 0 for v in done[n]]
        t0, t1 = reorder(where, factors, front, share, chips, segments)
        flat = [v for pair in ones for v in pair]

        def joined(bit_ref, refs, columns):
            parts = []
            zero = bit_ref[0] == 0
            for a, b in zip(refs[::2], refs[1::2]):
                a, b = a[:, columns], b[:, columns]
                parts.append((jnp.where(zero, a, b), jnp.where(zero, b, a)))
            ones = [parts[0][0]] + [p for pair in parts[1:] for p in pair]
            return jnp.concatenate(ones), parts[0][1]

        def make_one(bit_ref, *refs):
            return joined(bit_ref, refs, slice(0, nc))[0]

        def make_zero(bit_ref, scaled_ref, *refs):
            ones_refs, zero_refs = refs[: len(flat)], refs[len(flat) :]
            scaled = scaled_ref[...]
            turned_gram = joined(bit_ref, ones_refs, slice(nc, nc + half))[0]
            parts = [joined(bit_ref, ones_refs[:2], slice(0, nc))[1] - full_dot(turned_gram, scaled, TN)]
            later = jnp.concatenate([a[...] + b[...] for a, b in zip(zero_refs[::2], zero_refs[1::2])])
            parts.append(later[:, :nc] - full_dot(later[:, nc:], scaled))
            return jnp.concatenate(parts)

        current, scaled = update("update_one", make_one, [bit, *flat], t1, all_ones, current, False)
        return update("update_zero", make_zero, [bit, scaled, *flat, *zeros], t0, all_zeros, current, True)

    return local


def solution(mesh):
    placed = (P("groups", "col", "row"), P("groups", None, None), P(("groups", "row"), "col"))
    local = make_local(mesh.shape["col"] // 2, mesh.shape["row"])
    return jax.shard_map(
        local, mesh=mesh, in_specs=placed, out_specs=P(("groups", "row"), "col"), check_vma=False
    )
```

time: 218 us -> 124 us (0.57)
  waiting for transfers between devices: 140 us -> 34.3 us
  matrix products: 61.2 us -> 0 us
  Pallas kernels: 0 us -> 47.7 us
  starting transfers between devices: 0.26 us -> 25.7 us
  between operations: 13.2 us -> 0.44 us
  local copies, waits for them, and re-layouts: 3.41 us -> 15.2 us
    psum x2 -> x0, waiting for transfers between devices: 76.6 us -> none  [local(): summed = lax.psum(partial_value, 'row')]
    all_gather x1 -> x0, waiting for transfers between devices: 62.6 us -> none  [local(): full = lax.all_gather(vectors, 'col', axis=1, tiled=True)]
    dot_general x6 -> x0, matrix products: 61.2 us -> none  [the longest x2 36.7 us: local(): current = current - jnp.dot(reflector.T, scaled, precision=HIGH)]
    pallas_call x0 -> x14, Pallas kernels: none -> 47.7 us  [call(): pl.pallas_call(body, in_specs=specs, out_specs=out_specs, out_shape=outs,...]
    ppermute x0 -> x24, waiting for transfers between devices: none -> 34.3 us  [the longest x13 30.6 us: row_swap(): return lax.ppermute(value, 'row', [(i, i ^ step) for i in range(rows)])]
    ppermute x0 -> x24, starting transfers between devices: none -> 25.7 us  [the longest x13 18.4 us: row_swap(): return lax.ppermute(value, 'row', [(i, i ^ step) for i in range(rows)])]
    unnamed x8 -> x28, local copies, waits for them, and re-layouts: 3.41 us -> 15 us
  transfers between devices with their start and end apart: 3 -> 24, of which waited for: 3 -> 12; matrix products, arithmetic and copies ran while one was open for 0% -> 0% of each run, Pallas kernels for 0% -> 31%
where the time goes in v3:
time: 124 us; the launch traced here: 123 us
  Pallas kernels  47.7 us (38%)
  waiting for transfers between devices  34.3 us (28%)
  starting transfers between devices  25.7 us (21%)
  local copies, waits for them, and re-layouts  15.2 us (12%)
    pallas_call x14, Pallas kernels, call(): pl.pallas_call(body, in_specs=specs, out_specs=out_specs, out_shape=outs,...  47.7 us
    ppermute x13, waiting for transfers between devices, row_swap(): return lax.ppermute(value, 'row', [(i, i ^ step) for i in range(rows)])  30.6 us
    ppermute x13, starting transfers between devices, row_swap(): return lax.ppermute(value, 'row', [(i, i ^ step) for i in range(rows)])  18.4 us
    unnamed x28, local copies, waits for them, and re-layouts  15 us
    ppermute x4, starting transfers between devices, from_chip(): lax.ppermute(value, 'col', [((i + 2 * step) % cols, i) for i in range(col...  5.71 us
    ppermute x4, waiting for transfers between devices, from_chip(): lax.ppermute(value, 'col', [((i + 2 * step) % cols, i) for i in range(col...  2.96 us
  transfers between devices with their start and end apart: 24, of which 12 were waited for; matrix products, arithmetic and copies ran while one was open for 0% of the time, Pallas kernels for 31%

profile of v3, /device:TPU:0, one launch (start us, length us, event | category | flops | bytes accessed | tf_op | source)
XLA Modules:
  0.0 123.5 jit_solution(5317167211958436951)
XLA Ops:
  0.1 1.6 %copy-done.6 = f32[2,64,4096]{2,1,0:T(8,128)S(1)} copy-done((f32[2,64,4096]{2,1,0:T(8,128)S(1)}, f32[2,64,4096]{2,1,0:T(8,128)}, u32[]{:S(2)}) %copy-start.6) | copy-done | bytes 2097176
  1.7 1.4 %cut_0.1.refs_0_ = f32[32,4096]{1,0:T(8,128)} custom-call(s32[5]{0:T(128)S(1)} %stack.19.where_ref, f32[2,64,4096]{2,1,0:T(8,128)S(1)} %copy-done.6), custom_call_target="tpu_custom_call" | custom-call | flops 1 | bytes 1 | tf_op jit(solution)/shard_map/cut_0/pallas_call | solution.py:21
  4.5 2.6 %collective-permute-start.4 = (f32[32,4096]{1,0:T(8,128)}, f32[32,4096]{1,0:T(8,128)S(1)}, u32[]{:S(2)}, u32[]{:S(2)}) collective-permute-start(f32[32,4096]{1,0:T(8,128)} %cut_0.1.refs_0_), channel_id=1, source_target_pairs={{2,0},{3,1},{0,2},{1,3},{6,4},{7,5},{4,6},{5,7},{10,8},{11,9},{8,1... | collective-permute-start | bytes 1572872 | tf_op jit(solution)/shard_map/ppermute | solution.py:221
  7.1 3.4 %copy-done.10 = f32[4096,512]{1,0:T(8,128)S(1)} copy-done((f32[4096,512]{1,0:T(8,128)S(1)}, f32[4096,512]{1,0:T(8,128)}, u32[]{:S(2)}) %copy-start.10) | copy-done | bytes 8388632
  10.5 1.7 %load.1 = (f32[4096,512]{1,0:T(8,128)S(1)}, bf16[4096,512]{1,0:T(8,128)(2,1)S(1)}, bf16[4096,512]{1,0:T(8,128)(2,1)S(1)}) custom-call(f32[4096,512]{1,0:T(8,128)S(1)} %copy-done.10), custom_call_target="tpu_custom_call" | custom-call | flops 1 | bytes 1 | tf_op jit(solution)/shard_map/load/pallas_call | solution.py:21
  12.2 3.4 %copy-done.9 = f32[4096,512]{1,0:T(8,128)} copy-done((f32[4096,512]{1,0:T(8,128)}, f32[4096,512]{1,0:T(8,128)S(1)}, u32[]{:S(2)}) %copy-start.9) | copy-done | bytes 8388632
  15.6 1.9 %cut_1.1 = f32[32,4096]{1,0:T(8,128)} custom-call(s32[5]{0:T(128)S(1)} %stack.19.where_ref, f32[2,64,4096]{2,1,0:T(8,128)S(1)} %copy-done.7, bf16[4096,512]{1,0:T(8,128)(2,1)S(1)} %get-tuple-element.24.refs_7_.refs_6_.refs_0_.refs_10_), custom_call_target="tpu_custom_call" | custom-call | flops 1 | bytes 1 | tf_op jit(solution)/shard_map/cut_1/pallas_call | solution.py:21
  17.7 2.0 %copy-done = bf16[4096,512]{1,0:T(8,128)(2,1)} copy-done((bf16[4096,512]{1,0:T(8,128)(2,1)}, bf16[4096,512]{1,0:T(8,128)(2,1)S(1)}, u32[]{:S(2)}) %copy-start) | copy-done | bytes 4194328
  19.9 2.2 %copy-done.1 = bf16[4096,512]{1,0:T(8,128)(2,1)S(1)} copy-done((bf16[4096,512]{1,0:T(8,128)(2,1)S(1)}, bf16[4096,512]{1,0:T(8,128)(2,1)}, u32[]{:S(2)}) %copy-start.1) | copy-done | bytes 4194328
  22.1 2.2 %copy-done.4 = bf16[4096,512]{1,0:T(8,128)(2,1)S(1)} copy-done((bf16[4096,512]{1,0:T(8,128)(2,1)S(1)}, bf16[4096,512]{1,0:T(8,128)(2,1)}, u32[]{:S(2)}) %copy-start.4) | copy-done | bytes 4194328
  24.3 8.0 %project_own.1 = (f32[128,640]{1,0:T(8,128)S(1)}, f32[128,640]{1,0:T(8,128)S(1)}) custom-call(s32[1]{0:T(128)} %bitcast.refs_0_, f32[128,4096]{1,0:T(8,128)S(1)} %cut_own.1.refs_1_.refs_3_.refs_5_.refs_4_.refs_2_.refs_8_.refs_13_, f32[128,4096]{1,0:T(8,128)} %collective-permute-done.refs_2_.refs_4_.refs_6_.refs_5_.refs_3_.refs_9_.refs_14_, ...), custom_call_target="tpu_custom_call" | custom-call | flops 1 | bytes 1 | tf_op jit(solution)/shard_map/project_own/pallas_call | solution.py:21
  32.3 2.0 %collective-permute-start.1 = (f32[128,640]{1,0:T(8,128)S(1)}, f32[128,640]{1,0:T(8,128)S(1)}, u32[]{:S(2)}, u32[]{:S(2)}) collective-permute-start(f32[128,640]{1,0:T(8,128)S(1)} %get-tuple-element.27), channel_id=1, source_target_pairs={{0,4},{4,0},{8,12},{12,8},{1,5},{5,1},{9,13},{13,9},{2,6},{6,2},{1... | collective-permute-start | bytes 983048 | tf_op jit(solution)/shard_map/ppermute | solution.py:224
  35.8 1.6 %collective-permute-start.17 = (f32[40,4096]{1,0:T(8,128)S(1)}, f32[40,4096]{1,0:T(8,128)S(1)}, u32[]{:S(2)}, u32[]{:S(2)}) collective-permute-start(f32[40,4096]{1,0:T(8,128)S(1)} %cut_2.1), channel_id=1, source_target_pairs={{2,0},{3,1},{0,2},{1,3},{6,4},{7,5},{4,6},{5,7},{10,8},{11,9},{8,1... | collective-permute-start | bytes 1966088 | tf_op jit(solution)/shard_map/ppermute | solution.py:221
  37.4 3.8 %project_one_0.1 = (f32[32,640]{1,0:T(8,128)S(1)}, f32[32,640]{1,0:T(8,128)S(1)}) custom-call(s32[1]{0:T(128)} %bitcast.refs_0_, f32[32,4096]{1,0:T(8,128)S(1)} %collective-permute-done.4.refs_1_.refs_4_.refs_10_, f32[16,4096]{1,0:T(8,128)S(1)} %collective-permute-done.5.refs_2_.refs_5_.refs_11_, ...), custom_call_target="tpu_custom_call" | custom-call | flops 1 | bytes 1 | tf_op jit(solution)/shard_map/project_one_0/pallas_call | solution.py:21
  42.2 2.8 %collective-permute-start.2 = (f32[128,640]{1,0:T(8,128)S(1)}, f32[128,640]{1,0:T(8,128)S(1)}, u32[]{:S(2)}, u32[]{:S(2)}) collective-permute-start(f32[128,640]{1,0:T(8,128)S(1)} %add.34), channel_id=1, source_target_pairs={{0,8},{4,12},{8,0},{12,4},{1,9},{5,13},{9,1},{13,5},{2,10},{6,14},... | collective-permute-start | bytes 983048 | tf_op jit(solution)/shard_map/ppermute | solution.py:224
  45.6 1.6 %collective-permute-start.7 = (f32[32,640]{1,0:T(8,128)S(1)}, f32[32,640]{1,0:T(8,128)S(1)}, u32[]{:S(2)}, u32[]{:S(2)}) collective-permute-start(f32[32,640]{1,0:T(8,128)S(1)} %get-tuple-element.30), channel_id=1, source_target_pairs={{0,4},{4,0},{8,12},{12,8},{1,5},{5,1},{9,13},{13,9},{2,6},{6,2},{1... | collective-permute-start | bytes 245768 | tf_op jit(solution)/shard_map/ppermute | solution.py:224
  47.2 3.8 %project_one_1.1 = (f32[32,640]{1,0:T(8,128)S(1)}, f32[32,640]{1,0:T(8,128)S(1)}) custom-call(s32[1]{0:T(128)} %bitcast.refs_0_, f32[32,4096]{1,0:T(8,128)S(1)} %collective-permute-done.10.refs_1_.refs_7_.refs_13_, f32[16,4096]{1,0:T(8,128)S(1)} %collective-permute-done.11.refs_2_.refs_8_.refs_14_, ...), custom_call_target="tpu_custom_call" | custom-call | flops 1 | bytes 1 | tf_op jit(solution)/shard_map/project_one_1/pallas_call | solution.py:21
  51.0 1.6 %collective-permute-done.17.refs_0_.refs_15_ = f32[40,4096]{1,0:T(8,128)S(1)} collective-permute-done((f32[40,4096]{1,0:T(8,128)S(1)}, f32[40,4096]{1,0:T(8,128)S(1)}, u32[]{:S(2)}, u32[]{:S(2)}) %collective-permute-start.17) | collective-permute-done | bytes 655392 | tf_op jit(solution)/shard_map/ppermute | solution.py:221
  52.9 6.1 %collective-permute-done.2 = f32[128,640]{1,0:T(8,128)S(1)} collective-permute-done((f32[128,640]{1,0:T(8,128)S(1)}, f32[128,640]{1,0:T(8,128)S(1)}, u32[]{:S(2)}, u32[]{:S(2)}) %collective-permute-start.2) | collective-permute-done | bytes 327712 | tf_op jit(solution)/shard_map/ppermute | solution.py:224
  60.0 1.5 %collective-permute-start.16 = (f32[24,4096]{1,0:T(8,128)S(1)}, f32[24,4096]{1,0:T(8,128)S(1)}, u32[]{:S(2)}, u32[]{:S(2)}) collective-permute-start(f32[24,4096]{1,0:T(8,128)S(1)} %cut_3.1), channel_id=1, source_target_pairs={{2,0},{3,1},{0,2},{1,3},{6,4},{7,5},{4,6},{5,7},{10,8},{11,9},{8,1... | collective-permute-start | bytes 1179656 | tf_op jit(solution)/shard_map/ppermute | solution.py:221
  62.3 3.4 %collective-permute-start.8 = (f32[32,640]{1,0:T(8,128)S(1)}, f32[32,640]{1,0:T(8,128)S(1)}, u32[]{:S(2)}, u32[]{:S(2)}) collective-permute-start(f32[32,640]{1,0:T(8,128)S(1)} %add.36), channel_id=1, source_target_pairs={{0,8},{4,12},{8,0},{12,4},{1,9},{5,13},{9,1},{13,5},{2,10},{6,14},... | collective-permute-start | bytes 245768 | tf_op jit(solution)/shard_map/ppermute | solution.py:224
  65.7 4.5 %project_zero_2.1 = f32[80,768]{1,0:T(8,128)S(1)} custom-call(f32[40,4096]{1,0:T(8,128)S(1)} %collective-permute-done.17.refs_0_.refs_15_, f32[40,4096]{1,0:T(8,128)S(1)} %collective-permute-done.18.refs_1_.refs_16_, f32[128,4096]{1,0:T(8,128)S(1)} %cut_own.1.refs_1_.refs_3_.refs_5_.refs_4_.refs_2_.refs_8_.refs_13_, ...), custom_call_target="tpu_custom_call" | custom-call | flops 1 | bytes 1 | tf_op jit(solution)/shard_map/project_zero_2/pallas_call | solution.py:21
  72.1 2.9 %collective-permute-done.13 = f32[32,640]{1,0:T(8,128)S(1)} collective-permute-done((f32[32,640]{1,0:T(8,128)S(1)}, f32[32,640]{1,0:T(8,128)S(1)}, u32[]{:S(2)}, u32[]{:S(2)}) %collective-permute-start.13) | collective-permute-done | bytes 81952 | tf_op jit(solution)/shard_map/ppermute | solution.py:224
  76.7 4.3 %project_zero_3.1.refs_0_ = f32[48,768]{1,0:T(8,128)S(1)} custom-call(f32[24,4096]{1,0:T(8,128)S(1)} %collective-permute-done.16.refs_0_.refs_17_, f32[24,4096]{1,0:T(8,128)S(1)} %collective-permute-done.19.refs_1_.refs_18_, f32[128,4096]{1,0:T(8,128)S(1)} %cut_own.1.refs_1_.refs_3_.refs_5_.refs_4_.refs_2_.refs_8_.refs_13_, ...), custom_call_target="tpu_custom_call" | custom-call | flops 1 | bytes 1 | tf_op jit(solution)/shard_map/project_zero_3/pallas_call | solution.py:21
  83.3 2.4 %collective-permute-start.21 = (f32[80,768]{1,0:T(8,128)S(1)}, f32[80,768]{1,0:T(8,128)S(1)}, u32[]{:S(2)}, u32[]{:S(2)}) collective-permute-start(f32[80,768]{1,0:T(8,128)S(1)} %add.40.refs_8_), channel_id=1, source_target_pairs={{0,8},{4,12},{8,0},{12,4},{1,9},{5,13},{9,1},{13,5},{2,10},{6,14},... | collective-permute-start | bytes 737288 | tf_op jit(solution)/shard_map/ppermute | solution.py:224
  86.4 2.2 %collective-permute-done.22 = f32[48,768]{1,0:T(8,128)S(1)} collective-permute-done((f32[48,768]{1,0:T(8,128)S(1)}, f32[48,768]{1,0:T(8,128)S(1)}, u32[]{:S(2)}, u32[]{:S(2)}) %collective-permute-start.22) | collective-permute-done | bytes 147488 | tf_op jit(solution)/shard_map/ppermute | solution.py:224
  88.6 1.5 %collective-permute-start.23 = (f32[48,768]{1,0:T(8,128)S(1)}, f32[48,768]{1,0:T(8,128)S(1)}, u32[]{:S(2)}, u32[]{:S(2)}) collective-permute-start(f32[48,768]{1,0:T(8,128)S(1)} %add.41.refs_10_), channel_id=1, source_target_pairs={{0,8},{4,12},{8,0},{12,4},{1,9},{5,13},{9,1},{13,5},{2,10},{6,14},... | collective-permute-start | bytes 442376 | tf_op jit(solution)/shard_map/ppermute | solution.py:224
  91.2 13.9 %collective-permute-done.14 = f32[32,640]{1,0:T(8,128)S(1)} collective-permute-done((f32[32,640]{1,0:T(8,128)S(1)}, f32[32,640]{1,0:T(8,128)S(1)}, u32[]{:S(2)}, u32[]{:S(2)}) %collective-permute-start.14) | collective-permute-done | bytes 81952 | tf_op jit(solution)/shard_map/ppermute | solution.py:224
  105.2 2.0 %reorder.1 = (f32[256,256]{1,0:T(8,128)S(1)}, f32[256,256]{1,0:T(8,128)S(1)}) custom-call(s32[5]{0:T(128)S(1)} %stack.19.where_ref, f32[2,256,256]{2,1,0:T(8,128)S(1)} %copy-done.11, f32[48,768]{1,0:T(8,128)S(1)} %project_zero_3.1.refs_0_), custom_call_target="tpu_custom_call" | custom-call | flops 1 | bytes 1 | tf_op jit(solution)/shard_map/reorder/pallas_call | solution.py:21
  107.2 2.4 %collective-permute-done.15.refs_6_.refs_7_ = f32[32,640]{1,0:T(8,128)S(1)} collective-permute-done((f32[32,640]{1,0:T(8,128)S(1)}, f32[32,640]{1,0:T(8,128)S(1)}, u32[]{:S(2)}, u32[]{:S(2)}) %collective-permute-start.15) | collective-permute-done | bytes 81952 | tf_op jit(solution)/shard_map/ppermute | solution.py:224
  109.6 5.9 %update_one.1 = (f32[4096,512]{1,0:T(8,128)S(1)}, f32[256,512]{1,0:T(8,128)S(1)}) custom-call(s32[1]{0:T(128)} %bitcast.refs_0_, f32[128,640]{1,0:T(8,128)S(1)} %add.35.refs_1_.refs_2_, f32[128,640]{1,0:T(8,128)S(1)} %collective-permute-done.3.refs_2_.refs_3_, f32[32,640]{1,0:T(8,128)S(1)} %add.37.refs_3_.refs_4_, ...), custom_call_target="tpu_custom_call" | custom-call | flops 1 | bytes 1 | tf_op jit(solution)/shard_map/update_one/pallas_call | solution.py:21
  115.6 7.7 %update_zero.1 = f32[4096,512]{1,0:T(8,128)} custom-call(s32[1]{0:T(128)} %bitcast.refs_0_, f32[256,512]{1,0:T(8,128)S(1)} %get-tuple-element.38.refs_1_, f32[128,640]{1,0:T(8,128)S(1)} %add.35.refs_1_.refs_2_, f32[128,640]{1,0:T(8,128)S(1)} %collective-permute-done.3.refs_2_.refs_3_, f32[32,640]{1,0:T(8,128)S(1)} %add.37.refs_3_.refs_4_, ...), custom_call_target="tpu_custom_call" | custom-call | flops 1 | bytes 1 | tf_op jit(solution)/shard_map/update_zero/pallas_call | solution.py:21
  (70 shorter events, 14.8 us)
Async XLA Ops:
  4.0 11.6 %copy-start.7 = (f32[2,64,4096]{2,1,0:T(8,128)S(1)}, f32[2,64,4096]{2,1,0:T(8,128)}, u32[]{:S(2)}) copy-start(f32[2,64,4096]{2,1,0:T(8,128)} %in_ref.11) | copy-start | bytes 6291460
  4.0 15.9 %collective-permute-start = (f32[128,4096]{1,0:T(8,128)S(1)}, f32[128,4096]{1,0:T(8,128)}, u32[]{:S(2)}, u32[]{:S(2)}) collective-permute-start(f32[128,4096]{1,0:T(8,128)S(1)} %cut_own.1.refs_1_.refs_3_.refs_5_.refs_4_.refs_2_.refs_8_.refs_13_), channel_id=1, source_target_pairs={{0,1},{1,0},{2,3},{3,2},{4,5},{5,4},{6,7},{7,6},{8,9},{9,8},{10,11... | collective-permute-start | bytes 6291464 | tf_op jit(solution)/shard_map/ppermute | solution.py:218
  4.5 29.9 %collective-permute-start.4 = (f32[32,4096]{1,0:T(8,128)}, f32[32,4096]{1,0:T(8,128)S(1)}, u32[]{:S(2)}, u32[]{:S(2)}) collective-permute-start(f32[32,4096]{1,0:T(8,128)} %cut_0.1.refs_0_), channel_id=1, source_target_pairs={{2,0},{3,1},{0,2},{1,3},{6,4},{7,5},{4,6},{5,7},{10,8},{11,9},{8,1... | collective-permute-start | bytes 1572872 | tf_op jit(solution)/shard_map/ppermute | solution.py:221
  12.2 3.4 %copy-start.9 = (f32[4096,512]{1,0:T(8,128)}, f32[4096,512]{1,0:T(8,128)S(1)}, u32[]{:S(2)}) copy-start(f32[4096,512]{1,0:T(8,128)S(1)} %get-tuple-element.37.refs_16_) | copy-start | bytes 25165828
  19.8 25.2 %collective-permute-start.10 = (f32[32,4096]{1,0:T(8,128)}, f32[32,4096]{1,0:T(8,128)S(1)}, u32[]{:S(2)}, u32[]{:S(2)}) collective-permute-start(f32[32,4096]{1,0:T(8,128)} %cut_1.1), channel_id=1, source_target_pairs={{2,0},{3,1},{0,2},{1,3},{6,4},{7,5},{4,6},{5,7},{10,8},{11,9},{8,1... | collective-permute-start | bytes 1572872 | tf_op jit(solution)/shard_map/ppermute | solution.py:221
  24.3 10.7 %copy-start.2 = (bf16[4096,512]{1,0:T(8,128)(2,1)S(1)}, bf16[4096,512]{1,0:T(8,128)(2,1)}, u32[]{:S(2)}) copy-start(bf16[4096,512]{1,0:T(8,128)(2,1)} %copy-done) | copy-start | bytes 12582916
  24.3 10.7 %copy-start.8 = (f32[2,64,4096]{2,1,0:T(8,128)S(1)}, f32[2,64,4096]{2,1,0:T(8,128)}, u32[]{:S(2)}) copy-start(f32[2,64,4096]{2,1,0:T(8,128)} %in_ref.11) | copy-start | bytes 6291460
  32.3 5.1 %copy-start.5 = (bf16[4096,512]{1,0:T(8,128)(2,1)S(1)}, bf16[4096,512]{1,0:T(8,128)(2,1)}, u32[]{:S(2)}) copy-start(bf16[4096,512]{1,0:T(8,128)(2,1)} %copy-done.3) | copy-start | bytes 12582916
  32.3 9.8 %collective-permute-start.1 = (f32[128,640]{1,0:T(8,128)S(1)}, f32[128,640]{1,0:T(8,128)S(1)}, u32[]{:S(2)}, u32[]{:S(2)}) collective-permute-start(f32[128,640]{1,0:T(8,128)S(1)} %get-tuple-element.27), channel_id=1, source_target_pairs={{0,4},{4,0},{8,12},{12,8},{1,5},{5,1},{9,13},{13,9},{2,6},{6,2},{1... | collective-permute-start | bytes 983048 | tf_op jit(solution)/shard_map/ppermute | solution.py:224
  34.4 3.0 %collective-permute-start.5 = (f32[16,4096]{1,0:T(8,128)S(1)}, f32[16,4096]{1,0:T(8,128)S(1)}, u32[]{:S(2)}, u32[]{:S(2)}) collective-permute-start(f32[16,4096]{1,0:T(8,128)S(1)} %get-tuple-element.44), channel_id=1, source_target_pairs={{0,1},{1,0},{2,3},{3,2},{4,5},{5,4},{6,7},{7,6},{8,9},{9,8},{10,11... | collective-permute-start | bytes 786440 | tf_op jit(solution)/shard_map/ppermute | solution.py:218
  34.5 2.9 %collective-permute-start.6 = (f32[16,4096]{1,0:T(8,128)S(1)}, f32[16,4096]{1,0:T(8,128)S(1)}, u32[]{:S(2)}, u32[]{:S(2)}) collective-permute-start(f32[16,4096]{1,0:T(8,128)S(1)} %get-tuple-element.43), channel_id=1, source_target_pairs={{0,1},{1,0},{2,3},{3,2},{4,5},{5,4},{6,7},{7,6},{8,9},{9,8},{10,11... | collective-permute-start | bytes 786440 | tf_op jit(solution)/shard_map/ppermute | solution.py:218
  35.8 16.8 %collective-permute-start.17 = (f32[40,4096]{1,0:T(8,128)S(1)}, f32[40,4096]{1,0:T(8,128)S(1)}, u32[]{:S(2)}, u32[]{:S(2)}) collective-permute-start(f32[40,4096]{1,0:T(8,128)S(1)} %cut_2.1), channel_id=1, source_target_pairs={{2,0},{3,1},{0,2},{1,3},{6,4},{7,5},{4,6},{5,7},{10,8},{11,9},{8,1... | collective-permute-start | bytes 1966088 | tf_op jit(solution)/shard_map/ppermute | solution.py:221
  42.2 16.9 %collective-permute-start.2 = (f32[128,640]{1,0:T(8,128)S(1)}, f32[128,640]{1,0:T(8,128)S(1)}, u32[]{:S(2)}, u32[]{:S(2)}) collective-permute-start(f32[128,640]{1,0:T(8,128)S(1)} %add.34), channel_id=1, source_target_pairs={{0,8},{4,12},{8,0},{12,4},{1,9},{5,13},{9,1},{13,5},{2,10},{6,14},... | collective-permute-start | bytes 983048 | tf_op jit(solution)/shard_map/ppermute | solution.py:224
  45.0 2.2 %collective-permute-start.11 = (f32[16,4096]{1,0:T(8,128)S(1)}, f32[16,4096]{1,0:T(8,128)S(1)}, u32[]{:S(2)}, u32[]{:S(2)}) collective-permute-start(f32[16,4096]{1,0:T(8,128)S(1)} %get-tuple-element.42), channel_id=1, source_target_pairs={{0,1},{1,0},{2,3},{3,2},{4,5},{5,4},{6,7},{7,6},{8,9},{9,8},{10,11... | collective-permute-start | bytes 786440 | tf_op jit(solution)/shard_map/ppermute | solution.py:218
  45.1 2.1 %collective-permute-start.12 = (f32[16,4096]{1,0:T(8,128)S(1)}, f32[16,4096]{1,0:T(8,128)S(1)}, u32[]{:S(2)}, u32[]{:S(2)}) collective-permute-start(f32[16,4096]{1,0:T(8,128)S(1)} %get-tuple-element.41), channel_id=1, source_target_pairs={{0,1},{1,0},{2,3},{3,2},{4,5},{5,4},{6,7},{7,6},{8,9},{9,8},{10,11... | collective-permute-start | bytes 786440 | tf_op jit(solution)/shard_map/ppermute | solution.py:218
  45.6 7.3 %collective-permute-start.7 = (f32[32,640]{1,0:T(8,128)S(1)}, f32[32,640]{1,0:T(8,128)S(1)}, u32[]{:S(2)}, u32[]{:S(2)}) collective-permute-start(f32[32,640]{1,0:T(8,128)S(1)} %get-tuple-element.30), channel_id=1, source_target_pairs={{0,4},{4,0},{8,12},{12,8},{1,5},{5,1},{9,13},{13,9},{2,6},{6,2},{1... | collective-permute-start | bytes 245768 | tf_op jit(solution)/shard_map/ppermute | solution.py:224
  59.1 6.7 %collective-permute-start.18 = (f32[40,4096]{1,0:T(8,128)S(1)}, f32[40,4096]{1,0:T(8,128)S(1)}, u32[]{:S(2)}, u32[]{:S(2)}) collective-permute-start(f32[40,4096]{1,0:T(8,128)S(1)} %collective-permute-done.17.refs_0_.refs_15_), channel_id=1, source_target_pairs={{0,1},{1,0},{2,3},{3,2},{4,5},{5,4},{6,7},{7,6},{8,9},{9,8},{10,11... | collective-permute-start | bytes 1966088 | tf_op jit(solution)/shard_map/ppermute | solution.py:218
  60.0 11.6 %collective-permute-start.16 = (f32[24,4096]{1,0:T(8,128)S(1)}, f32[24,4096]{1,0:T(8,128)S(1)}, u32[]{:S(2)}, u32[]{:S(2)}) collective-permute-start(f32[24,4096]{1,0:T(8,128)S(1)} %cut_3.1), channel_id=1, source_target_pairs={{2,0},{3,1},{0,2},{1,3},{6,4},{7,5},{4,6},{5,7},{10,8},{11,9},{8,1... | collective-permute-start | bytes 1179656 | tf_op jit(solution)/shard_map/ppermute | solution.py:221
  61.5 13.4 %collective-permute-start.3 = (f32[128,640]{1,0:T(8,128)S(1)}, f32[128,640]{1,0:T(8,128)S(1)}, u32[]{:S(2)}, u32[]{:S(2)}) collective-permute-start(f32[128,640]{1,0:T(8,128)S(1)} %add.35.refs_1_.refs_2_), channel_id=1, source_target_pairs={{0,4},{4,0},{8,12},{12,8},{1,5},{5,1},{9,13},{13,9},{2,6},{6,2},{1... | collective-permute-start | bytes 983048 | tf_op jit(solution)/shard_map/ppermute | solution.py:224
  62.3 9.8 %collective-permute-start.8 = (f32[32,640]{1,0:T(8,128)S(1)}, f32[32,640]{1,0:T(8,128)S(1)}, u32[]{:S(2)}, u32[]{:S(2)}) collective-permute-start(f32[32,640]{1,0:T(8,128)S(1)} %add.36), channel_id=1, source_target_pairs={{0,8},{4,12},{8,0},{12,4},{1,9},{5,13},{9,1},{13,5},{2,10},{6,14},... | collective-permute-start | bytes 245768 | tf_op jit(solution)/shard_map/ppermute | solution.py:224
  65.7 9.2 %collective-permute-start.13 = (f32[32,640]{1,0:T(8,128)S(1)}, f32[32,640]{1,0:T(8,128)S(1)}, u32[]{:S(2)}, u32[]{:S(2)}) collective-permute-start(f32[32,640]{1,0:T(8,128)S(1)} %get-tuple-element.33), channel_id=1, source_target_pairs={{0,4},{4,0},{8,12},{12,8},{1,5},{5,1},{9,13},{13,9},{2,6},{6,2},{1... | collective-permute-start | bytes 245768 | tf_op jit(solution)/shard_map/ppermute | solution.py:224
  65.7 43.9 %slice-start = ((s8[8388608]{0:T(1024)(128)(4,1)}), s8[4194304]{0:T(1024)(128)(4,1)S(1)}, s32[]{:S(2)}) async-start(s8[8388608]{0:T(1024)(128)(4,1)} %bitcast.5), calls=%async_computation | async-start | bytes 8388608
  70.2 35.0 %copy-start.11 = (f32[2,256,256]{2,1,0:T(8,128)S(1)}, f32[2,256,256]{2,1,0:T(8,128)}, u32[]{:S(2)}) copy-start(f32[2,256,256]{2,1,0:T(8,128)} %in_ref.12) | copy-start | bytes 1572868
  70.3 39.4 %slice-start.1 = ((s8[8388608]{0:T(1024)(128)(4,1)}), s8[4194304]{0:T(1024)(128)(4,1)S(1)}, s32[]{:S(2)}) async-start(s8[8388608]{0:T(1024)(128)(4,1)} %bitcast.5), calls=%async_computation.1 | async-start | bytes 8388608
  74.9 1.7 %collective-permute-start.19 = (f32[24,4096]{1,0:T(8,128)S(1)}, f32[24,4096]{1,0:T(8,128)S(1)}, u32[]{:S(2)}, u32[]{:S(2)}) collective-permute-start(f32[24,4096]{1,0:T(8,128)S(1)} %collective-permute-done.16.refs_0_.refs_17_), channel_id=1, source_target_pairs={{0,1},{1,0},{2,3},{3,2},{4,5},{5,4},{6,7},{7,6},{8,9},{9,8},{10,11... | collective-permute-start | bytes 1179656 | tf_op jit(solution)/shard_map/ppermute | solution.py:218
  74.9 8.4 %collective-permute-start.20 = (f32[80,768]{1,0:T(8,128)S(1)}, f32[80,768]{1,0:T(8,128)S(1)}, u32[]{:S(2)}, u32[]{:S(2)}) collective-permute-start(f32[80,768]{1,0:T(8,128)S(1)} %project_zero_2.1), channel_id=1, source_target_pairs={{0,4},{4,0},{8,12},{12,8},{1,5},{5,1},{9,13},{13,9},{2,6},{6,2},{1... | collective-permute-start | bytes 737288 | tf_op jit(solution)/shard_map/ppermute | solution.py:224
  81.0 7.6 %collective-permute-start.22 = (f32[48,768]{1,0:T(8,128)S(1)}, f32[48,768]{1,0:T(8,128)S(1)}, u32[]{:S(2)}, u32[]{:S(2)}) collective-permute-start(f32[48,768]{1,0:T(8,128)S(1)} %project_zero_3.1.refs_0_), channel_id=1, source_target_pairs={{0,4},{4,0},{8,12},{12,8},{1,5},{5,1},{9,13},{13,9},{2,6},{6,2},{1... | collective-permute-start | bytes 442376 | tf_op jit(solution)/shard_map/ppermute | solution.py:224
  83.3 32.2 %collective-permute-start.21 = (f32[80,768]{1,0:T(8,128)S(1)}, f32[80,768]{1,0:T(8,128)S(1)}, u32[]{:S(2)}, u32[]{:S(2)}) collective-permute-start(f32[80,768]{1,0:T(8,128)S(1)} %add.40.refs_8_), channel_id=1, source_target_pairs={{0,8},{4,12},{8,0},{12,4},{1,9},{5,13},{9,1},{13,5},{2,10},{6,14},... | collective-permute-start | bytes 737288 | tf_op jit(solution)/shard_map/ppermute | solution.py:224
  85.7 19.4 %collective-permute-start.14 = (f32[32,640]{1,0:T(8,128)S(1)}, f32[32,640]{1,0:T(8,128)S(1)}, u32[]{:S(2)}, u32[]{:S(2)}) collective-permute-start(f32[32,640]{1,0:T(8,128)S(1)} %add.38), channel_id=1, source_target_pairs={{0,8},{4,12},{8,0},{12,4},{1,9},{5,13},{9,1},{13,5},{2,10},{6,14},... | collective-permute-start | bytes 245768 | tf_op jit(solution)/shard_map/ppermute | solution.py:224
  88.6 27.0 %collective-permute-start.23 = (f32[48,768]{1,0:T(8,128)S(1)}, f32[48,768]{1,0:T(8,128)S(1)}, u32[]{:S(2)}, u32[]{:S(2)}) collective-permute-start(f32[48,768]{1,0:T(8,128)S(1)} %add.41.refs_10_), channel_id=1, source_target_pairs={{0,8},{4,12},{8,0},{12,4},{1,9},{5,13},{9,1},{13,5},{2,10},{6,14},... | collective-permute-start | bytes 442376 | tf_op jit(solution)/shard_map/ppermute | solution.py:224
  90.1 17.1 %collective-permute-start.9 = (f32[32,640]{1,0:T(8,128)S(1)}, f32[32,640]{1,0:T(8,128)S(1)}, u32[]{:S(2)}, u32[]{:S(2)}) collective-permute-start(f32[32,640]{1,0:T(8,128)S(1)} %add.37.refs_3_.refs_4_), channel_id=1, source_target_pairs={{0,4},{4,0},{8,12},{12,8},{1,5},{5,1},{9,13},{13,9},{2,6},{6,2},{1... | collective-permute-start | bytes 245768 | tf_op jit(solution)/shard_map/ppermute | solution.py:224
  105.1 4.5 %collective-permute-start.15 = (f32[32,640]{1,0:T(8,128)S(1)}, f32[32,640]{1,0:T(8,128)S(1)}, u32[]{:S(2)}, u32[]{:S(2)}) collective-permute-start(f32[32,640]{1,0:T(8,128)S(1)} %add.39.refs_5_.refs_6_), channel_id=1, source_target_pairs={{0,4},{4,0},{8,12},{12,8},{1,5},{5,1},{9,13},{13,9},{2,6},{6,2},{1... | collective-permute-start | bytes 245768 | tf_op jit(solution)/shard_map/ppermute | solution.py:224
  (6 other events, 13.5 us)

commit v4 on v3

v4 whole, which is shorter than its diff:
```python
import jax
import jax.numpy as jnp
from jax import lax
from jax.experimental import pallas as pl
from jax.experimental.pallas import tpu as pltpu
from jax.sharding import PartitionSpec as P

F32, BF16 = jnp.float32, jnp.bfloat16
PIECES = ((1, 0, 32, True), (1, 32, 64, True), (0, 0, 48, True), (0, 48, 64, False))
SWAP_PARTS = 2
NN = (((1,), (0,)), ((), ()))
NT = (((1,), (1,)), ((), ()))
TN = (((0,), (0,)), ((), ()))
SCALARS = pl.BlockSpec(memory_space=pltpu.SMEM)
VMEM = pl.BlockSpec(memory_space=pltpu.VMEM)
HBM = pl.BlockSpec(memory_space=pltpu.HBM)


def call(body, name, ins, specs, outs, out_specs, scratch=(), mib=8):
    return pl.pallas_call(
        body,
        in_specs=specs,
        out_specs=out_specs,
        out_shape=outs,
        scratch_shapes=list(scratch),
        compiler_params=pltpu.CompilerParams(vmem_limit_bytes=mib * 1024 * 1024),
        cost_estimate=pl.CostEstimate(flops=1, bytes_accessed=1, transcendentals=0),
        name=name,
    )(*ins)


def array(*shape, dtype=F32):
    return jax.ShapeDtypeStruct(shape, dtype)


def split(value):
    high = value.astype(BF16)
    return high, (value - high.astype(F32)).astype(BF16)


def dot(a, b, dims=NN):
    return lax.dot_general(a, b, dims, preferred_element_type=F32)


def full_dot(a, b, dims=NN):
    return lax.dot_general(a, b, dims, precision=lax.Precision.HIGHEST, preferred_element_type=F32)


def three(vh, vl, bh, bl, dims):
    rows = vh.shape[0]
    first = dot(jnp.concatenate([vh, vl]), bh, dims)
    return first[:rows] + first[rows:] + dot(vh, bl, dims)


def steps_of(here, step):
    step = min(here, step)
    return [pl.ds(at, step) for at in range(0, here, step)]


def cut(where, vectors, first):
    _, share, here = vectors.shape
    block, low, high = first
    begin = (1 - block) * share + low

    def body(where_ref, in_ref, piece, mine, sems):
        copies = [
            pltpu.make_async_copy(in_ref.at[k], mine.at[(1 - k) * share : (2 - k) * share], sems.at[k]) for k in (0, 1)
        ]
        copies[1].start()
        copies[0].start()
        for k in (1, 0):
            copies[k].wait()
            shape = (share, here)
            along = lax.broadcasted_iota(jnp.int32, shape, 0) + (where_ref[0] + k * where_ref[2])
            across = lax.broadcasted_iota(jnp.int32, shape, 1) + where_ref[1]
            rows = slice((1 - k) * share, (2 - k) * share)
            mine[rows] = jnp.where(across >= along, mine[rows], 0.0)
        piece[...] = mine[begin : begin + high - low]

    outs = [array(high - low, here), array(2 * share, here)]
    return call(body, "cut", (where, vectors), [SCALARS, HBM], outs, [VMEM] * 2, [pltpu.SemaphoreType.DMA((2,))], 56)


def parts_of(mine, places):
    here = mine.shape[1]

    def body(in_ref, *refs):
        for (low, high), out in zip(places, refs):
            out[...] = in_ref[low:high]

    outs = [array(high - low, here) for low, high in places]
    return call(body, "parts", (mine,), [VMEM], outs, [VMEM] * len(outs), mib=2)


def load(eigvecs):
    here, nc = eigvecs.shape
    steps = steps_of(here, 512)

    def body(in_ref, high, low, held, sems):
        copies = [pltpu.make_async_copy(in_ref.at[ds], held.at[ds], sems.at[n]) for n, ds in enumerate(steps)]
        for copy in copies:
            copy.start()
        for copy, ds in zip(copies, steps):
            copy.wait()
            high[ds, :], low[ds, :] = split(held[ds, :])

    scratch = [pltpu.VMEM((here, nc), F32), pltpu.SemaphoreType.DMA((len(steps),))]
    return call(body, "load", (eigvecs,), [HBM], [array(here, nc, dtype=BF16)] * 2, [VMEM] * 2, scratch, 44)


def rows_of(refs, pieces, ds):
    return jnp.concatenate([ref[at : at + count, ds] for ref, (_, count, at) in zip(refs, pieces)])


def project(name, rows, partners, high, low, bit=None, gram_rows=None):
    here, nc = high.shape
    height = sum(count for _, count, _ in rows)
    extra = sum(count for _, count, _ in partners)
    some = height if gram_rows is None else gram_rows
    steps = steps_of(here, 512)

    def body(*refs):
        refs = list(refs)
        acc = refs.pop()
        bit_ref = refs.pop(0) if bit is not None else None
        row_refs, refs = refs[: len(rows)], refs[len(rows) :]
        partner_refs, refs = refs[: len(partners)], refs[len(partners) :]
        high_ref, low_ref = refs[:2]
        outs = refs[2:]
        for n, ds in enumerate(steps):
            vh, vl = split(rows_of(row_refs, rows, ds))
            main = three(vh, vl, high_ref[ds, :], low_ref[ds, :], NN)
            gram = three(vh[:some], vl[:some], *split(rows_of(partner_refs, partners, ds)), NT)
            if n == 0:
                acc[:, :nc], acc[:some, nc:] = main, gram
                if some < height:
                    acc[some:, nc:] = jnp.zeros((height - some, extra), F32)
            else:
                acc[:, :nc] += main
                acc[:some, nc:] += gram
        if bit is None:
            outs[0][...] = acc[...]
        else:
            half = height // 2
            zero = bit_ref[5] == 0
            outs[0][...] = jnp.where(zero, acc[:half], acc[half:])
            outs[1][...] = jnp.where(zero, acc[half:], acc[:half])

    outputs = 1 if bit is None else 2
    arrays = [r[0] for r in rows + partners] + [high, low]
    return call(
        body,
        name,
        ([] if bit is None else [bit]) + arrays,
        ([] if bit is None else [SCALARS]) + [VMEM] * len(arrays),
        [array(height // outputs, nc + extra)] * outputs,
        [VMEM] * outputs,
        [pltpu.VMEM((height, nc + extra), F32)],
    )


def reorder(where, factors, share, chips, segments):
    width = factors.shape[1]

    def body(where_ref, in_ref, *outs):
        chip, core = where_ref[3], where_ref[4]
        for block, out in enumerate(outs):
            picks = []
            for step, other, low, high in segments[block]:
                at = (lax.rem(chip + step, chips) * 2 + (core + other) % 2) * share + low
                shape = (high - low, width)
                same = lax.broadcasted_iota(jnp.int32, shape, 1) == lax.broadcasted_iota(jnp.int32, shape, 0) + at
                picks.append(jnp.where(same, 1.0, 0.0))
            pick = jnp.concatenate(picks)
            out[...] = full_dot(full_dot(pick, in_ref[block]), pick, NT)

    return call(body, "reorder", (where, factors), [SCALARS, VMEM], [array(width, width)] * 2, [VMEM] * 2)


def update(name, make, ins, factor, pieces, current, last):
    here, nc = current.shape
    width = factor.shape[0]
    steps = steps_of(here, 256)

    def body(*refs):
        in_refs, refs = refs[: len(ins)], refs[len(ins) :]
        factor_ref, refs = refs[0], refs[1:]
        piece_refs, refs = refs[: len(pieces)], refs[len(pieces) :]
        cur_ref, out = refs[:2]
        loads = []
        if not last:
            held, sems = refs[3:]
            loads = [pltpu.make_async_copy(cur_ref.at[ds], held.at[ds], sems.at[n]) for n, ds in enumerate(steps)]
            for copy in loads:
                copy.start()
            cur_ref = held
        scaled = full_dot(factor_ref[...], make(*in_refs))
        sh, sl = split(scaled)
        if not last:
            refs[2][...] = scaled
        copies = []
        for n, ds in enumerate(steps):
            vh, vl = split(rows_of(piece_refs, pieces, ds))
            if loads:
                loads[n].wait()
            new = cur_ref[ds, :] - (dot(vh, sh, TN) + dot(vh, sl, TN) + dot(vl, sh, TN))
            if last:
                held, sems = refs[2:]
                held[ds, :] = new
                copies.append(pltpu.make_async_copy(held.at[ds], out.at[ds], sems.at[n]))
                copies[-1].start()
            else:
                out[ds, :] = new
        for copy in copies:
            copy.wait()

    specs = [SCALARS if v.dtype == jnp.int32 else VMEM for v in ins] + [VMEM] * (len(pieces) + 1)
    specs.append(VMEM if last else HBM)
    args = [*ins, factor, *[p[0] for p in pieces], current]
    scratch = [pltpu.VMEM((here, nc), F32), pltpu.SemaphoreType.DMA((len(steps),))]
    if last:
        return call(body, name, args, specs, array(here, nc), HBM, scratch, 13)
    return call(body, name, args, specs, [array(here, nc), array(width, nc)], [VMEM] * 2, scratch, 13)


def make_local(chips, rows):
    cols = 2 * chips

    def core_swap(value):
        return lax.ppermute(value, "col", [(i, i ^ 1) for i in range(cols)])

    def from_chip(value, step):
        return lax.ppermute(value, "col", [((i + 2 * step) % cols, i) for i in range(cols)])

    def row_swap(value, step):
        return lax.ppermute(value, "row", [(i, i ^ step) for i in range(rows)])

    def sums(value, send=None):
        step, got = 1, None
        if send is not None:
            got = row_swap(send, 1)
            yield got
            step = 2
        while step < rows:
            value = value if got is None else value + got
            got = row_swap(value, step)
            yield got
            step *= 2
        if send is not None:
            value = value + got
            got = row_swap(value, 1)
            yield got
        return value, got

    def local(vectors, factors, eigvecs):
        share, here = vectors.shape[1:]
        nc = eigvecs.shape[1]
        width = share * cols
        half = 2 * share
        col, row = lax.axis_index("col"), lax.axis_index("row")
        where = jnp.stack([col * share, row * here, jnp.int32(width), col // 2, col % 2, row % 2]).astype(jnp.int32)
        bit = where
        pieces = []
        for block, low, high, _ in PIECES:
            low, high = low * share // 64 // 8 * 8, high * share // 64 // 8 * 8
            pieces.append((block, low, high))
        halves = {piece: chosen for piece, (*_, chosen) in zip(pieces, PIECES)}

        def after(value, *others):
            return lax.optimization_barrier((value, *others))[0]

        sent, mine = cut(where, vectors, pieces[0])
        far = [(step, pieces[0], from_chip(sent, step)) for step in range(1, chips)]
        sib = core_swap(mine)
        high, low = load(after(eigvecs, mine))
        places = [((1 - block) * share + a, (1 - block) * share + b) for block, a, b in pieces[1:]]
        for piece, sent in zip(pieces[1:], parts_of(after(mine, high), places)):
            far += [(step, piece, from_chip(sent, step)) for step in range(1, chips)]
        own = {1: [(mine, share, 0), (sib, share, 0)], 0: [(mine, share, share), (sib, share, share)]}
        segments = {k: [(0, 0, 0, share), (0, 1, 0, share)] for k in (0, 1)}
        all_ones, all_zeros = list(own[1]), list(own[0])
        running, done, waits = [], {}, ()

        def advance():
            got = []
            for key, chain in list(running):
                try:
                    got.append(next(chain))
                except StopIteration as end:
                    done[key] = end.value
                    running.remove((key, chain))
            return got

        front = project("project_own", own[1] + own[0], own[0], high, low, bit, half)
        running.append(("own", sums(*front)))
        for n, (step, (block, first, final), value) in enumerate(far):
            value = after(value, *front, *waits)
            waits = advance()
            split_rows = halves[block, first, final]
            pair = [(value, final - first, 0)]
            parts = SWAP_PARTS if (final - first) % (8 * SWAP_PARTS) == 0 else 1
            each = (final - first) // parts
            for part in range(parts):
                pair.append((core_swap(value[part * each : (part + 1) * each]), each, 0))
            segments[block] += [(step, 0, first, final), (step, 1, first, final)]
            if block == 1:
                all_ones += pair
                front = project(f"project_one_{n}", pair, own[0], high, low, bit if split_rows else None)
            else:
                all_zeros += pair
                front = project(f"project_zero_{n}", pair, all_ones, high, low, bit if split_rows else None)
            running.append((n, sums(*front)))
        while running:
            advance()
        ones = [("own", True)] + [(n, halves[f[1]]) for n, f in enumerate(far) if f[1][0] == 1]
        zeros = [(n, halves[f[1]]) for n, f in enumerate(far) if f[1][0] == 0]
        t0, t1 = reorder(where, after(factors, *front), share, chips, segments)
        ones_flat, zeros_flat = ([v for key, _ in group for v in done[key]] for group in (ones, zeros))

        def joined(where_ref, refs, group, columns):
            parts = []
            zero = where_ref[5] == 0
            for a, b, (_, chosen) in zip(refs[::2], refs[1::2], group):
                a, b = a[:, columns], b[:, columns]
                parts += [jnp.where(zero, a, b), jnp.where(zero, b, a)] if chosen else [a + b]
            return parts

        def make_one(where_ref, *refs):
            parts = joined(where_ref, refs, ones, slice(0, nc))
            return jnp.concatenate(parts[:1] + parts[2:])

        def make_zero(where_ref, scaled_ref, *refs):
            ones_refs, zero_refs = refs[: len(ones_flat)], refs[len(ones_flat) :]
            scaled = scaled_ref[...]
            parts = joined(where_ref, ones_refs, ones, slice(nc, nc + half))
            turned_gram = jnp.concatenate(parts[:1] + parts[2:])
            front = joined(where_ref, ones_refs[:2], ones[:1], slice(0, nc))[1] - full_dot(turned_gram, scaled, TN)
            later = jnp.concatenate(joined(where_ref, zero_refs, zeros, slice(None)))
            return jnp.concatenate([front, later[:, :nc] - full_dot(later[:, nc:], scaled)])

        current, scaled = update("update_one", make_one, [bit, *ones_flat], t1, all_ones, eigvecs, False)
        ins = [bit, scaled, *ones_flat, *zeros_flat]
        return update("update_zero", make_zero, ins, t0, all_zeros, current, True)

    return local


def solution(mesh):
    placed = (P("groups", "col", "row"), P("groups", None, None), P(("groups", "row"), "col"))
    local = make_local(mesh.shape["col"] // 2, mesh.shape["row"])
    return jax.shard_map(
        local, mesh=mesh, in_specs=placed, out_specs=P(("groups", "row"), "col"), check_vma=False
    )
```

time: 124 us -> 106 us (0.85)
  local copies, waits for them, and re-layouts: 15.2 us -> 4.13 us
  starting transfers between devices: 25.7 us -> 34.2 us
  waiting for transfers between devices: 34.3 us -> 26 us
  Pallas kernels: 47.7 us -> 40.9 us
    ppermute x13 -> x14, waiting for transfers between devices: 30.6 us -> 9.83 us  [row_swap(): return lax.ppermute(value, 'row', [(i, i ^ step) for i in range(rows)])]
    ppermute x4, waiting for transfers between devices: 2.96 us -> 16.1 us  [from_chip(): lax.ppermute(value, 'col', [((i + 2 * step) % cols, i) for i in range(col...]
    unnamed x28 -> x8, local copies, waits for them, and re-layouts: 15 us -> 3.4 us
    pallas_call x14 -> x11, Pallas kernels: 47.7 us -> 40.9 us  [call(): pl.pallas_call(body, in_specs=specs, out_specs=out_specs, out_shape=outs,...]
    ppermute x13 -> x14, starting transfers between devices: 18.4 us -> 24.9 us  [row_swap(): return lax.ppermute(value, 'row', [(i, i ^ step) for i in range(rows)])]
    ppermute x7 -> x9, starting transfers between devices: 1.66 us -> 2.79 us  [core_swap(): return lax.ppermute(value, 'col', [(i, i ^ 1) for i in range(cols)])]
  transfers between devices with their start and end apart: 24 -> 27, of which waited for: 12 -> 10; matrix products, arithmetic and copies ran while one was open for 0% -> 0% of each run, Pallas kernels for 31% -> 29%
where the time goes in v4:
time: 106 us
  Pallas kernels  40.9 us (39%)
  starting transfers between devices  34.2 us (32%)
  waiting for transfers between devices  26 us (25%)
  local copies, waits for them, and re-layouts  4.13 us (4%)
    pallas_call x11, Pallas kernels, call(): pl.pallas_call(body, in_specs=specs, out_specs=out_specs, out_shape=outs,...  40.9 us
    ppermute x14, starting transfers between devices, row_swap(): return lax.ppermute(value, 'row', [(i, i ^ step) for i in range(rows)])  24.9 us
    ppermute x4, waiting for transfers between devices, from_chip(): lax.ppermute(value, 'col', [((i + 2 * step) % cols, i) for i in range(col...  16.1 us
    ppermute x14, waiting for transfers between devices, row_swap(): return lax.ppermute(value, 'row', [(i, i ^ step) for i in range(rows)])  9.83 us
    ppermute x4, starting transfers between devices, from_chip(): lax.ppermute(value, 'col', [((i + 2 * step) % cols, i) for i in range(col...  6.43 us
    unnamed x8, local copies, waits for them, and re-layouts  3.4 us
    ppermute x9, starting transfers between devices, core_swap(): return lax.ppermute(value, 'col', [(i, i ^ 1) for i in range(cols)])  2.79 us
  transfers between devices with their start and end apart: 27, of which 10 were waited for; matrix products, arithmetic and copies ran while one was open for 0% of the time, Pallas kernels for 29%

profile of v4, /device:TPU:0, one launch (start us, length us, event | category | flops | bytes accessed | tf_op | source)
XLA Modules:
  0.0 105.7 jit_solution(12351116582680707261)
XLA Ops:
  0.6 3.8 %cut.1 = (f32[32,4096]{1,0:T(8,128)}, f32[128,4096]{1,0:T(8,128)}) custom-call(s32[6]{0:T(128)} %stack.23.where_ref.refs_0_, f32[2,64,4096]{2,1,0:T(8,128)} %in_ref.1), custom_call_target="tpu_custom_call" | custom-call | flops 1 | bytes 1 | tf_op jit(solution)/shard_map/cut/pallas_call | solution.py:20
  4.9 2.6 %collective-permute-start.4 = (f32[32,4096]{1,0:T(8,128)}, f32[32,4096]{1,0:T(8,128)S(1)}, u32[]{:S(2)}, u32[]{:S(2)}) collective-permute-start(f32[32,4096]{1,0:T(8,128)} %get-tuple-element.37), channel_id=1, source_target_pairs={{2,0},{3,1},{0,2},{1,3},{6,4},{7,5},{4,6},{5,7},{10,8},{11,9},{8,1... | collective-permute-start | bytes 1572872 | tf_op jit(solution)/shard_map/ppermute | solution.py:233
  7.5 3.6 %load.1 = (bf16[4096,512]{1,0:T(8,128)(2,1)S(1)}, bf16[4096,512]{1,0:T(8,128)(2,1)S(1)}) custom-call(f32[4096,512]{1,0:T(8,128)} %refs_16_.1), custom_call_target="tpu_custom_call" | custom-call | flops 1 | bytes 1 | tf_op jit(solution)/shard_map/load/pallas_call | solution.py:20
  11.7 4.8 %project_own.1 = (f32[128,640]{1,0:T(8,128)S(1)}, f32[128,640]{1,0:T(8,128)S(1)}) custom-call(s32[6]{0:T(128)S(1)} %copy-done.3, f32[128,4096]{1,0:T(8,128)S(1)} %copy-done, f32[128,4096]{1,0:T(8,128)S(1)} %collective-permute-done.refs_2_.refs_4_.refs_6_.refs_5_.refs_9_.refs_14_, f32[128,4096]{1,0:T(8,128)S(1)} %copy-done, ...), custom_call_target="tpu_custom_call" | custom-call | flops 1 | bytes 1 | tf_op jit(solution)/shard_map/project_own/pallas_call | solution.py:20
  16.4 1.9 %collective-permute-start.1 = (f32[128,640]{1,0:T(8,128)S(1)}, f32[128,640]{1,0:T(8,128)S(1)}, u32[]{:S(2)}, u32[]{:S(2)}) collective-permute-start(f32[128,640]{1,0:T(8,128)S(1)} %get-tuple-element.36), channel_id=1, source_target_pairs={{0,4},{4,0},{8,12},{12,8},{1,5},{5,1},{9,13},{13,9},{2,6},{6,2},{1... | collective-permute-start | bytes 983048 | tf_op jit(solution)/shard_map/ppermute | solution.py:236
  18.3 2.2 %collective-permute-done.4.refs_1_.refs_6_.refs_5_.refs_10_ = f32[32,4096]{1,0:T(8,128)S(1)} collective-permute-done((f32[32,4096]{1,0:T(8,128)}, f32[32,4096]{1,0:T(8,128)S(1)}, u32[]{:S(2)}, u32[]{:S(2)}) %collective-permute-start.4) | collective-permute-done | bytes 524320 | tf_op jit(solution)/shard_map/ppermute | solution.py:233
  21.1 2.0 %collective-permute-start.17 = (f32[48,4096]{1,0:T(8,128)S(1)}, f32[48,4096]{1,0:T(8,128)S(1)}, u32[]{:S(2)}, u32[]{:S(2)}) collective-permute-start(f32[48,4096]{1,0:T(8,128)S(1)} %get-tuple-element.47), channel_id=1, source_target_pairs={{2,0},{3,1},{0,2},{1,3},{6,4},{7,5},{4,6},{5,7},{10,8},{11,9},{8,1... | collective-permute-start | bytes 2359304 | tf_op jit(solution)/shard_map/ppermute | solution.py:233
  23.1 2.7 %project_one_0.1 = (f32[32,640]{1,0:T(8,128)S(1)}, f32[32,640]{1,0:T(8,128)S(1)}) custom-call(s32[6]{0:T(128)S(1)} %copy-done.3, f32[32,4096]{1,0:T(8,128)S(1)} %collective-permute-done.4.refs_1_.refs_6_.refs_5_.refs_10_, f32[16,4096]{1,0:T(8,128)S(1)} %collective-permute-done.5.refs_2_.refs_7_.refs_6_.refs_11_, ...), custom_call_target="tpu_custom_call" | custom-call | flops 1 | bytes 1 | tf_op jit(solution)/shard_map/project_one_0/pallas_call | solution.py:20
  26.4 2.7 %collective-permute-start.2 = (f32[128,640]{1,0:T(8,128)S(1)}, f32[128,640]{1,0:T(8,128)S(1)}, u32[]{:S(2)}, u32[]{:S(2)}) collective-permute-start(f32[128,640]{1,0:T(8,128)S(1)} %add.37), channel_id=1, source_target_pairs={{0,8},{4,12},{8,0},{12,4},{1,9},{5,13},{9,1},{13,5},{2,10},{6,14},... | collective-permute-start | bytes 983048 | tf_op jit(solution)/shard_map/ppermute | solution.py:236
  29.0 2.7 %collective-permute-done.10.refs_1_.refs_9_.refs_8_.refs_13_ = f32[32,4096]{1,0:T(8,128)S(1)} collective-permute-done((f32[32,4096]{1,0:T(8,128)S(1)}, f32[32,4096]{1,0:T(8,128)S(1)}, u32[]{:S(2)}, u32[]{:S(2)}) %collective-permute-start.10) | collective-permute-done | bytes 524320 | tf_op jit(solution)/shard_map/ppermute | solution.py:233
  32.3 2.0 %collective-permute-start.7 = (f32[32,640]{1,0:T(8,128)S(1)}, f32[32,640]{1,0:T(8,128)S(1)}, u32[]{:S(2)}, u32[]{:S(2)}) collective-permute-start(f32[32,640]{1,0:T(8,128)S(1)} %get-tuple-element.40), channel_id=1, source_target_pairs={{0,4},{4,0},{8,12},{12,8},{1,5},{5,1},{9,13},{13,9},{2,6},{6,2},{1... | collective-permute-start | bytes 245768 | tf_op jit(solution)/shard_map/ppermute | solution.py:236
  34.4 2.7 %project_one_1.1 = (f32[32,640]{1,0:T(8,128)S(1)}, f32[32,640]{1,0:T(8,128)S(1)}) custom-call(s32[6]{0:T(128)S(1)} %copy-done.3, f32[32,4096]{1,0:T(8,128)S(1)} %collective-permute-done.10.refs_1_.refs_9_.refs_8_.refs_13_, f32[16,4096]{1,0:T(8,128)S(1)} %collective-permute-done.11.refs_2_.refs_10_.refs_9_.refs_14_, ...), custom_call_target="tpu_custom_call" | custom-call | flops 1 | bytes 1 | tf_op jit(solution)/shard_map/project_one_1/pallas_call | solution.py:20
  37.1 11.2 %collective-permute-done.17.refs_1_.refs_15_ = f32[48,4096]{1,0:T(8,128)S(1)} collective-permute-done((f32[48,4096]{1,0:T(8,128)S(1)}, f32[48,4096]{1,0:T(8,128)S(1)}, u32[]{:S(2)}, u32[]{:S(2)}) %collective-permute-start.17) | collective-permute-done | bytes 786464 | tf_op jit(solution)/shard_map/ppermute | solution.py:233
  49.0 1.9 %collective-permute-start.3 = (f32[128,640]{1,0:T(8,128)S(1)}, f32[128,640]{1,0:T(8,128)S(1)}, u32[]{:S(2)}, u32[]{:S(2)}) collective-permute-start(f32[128,640]{1,0:T(8,128)S(1)} %add.38.refs_1_.refs_2_), channel_id=1, source_target_pairs={{0,4},{4,0},{8,12},{12,8},{1,5},{5,1},{9,13},{13,9},{2,6},{6,2},{1... | collective-permute-start | bytes 983048 | tf_op jit(solution)/shard_map/ppermute | solution.py:236
  50.9 1.5 %collective-permute-start.16 = (f32[16,4096]{1,0:T(8,128)S(1)}, f32[16,4096]{1,0:T(8,128)S(1)}, u32[]{:S(2)}, u32[]{:S(2)}) collective-permute-start(f32[16,4096]{1,0:T(8,128)S(1)} %get-tuple-element.46), channel_id=1, source_target_pairs={{2,0},{3,1},{0,2},{1,3},{6,4},{7,5},{4,6},{5,7},{10,8},{11,9},{8,1... | collective-permute-start | bytes 786440 | tf_op jit(solution)/shard_map/ppermute | solution.py:233
  52.4 2.7 %collective-permute-start.8 = (f32[32,640]{1,0:T(8,128)S(1)}, f32[32,640]{1,0:T(8,128)S(1)}, u32[]{:S(2)}, u32[]{:S(2)}) collective-permute-start(f32[32,640]{1,0:T(8,128)S(1)} %add.39), channel_id=1, source_target_pairs={{0,8},{4,12},{8,0},{12,4},{1,9},{5,13},{9,1},{13,5},{2,10},{6,14},... | collective-permute-start | bytes 245768 | tf_op jit(solution)/shard_map/ppermute | solution.py:236
  55.5 3.7 %project_zero_2.1 = (f32[48,768]{1,0:T(8,128)S(1)}, f32[48,768]{1,0:T(8,128)S(1)}) custom-call(s32[6]{0:T(128)S(1)} %copy-done.3, f32[48,4096]{1,0:T(8,128)S(1)} %collective-permute-done.17.refs_1_.refs_15_, f32[24,4096]{1,0:T(8,128)S(1)} %collective-permute-done.18.refs_2_.refs_16_, f32[24,4096]{1,0:T(8,128)S(1)} %collective-permute-done.19.refs_3_.refs_17_, ...), custom_call_target="tpu_custom_call" | custom-call | flops 1 | bytes 1 | tf_op jit(solution)/shard_map/project_zero_2/pallas_call | solution.py:20
  59.2 1.7 %collective-permute-start.22 = (f32[48,768]{1,0:T(8,128)S(1)}, f32[48,768]{1,0:T(8,128)S(1)}, u32[]{:S(2)}, u32[]{:S(2)}) collective-permute-start(f32[48,768]{1,0:T(8,128)S(1)} %get-tuple-element.50), channel_id=1, source_target_pairs={{0,4},{4,0},{8,12},{12,8},{1,5},{5,1},{9,13},{13,9},{2,6},{6,2},{1... | collective-permute-start | bytes 442376 | tf_op jit(solution)/shard_map/ppermute | solution.py:236
  60.8 2.3 %collective-permute-done.13 = f32[32,640]{1,0:T(8,128)S(1)} collective-permute-done((f32[32,640]{1,0:T(8,128)S(1)}, f32[32,640]{1,0:T(8,128)S(1)}, u32[]{:S(2)}, u32[]{:S(2)}) %collective-permute-start.13) | collective-permute-done | bytes 81952 | tf_op jit(solution)/shard_map/ppermute | solution.py:236
  63.7 1.8 %collective-permute-done.22 = f32[48,768]{1,0:T(8,128)S(1)} collective-permute-done((f32[48,768]{1,0:T(8,128)S(1)}, f32[48,768]{1,0:T(8,128)S(1)}, u32[]{:S(2)}, u32[]{:S(2)}) %collective-permute-start.22) | collective-permute-done | bytes 147488 | tf_op jit(solution)/shard_map/ppermute | solution.py:236
  65.5 2.8 %collective-permute-start.23 = (f32[48,768]{1,0:T(8,128)S(1)}, f32[48,768]{1,0:T(8,128)S(1)}, u32[]{:S(2)}, u32[]{:S(2)}) collective-permute-start(f32[48,768]{1,0:T(8,128)S(1)} %add.43), channel_id=1, source_target_pairs={{0,8},{4,12},{8,0},{12,4},{1,9},{5,13},{9,1},{13,5},{2,10},{6,14},... | collective-permute-start | bytes 442376 | tf_op jit(solution)/shard_map/ppermute | solution.py:236
  68.4 2.7 %project_zero_3.1 = f32[32,768]{1,0:T(8,128)S(1)} custom-call(f32[16,4096]{1,0:T(8,128)S(1)} %collective-permute-done.16.refs_0_.refs_18_, f32[8,4096]{1,0:T(8,128)S(1)} %collective-permute-done.20.refs_1_.refs_19_, f32[8,4096]{1,0:T(8,128)S(1)} %collective-permute-done.21.refs_2_.refs_20_, f32[128,4096]{1,0:T(8,128)S(1)} %copy-done, ...), custom_call_target="tpu_custom_call" | custom-call | flops 1 | bytes 1 | tf_op jit(solution)/shard_map/project_zero_3/pallas_call | solution.py:20
  71.1 1.6 %collective-permute-start.25 = (f32[32,768]{1,0:T(8,128)S(1)}, f32[32,768]{1,0:T(8,128)S(1)}, u32[]{:S(2)}, u32[]{:S(2)}) collective-permute-start(f32[32,768]{1,0:T(8,128)S(1)} %project_zero_3.1), channel_id=1, source_target_pairs={{0,4},{4,0},{8,12},{12,8},{1,5},{5,1},{9,13},{13,9},{2,6},{6,2},{1... | collective-permute-start | bytes 294920 | tf_op jit(solution)/shard_map/ppermute | solution.py:236
  73.1 1.8 %collective-permute-done.23 = f32[48,768]{1,0:T(8,128)S(1)} collective-permute-done((f32[48,768]{1,0:T(8,128)S(1)}, f32[48,768]{1,0:T(8,128)S(1)}, u32[]{:S(2)}, u32[]{:S(2)}) %collective-permute-start.23) | collective-permute-done | bytes 147488 | tf_op jit(solution)/shard_map/ppermute | solution.py:236
  74.9 1.7 %collective-permute-start.24 = (f32[48,768]{1,0:T(8,128)S(1)}, f32[48,768]{1,0:T(8,128)S(1)}, u32[]{:S(2)}, u32[]{:S(2)}) collective-permute-start(f32[48,768]{1,0:T(8,128)S(1)} %add.44.refs_8_), channel_id=1, source_target_pairs={{0,4},{4,0},{8,12},{12,8},{1,5},{5,1},{9,13},{13,9},{2,6},{6,2},{1... | collective-permute-start | bytes 442376 | tf_op jit(solution)/shard_map/ppermute | solution.py:236
  76.6 1.3 %collective-permute-done.25 = f32[32,768]{1,0:T(8,128)S(1)} collective-permute-done((f32[32,768]{1,0:T(8,128)S(1)}, f32[32,768]{1,0:T(8,128)S(1)}, u32[]{:S(2)}, u32[]{:S(2)}) %collective-permute-start.25) | collective-permute-done | bytes 98336 | tf_op jit(solution)/shard_map/ppermute | solution.py:236
  77.9 3.1 %collective-permute-start.26 = (f32[32,768]{1,0:T(8,128)S(1)}, f32[32,768]{1,0:T(8,128)S(1)}, u32[]{:S(2)}, u32[]{:S(2)}) collective-permute-start(f32[32,768]{1,0:T(8,128)S(1)} %add.45.refs_10_), channel_id=1, source_target_pairs={{0,8},{4,12},{8,0},{12,4},{1,9},{5,13},{9,1},{13,5},{2,10},{6,14},... | collective-permute-start | bytes 294920 | tf_op jit(solution)/shard_map/ppermute | solution.py:236
  81.1 2.1 %collective-permute-start.15 = (f32[32,640]{1,0:T(8,128)S(1)}, f32[32,640]{1,0:T(8,128)S(1)}, u32[]{:S(2)}, u32[]{:S(2)}) collective-permute-start(f32[32,640]{1,0:T(8,128)S(1)} %add.42.refs_5_.refs_6_), channel_id=1, source_target_pairs={{0,4},{4,0},{8,12},{12,8},{1,5},{5,1},{9,13},{13,9},{2,6},{6,2},{1... | collective-permute-start | bytes 245768 | tf_op jit(solution)/shard_map/ppermute | solution.py:236
  83.2 2.0 %reorder.1 = (f32[256,256]{1,0:T(8,128)S(1)}, f32[256,256]{1,0:T(8,128)S(1)}) custom-call(s32[6]{0:T(128)S(1)} %copy-done.3, f32[2,256,256]{2,1,0:T(8,128)S(1)} %copy-done.2), custom_call_target="tpu_custom_call" | custom-call | flops 1 | bytes 1 | tf_op jit(solution)/shard_map/reorder/pallas_call | solution.py:20
  87.3 3.4 %copy-done.1 = f32[4096,512]{1,0:T(8,128)S(1)} copy-done((f32[4096,512]{1,0:T(8,128)S(1)}, f32[4096,512]{1,0:T(8,128)}, u32[]{:S(2)}) %copy-start.1) | copy-done | bytes 8388632
  90.6 8.3 %update_one.1 = (f32[4096,512]{1,0:T(8,128)S(1)}, f32[256,512]{1,0:T(8,128)S(1)}) custom-call(s32[6]{0:T(128)S(1)} %copy-done.3, f32[128,640]{1,0:T(8,128)S(1)} %add.38.refs_1_.refs_2_, f32[128,640]{1,0:T(8,128)S(1)} %collective-permute-done.3.refs_2_.refs_3_, f32[32,640]{1,0:T(8,128)S(1)} %add.40.refs_3_.refs_4_, ...), custom_call_target="tpu_custom_call" | custom-call | flops 1 | bytes 1 | tf_op jit(solution)/shard_map/update_one/pallas_call | solution.py:20
  99.0 6.5 %update_zero.1 = f32[4096,512]{1,0:T(8,128)} custom-call(s32[6]{0:T(128)S(1)} %copy-done.3, f32[256,512]{1,0:T(8,128)S(1)} %get-tuple-element.54.refs_1_, f32[128,640]{1,0:T(8,128)S(1)} %add.38.refs_1_.refs_2_, f32[128,640]{1,0:T(8,128)S(1)} %collective-permute-done.3.refs_2_.refs_3_, f32[32,640]{1,0:T(8,128)S(1)} %add.40.refs_3_.refs_4_, ...), custom_call_target="tpu_custom_call" | custom-call | flops 1 | bytes 1 | tf_op jit(solution)/shard_map/update_zero/pallas_call | solution.py:20
  (55 shorter events, 7.8 us)
Async XLA Ops:
  4.4 7.3 %collective-permute-start = (f32[128,4096]{1,0:T(8,128)}, f32[128,4096]{1,0:T(8,128)S(1)}, u32[]{:S(2)}, u32[]{:S(2)}) collective-permute-start(f32[128,4096]{1,0:T(8,128)} %get-tuple-element.41.refs_1_.refs_3_.refs_5_.refs_4_.in_ref.refs_8_.refs_13_), channel_id=1, source_target_pairs={{0,1},{1,0},{2,3},{3,2},{4,5},{5,4},{6,7},{7,6},{8,9},{9,8},{10,11... | collective-permute-start | bytes 6291464 | tf_op jit(solution)/shard_map/ppermute | solution.py:230
  4.9 6.2 %copy-start = (f32[128,4096]{1,0:T(8,128)S(1)}, f32[128,4096]{1,0:T(8,128)}, u32[]{:S(2)}) copy-start(f32[128,4096]{1,0:T(8,128)} %get-tuple-element.41.refs_1_.refs_3_.refs_5_.refs_4_.in_ref.refs_8_.refs_13_) | copy-start | bytes 6291460
  4.9 6.7 %copy-start.3 = (s32[6]{0:T(128)S(1)}, s32[6]{0:T(128)}, u32[]{:S(2)}) copy-start(s32[6]{0:T(128)} %stack.23.where_ref.refs_0_) | copy-start | bytes 76
  4.9 15.6 %collective-permute-start.4 = (f32[32,4096]{1,0:T(8,128)}, f32[32,4096]{1,0:T(8,128)S(1)}, u32[]{:S(2)}, u32[]{:S(2)}) collective-permute-start(f32[32,4096]{1,0:T(8,128)} %get-tuple-element.37), channel_id=1, source_target_pairs={{2,0},{3,1},{0,2},{1,3},{6,4},{7,5},{4,6},{5,7},{10,8},{11,9},{8,1... | collective-permute-start | bytes 1572872 | tf_op jit(solution)/shard_map/ppermute | solution.py:233
  11.2 20.5 %collective-permute-start.10 = (f32[32,4096]{1,0:T(8,128)S(1)}, f32[32,4096]{1,0:T(8,128)S(1)}, u32[]{:S(2)}, u32[]{:S(2)}) collective-permute-start(f32[32,4096]{1,0:T(8,128)S(1)} %get-tuple-element.42), channel_id=1, source_target_pairs={{2,0},{3,1},{0,2},{1,3},{6,4},{7,5},{4,6},{5,7},{10,8},{11,9},{8,1... | collective-permute-start | bytes 1572872 | tf_op jit(solution)/shard_map/ppermute | solution.py:233
  16.4 9.9 %collective-permute-start.1 = (f32[128,640]{1,0:T(8,128)S(1)}, f32[128,640]{1,0:T(8,128)S(1)}, u32[]{:S(2)}, u32[]{:S(2)}) collective-permute-start(f32[128,640]{1,0:T(8,128)S(1)} %get-tuple-element.36), channel_id=1, source_target_pairs={{0,4},{4,0},{8,12},{12,8},{1,5},{5,1},{9,13},{13,9},{2,6},{6,2},{1... | collective-permute-start | bytes 983048 | tf_op jit(solution)/shard_map/ppermute | solution.py:236
  20.5 2.5 %collective-permute-start.6 = (f32[16,4096]{1,0:T(8,128)S(1)}, f32[16,4096]{1,0:T(8,128)S(1)}, u32[]{:S(2)}, u32[]{:S(2)}) collective-permute-start(f32[16,4096]{1,0:T(8,128)S(1)} %get-tuple-element.61), channel_id=1, source_target_pairs={{0,1},{1,0},{2,3},{3,2},{4,5},{5,4},{6,7},{7,6},{8,9},{9,8},{10,11... | collective-permute-start | bytes 786440 | tf_op jit(solution)/shard_map/ppermute | solution.py:230
  20.6 2.5 %collective-permute-start.5 = (f32[16,4096]{1,0:T(8,128)S(1)}, f32[16,4096]{1,0:T(8,128)S(1)}, u32[]{:S(2)}, u32[]{:S(2)}) collective-permute-start(f32[16,4096]{1,0:T(8,128)S(1)} %get-tuple-element.62), channel_id=1, source_target_pairs={{0,1},{1,0},{2,3},{3,2},{4,5},{5,4},{6,7},{7,6},{8,9},{9,8},{10,11... | collective-permute-start | bytes 786440 | tf_op jit(solution)/shard_map/ppermute | solution.py:230
  21.1 27.2 %collective-permute-start.17 = (f32[48,4096]{1,0:T(8,128)S(1)}, f32[48,4096]{1,0:T(8,128)S(1)}, u32[]{:S(2)}, u32[]{:S(2)}) collective-permute-start(f32[48,4096]{1,0:T(8,128)S(1)} %get-tuple-element.47), channel_id=1, source_target_pairs={{2,0},{3,1},{0,2},{1,3},{6,4},{7,5},{4,6},{5,7},{10,8},{11,9},{8,1... | collective-permute-start | bytes 2359304 | tf_op jit(solution)/shard_map/ppermute | solution.py:233
  26.4 22.0 %collective-permute-start.2 = (f32[128,640]{1,0:T(8,128)S(1)}, f32[128,640]{1,0:T(8,128)S(1)}, u32[]{:S(2)}, u32[]{:S(2)}) collective-permute-start(f32[128,640]{1,0:T(8,128)S(1)} %add.37), channel_id=1, source_target_pairs={{0,8},{4,12},{8,0},{12,4},{1,9},{5,13},{9,1},{13,5},{2,10},{6,14},... | collective-permute-start | bytes 983048 | tf_op jit(solution)/shard_map/ppermute | solution.py:236
  31.8 2.6 %collective-permute-start.12 = (f32[16,4096]{1,0:T(8,128)S(1)}, f32[16,4096]{1,0:T(8,128)S(1)}, u32[]{:S(2)}, u32[]{:S(2)}) collective-permute-start(f32[16,4096]{1,0:T(8,128)S(1)} %get-tuple-element.59), channel_id=1, source_target_pairs={{0,1},{1,0},{2,3},{3,2},{4,5},{5,4},{6,7},{7,6},{8,9},{9,8},{10,11... | collective-permute-start | bytes 786440 | tf_op jit(solution)/shard_map/ppermute | solution.py:230
  31.8 2.5 %collective-permute-start.11 = (f32[16,4096]{1,0:T(8,128)S(1)}, f32[16,4096]{1,0:T(8,128)S(1)}, u32[]{:S(2)}, u32[]{:S(2)}) collective-permute-start(f32[16,4096]{1,0:T(8,128)S(1)} %get-tuple-element.60), channel_id=1, source_target_pairs={{0,1},{1,0},{2,3},{3,2},{4,5},{5,4},{6,7},{7,6},{8,9},{9,8},{10,11... | collective-permute-start | bytes 786440 | tf_op jit(solution)/shard_map/ppermute | solution.py:230
  32.3 16.0 %collective-permute-start.7 = (f32[32,640]{1,0:T(8,128)S(1)}, f32[32,640]{1,0:T(8,128)S(1)}, u32[]{:S(2)}, u32[]{:S(2)}) collective-permute-start(f32[32,640]{1,0:T(8,128)S(1)} %get-tuple-element.40), channel_id=1, source_target_pairs={{0,4},{4,0},{8,12},{12,8},{1,5},{5,1},{9,13},{13,9},{2,6},{6,2},{1... | collective-permute-start | bytes 245768 | tf_op jit(solution)/shard_map/ppermute | solution.py:236
  48.4 6.7 %collective-permute-start.19 = (f32[24,4096]{1,0:T(8,128)S(1)}, f32[24,4096]{1,0:T(8,128)S(1)}, u32[]{:S(2)}, u32[]{:S(2)}) collective-permute-start(f32[24,4096]{1,0:T(8,128)S(1)} %get-tuple-element.57), channel_id=1, source_target_pairs={{0,1},{1,0},{2,3},{3,2},{4,5},{5,4},{6,7},{7,6},{8,9},{9,8},{10,11... | collective-permute-start | bytes 1179656 | tf_op jit(solution)/shard_map/ppermute | solution.py:230
  48.4 7.1 %collective-permute-start.18 = (f32[24,4096]{1,0:T(8,128)S(1)}, f32[24,4096]{1,0:T(8,128)S(1)}, u32[]{:S(2)}, u32[]{:S(2)}) collective-permute-start(f32[24,4096]{1,0:T(8,128)S(1)} %get-tuple-element.58), channel_id=1, source_target_pairs={{0,1},{1,0},{2,3},{3,2},{4,5},{5,4},{6,7},{7,6},{8,9},{9,8},{10,11... | collective-permute-start | bytes 1179656 | tf_op jit(solution)/shard_map/ppermute | solution.py:230
  49.0 14.1 %collective-permute-start.3 = (f32[128,640]{1,0:T(8,128)S(1)}, f32[128,640]{1,0:T(8,128)S(1)}, u32[]{:S(2)}, u32[]{:S(2)}) collective-permute-start(f32[128,640]{1,0:T(8,128)S(1)} %add.38.refs_1_.refs_2_), channel_id=1, source_target_pairs={{0,4},{4,0},{8,12},{12,8},{1,5},{5,1},{9,13},{13,9},{2,6},{6,2},{1... | collective-permute-start | bytes 983048 | tf_op jit(solution)/shard_map/ppermute | solution.py:236
  50.9 9.9 %collective-permute-start.16 = (f32[16,4096]{1,0:T(8,128)S(1)}, f32[16,4096]{1,0:T(8,128)S(1)}, u32[]{:S(2)}, u32[]{:S(2)}) collective-permute-start(f32[16,4096]{1,0:T(8,128)S(1)} %get-tuple-element.46), channel_id=1, source_target_pairs={{2,0},{3,1},{0,2},{1,3},{6,4},{7,5},{4,6},{5,7},{10,8},{11,9},{8,1... | collective-permute-start | bytes 786440 | tf_op jit(solution)/shard_map/ppermute | solution.py:233
  52.4 8.4 %collective-permute-start.8 = (f32[32,640]{1,0:T(8,128)S(1)}, f32[32,640]{1,0:T(8,128)S(1)}, u32[]{:S(2)}, u32[]{:S(2)}) collective-permute-start(f32[32,640]{1,0:T(8,128)S(1)} %add.39), channel_id=1, source_target_pairs={{0,8},{4,12},{8,0},{12,4},{1,9},{5,13},{9,1},{13,5},{2,10},{6,14},... | collective-permute-start | bytes 245768 | tf_op jit(solution)/shard_map/ppermute | solution.py:236
  55.1 8.1 %collective-permute-start.13 = (f32[32,640]{1,0:T(8,128)S(1)}, f32[32,640]{1,0:T(8,128)S(1)}, u32[]{:S(2)}, u32[]{:S(2)}) collective-permute-start(f32[32,640]{1,0:T(8,128)S(1)} %get-tuple-element.45), channel_id=1, source_target_pairs={{0,4},{4,0},{8,12},{12,8},{1,5},{5,1},{9,13},{13,9},{2,6},{6,2},{1... | collective-permute-start | bytes 245768 | tf_op jit(solution)/shard_map/ppermute | solution.py:236
  59.2 6.3 %collective-permute-start.22 = (f32[48,768]{1,0:T(8,128)S(1)}, f32[48,768]{1,0:T(8,128)S(1)}, u32[]{:S(2)}, u32[]{:S(2)}) collective-permute-start(f32[48,768]{1,0:T(8,128)S(1)} %get-tuple-element.50), channel_id=1, source_target_pairs={{0,4},{4,0},{8,12},{12,8},{1,5},{5,1},{9,13},{13,9},{2,6},{6,2},{1... | collective-permute-start | bytes 442376 | tf_op jit(solution)/shard_map/ppermute | solution.py:236
  63.1 5.2 %collective-permute-start.21 = (f32[8,4096]{1,0:T(8,128)S(1)}, f32[8,4096]{1,0:T(8,128)S(1)}, u32[]{:S(2)}, u32[]{:S(2)}) collective-permute-start(f32[8,4096]{1,0:T(8,128)S(1)} %get-tuple-element.63), channel_id=1, source_target_pairs={{0,1},{1,0},{2,3},{3,2},{4,5},{5,4},{6,7},{7,6},{8,9},{9,8},{10,11... | collective-permute-start | bytes 393224 | tf_op jit(solution)/shard_map/ppermute | solution.py:230
  63.2 5.2 %collective-permute-start.20 = (f32[8,4096]{1,0:T(8,128)S(1)}, f32[8,4096]{1,0:T(8,128)S(1)}, u32[]{:S(2)}, u32[]{:S(2)}) collective-permute-start(f32[8,4096]{1,0:T(8,128)S(1)} %get-tuple-element.64), channel_id=1, source_target_pairs={{0,1},{1,0},{2,3},{3,2},{4,5},{5,4},{6,7},{7,6},{8,9},{9,8},{10,11... | collective-permute-start | bytes 393224 | tf_op jit(solution)/shard_map/ppermute | solution.py:230
  65.5 17.7 %copy-start.2 = (f32[2,256,256]{2,1,0:T(8,128)S(1)}, f32[2,256,256]{2,1,0:T(8,128)}, u32[]{:S(2)}) copy-start(f32[2,256,256]{2,1,0:T(8,128)} %in_ref.3) | copy-start | bytes 1572868
  65.5 9.3 %collective-permute-start.23 = (f32[48,768]{1,0:T(8,128)S(1)}, f32[48,768]{1,0:T(8,128)S(1)}, u32[]{:S(2)}, u32[]{:S(2)}) collective-permute-start(f32[48,768]{1,0:T(8,128)S(1)} %add.43), channel_id=1, source_target_pairs={{0,8},{4,12},{8,0},{12,4},{1,9},{5,13},{9,1},{13,5},{2,10},{6,14},... | collective-permute-start | bytes 442376 | tf_op jit(solution)/shard_map/ppermute | solution.py:236
  71.1 6.8 %collective-permute-start.25 = (f32[32,768]{1,0:T(8,128)S(1)}, f32[32,768]{1,0:T(8,128)S(1)}, u32[]{:S(2)}, u32[]{:S(2)}) collective-permute-start(f32[32,768]{1,0:T(8,128)S(1)} %project_zero_3.1), channel_id=1, source_target_pairs={{0,4},{4,0},{8,12},{12,8},{1,5},{5,1},{9,13},{13,9},{2,6},{6,2},{1... | collective-permute-start | bytes 294920 | tf_op jit(solution)/shard_map/ppermute | solution.py:236
  72.7 8.4 %collective-permute-start.14 = (f32[32,640]{1,0:T(8,128)S(1)}, f32[32,640]{1,0:T(8,128)S(1)}, u32[]{:S(2)}, u32[]{:S(2)}) collective-permute-start(f32[32,640]{1,0:T(8,128)S(1)} %add.41), channel_id=1, source_target_pairs={{0,8},{4,12},{8,0},{12,4},{1,9},{5,13},{9,1},{13,5},{2,10},{6,14},... | collective-permute-start | bytes 245768 | tf_op jit(solution)/shard_map/ppermute | solution.py:236
  74.9 24.1 %collective-permute-start.24 = (f32[48,768]{1,0:T(8,128)S(1)}, f32[48,768]{1,0:T(8,128)S(1)}, u32[]{:S(2)}, u32[]{:S(2)}) collective-permute-start(f32[48,768]{1,0:T(8,128)S(1)} %add.44.refs_8_), channel_id=1, source_target_pairs={{0,4},{4,0},{8,12},{12,8},{1,5},{5,1},{9,13},{13,9},{2,6},{6,2},{1... | collective-permute-start | bytes 442376 | tf_op jit(solution)/shard_map/ppermute | solution.py:236
  77.9 21.0 %collective-permute-start.26 = (f32[32,768]{1,0:T(8,128)S(1)}, f32[32,768]{1,0:T(8,128)S(1)}, u32[]{:S(2)}, u32[]{:S(2)}) collective-permute-start(f32[32,768]{1,0:T(8,128)S(1)} %add.45.refs_10_), channel_id=1, source_target_pairs={{0,8},{4,12},{8,0},{12,4},{1,9},{5,13},{9,1},{13,5},{2,10},{6,14},... | collective-permute-start | bytes 294920 | tf_op jit(solution)/shard_map/ppermute | solution.py:236
  81.0 5.4 %collective-permute-start.9 = (f32[32,640]{1,0:T(8,128)S(1)}, f32[32,640]{1,0:T(8,128)S(1)}, u32[]{:S(2)}, u32[]{:S(2)}) collective-permute-start(f32[32,640]{1,0:T(8,128)S(1)} %add.40.refs_3_.refs_4_), channel_id=1, source_target_pairs={{0,4},{4,0},{8,12},{12,8},{1,5},{5,1},{9,13},{13,9},{2,6},{6,2},{1... | collective-permute-start | bytes 245768 | tf_op jit(solution)/shard_map/ppermute | solution.py:236
  81.1 6.1 %collective-permute-start.15 = (f32[32,640]{1,0:T(8,128)S(1)}, f32[32,640]{1,0:T(8,128)S(1)}, u32[]{:S(2)}, u32[]{:S(2)}) collective-permute-start(f32[32,640]{1,0:T(8,128)S(1)} %add.42.refs_5_.refs_6_), channel_id=1, source_target_pairs={{0,4},{4,0},{8,12},{12,8},{1,5},{5,1},{9,13},{13,9},{2,6},{6,2},{1... | collective-permute-start | bytes 245768 | tf_op jit(solution)/shard_map/ppermute | solution.py:236
  87.3 3.4 %copy-start.1 = (f32[4096,512]{1,0:T(8,128)S(1)}, f32[4096,512]{1,0:T(8,128)}, u32[]{:S(2)}) copy-start(f32[4096,512]{1,0:T(8,128)} %refs_16_.1) | copy-start | bytes 25165828

commit v5 on v4

--- a/solution.py
+++ b/solution.py
@@ -6,7 +6,7 @@
 from jax.sharding import PartitionSpec as P
 
 F32, BF16 = jnp.float32, jnp.bfloat16
-PIECES = ((1, 0, 32, True), (1, 32, 64, True), (0, 0, 48, True), (0, 48, 64, False))
+PIECES = ((1, 0, 64, True), (0, 0, 48, True), (0, 48, 64, False))
 SWAP_PARTS = 2
 NN = (((1,), (0,)), ((), ()))
 NT = (((1,), (1,)), ((), ()))
@@ -52,6 +52,11 @@
     return first[:rows] + first[rows:] + dot(vh, bl, dims)
 
 
+def short_dot(a, b, dims=NN):
+    (ah, al), (bh, bl) = split(a), split(b)
+    return dot(ah, bh, dims) + dot(ah, bl, dims) + dot(al, bh, dims)
+
+
 def steps_of(here, step):
     step = min(here, step)
     return [pl.ds(at, step) for at in range(0, here, step)]
@@ -62,23 +67,27 @@
     block, low, high = first
     begin = (1 - block) * share + low
 
+    strip = min(share, 16)
+    strips = [(k, at) for k in (1, 0) for at in range(0, share, strip)]
+
     def body(where_ref, in_ref, piece, mine, sems):
-        copies = [
-            pltpu.make_async_copy(in_ref.at[k], mine.at[(1 - k) * share : (2 - k) * share], sems.at[k]) for k in (0, 1)
-        ]
-        copies[1].start()
-        copies[0].start()
-        for k in (1, 0):
-            copies[k].wait()
-            shape = (share, here)
-            along = lax.broadcasted_iota(jnp.int32, shape, 0) + (where_ref[0] + k * where_ref[2])
+        copies = []
+        for n, (k, at) in enumerate(strips):
+            to = mine.at[(1 - k) * share + at : (1 - k) * share + at + strip]
+            copies.append(pltpu.make_async_copy(in_ref.at[k, at : at + strip], to, sems.at[n]))
+            copies[-1].start()
+        for copy, (k, at) in zip(copies, strips):
+            copy.wait()
+            shape = (strip, here)
+            along = lax.broadcasted_iota(jnp.int32, shape, 0) + (where_ref[0] + at + k * where_ref[2])
             across = lax.broadcasted_iota(jnp.int32, shape, 1) + where_ref[1]
-            rows = slice((1 - k) * share, (2 - k) * share)
+            rows = slice((1 - k) * share + at, (1 - k) * share + at + strip)
             mine[rows] = jnp.where(across >= along, mine[rows], 0.0)
         piece[...] = mine[begin : begin + high - low]
 
     outs = [array(high - low, here), array(2 * share, here)]
-    return call(body, "cut", (where, vectors), [SCALARS, HBM], outs, [VMEM] * 2, [pltpu.SemaphoreType.DMA((2,))], 56)
+    sems = [pltpu.SemaphoreType.DMA((len(strips),))]
+    return call(body, "cut", (where, vectors), [SCALARS, HBM], outs, [VMEM] * 2, sems, 56)
 
 
 def parts_of(mine, places):
@@ -178,7 +187,7 @@
 
 
 def update(name, make, ins, factor, pieces, current, last):
-    here, nc = current.shape
+    here, nc = current[0].shape
     width = factor.shape[0]
     steps = steps_of(here, 256)
 
@@ -186,26 +195,21 @@
         in_refs, refs = refs[: len(ins)], refs[len(ins) :]
         factor_ref, refs = refs[0], refs[1:]
         piece_refs, refs = refs[: len(pieces)], refs[len(pieces) :]
-        cur_ref, out = refs[:2]
-        loads = []
-        if not last:
-            held, sems = refs[3:]
-            loads = [pltpu.make_async_copy(cur_ref.at[ds], held.at[ds], sems.at[n]) for n, ds in enumerate(steps)]
-            for copy in loads:
-                copy.start()
-            cur_ref = held
-        scaled = full_dot(factor_ref[...], make(*in_refs))
+        cur_refs, refs = refs[: len(current)], refs[len(current) :]
+        out = refs[0]
+        scaled = short_dot(factor_ref[...], make(*in_refs))
         sh, sl = split(scaled)
         if not last:
-            refs[2][...] = scaled
+            refs[1][...] = scaled
         copies = []
         for n, ds in enumerate(steps):
             vh, vl = split(rows_of(piece_refs, pieces, ds))
-            if loads:
-                loads[n].wait()
-            new = cur_ref[ds, :] - (dot(vh, sh, TN) + dot(vh, sl, TN) + dot(vl, sh, TN))
+            new = cur_refs[0][ds, :].astype(F32)
+            for ref in cur_refs[1:]:
+                new += ref[ds, :].astype(F32)
+            new -= dot(vh, sh, TN) + dot(vh, sl, TN) + dot(vl, sh, TN)
             if last:
-                held, sems = refs[2:]
+                held, sems = refs[1:]
                 held[ds, :] = new
                 copies.append(pltpu.make_async_copy(held.at[ds], out.at[ds], sems.at[n]))
                 copies[-1].start()
@@ -214,13 +218,12 @@
         for copy in copies:
             copy.wait()
 
-    specs = [SCALARS if v.dtype == jnp.int32 else VMEM for v in ins] + [VMEM] * (len(pieces) + 1)
-    specs.append(VMEM if last else HBM)
-    args = [*ins, factor, *[p[0] for p in pieces], current]
-    scratch = [pltpu.VMEM((here, nc), F32), pltpu.SemaphoreType.DMA((len(steps),))]
+    args = [*ins, factor, *[p[0] for p in pieces], *current]
+    specs = [SCALARS if v.dtype == jnp.int32 else VMEM for v in args]
     if last:
+        scratch = [pltpu.VMEM((here, nc), F32), pltpu.SemaphoreType.DMA((len(steps),))]
         return call(body, name, args, specs, array(here, nc), HBM, scratch, 13)
-    return call(body, name, args, specs, [array(here, nc), array(width, nc)], [VMEM] * 2, scratch, 13)
+    return call(body, name, args, specs, [array(here, nc), array(width, nc)], [VMEM] * 2)
 
 
 def make_local(chips, rows):
@@ -238,18 +241,15 @@
     def sums(value, send=None):
         step, got = 1, None
         if send is not None:
-            got = row_swap(send, 1)
-            yield got
+            got = yield row_swap(send, 1)
             step = 2
         while step < rows:
             value = value if got is None else value + got
-            got = row_swap(value, step)
-            yield got
+            got = yield row_swap(value, step)
             step *= 2
         if send is not None:
             value = value + got
-            got = row_swap(value, 1)
-            yield got
+            got = yield row_swap(value, 1)
         return value, got
 
     def local(vectors, factors, eigvecs):
@@ -279,23 +279,29 @@
         own = {1: [(mine, share, 0), (sib, share, 0)], 0: [(mine, share, share), (sib, share, share)]}
         segments = {k: [(0, 0, 0, share), (0, 1, 0, share)] for k in (0, 1)}
         all_ones, all_zeros = list(own[1]), list(own[0])
-        running, done, waits = [], {}, ()
-
-        def advance():
-            got = []
-            for key, chain in list(running):
+        running, flying, done = {}, {}, {}
+
+        def start(*names):
+            for name in names:
+                if name not in running:
+                    continue
                 try:
-                    got.append(next(chain))
+                    flying[name] = running[name].send(flying.pop(name, None))
                 except StopIteration as end:
-                    done[key] = end.value
-                    running.remove((key, chain))
-            return got
+                    done[name] = end.value
+                    del running[name]
+
+        def arrived(*names):
+            return [flying[name] for name in names if name in flying]
 
         front = project("project_own", own[1] + own[0], own[0], high, low, bit, half)
-        running.append(("own", sums(*front)))
+        running["own"] = sums(*front)
+        start("own")
+        last = len(far) - 1
         for n, (step, (block, first, final), value) in enumerate(far):
-            value = after(value, *front, *waits)
-            waits = advance()
+            waits = list(running) if n < last or last != 2 else []
+            value = after(value, *front, *arrived(*waits))
+            start(*waits)
             split_rows = halves[block, first, final]
             pair = [(value, final - first, 0)]
             parts = SWAP_PARTS if (final - first) % (8 * SWAP_PARTS) == 0 else 1
@@ -303,15 +309,22 @@
             for part in range(parts):
                 pair.append((core_swap(value[part * each : (part + 1) * each]), each, 0))
             segments[block] += [(step, 0, first, final), (step, 1, first, final)]
+            ready = high
+            if n == last == 2:
+                ready = after(high, *arrived(0, 1))
+                start(0, 1)
             if block == 1:
                 all_ones += pair
-                front = project(f"project_one_{n}", pair, own[0], high, low, bit if split_rows else None)
+                front = project(f"project_one_{n}", pair, own[0], ready, low, bit if split_rows else None)
             else:
                 all_zeros += pair
-                front = project(f"project_zero_{n}", pair, all_ones, high, low, bit if split_rows else None)
-            running.append((n, sums(*front)))
+                front = project(f"project_zero_{n}", pair, all_ones, ready, low, bit if split_rows else None)
+            running[n] = sums(*front)
+            start(n)
+        if last in flying:
+            flying[last] = after(flying[last], *arrived("own", 0))
         while running:
-            advance()
+            start(*list(running))
         ones = [("own", True)] + [(n, halves[f[1]]) for n, f in enumerate(far) if f[1][0] == 1]
         zeros = [(n, halves[f[1]]) for n, f in enumerate(far) if f[1][0] == 0]
         t0, t1 = reorder(where, after(factors, *front), share, chips, segments)
@@ -334,13 +347,13 @@
             scaled = scaled_ref[...]
             parts = joined(where_ref, ones_refs, ones, slice(nc, nc + half))
             turned_gram = jnp.concatenate(parts[:1] + parts[2:])
-            front = joined(where_ref, ones_refs[:2], ones[:1], slice(0, nc))[1] - full_dot(turned_gram, scaled, TN)
+            front = joined(where_ref, ones_refs[:2], ones[:1], slice(0, nc))[1] - short_dot(turned_gram, scaled, TN)
             later = jnp.concatenate(joined(where_ref, zero_refs, zeros, slice(None)))
-            return jnp.concatenate([front, later[:, :nc] - full_dot(later[:, nc:], scaled)])
-
-        current, scaled = update("update_one", make_one, [bit, *ones_flat], t1, all_ones, eigvecs, False)
+            return jnp.concatenate([front, later[:, :nc] - short_dot(later[:, nc:], scaled)])
+
+        current, scaled = update("update_one", make_one, [bit, *ones_flat], t1, all_ones, [high, low], False)
         ins = [bit, scaled, *ones_flat, *zeros_flat]
-        return update("update_zero", make_zero, ins, t0, all_zeros, current, True)
+        return update("update_zero", make_zero, ins, t0, all_zeros, [current], True)
 
     return local
 

time: 106 us -> 96.1 us (0.907)
  starting transfers between devices: 34.2 us -> 25 us
  waiting for transfers between devices: 26 us -> 35.2 us
  Pallas kernels: 40.9 us -> 34.5 us
  local copies, waits for them, and re-layouts: 4.13 us -> 0.82 us
    ppermute x14 -> x11, starting transfers between devices: 24.9 us -> 18 us  [row_swap(): return lax.ppermute(value, 'row', [(i, i ^ step) for i in range(rows)])]
    pallas_call x11 -> x10, Pallas kernels: 40.9 us -> 34.5 us  [call(): pl.pallas_call(body, in_specs=specs, out_specs=out_specs, out_shape=outs,...]
    ppermute x4 -> x3, waiting for transfers between devices: 16.1 us -> 21.3 us  [from_chip(): lax.ppermute(value, 'col', [((i + 2 * step) % cols, i) for i in range(col...]
    ppermute x14 -> x11, waiting for transfers between devices: 9.83 us -> 13.8 us  [row_swap(): return lax.ppermute(value, 'row', [(i, i ^ step) for i in range(rows)])]
    unnamed x8 -> x6, local copies, waits for them, and re-layouts: 3.4 us -> 0.01 us
    ppermute x4 -> x3, starting transfers between devices: 6.43 us -> 4.81 us  [from_chip(): lax.ppermute(value, 'col', [((i + 2 * step) % cols, i) for i in range(col...]
    ppermute x9 -> x7, starting transfers between devices: 2.79 us -> 2.22 us  [core_swap(): return lax.ppermute(value, 'col', [(i, i ^ 1) for i in range(cols)])]
  transfers between devices with their start and end apart: 27 -> 21, of which waited for: 10 -> 7; matrix products, arithmetic and copies ran while one was open for 0% -> 0% of each run, Pallas kernels for 29% -> 26%
where the time goes in v5:
time: 96.1 us; the launch traced here: 96 us
  waiting for transfers between devices  35.2 us (37%)
  Pallas kernels  34.5 us (36%)
  starting transfers between devices  25 us (26%)
    pallas_call x10, Pallas kernels, call(): pl.pallas_call(body, in_specs=specs, out_specs=out_specs, out_shape=outs,...  34.5 us
    ppermute x3, waiting for transfers between devices, from_chip(): lax.ppermute(value, 'col', [((i + 2 * step) % cols, i) for i in range(col...  21.3 us
    ppermute x11, starting transfers between devices, row_swap(): return lax.ppermute(value, 'row', [(i, i ^ step) for i in range(rows)])  18 us
    ppermute x11, waiting for transfers between devices, row_swap(): return lax.ppermute(value, 'row', [(i, i ^ step) for i in range(rows)])  13.8 us
    ppermute x3, starting transfers between devices, from_chip(): lax.ppermute(value, 'col', [((i + 2 * step) % cols, i) for i in range(col...  4.81 us
    ppermute x7, starting transfers between devices, core_swap(): return lax.ppermute(value, 'col', [(i, i ^ 1) for i in range(cols)])  2.22 us
  transfers between devices with their start and end apart: 21, of which 7 were waited for; matrix products, arithmetic and copies ran while one was open for 0% of the time, Pallas kernels for 26%

profile of v5, /device:TPU:0, one launch (start us, length us, event | category | flops | bytes accessed | tf_op | source)
XLA Modules:
  0.0 96.0 jit_solution(12097155141109032774)
XLA Ops:
  0.0 0.7 stack.23.where_ref.refs_0_
  0.7 4.0 %cut.1 = (f32[64,4096]{1,0:T(8,128)}, f32[128,4096]{1,0:T(8,128)}) custom-call(s32[6]{0:T(128)} %stack.23.where_ref.refs_0_, f32[2,64,4096]{2,1,0:T(8,128)} %in_ref.1), custom_call_target="tpu_custom_call" | custom-call | flops 1 | bytes 1 | tf_op jit(solution)/shard_map/cut/pallas_call | solution.py:20
  4.6 0.5 collective-permute-start
  5.1 2.6 %collective-permute-start.4 = (f32[64,4096]{1,0:T(8,128)}, f32[64,4096]{1,0:T(8,128)S(1)}, u32[]{:S(2)}, u32[]{:S(2)}) collective-permute-start(f32[64,4096]{1,0:T(8,128)} %get-tuple-element.35), channel_id=1, source_target_pairs={{2,0},{3,1},{0,2},{1,3},{6,4},{7,5},{4,6},{5,7},{10,8},{11,9},{8,1... | collective-permute-start | bytes 3145736 | tf_op jit(solution)/shard_map/ppermute | solution.py:236
  7.7 3.6 %load.1 = (bf16[4096,512]{1,0:T(8,128)(2,1)S(1)}, bf16[4096,512]{1,0:T(8,128)(2,1)S(1)}) custom-call(f32[4096,512]{1,0:T(8,128)} %in_ref.2), custom_call_target="tpu_custom_call" | custom-call | flops 1 | bytes 1 | tf_op jit(solution)/shard_map/load/pallas_call | solution.py:20
  11.4 4.8 %project_own.1 = (f32[128,640]{1,0:T(8,128)S(1)}, f32[128,640]{1,0:T(8,128)S(1)}) custom-call(s32[6]{0:T(128)S(1)} %copy-done.2, f32[128,4096]{1,0:T(8,128)S(1)} %copy-done, f32[128,4096]{1,0:T(8,128)S(1)} %collective-permute-done.refs_2_.refs_4_.refs_6_.refs_5_.refs_7_.refs_12_, f32[128,4096]{1,0:T(8,128)S(1)} %copy-done, ...), custom_call_target="tpu_custom_call" | custom-call | flops 1 | bytes 1 | tf_op jit(solution)/shard_map/project_own/pallas_call | solution.py:20
  16.1 1.6 %collective-permute-start.1 = (f32[128,640]{1,0:T(8,128)S(1)}, f32[128,640]{1,0:T(8,128)S(1)}, u32[]{:S(2)}, u32[]{:S(2)}) collective-permute-start(f32[128,640]{1,0:T(8,128)S(1)} %get-tuple-element.34), channel_id=1, source_target_pairs={{0,4},{4,0},{8,12},{12,8},{1,5},{5,1},{9,13},{13,9},{2,6},{6,2},{1... | collective-permute-start | bytes 983048 | tf_op jit(solution)/shard_map/ppermute | solution.py:239
  17.9 0.7 collective-permute-start.11
  18.5 13.4 %collective-permute-done.4.refs_1_.refs_6_.refs_5_.refs_8_ = f32[64,4096]{1,0:T(8,128)S(1)} collective-permute-done((f32[64,4096]{1,0:T(8,128)}, f32[64,4096]{1,0:T(8,128)S(1)}, u32[]{:S(2)}, u32[]{:S(2)}) %collective-permute-start.4) | collective-permute-done | bytes 1048608 | tf_op jit(solution)/shard_map/ppermute | solution.py:236
  32.1 0.5 collective-permute-start.6
  32.6 3.1 %collective-permute-start.2 = (f32[128,640]{1,0:T(8,128)S(1)}, f32[128,640]{1,0:T(8,128)S(1)}, u32[]{:S(2)}, u32[]{:S(2)}) collective-permute-start(f32[128,640]{1,0:T(8,128)S(1)} %add.31), channel_id=1, source_target_pairs={{0,8},{4,12},{8,0},{12,4},{1,9},{5,13},{9,1},{13,5},{2,10},{6,14},... | collective-permute-start | bytes 983048 | tf_op jit(solution)/shard_map/ppermute | solution.py:239
  35.8 3.2 %project_one_0.1 = (f32[64,640]{1,0:T(8,128)S(1)}, f32[64,640]{1,0:T(8,128)S(1)}) custom-call(s32[6]{0:T(128)S(1)} %copy-done.2, f32[64,4096]{1,0:T(8,128)S(1)} %collective-permute-done.4.refs_1_.refs_6_.refs_5_.refs_8_, f32[32,4096]{1,0:T(8,128)S(1)} %collective-permute-done.5.refs_2_.refs_7_.refs_6_.refs_9_, ...), custom_call_target="tpu_custom_call" | custom-call | flops 1 | bytes 1 | tf_op jit(solution)/shard_map/project_one_0/pallas_call | solution.py:20
  39.0 1.6 %collective-permute-start.7 = (f32[64,640]{1,0:T(8,128)S(1)}, f32[64,640]{1,0:T(8,128)S(1)}, u32[]{:S(2)}, u32[]{:S(2)}) collective-permute-start(f32[64,640]{1,0:T(8,128)S(1)} %get-tuple-element.38), channel_id=1, source_target_pairs={{0,4},{4,0},{8,12},{12,8},{1,5},{5,1},{9,13},{13,9},{2,6},{6,2},{1... | collective-permute-start | bytes 491528 | tf_op jit(solution)/shard_map/ppermute | solution.py:239
  40.6 7.9 %collective-permute-done.11.refs_1_.refs_13_ = f32[48,4096]{1,0:T(8,128)S(1)} collective-permute-done((f32[48,4096]{1,0:T(8,128)S(1)}, f32[48,4096]{1,0:T(8,128)S(1)}, u32[]{:S(2)}, u32[]{:S(2)}) %collective-permute-start.11) | collective-permute-done | bytes 786464 | tf_op jit(solution)/shard_map/ppermute | solution.py:236
  48.5 2.3 %collective-permute-done.2 = f32[128,640]{1,0:T(8,128)S(1)} collective-permute-done((f32[128,640]{1,0:T(8,128)S(1)}, f32[128,640]{1,0:T(8,128)S(1)}, u32[]{:S(2)}, u32[]{:S(2)}) %collective-permute-start.2) | collective-permute-done | bytes 327712 | tf_op jit(solution)/shard_map/ppermute | solution.py:239
  50.9 0.5 collective-permute-start.13
  51.4 1.5 %collective-permute-start.10 = (f32[16,4096]{1,0:T(8,128)S(1)}, f32[16,4096]{1,0:T(8,128)S(1)}, u32[]{:S(2)}, u32[]{:S(2)}) collective-permute-start(f32[16,4096]{1,0:T(8,128)S(1)} %get-tuple-element.40), channel_id=1, source_target_pairs={{2,0},{3,1},{0,2},{1,3},{6,4},{7,5},{4,6},{5,7},{10,8},{11,9},{8,1... | collective-permute-start | bytes 786440 | tf_op jit(solution)/shard_map/ppermute | solution.py:236
  53.0 0.7 collective-permute-start.3
  53.8 4.4 %collective-permute-start.8 = (f32[64,640]{1,0:T(8,128)S(1)}, f32[64,640]{1,0:T(8,128)S(1)}, u32[]{:S(2)}, u32[]{:S(2)}) collective-permute-start(f32[64,640]{1,0:T(8,128)S(1)} %add.33), channel_id=1, source_target_pairs={{0,8},{4,12},{8,0},{12,4},{1,9},{5,13},{9,1},{13,5},{2,10},{6,14},... | collective-permute-start | bytes 491528 | tf_op jit(solution)/shard_map/ppermute | solution.py:239
  58.1 3.5 %project_zero_1.1 = (f32[48,768]{1,0:T(8,128)S(1)}, f32[48,768]{1,0:T(8,128)S(1)}) custom-call(s32[6]{0:T(128)S(1)} %copy-done.2, f32[48,4096]{1,0:T(8,128)S(1)} %collective-permute-done.11.refs_1_.refs_13_, f32[24,4096]{1,0:T(8,128)S(1)} %collective-permute-done.12.refs_2_.refs_14_, f32[24,4096]{1,0:T(8,128)S(1)} %collective-permute-done.13.refs_3_.refs_15_, ...), custom_call_target="tpu_custom_call" | custom-call | flops 1 | bytes 1 | tf_op jit(solution)/shard_map/project_zero_1/pallas_call | solution.py:20
  61.8 0.5 collective-permute-start.15
  62.3 6.9 %collective-permute-done.16 = f32[48,768]{1,0:T(8,128)S(1)} collective-permute-done((f32[48,768]{1,0:T(8,128)S(1)}, f32[48,768]{1,0:T(8,128)S(1)}, u32[]{:S(2)}, u32[]{:S(2)}) %collective-permute-start.16) | collective-permute-done | bytes 147488 | tf_op jit(solution)/shard_map/ppermute | solution.py:239
  69.2 3.3 %collective-permute-start.17 = (f32[48,768]{1,0:T(8,128)S(1)}, f32[48,768]{1,0:T(8,128)S(1)}, u32[]{:S(2)}, u32[]{:S(2)}) collective-permute-start(f32[48,768]{1,0:T(8,128)S(1)} %add.35), channel_id=1, source_target_pairs={{0,8},{4,12},{8,0},{12,4},{1,9},{5,13},{9,1},{13,5},{2,10},{6,14},... | collective-permute-start | bytes 442376 | tf_op jit(solution)/shard_map/ppermute | solution.py:239
  72.5 1.8 %collective-permute-start.9 = (f32[64,640]{1,0:T(8,128)S(1)}, f32[64,640]{1,0:T(8,128)S(1)}, u32[]{:S(2)}, u32[]{:S(2)}) collective-permute-start(f32[64,640]{1,0:T(8,128)S(1)} %add.34.refs_3_.refs_4_), channel_id=1, source_target_pairs={{0,4},{4,0},{8,12},{12,8},{1,5},{5,1},{9,13},{13,9},{2,6},{6,2},{1... | collective-permute-start | bytes 491528 | tf_op jit(solution)/shard_map/ppermute | solution.py:239
  74.3 2.9 %project_zero_2.1 = f32[32,768]{1,0:T(8,128)S(1)} custom-call(f32[16,4096]{1,0:T(8,128)S(1)} %collective-permute-done.10.refs_0_.refs_16_, f32[8,4096]{1,0:T(8,128)S(1)} %collective-permute-done.14.refs_1_.refs_17_, f32[8,4096]{1,0:T(8,128)S(1)} %collective-permute-done.15.refs_2_.refs_18_, f32[128,4096]{1,0:T(8,128)S(1)} %copy-done, ...), custom_call_target="tpu_custom_call" | custom-call | flops 1 | bytes 1 | tf_op jit(solution)/shard_map/project_zero_2/pallas_call | solution.py:20
  77.5 1.4 %collective-permute-done.17 = f32[48,768]{1,0:T(8,128)S(1)} collective-permute-done((f32[48,768]{1,0:T(8,128)S(1)}, f32[48,768]{1,0:T(8,128)S(1)}, u32[]{:S(2)}, u32[]{:S(2)}) %collective-permute-start.17) | collective-permute-done | bytes 147488 | tf_op jit(solution)/shard_map/ppermute | solution.py:239
  79.0 0.7 collective-permute-start.18
  79.7 1.0 %collective-permute-done.9.refs_4_.refs_5_ = f32[64,640]{1,0:T(8,128)S(1)} collective-permute-done((f32[64,640]{1,0:T(8,128)S(1)}, f32[64,640]{1,0:T(8,128)S(1)}, u32[]{:S(2)}, u32[]{:S(2)}) %collective-permute-start.9) | collective-permute-done | bytes 163872 | tf_op jit(solution)/shard_map/ppermute | solution.py:239
  80.7 2.3 %collective-permute-done.19 = f32[32,768]{1,0:T(8,128)S(1)} collective-permute-done((f32[32,768]{1,0:T(8,128)S(1)}, f32[32,768]{1,0:T(8,128)S(1)}, u32[]{:S(2)}, u32[]{:S(2)}) %collective-permute-start.19) | collective-permute-done | bytes 98336 | tf_op jit(solution)/shard_map/ppermute | solution.py:239
  83.2 2.0 %reorder.1 = (f32[256,256]{1,0:T(8,128)S(1)}, f32[256,256]{1,0:T(8,128)S(1)}) custom-call(s32[6]{0:T(128)S(1)} %copy-done.2, f32[2,256,256]{2,1,0:T(8,128)S(1)} %copy-done.1), custom_call_target="tpu_custom_call" | custom-call | flops 1 | bytes 1 | tf_op jit(solution)/shard_map/reorder/pallas_call | solution.py:20
  85.2 4.6 %update_one.1 = (f32[4096,512]{1,0:T(8,128)S(1)}, f32[256,512]{1,0:T(8,128)S(1)}) custom-call(s32[6]{0:T(128)S(1)} %copy-done.2, f32[128,640]{1,0:T(8,128)S(1)} %add.32.refs_1_.refs_2_, f32[128,640]{1,0:T(8,128)S(1)} %collective-permute-done.3.refs_2_.refs_3_, f32[64,640]{1,0:T(8,128)S(1)} %add.34.refs_3_.refs_4_, ...), custom_call_target="tpu_custom_call" | custom-call | flops 1 | bytes 1 | tf_op jit(solution)/shard_map/update_one/pallas_call | solution.py:20
  89.8 6.0 %update_zero.1 = f32[4096,512]{1,0:T(8,128)} custom-call(s32[6]{0:T(128)S(1)} %copy-done.2, f32[256,512]{1,0:T(8,128)S(1)} %get-tuple-element.49.refs_1_, f32[128,640]{1,0:T(8,128)S(1)} %add.32.refs_1_.refs_2_, f32[128,640]{1,0:T(8,128)S(1)} %collective-permute-done.3.refs_2_.refs_3_, f32[64,640]{1,0:T(8,128)S(1)} %add.34.refs_3_.refs_4_, ...), custom_call_target="tpu_custom_call" | custom-call | flops 1 | bytes 1 | tf_op jit(solution)/shard_map/update_zero/pallas_call | solution.py:20
  (37 shorter events, 1.3 us)
Async XLA Ops:
  4.6 6.7 %collective-permute-start = (f32[128,4096]{1,0:T(8,128)}, f32[128,4096]{1,0:T(8,128)S(1)}, u32[]{:S(2)}, u32[]{:S(2)}) collective-permute-start(f32[128,4096]{1,0:T(8,128)} %get-tuple-element.39.refs_1_.refs_3_.refs_5_.refs_4_.in_ref.refs_6_.refs_11_), channel_id=1, source_target_pairs={{0,1},{1,0},{2,3},{3,2},{4,5},{5,4},{6,7},{7,6},{8,9},{9,8},{10,11... | collective-permute-start | bytes 6291464 | tf_op jit(solution)/shard_map/ppermute | solution.py:233
  5.1 6.2 %copy-start = (f32[128,4096]{1,0:T(8,128)S(1)}, f32[128,4096]{1,0:T(8,128)}, u32[]{:S(2)}) copy-start(f32[128,4096]{1,0:T(8,128)} %get-tuple-element.39.refs_1_.refs_3_.refs_5_.refs_4_.in_ref.refs_6_.refs_11_) | copy-start | bytes 6291460
  5.1 6.2 %copy-start.2 = (s32[6]{0:T(128)S(1)}, s32[6]{0:T(128)}, u32[]{:S(2)}) copy-start(s32[6]{0:T(128)} %stack.23.where_ref.refs_0_) | copy-start | bytes 76
  5.1 26.8 %collective-permute-start.4 = (f32[64,4096]{1,0:T(8,128)}, f32[64,4096]{1,0:T(8,128)S(1)}, u32[]{:S(2)}, u32[]{:S(2)}) collective-permute-start(f32[64,4096]{1,0:T(8,128)} %get-tuple-element.35), channel_id=1, source_target_pairs={{2,0},{3,1},{0,2},{1,3},{6,4},{7,5},{4,6},{5,7},{10,8},{11,9},{8,1... | collective-permute-start | bytes 3145736 | tf_op jit(solution)/shard_map/ppermute | solution.py:236
  16.1 15.8 %collective-permute-start.1 = (f32[128,640]{1,0:T(8,128)S(1)}, f32[128,640]{1,0:T(8,128)S(1)}, u32[]{:S(2)}, u32[]{:S(2)}) collective-permute-start(f32[128,640]{1,0:T(8,128)S(1)} %get-tuple-element.34), channel_id=1, source_target_pairs={{0,4},{4,0},{8,12},{12,8},{1,5},{5,1},{9,13},{13,9},{2,6},{6,2},{1... | collective-permute-start | bytes 983048 | tf_op jit(solution)/shard_map/ppermute | solution.py:239
  17.9 30.7 %collective-permute-start.11 = (f32[48,4096]{1,0:T(8,128)S(1)}, f32[48,4096]{1,0:T(8,128)S(1)}, u32[]{:S(2)}, u32[]{:S(2)}) collective-permute-start(f32[48,4096]{1,0:T(8,128)S(1)} %get-tuple-element.41), channel_id=1, source_target_pairs={{2,0},{3,1},{0,2},{1,3},{6,4},{7,5},{4,6},{5,7},{10,8},{11,9},{8,1... | collective-permute-start | bytes 2359304 | tf_op jit(solution)/shard_map/ppermute | solution.py:236
  32.0 3.7 %collective-permute-start.5 = (f32[32,4096]{1,0:T(8,128)S(1)}, f32[32,4096]{1,0:T(8,128)S(1)}, u32[]{:S(2)}, u32[]{:S(2)}) collective-permute-start(f32[32,4096]{1,0:T(8,128)S(1)} %get-tuple-element.54), channel_id=1, source_target_pairs={{0,1},{1,0},{2,3},{3,2},{4,5},{5,4},{6,7},{7,6},{8,9},{9,8},{10,11... | collective-permute-start | bytes 1572872 | tf_op jit(solution)/shard_map/ppermute | solution.py:233
  32.1 3.7 %collective-permute-start.6 = (f32[32,4096]{1,0:T(8,128)S(1)}, f32[32,4096]{1,0:T(8,128)S(1)}, u32[]{:S(2)}, u32[]{:S(2)}) collective-permute-start(f32[32,4096]{1,0:T(8,128)S(1)} %get-tuple-element.53), channel_id=1, source_target_pairs={{0,1},{1,0},{2,3},{3,2},{4,5},{5,4},{6,7},{7,6},{8,9},{9,8},{10,11... | collective-permute-start | bytes 1572872 | tf_op jit(solution)/shard_map/ppermute | solution.py:233
  32.6 18.2 %collective-permute-start.2 = (f32[128,640]{1,0:T(8,128)S(1)}, f32[128,640]{1,0:T(8,128)S(1)}, u32[]{:S(2)}, u32[]{:S(2)}) collective-permute-start(f32[128,640]{1,0:T(8,128)S(1)} %add.31), channel_id=1, source_target_pairs={{0,8},{4,12},{8,0},{12,4},{1,9},{5,13},{9,1},{13,5},{2,10},{6,14},... | collective-permute-start | bytes 983048 | tf_op jit(solution)/shard_map/ppermute | solution.py:239
  39.0 11.8 %collective-permute-start.7 = (f32[64,640]{1,0:T(8,128)S(1)}, f32[64,640]{1,0:T(8,128)S(1)}, u32[]{:S(2)}, u32[]{:S(2)}) collective-permute-start(f32[64,640]{1,0:T(8,128)S(1)} %get-tuple-element.38), channel_id=1, source_target_pairs={{0,4},{4,0},{8,12},{12,8},{1,5},{5,1},{9,13},{13,9},{2,6},{6,2},{1... | collective-permute-start | bytes 491528 | tf_op jit(solution)/shard_map/ppermute | solution.py:239
  50.9 7.3 %collective-permute-start.12 = (f32[24,4096]{1,0:T(8,128)S(1)}, f32[24,4096]{1,0:T(8,128)S(1)}, u32[]{:S(2)}, u32[]{:S(2)}) collective-permute-start(f32[24,4096]{1,0:T(8,128)S(1)} %get-tuple-element.56), channel_id=1, source_target_pairs={{0,1},{1,0},{2,3},{3,2},{4,5},{5,4},{6,7},{7,6},{8,9},{9,8},{10,11... | collective-permute-start | bytes 1179656 | tf_op jit(solution)/shard_map/ppermute | solution.py:233
  50.9 7.2 %collective-permute-start.13 = (f32[24,4096]{1,0:T(8,128)S(1)}, f32[24,4096]{1,0:T(8,128)S(1)}, u32[]{:S(2)}, u32[]{:S(2)}) collective-permute-start(f32[24,4096]{1,0:T(8,128)S(1)} %get-tuple-element.55), channel_id=1, source_target_pairs={{0,1},{1,0},{2,3},{3,2},{4,5},{5,4},{6,7},{7,6},{8,9},{9,8},{10,11... | collective-permute-start | bytes 1179656 | tf_op jit(solution)/shard_map/ppermute | solution.py:233
  51.4 10.3 %collective-permute-start.10 = (f32[16,4096]{1,0:T(8,128)S(1)}, f32[16,4096]{1,0:T(8,128)S(1)}, u32[]{:S(2)}, u32[]{:S(2)}) collective-permute-start(f32[16,4096]{1,0:T(8,128)S(1)} %get-tuple-element.40), channel_id=1, source_target_pairs={{2,0},{3,1},{0,2},{1,3},{6,4},{7,5},{4,6},{5,7},{10,8},{11,9},{8,1... | collective-permute-start | bytes 786440 | tf_op jit(solution)/shard_map/ppermute | solution.py:236
  53.0 26.7 %collective-permute-start.3 = (f32[128,640]{1,0:T(8,128)S(1)}, f32[128,640]{1,0:T(8,128)S(1)}, u32[]{:S(2)}, u32[]{:S(2)}) collective-permute-start(f32[128,640]{1,0:T(8,128)S(1)} %add.32.refs_1_.refs_2_), channel_id=1, source_target_pairs={{0,4},{4,0},{8,12},{12,8},{1,5},{5,1},{9,13},{13,9},{2,6},{6,2},{1... | collective-permute-start | bytes 983048 | tf_op jit(solution)/shard_map/ppermute | solution.py:239
  53.8 18.7 %collective-permute-start.8 = (f32[64,640]{1,0:T(8,128)S(1)}, f32[64,640]{1,0:T(8,128)S(1)}, u32[]{:S(2)}, u32[]{:S(2)}) collective-permute-start(f32[64,640]{1,0:T(8,128)S(1)} %add.33), channel_id=1, source_target_pairs={{0,8},{4,12},{8,0},{12,4},{1,9},{5,13},{9,1},{13,5},{2,10},{6,14},... | collective-permute-start | bytes 491528 | tf_op jit(solution)/shard_map/ppermute | solution.py:239
  61.6 7.5 %collective-permute-start.16 = (f32[48,768]{1,0:T(8,128)S(1)}, f32[48,768]{1,0:T(8,128)S(1)}, u32[]{:S(2)}, u32[]{:S(2)}) collective-permute-start(f32[48,768]{1,0:T(8,128)S(1)} %get-tuple-element.44), channel_id=1, source_target_pairs={{0,4},{4,0},{8,12},{12,8},{1,5},{5,1},{9,13},{13,9},{2,6},{6,2},{1... | collective-permute-start | bytes 442376 | tf_op jit(solution)/shard_map/ppermute | solution.py:239
  61.7 12.6 %collective-permute-start.14 = (f32[8,4096]{1,0:T(8,128)S(1)}, f32[8,4096]{1,0:T(8,128)S(1)}, u32[]{:S(2)}, u32[]{:S(2)}) collective-permute-start(f32[8,4096]{1,0:T(8,128)S(1)} %get-tuple-element.58), channel_id=1, source_target_pairs={{0,1},{1,0},{2,3},{3,2},{4,5},{5,4},{6,7},{7,6},{8,9},{9,8},{10,11... | collective-permute-start | bytes 393224 | tf_op jit(solution)/shard_map/ppermute | solution.py:233
  61.8 12.5 %collective-permute-start.15 = (f32[8,4096]{1,0:T(8,128)S(1)}, f32[8,4096]{1,0:T(8,128)S(1)}, u32[]{:S(2)}, u32[]{:S(2)}) collective-permute-start(f32[8,4096]{1,0:T(8,128)S(1)} %get-tuple-element.57), channel_id=1, source_target_pairs={{0,1},{1,0},{2,3},{3,2},{4,5},{5,4},{6,7},{7,6},{8,9},{9,8},{10,11... | collective-permute-start | bytes 393224 | tf_op jit(solution)/shard_map/ppermute | solution.py:233
  69.2 9.8 %collective-permute-start.17 = (f32[48,768]{1,0:T(8,128)S(1)}, f32[48,768]{1,0:T(8,128)S(1)}, u32[]{:S(2)}, u32[]{:S(2)}) collective-permute-start(f32[48,768]{1,0:T(8,128)S(1)} %add.35), channel_id=1, source_target_pairs={{0,8},{4,12},{8,0},{12,4},{1,9},{5,13},{9,1},{13,5},{2,10},{6,14},... | collective-permute-start | bytes 442376 | tf_op jit(solution)/shard_map/ppermute | solution.py:239
  72.5 10.7 %copy-start.1 = (f32[2,256,256]{2,1,0:T(8,128)S(1)}, f32[2,256,256]{2,1,0:T(8,128)}, u32[]{:S(2)}) copy-start(f32[2,256,256]{2,1,0:T(8,128)} %in_ref.3) | copy-start | bytes 1572868
  72.5 8.2 %collective-permute-start.9 = (f32[64,640]{1,0:T(8,128)S(1)}, f32[64,640]{1,0:T(8,128)S(1)}, u32[]{:S(2)}, u32[]{:S(2)}) collective-permute-start(f32[64,640]{1,0:T(8,128)S(1)} %add.34.refs_3_.refs_4_), channel_id=1, source_target_pairs={{0,4},{4,0},{8,12},{12,8},{1,5},{5,1},{9,13},{13,9},{2,6},{6,2},{1... | collective-permute-start | bytes 491528 | tf_op jit(solution)/shard_map/ppermute | solution.py:239
  77.2 5.8 %collective-permute-start.19 = (f32[32,768]{1,0:T(8,128)S(1)}, f32[32,768]{1,0:T(8,128)S(1)}, u32[]{:S(2)}, u32[]{:S(2)}) collective-permute-start(f32[32,768]{1,0:T(8,128)S(1)} %project_zero_2.1), channel_id=1, source_target_pairs={{0,4},{4,0},{8,12},{12,8},{1,5},{5,1},{9,13},{13,9},{2,6},{6,2},{1... | collective-permute-start | bytes 294920 | tf_op jit(solution)/shard_map/ppermute | solution.py:239
  79.0 10.8 %collective-permute-start.18 = (f32[48,768]{1,0:T(8,128)S(1)}, f32[48,768]{1,0:T(8,128)S(1)}, u32[]{:S(2)}, u32[]{:S(2)}) collective-permute-start(f32[48,768]{1,0:T(8,128)S(1)} %add.36.refs_6_), channel_id=1, source_target_pairs={{0,4},{4,0},{8,12},{12,8},{1,5},{5,1},{9,13},{13,9},{2,6},{6,2},{1... | collective-permute-start | bytes 442376 | tf_op jit(solution)/shard_map/ppermute | solution.py:239
  83.0 6.8 %collective-permute-start.20 = (f32[32,768]{1,0:T(8,128)S(1)}, f32[32,768]{1,0:T(8,128)S(1)}, u32[]{:S(2)}, u32[]{:S(2)}) collective-permute-start(f32[32,768]{1,0:T(8,128)S(1)} %add.37.refs_8_), channel_id=1, source_target_pairs={{0,8},{4,12},{8,0},{12,4},{1,9},{5,13},{9,1},{13,5},{2,10},{6,14},... | collective-permute-start | bytes 294920 | tf_op jit(solution)/shard_map/ppermute | solution.py:239

commit v6 on v5

--- a/solution.py
+++ b/solution.py
@@ -6,8 +6,8 @@
 from jax.sharding import PartitionSpec as P
 
 F32, BF16 = jnp.float32, jnp.bfloat16
-PIECES = ((1, 0, 64, True), (0, 0, 48, True), (0, 48, 64, False))
-SWAP_PARTS = 2
+PIECES = ((1, 0, 64, True), (0, 0, 40, True), (0, 40, 64, False))
+SWAP_ROWS = (16, 16, 32)
 NN = (((1,), (0,)), ((), ()))
 NT = (((1,), (1,)), ((), ()))
 TN = (((0,), (0,)), ((), ()))
@@ -62,32 +62,28 @@
     return [pl.ds(at, step) for at in range(0, here, step)]
 
 
-def cut(where, vectors, first):
+def cut(where, vectors, width):
     _, share, here = vectors.shape
-    block, low, high = first
-    begin = (1 - block) * share + low
-
     strip = min(share, 16)
     strips = [(k, at) for k in (1, 0) for at in range(0, share, strip)]
 
-    def body(where_ref, in_ref, piece, mine, sems):
+    def body(where_ref, in_ref, zeros, ones, sems):
+        outs = (zeros, ones)
         copies = []
         for n, (k, at) in enumerate(strips):
-            to = mine.at[(1 - k) * share + at : (1 - k) * share + at + strip]
-            copies.append(pltpu.make_async_copy(in_ref.at[k, at : at + strip], to, sems.at[n]))
+            ds = pl.ds(at, strip)
+            copies.append(pltpu.make_async_copy(in_ref.at[k, ds], outs[k].at[ds], sems.at[n]))
             copies[-1].start()
         for copy, (k, at) in zip(copies, strips):
             copy.wait()
-            shape = (strip, here)
+            shape = (strip, min(here, (k + 1) * width))
             along = lax.broadcasted_iota(jnp.int32, shape, 0) + (where_ref[0] + at + k * where_ref[2])
             across = lax.broadcasted_iota(jnp.int32, shape, 1) + where_ref[1]
-            rows = slice((1 - k) * share + at, (1 - k) * share + at + strip)
-            mine[rows] = jnp.where(across >= along, mine[rows], 0.0)
-        piece[...] = mine[begin : begin + high - low]
-
-    outs = [array(high - low, here), array(2 * share, here)]
+            part = outs[k][at : at + strip, : shape[1]]
+            outs[k][at : at + strip, : shape[1]] = jnp.where(across >= along, part, 0.0)
+
     sems = [pltpu.SemaphoreType.DMA((len(strips),))]
-    return call(body, "cut", (where, vectors), [SCALARS, HBM], outs, [VMEM] * 2, sems, 56)
+    return call(body, "cut", (where, vectors), [SCALARS, HBM], [array(share, here)] * 2, [VMEM] * 2, sems, 4)
 
 
 def parts_of(mine, places):
@@ -121,11 +117,10 @@
     return jnp.concatenate([ref[at : at + count, ds] for ref, (_, count, at) in zip(refs, pieces)])
 
 
-def project(name, rows, partners, high, low, bit=None, gram_rows=None):
+def project(name, rows, partners, high, low, bit=None):
     here, nc = high.shape
     height = sum(count for _, count, _ in rows)
     extra = sum(count for _, count, _ in partners)
-    some = height if gram_rows is None else gram_rows
     steps = steps_of(here, 512)
 
     def body(*refs):
@@ -139,14 +134,13 @@
         for n, ds in enumerate(steps):
             vh, vl = split(rows_of(row_refs, rows, ds))
             main = three(vh, vl, high_ref[ds, :], low_ref[ds, :], NN)
-            gram = three(vh[:some], vl[:some], *split(rows_of(partner_refs, partners, ds)), NT)
+            if partners:
+                gram = three(vh, vl, *split(rows_of(partner_refs, partners, ds)), NT)
+                main = jnp.concatenate([main, gram], axis=1)
             if n == 0:
-                acc[:, :nc], acc[:some, nc:] = main, gram
-                if some < height:
-                    acc[some:, nc:] = jnp.zeros((height - some, extra), F32)
+                acc[...] = main
             else:
-                acc[:, :nc] += main
-                acc[:some, nc:] += gram
+                acc[...] += main
         if bit is None:
             outs[0][...] = acc[...]
         else:
@@ -264,20 +258,23 @@
         for block, low, high, _ in PIECES:
             low, high = low * share // 64 // 8 * 8, high * share // 64 // 8 * 8
             pieces.append((block, low, high))
+        swap_rows = dict(zip(pieces, SWAP_ROWS))
         halves = {piece: chosen for piece, (*_, chosen) in zip(pieces, PIECES)}
 
         def after(value, *others):
             return lax.optimization_barrier((value, *others))[0]
 
-        sent, mine = cut(where, vectors, pieces[0])
-        far = [(step, pieces[0], from_chip(sent, step)) for step in range(1, chips)]
-        sib = core_swap(mine)
-        high, low = load(after(eigvecs, mine))
-        places = [((1 - block) * share + a, (1 - block) * share + b) for block, a, b in pieces[1:]]
-        for piece, sent in zip(pieces[1:], parts_of(after(mine, high), places)):
+        mine = cut(where, vectors, width)
+        whole = [(step, pieces[0], from_chip(mine[1], step)) for step in range(1, chips)]
+        sib = [core_swap(m) for m in mine]
+        high, low = load(after(eigvecs, *mine))
+        far, places = whole, [(a, b) for _, a, b in pieces[1:]]
+        for piece, sent in zip(pieces[1:], parts_of(after(mine[0], high), places)):
             far += [(step, piece, from_chip(sent, step)) for step in range(1, chips)]
-        own = {1: [(mine, share, 0), (sib, share, 0)], 0: [(mine, share, share), (sib, share, share)]}
+        own = {k: [(mine[k], share, 0), (sib[k], share, 0)] for k in (0, 1)}
         segments = {k: [(0, 0, 0, share), (0, 1, 0, share)] for k in (0, 1)}
+        for step, (block, a, b), _ in far:
+            segments[block] += [(step, 0, a, b), (step, 1, a, b)]
         all_ones, all_zeros = list(own[1]), list(own[0])
         running, flying, done = {}, {}, {}
 
@@ -294,40 +291,43 @@
         def arrived(*names):
             return [flying[name] for name in names if name in flying]
 
-        front = project("project_own", own[1] + own[0], own[0], high, low, bit, half)
-        running["own"] = sums(*front)
-        start("own")
+        keep, send = project("project_own1", own[1], own[0], high, low, bit)
+        running["own1"] = sums(keep, send)
+        start("own1")
+        front = project("project_own0", own[0], [], after(high, keep), low, bit)
+        running["own0"] = sums(*front)
+        start("own0")
+        t0, t1 = reorder(where, after(factors, *front), share, chips, segments)
+        front = (*front, t0)
         last = len(far) - 1
         for n, (step, (block, first, final), value) in enumerate(far):
-            waits = list(running) if n < last or last != 2 else []
+            waits = list(running) if last != 2 else (("own1", "own0"), ("own1", 0, "own0"), ("own1",))[n]
             value = after(value, *front, *arrived(*waits))
-            start(*waits)
+            start(*waits if last != 2 else (("own1", "own0"), ("own1",), ())[n])
             split_rows = halves[block, first, final]
             pair = [(value, final - first, 0)]
-            parts = SWAP_PARTS if (final - first) % (8 * SWAP_PARTS) == 0 else 1
-            each = (final - first) // parts
-            for part in range(parts):
-                pair.append((core_swap(value[part * each : (part + 1) * each]), each, 0))
-            segments[block] += [(step, 0, first, final), (step, 1, first, final)]
-            ready = high
-            if n == last == 2:
-                ready = after(high, *arrived(0, 1))
-                start(0, 1)
+            for at in range(0, final - first, swap_rows[block, first, final]):
+                upto = min(at + swap_rows[block, first, final], final - first)
+                pair.append((core_swap(value[at:upto]), upto - at, 0))
             if block == 1:
                 all_ones += pair
-                front = project(f"project_one_{n}", pair, own[0], ready, low, bit if split_rows else None)
+                front = project(f"project_one_{n}", pair, own[0], high, low, bit if split_rows else None)
             else:
                 all_zeros += pair
-                front = project(f"project_zero_{n}", pair, all_ones, ready, low, bit if split_rows else None)
+                front = project(f"project_zero_{n}", pair, all_ones, high, low, bit if split_rows else None)
             running[n] = sums(*front)
             start(n)
-        if last in flying:
-            flying[last] = after(flying[last], *arrived("own", 0))
+            if n == 1 and last == 2:
+                flying[0] = after(flying[0], *front)
+                start(0)
+        if last == 2:
+            flying["own0"] = after(flying["own0"], *front)
+            flying[last] = after(flying[last], *arrived(0))
+            start("own0", 0)
         while running:
             start(*list(running))
-        ones = [("own", True)] + [(n, halves[f[1]]) for n, f in enumerate(far) if f[1][0] == 1]
-        zeros = [(n, halves[f[1]]) for n, f in enumerate(far) if f[1][0] == 0]
-        t0, t1 = reorder(where, after(factors, *front), share, chips, segments)
+        ones = [("own1", True)] + [(n, halves[f[1]]) for n, f in enumerate(far) if f[1][0] == 1]
+        zeros = [("own0", True)] + [(n, halves[f[1]]) for n, f in enumerate(far) if f[1][0] == 0]
         ones_flat, zeros_flat = ([v for key, _ in group for v in done[key]] for group in (ones, zeros))
 
         def joined(where_ref, refs, group, columns):
@@ -339,16 +339,15 @@
             return parts
 
         def make_one(where_ref, *refs):
-            parts = joined(where_ref, refs, ones, slice(0, nc))
-            return jnp.concatenate(parts[:1] + parts[2:])
+            return jnp.concatenate(joined(where_ref, refs, ones, slice(0, nc)))
 
         def make_zero(where_ref, scaled_ref, *refs):
             ones_refs, zero_refs = refs[: len(ones_flat)], refs[len(ones_flat) :]
             scaled = scaled_ref[...]
-            parts = joined(where_ref, ones_refs, ones, slice(nc, nc + half))
-            turned_gram = jnp.concatenate(parts[:1] + parts[2:])
-            front = joined(where_ref, ones_refs[:2], ones[:1], slice(0, nc))[1] - short_dot(turned_gram, scaled, TN)
-            later = jnp.concatenate(joined(where_ref, zero_refs, zeros, slice(None)))
+            turned_gram = jnp.concatenate(joined(where_ref, ones_refs, ones, slice(nc, nc + half)))
+            front = jnp.concatenate(joined(where_ref, zero_refs[:2], zeros[:1], slice(None)))
+            later = jnp.concatenate(joined(where_ref, zero_refs[2:], zeros[1:], slice(None)))
+            front -= short_dot(turned_gram, scaled, TN)
             return jnp.concatenate([front, later[:, :nc] - short_dot(later[:, nc:], scaled)])
 
         current, scaled = update("update_one", make_one, [bit, *ones_flat], t1, all_ones, [high, low], False)

time: 96.1 us -> 90.3 us (0.940)
  waiting for transfers between devices: 35.2 us -> 29 us
  Pallas kernels: 34.5 us -> 31.9 us
  starting transfers between devices: 25 us -> 27 us
  local copies, waits for them, and re-layouts: 0.82 us -> 1.79 us
    ppermute x3, waiting for transfers between devices: 21.3 us -> 11.9 us  [from_chip(): lax.ppermute(value, 'col', [((i + 2 * step) % cols, i) for i in range(col...]
    pallas_call x10 -> x11, Pallas kernels: 34.5 us -> 31.9 us  [call(): pl.pallas_call(body, in_specs=specs, out_specs=out_specs, out_shape=outs,...]
    ppermute x11 -> x14, starting transfers between devices: 18 us -> 20.1 us  [row_swap(): return lax.ppermute(value, 'row', [(i, i ^ step) for i in range(rows)])]
    ppermute x7 -> x10, waiting for transfers between devices: 0.02 us -> 1.85 us  [core_swap(): return lax.ppermute(value, 'col', [(i, i ^ 1) for i in range(cols)])]
    unnamed x6 -> x4, local copies, waits for them, and re-layouts: 0.01 us -> 1.6 us
    ppermute x11 -> x14, waiting for transfers between devices: 13.8 us -> 15.3 us  [row_swap(): return lax.ppermute(value, 'row', [(i, i ^ step) for i in range(rows)])]
    ppermute x7 -> x10, starting transfers between devices: 2.22 us -> 2.32 us  [core_swap(): return lax.ppermute(value, 'col', [(i, i ^ 1) for i in range(cols)])]
  transfers between devices with their start and end apart: 21 -> 27, of which waited for: 7 -> 12; matrix products, arithmetic and copies ran while one was open for 0% -> 0% of each run, Pallas kernels for 26% -> 28%
where the time goes in v6:
time: 90.3 us; the launch traced here: 90.2 us
  Pallas kernels  31.9 us (35%)
  waiting for transfers between devices  29 us (32%)
  starting transfers between devices  27 us (30%)
  local copies, waits for them, and re-layouts  1.79 us (2%)
    pallas_call x11, Pallas kernels, call(): pl.pallas_call(body, in_specs=specs, out_specs=out_specs, out_shape=outs,...  31.9 us
    ppermute x14, starting transfers between devices, row_swap(): return lax.ppermute(value, 'row', [(i, i ^ step) for i in range(rows)])  20.1 us
    ppermute x14, waiting for transfers between devices, row_swap(): return lax.ppermute(value, 'row', [(i, i ^ step) for i in range(rows)])  15.3 us
    ppermute x3, waiting for transfers between devices, from_chip(): lax.ppermute(value, 'col', [((i + 2 * step) % cols, i) for i in range(col...  11.9 us
    ppermute x3, starting transfers between devices, from_chip(): lax.ppermute(value, 'col', [((i + 2 * step) % cols, i) for i in range(col...  4.58 us
    ppermute x10, starting transfers between devices, core_swap(): return lax.ppermute(value, 'col', [(i, i ^ 1) for i in range(cols)])  2.32 us
    ppermute x10, waiting for transfers between devices, core_swap(): return lax.ppermute(value, 'col', [(i, i ^ 1) for i in range(cols)])  1.85 us
  transfers between devices with their start and end apart: 27, of which 12 were waited for; matrix products, arithmetic and copies ran while one was open for 0% of the time, Pallas kernels for 28%

profile of v6, /device:TPU:0, one launch (start us, length us, event | category | flops | bytes accessed | tf_op | source)
XLA Modules:
  0.0 90.2 jit_solution(6968155095022079724)
XLA Ops:
  0.1 1.6 %copy-done = f32[2,64,4096]{2,1,0:T(8,128)S(1)} copy-done((f32[2,64,4096]{2,1,0:T(8,128)S(1)}, f32[2,64,4096]{2,1,0:T(8,128)}, u32[]{:S(2)}) %copy-start) | copy-done | bytes 2097176
  1.7 0.8 cut.1
  3.1 2.9 %collective-permute-start.5 = (f32[64,4096]{1,0:T(8,128)S(1)}, f32[64,4096]{1,0:T(8,128)S(1)}, u32[]{:S(2)}, u32[]{:S(2)}) collective-permute-start(f32[64,4096]{1,0:T(8,128)S(1)} %get-tuple-element.33.refs_1_.refs_5_.refs_6_.refs_2_), channel_id=1, source_target_pairs={{2,0},{3,1},{0,2},{1,3},{6,4},{7,5},{4,6},{5,7},{10,8},{11,9},{8,1... | collective-permute-start | bytes 3145736 | tf_op jit(solution)/shard_map/ppermute | solution.py:230
  6.0 3.6 %load.1 = (bf16[4096,512]{1,0:T(8,128)(2,1)S(1)}, bf16[4096,512]{1,0:T(8,128)(2,1)S(1)}) custom-call(f32[4096,512]{1,0:T(8,128)} %in_ref.2), custom_call_target="tpu_custom_call" | custom-call | flops 1 | bytes 1 | tf_op jit(solution)/shard_map/load/pallas_call | solution.py:20
  9.7 3.2 %project_own1.1 = (f32[64,640]{1,0:T(8,128)S(1)}, f32[64,640]{1,0:T(8,128)S(1)}) custom-call(s32[6]{0:T(128)S(1)} %stack.23.where_ref.refs_0_, f32[64,4096]{1,0:T(8,128)S(1)} %get-tuple-element.33.refs_1_.refs_5_.refs_6_.refs_2_, f32[64,4096]{1,0:T(8,128)S(1)} %collective-permute-done.refs_2_.refs_6_.refs_7_.refs_3_, ...), custom_call_target="tpu_custom_call" | custom-call | flops 1 | bytes 1 | tf_op jit(solution)/shard_map/project_own1/pallas_call | solution.py:20
  12.9 1.6 %collective-permute-start.2 = (f32[64,640]{1,0:T(8,128)S(1)}, f32[64,640]{1,0:T(8,128)S(1)}, u32[]{:S(2)}, u32[]{:S(2)}) collective-permute-start(f32[64,640]{1,0:T(8,128)S(1)} %get-tuple-element.39), channel_id=1, source_target_pairs={{0,4},{4,0},{8,12},{12,8},{1,5},{5,1},{9,13},{13,9},{2,6},{6,2},{1... | collective-permute-start | bytes 491528 | tf_op jit(solution)/shard_map/ppermute | solution.py:233
  14.5 2.3 %project_own0.1 = (f32[64,512]{1,0:T(8,128)S(1)}, f32[64,512]{1,0:T(8,128)S(1)}) custom-call(s32[6]{0:T(128)S(1)} %stack.23.where_ref.refs_0_, f32[64,4096]{1,0:T(8,128)S(1)} %get-tuple-element.48.refs_3_.refs_1_.refs_6_.in_ref.refs_13_, f32[64,4096]{1,0:T(8,128)S(1)} %collective-permute-done.1.refs_4_.refs_2_.refs_7_.refs_14_, ...), custom_call_target="tpu_custom_call" | custom-call | flops 1 | bytes 1 | tf_op jit(solution)/shard_map/project_own0/pallas_call | solution.py:20
  17.6 2.0 %reorder.1 = (f32[256,256]{1,0:T(8,128)S(1)}, f32[256,256]{1,0:T(8,128)S(1)}) custom-call(s32[6]{0:T(128)S(1)} %stack.23.where_ref.refs_0_, f32[2,256,256]{2,1,0:T(8,128)S(1)} %copy-done.1), custom_call_target="tpu_custom_call" | custom-call | flops 1 | bytes 1 | tf_op jit(solution)/shard_map/reorder/pallas_call | solution.py:20
  19.6 10.4 %collective-permute-done.5.refs_1_.refs_7_.refs_8_.refs_4_ = f32[64,4096]{1,0:T(8,128)S(1)} collective-permute-done((f32[64,4096]{1,0:T(8,128)S(1)}, f32[64,4096]{1,0:T(8,128)S(1)}, u32[]{:S(2)}, u32[]{:S(2)}) %collective-permute-start.5) | collective-permute-done | bytes 1048608 | tf_op jit(solution)/shard_map/ppermute | solution.py:230
  31.7 3.2 %collective-permute-start.3 = (f32[64,640]{1,0:T(8,128)S(1)}, f32[64,640]{1,0:T(8,128)S(1)}, u32[]{:S(2)}, u32[]{:S(2)}) collective-permute-start(f32[64,640]{1,0:T(8,128)S(1)} %add.37), channel_id=1, source_target_pairs={{0,8},{4,12},{8,0},{12,4},{1,9},{5,13},{9,1},{13,5},{2,10},{6,14},... | collective-permute-start | bytes 491528 | tf_op jit(solution)/shard_map/ppermute | solution.py:233
  34.8 3.2 %project_one_0.1 = (f32[64,640]{1,0:T(8,128)S(1)}, f32[64,640]{1,0:T(8,128)S(1)}) custom-call(s32[6]{0:T(128)S(1)} %stack.23.where_ref.refs_0_, f32[64,4096]{1,0:T(8,128)S(1)} %collective-permute-done.5.refs_1_.refs_7_.refs_8_.refs_4_, f32[16,4096]{1,0:T(8,128)S(1)} %collective-permute-done.7.refs_2_.refs_8_.refs_9_.refs_5_, ...), custom_call_target="tpu_custom_call" | custom-call | flops 1 | bytes 1 | tf_op jit(solution)/shard_map/project_one_0/pallas_call | solution.py:20
  38.0 1.6 %collective-permute-start.11 = (f32[64,640]{1,0:T(8,128)S(1)}, f32[64,640]{1,0:T(8,128)S(1)}, u32[]{:S(2)}, u32[]{:S(2)}) collective-permute-start(f32[64,640]{1,0:T(8,128)S(1)} %get-tuple-element.47), channel_id=1, source_target_pairs={{0,4},{4,0},{8,12},{12,8},{1,5},{5,1},{9,13},{13,9},{2,6},{6,2},{1... | collective-permute-start | bytes 491528 | tf_op jit(solution)/shard_map/ppermute | solution.py:233
  39.7 1.2 %collective-permute-start.13 = (f32[64,512]{1,0:T(8,128)S(1)}, f32[64,512]{1,0:T(8,128)S(1)}, u32[]{:S(2)}, u32[]{:S(2)}) collective-permute-start(f32[64,512]{1,0:T(8,128)S(1)} %add.39), channel_id=1, source_target_pairs={{0,8},{4,12},{8,0},{12,4},{1,9},{5,13},{9,1},{13,5},{2,10},{6,14},... | collective-permute-start | bytes 393224 | tf_op jit(solution)/shard_map/ppermute | solution.py:233
  40.9 1.5 %collective-permute-start.19 = (f32[24,4096]{1,0:T(8,128)S(1)}, f32[24,4096]{1,0:T(8,128)S(1)}, u32[]{:S(2)}, u32[]{:S(2)}) collective-permute-start(f32[24,4096]{1,0:T(8,128)S(1)} %get-tuple-element.56), channel_id=1, source_target_pairs={{2,0},{3,1},{0,2},{1,3},{6,4},{7,5},{4,6},{5,7},{10,8},{11,9},{8,1... | collective-permute-start | bytes 1179656 | tf_op jit(solution)/shard_map/ppermute | solution.py:230
  42.4 1.5 %collective-permute-done.12.refs_1_.refs_15_ = f32[40,4096]{1,0:T(8,128)S(1)} collective-permute-done((f32[40,4096]{1,0:T(8,128)S(1)}, f32[40,4096]{1,0:T(8,128)S(1)}, u32[]{:S(2)}, u32[]{:S(2)}) %collective-permute-start.12) | collective-permute-done | bytes 655392 | tf_op jit(solution)/shard_map/ppermute | solution.py:230
  43.8 4.8 %collective-permute-done.13 = f32[64,512]{1,0:T(8,128)S(1)} collective-permute-done((f32[64,512]{1,0:T(8,128)S(1)}, f32[64,512]{1,0:T(8,128)S(1)}, u32[]{:S(2)}, u32[]{:S(2)}) %collective-permute-start.13) | collective-permute-done | bytes 131104 | tf_op jit(solution)/shard_map/ppermute | solution.py:233
  50.1 1.3 %collective-permute-done.16.refs_4_.refs_18_ = f32[8,4096]{1,0:T(8,128)S(1)} collective-permute-done((f32[8,4096]{1,0:T(8,128)S(1)}, f32[8,4096]{1,0:T(8,128)S(1)}, u32[]{:S(2)}, u32[]{:S(2)}) %collective-permute-start.16) | collective-permute-done | bytes 131104 | tf_op jit(solution)/shard_map/ppermute | solution.py:227
  51.4 3.5 %project_zero_1.1 = (f32[40,768]{1,0:T(8,128)S(1)}, f32[40,768]{1,0:T(8,128)S(1)}) custom-call(s32[6]{0:T(128)S(1)} %stack.23.where_ref.refs_0_, f32[40,4096]{1,0:T(8,128)S(1)} %collective-permute-done.12.refs_1_.refs_15_, f32[16,4096]{1,0:T(8,128)S(1)} %collective-permute-done.14.refs_2_.refs_16_, f32[16,4096]{1,0:T(8,128)S(1)} %collective-permute-done.15.refs_3_.refs_17_, ...), custom_call_target="tpu_custom_call" | custom-call | flops 1 | bytes 1 | tf_op jit(solution)/shard_map/project_zero_1/pallas_call | solution.py:20
  54.9 1.1 %collective-permute-done.4.refs_2_.refs_3_ = f32[64,640]{1,0:T(8,128)S(1)} collective-permute-done((f32[64,640]{1,0:T(8,128)S(1)}, f32[64,640]{1,0:T(8,128)S(1)}, u32[]{:S(2)}, u32[]{:S(2)}) %collective-permute-start.4) | collective-permute-done | bytes 163872 | tf_op jit(solution)/shard_map/ppermute | solution.py:233
  56.0 1.0 %collective-permute-start.22 = (f32[40,768]{1,0:T(8,128)S(1)}, f32[40,768]{1,0:T(8,128)S(1)}, u32[]{:S(2)}, u32[]{:S(2)}) collective-permute-start(f32[40,768]{1,0:T(8,128)S(1)} %get-tuple-element.52), channel_id=1, source_target_pairs={{0,4},{4,0},{8,12},{12,8},{1,5},{5,1},{9,13},{13,9},{2,6},{6,2},{1... | collective-permute-start | bytes 368648 | tf_op jit(solution)/shard_map/ppermute | solution.py:233
  57.1 3.1 %collective-permute-start.17 = (f32[64,640]{1,0:T(8,128)S(1)}, f32[64,640]{1,0:T(8,128)S(1)}, u32[]{:S(2)}, u32[]{:S(2)}) collective-permute-start(f32[64,640]{1,0:T(8,128)S(1)} %add.40), channel_id=1, source_target_pairs={{0,8},{4,12},{8,0},{12,4},{1,9},{5,13},{9,1},{13,5},{2,10},{6,14},... | collective-permute-start | bytes 491528 | tf_op jit(solution)/shard_map/ppermute | solution.py:233
  60.2 2.7 %project_zero_2.1 = f32[48,768]{1,0:T(8,128)S(1)} custom-call(f32[24,4096]{1,0:T(8,128)S(1)} %collective-permute-done.19.refs_0_.refs_19_, f32[24,4096]{1,0:T(8,128)S(1)} %collective-permute-done.20.refs_1_.refs_20_, f32[64,4096]{1,0:T(8,128)S(1)} %get-tuple-element.33.refs_1_.refs_5_.refs_6_.refs_2_, ...), custom_call_target="tpu_custom_call" | custom-call | flops 1 | bytes 1 | tf_op jit(solution)/shard_map/project_zero_2/pallas_call | solution.py:20
  62.9 1.1 %collective-permute-start.25 = (f32[48,768]{1,0:T(8,128)S(1)}, f32[48,768]{1,0:T(8,128)S(1)}, u32[]{:S(2)}, u32[]{:S(2)}) collective-permute-start(f32[48,768]{1,0:T(8,128)S(1)} %project_zero_2.1), channel_id=1, source_target_pairs={{0,4},{4,0},{8,12},{12,8},{1,5},{5,1},{9,13},{13,9},{2,6},{6,2},{1... | collective-permute-start | bytes 442376 | tf_op jit(solution)/shard_map/ppermute | solution.py:233
  64.4 0.9 %collective-permute-start.23 = (f32[40,768]{1,0:T(8,128)S(1)}, f32[40,768]{1,0:T(8,128)S(1)}, u32[]{:S(2)}, u32[]{:S(2)}) collective-permute-start(f32[40,768]{1,0:T(8,128)S(1)} %add.43), channel_id=1, source_target_pairs={{0,8},{4,12},{8,0},{12,4},{1,9},{5,13},{9,1},{13,5},{2,10},{6,14},... | collective-permute-start | bytes 368648 | tf_op jit(solution)/shard_map/ppermute | solution.py:233
  65.4 3.5 %collective-permute-done.17 = f32[64,640]{1,0:T(8,128)S(1)} collective-permute-done((f32[64,640]{1,0:T(8,128)S(1)}, f32[64,640]{1,0:T(8,128)S(1)}, u32[]{:S(2)}, u32[]{:S(2)}) %collective-permute-start.17) | collective-permute-done | bytes 163872 | tf_op jit(solution)/shard_map/ppermute | solution.py:233
  68.9 1.2 %collective-permute-start.18 = (f32[64,640]{1,0:T(8,128)S(1)}, f32[64,640]{1,0:T(8,128)S(1)}, u32[]{:S(2)}, u32[]{:S(2)}) collective-permute-start(f32[64,640]{1,0:T(8,128)S(1)} %add.41.refs_3_.refs_4_), channel_id=1, source_target_pairs={{0,4},{4,0},{8,12},{12,8},{1,5},{5,1},{9,13},{13,9},{2,6},{6,2},{1... | collective-permute-start | bytes 491528 | tf_op jit(solution)/shard_map/ppermute | solution.py:233
  70.1 2.5 %collective-permute-done.25 = f32[48,768]{1,0:T(8,128)S(1)} collective-permute-done((f32[48,768]{1,0:T(8,128)S(1)}, f32[48,768]{1,0:T(8,128)S(1)}, u32[]{:S(2)}, u32[]{:S(2)}) %collective-permute-start.25) | collective-permute-done | bytes 147488 | tf_op jit(solution)/shard_map/ppermute | solution.py:233
  72.6 2.2 %collective-permute-start.26 = (f32[48,768]{1,0:T(8,128)S(1)}, f32[48,768]{1,0:T(8,128)S(1)}, u32[]{:S(2)}, u32[]{:S(2)}) collective-permute-start(f32[48,768]{1,0:T(8,128)S(1)} %add.45.refs_10_), channel_id=1, source_target_pairs={{0,8},{4,12},{8,0},{12,4},{1,9},{5,13},{9,1},{13,5},{2,10},{6,14},... | collective-permute-start | bytes 442376 | tf_op jit(solution)/shard_map/ppermute | solution.py:233
  74.9 2.1 %collective-permute-start.24 = (f32[40,768]{1,0:T(8,128)S(1)}, f32[40,768]{1,0:T(8,128)S(1)}, u32[]{:S(2)}, u32[]{:S(2)}) collective-permute-start(f32[40,768]{1,0:T(8,128)S(1)} %add.44.refs_8_), channel_id=1, source_target_pairs={{0,4},{4,0},{8,12},{12,8},{1,5},{5,1},{9,13},{13,9},{2,6},{6,2},{1... | collective-permute-start | bytes 368648 | tf_op jit(solution)/shard_map/ppermute | solution.py:233
  77.0 2.4 %collective-permute-done.18.refs_4_.refs_5_ = f32[64,640]{1,0:T(8,128)S(1)} collective-permute-done((f32[64,640]{1,0:T(8,128)S(1)}, f32[64,640]{1,0:T(8,128)S(1)}, u32[]{:S(2)}, u32[]{:S(2)}) %collective-permute-start.18) | collective-permute-done | bytes 163872 | tf_op jit(solution)/shard_map/ppermute | solution.py:233
  79.4 4.6 %update_one.1 = (f32[4096,512]{1,0:T(8,128)S(1)}, f32[256,512]{1,0:T(8,128)S(1)}) custom-call(s32[6]{0:T(128)S(1)} %stack.23.where_ref.refs_0_, f32[64,640]{1,0:T(8,128)S(1)} %add.38.refs_1_.refs_2_, f32[64,640]{1,0:T(8,128)S(1)} %collective-permute-done.4.refs_2_.refs_3_, f32[64,640]{1,0:T(8,128)S(1)} %add.41.refs_3_.refs_4_, ...), custom_call_target="tpu_custom_call" | custom-call | flops 1 | bytes 1 | tf_op jit(solution)/shard_map/update_one/pallas_call | solution.py:20
  84.1 5.9 %update_zero.1 = f32[4096,512]{1,0:T(8,128)} custom-call(s32[6]{0:T(128)S(1)} %stack.23.where_ref.refs_0_, f32[256,512]{1,0:T(8,128)S(1)} %get-tuple-element.55.refs_1_, f32[64,640]{1,0:T(8,128)S(1)} %add.38.refs_1_.refs_2_, f32[64,640]{1,0:T(8,128)S(1)} %collective-permute-done.4.refs_2_.refs_3_, f32[64,640]{1,0:T(8,128)S(1)} %add.41.refs_3_.refs_4_, ...), custom_call_target="tpu_custom_call" | custom-call | flops 1 | bytes 1 | tf_op jit(solution)/shard_map/update_zero/pallas_call | solution.py:20
  (50 shorter events, 5.3 us)
Async XLA Ops:
  0.1 1.6 %copy-start = (f32[2,64,4096]{2,1,0:T(8,128)S(1)}, f32[2,64,4096]{2,1,0:T(8,128)}, u32[]{:S(2)}) copy-start(f32[2,64,4096]{2,1,0:T(8,128)} %in_ref.1) | copy-start | bytes 6291460
  2.5 7.1 %collective-permute-start = (f32[64,4096]{1,0:T(8,128)S(1)}, f32[64,4096]{1,0:T(8,128)S(1)}, u32[]{:S(2)}, u32[]{:S(2)}) collective-permute-start(f32[64,4096]{1,0:T(8,128)S(1)} %get-tuple-element.33.refs_1_.refs_5_.refs_6_.refs_2_), channel_id=1, source_target_pairs={{0,1},{1,0},{2,3},{3,2},{4,5},{5,4},{6,7},{7,6},{8,9},{9,8},{10,11... | collective-permute-start | bytes 3145736 | tf_op jit(solution)/shard_map/ppermute | solution.py:227
  3.0 6.6 %collective-permute-start.1 = (f32[64,4096]{1,0:T(8,128)S(1)}, f32[64,4096]{1,0:T(8,128)S(1)}, u32[]{:S(2)}, u32[]{:S(2)}) collective-permute-start(f32[64,4096]{1,0:T(8,128)S(1)} %get-tuple-element.48.refs_3_.refs_1_.refs_6_.in_ref.refs_13_), channel_id=1, source_target_pairs={{0,1},{1,0},{2,3},{3,2},{4,5},{5,4},{6,7},{7,6},{8,9},{9,8},{10,11... | collective-permute-start | bytes 3145736 | tf_op jit(solution)/shard_map/ppermute | solution.py:227
  3.1 26.9 %collective-permute-start.5 = (f32[64,4096]{1,0:T(8,128)S(1)}, f32[64,4096]{1,0:T(8,128)S(1)}, u32[]{:S(2)}, u32[]{:S(2)}) collective-permute-start(f32[64,4096]{1,0:T(8,128)S(1)} %get-tuple-element.33.refs_1_.refs_5_.refs_6_.refs_2_), channel_id=1, source_target_pairs={{2,0},{3,1},{0,2},{1,3},{6,4},{7,5},{4,6},{5,7},{10,8},{11,9},{8,1... | collective-permute-start | bytes 3145736 | tf_op jit(solution)/shard_map/ppermute | solution.py:230
  12.8 4.7 %copy-start.1 = (f32[2,256,256]{2,1,0:T(8,128)S(1)}, f32[2,256,256]{2,1,0:T(8,128)}, u32[]{:S(2)}) copy-start(f32[2,256,256]{2,1,0:T(8,128)} %in_ref.3) | copy-start | bytes 1572868
  12.9 17.1 %collective-permute-start.2 = (f32[64,640]{1,0:T(8,128)S(1)}, f32[64,640]{1,0:T(8,128)S(1)}, u32[]{:S(2)}, u32[]{:S(2)}) collective-permute-start(f32[64,640]{1,0:T(8,128)S(1)} %get-tuple-element.39), channel_id=1, source_target_pairs={{0,4},{4,0},{8,12},{12,8},{1,5},{5,1},{9,13},{13,9},{2,6},{6,2},{1... | collective-permute-start | bytes 491528 | tf_op jit(solution)/shard_map/ppermute | solution.py:233
  16.8 13.2 %collective-permute-start.6 = (f32[64,512]{1,0:T(8,128)S(1)}, f32[64,512]{1,0:T(8,128)S(1)}, u32[]{:S(2)}, u32[]{:S(2)}) collective-permute-start(f32[64,512]{1,0:T(8,128)S(1)} %get-tuple-element.42), channel_id=1, source_target_pairs={{0,4},{4,0},{8,12},{12,8},{1,5},{5,1},{9,13},{13,9},{2,6},{6,2},{1... | collective-permute-start | bytes 393224 | tf_op jit(solution)/shard_map/ppermute | solution.py:233
  17.4 26.4 %collective-permute-start.12 = (f32[40,4096]{1,0:T(8,128)S(1)}, f32[40,4096]{1,0:T(8,128)S(1)}, u32[]{:S(2)}, u32[]{:S(2)}) collective-permute-start(f32[40,4096]{1,0:T(8,128)S(1)} %get-tuple-element.49), channel_id=1, source_target_pairs={{2,0},{3,1},{0,2},{1,3},{6,4},{7,5},{4,6},{5,7},{10,8},{11,9},{8,1... | collective-permute-start | bytes 1966088 | tf_op jit(solution)/shard_map/ppermute | solution.py:230
  30.1 1.6 %collective-permute-start.7 = (f32[16,4096]{1,0:T(8,128)S(1)}, f32[16,4096]{1,0:T(8,128)S(1)}, u32[]{:S(2)}, u32[]{:S(2)}) collective-permute-start(f32[16,4096]{1,0:T(8,128)S(1)} %get-tuple-element.64), channel_id=1, source_target_pairs={{0,1},{1,0},{2,3},{3,2},{4,5},{5,4},{6,7},{7,6},{8,9},{9,8},{10,11... | collective-permute-start | bytes 786440 | tf_op jit(solution)/shard_map/ppermute | solution.py:227
  30.1 4.7 %collective-permute-start.8 = (f32[16,4096]{1,0:T(8,128)S(1)}, f32[16,4096]{1,0:T(8,128)S(1)}, u32[]{:S(2)}, u32[]{:S(2)}) collective-permute-start(f32[16,4096]{1,0:T(8,128)S(1)} %get-tuple-element.63), channel_id=1, source_target_pairs={{0,1},{1,0},{2,3},{3,2},{4,5},{5,4},{6,7},{7,6},{8,9},{9,8},{10,11... | collective-permute-start | bytes 786440 | tf_op jit(solution)/shard_map/ppermute | solution.py:227
  30.6 4.2 %collective-permute-start.9 = (f32[16,4096]{1,0:T(8,128)S(1)}, f32[16,4096]{1,0:T(8,128)S(1)}, u32[]{:S(2)}, u32[]{:S(2)}) collective-permute-start(f32[16,4096]{1,0:T(8,128)S(1)} %get-tuple-element.62), channel_id=1, source_target_pairs={{0,1},{1,0},{2,3},{3,2},{4,5},{5,4},{6,7},{7,6},{8,9},{9,8},{10,11... | collective-permute-start | bytes 786440 | tf_op jit(solution)/shard_map/ppermute | solution.py:227
  30.7 4.1 %collective-permute-start.10 = (f32[16,4096]{1,0:T(8,128)S(1)}, f32[16,4096]{1,0:T(8,128)S(1)}, u32[]{:S(2)}, u32[]{:S(2)}) collective-permute-start(f32[16,4096]{1,0:T(8,128)S(1)} %get-tuple-element.61), channel_id=1, source_target_pairs={{0,1},{1,0},{2,3},{3,2},{4,5},{5,4},{6,7},{7,6},{8,9},{9,8},{10,11... | collective-permute-start | bytes 786440 | tf_op jit(solution)/shard_map/ppermute | solution.py:227
  31.7 16.9 %collective-permute-start.3 = (f32[64,640]{1,0:T(8,128)S(1)}, f32[64,640]{1,0:T(8,128)S(1)}, u32[]{:S(2)}, u32[]{:S(2)}) collective-permute-start(f32[64,640]{1,0:T(8,128)S(1)} %add.37), channel_id=1, source_target_pairs={{0,8},{4,12},{8,0},{12,4},{1,9},{5,13},{9,1},{13,5},{2,10},{6,14},... | collective-permute-start | bytes 491528 | tf_op jit(solution)/shard_map/ppermute | solution.py:233
  38.0 11.1 %collective-permute-start.11 = (f32[64,640]{1,0:T(8,128)S(1)}, f32[64,640]{1,0:T(8,128)S(1)}, u32[]{:S(2)}, u32[]{:S(2)}) collective-permute-start(f32[64,640]{1,0:T(8,128)S(1)} %get-tuple-element.47), channel_id=1, source_target_pairs={{0,4},{4,0},{8,12},{12,8},{1,5},{5,1},{9,13},{13,9},{2,6},{6,2},{1... | collective-permute-start | bytes 491528 | tf_op jit(solution)/shard_map/ppermute | solution.py:233
  39.7 8.9 %collective-permute-start.13 = (f32[64,512]{1,0:T(8,128)S(1)}, f32[64,512]{1,0:T(8,128)S(1)}, u32[]{:S(2)}, u32[]{:S(2)}) collective-permute-start(f32[64,512]{1,0:T(8,128)S(1)} %add.39), channel_id=1, source_target_pairs={{0,8},{4,12},{8,0},{12,4},{1,9},{5,13},{9,1},{13,5},{2,10},{6,14},... | collective-permute-start | bytes 393224 | tf_op jit(solution)/shard_map/ppermute | solution.py:233
  40.9 14.0 %collective-permute-start.19 = (f32[24,4096]{1,0:T(8,128)S(1)}, f32[24,4096]{1,0:T(8,128)S(1)}, u32[]{:S(2)}, u32[]{:S(2)}) collective-permute-start(f32[24,4096]{1,0:T(8,128)S(1)} %get-tuple-element.56), channel_id=1, source_target_pairs={{2,0},{3,1},{0,2},{1,3},{6,4},{7,5},{4,6},{5,7},{10,8},{11,9},{8,1... | collective-permute-start | bytes 1179656 | tf_op jit(solution)/shard_map/ppermute | solution.py:230
  49.2 2.2 %collective-permute-start.14 = (f32[16,4096]{1,0:T(8,128)S(1)}, f32[16,4096]{1,0:T(8,128)S(1)}, u32[]{:S(2)}, u32[]{:S(2)}) collective-permute-start(f32[16,4096]{1,0:T(8,128)S(1)} %get-tuple-element.66), channel_id=1, source_target_pairs={{0,1},{1,0},{2,3},{3,2},{4,5},{5,4},{6,7},{7,6},{8,9},{9,8},{10,11... | collective-permute-start | bytes 786440 | tf_op jit(solution)/shard_map/ppermute | solution.py:227
  49.3 2.1 %collective-permute-start.15 = (f32[16,4096]{1,0:T(8,128)S(1)}, f32[16,4096]{1,0:T(8,128)S(1)}, u32[]{:S(2)}, u32[]{:S(2)}) collective-permute-start(f32[16,4096]{1,0:T(8,128)S(1)} %get-tuple-element.65), channel_id=1, source_target_pairs={{0,1},{1,0},{2,3},{3,2},{4,5},{5,4},{6,7},{7,6},{8,9},{9,8},{10,11... | collective-permute-start | bytes 786440 | tf_op jit(solution)/shard_map/ppermute | solution.py:227
  49.8 6.2 %collective-permute-start.4 = (f32[64,640]{1,0:T(8,128)S(1)}, f32[64,640]{1,0:T(8,128)S(1)}, u32[]{:S(2)}, u32[]{:S(2)}) collective-permute-start(f32[64,640]{1,0:T(8,128)S(1)} %add.38.refs_1_.refs_2_), channel_id=1, source_target_pairs={{0,4},{4,0},{8,12},{12,8},{1,5},{5,1},{9,13},{13,9},{2,6},{6,2},{1... | collective-permute-start | bytes 491528 | tf_op jit(solution)/shard_map/ppermute | solution.py:233
  50.0 1.4 %collective-permute-start.16 = (f32[8,4096]{1,0:T(8,128)S(1)}, f32[8,4096]{1,0:T(8,128)S(1)}, u32[]{:S(2)}, u32[]{:S(2)}) collective-permute-start(f32[8,4096]{1,0:T(8,128)S(1)} %slice.27), channel_id=1, source_target_pairs={{0,1},{1,0},{2,3},{3,2},{4,5},{5,4},{6,7},{7,6},{8,9},{9,8},{10,11... | collective-permute-start | bytes 393224 | tf_op jit(solution)/shard_map/ppermute | solution.py:227
  56.0 4.2 %collective-permute-start.20 = (f32[24,4096]{1,0:T(8,128)S(1)}, f32[24,4096]{1,0:T(8,128)S(1)}, u32[]{:S(2)}, u32[]{:S(2)}) collective-permute-start(f32[24,4096]{1,0:T(8,128)S(1)} %collective-permute-done.19.refs_0_.refs_19_), channel_id=1, source_target_pairs={{0,1},{1,0},{2,3},{3,2},{4,5},{5,4},{6,7},{7,6},{8,9},{9,8},{10,11... | collective-permute-start | bytes 1179656 | tf_op jit(solution)/shard_map/ppermute | solution.py:227
  56.0 8.4 %collective-permute-start.22 = (f32[40,768]{1,0:T(8,128)S(1)}, f32[40,768]{1,0:T(8,128)S(1)}, u32[]{:S(2)}, u32[]{:S(2)}) collective-permute-start(f32[40,768]{1,0:T(8,128)S(1)} %get-tuple-element.52), channel_id=1, source_target_pairs={{0,4},{4,0},{8,12},{12,8},{1,5},{5,1},{9,13},{13,9},{2,6},{6,2},{1... | collective-permute-start | bytes 368648 | tf_op jit(solution)/shard_map/ppermute | solution.py:233
  57.1 11.8 %collective-permute-start.17 = (f32[64,640]{1,0:T(8,128)S(1)}, f32[64,640]{1,0:T(8,128)S(1)}, u32[]{:S(2)}, u32[]{:S(2)}) collective-permute-start(f32[64,640]{1,0:T(8,128)S(1)} %add.40), channel_id=1, source_target_pairs={{0,8},{4,12},{8,0},{12,4},{1,9},{5,13},{9,1},{13,5},{2,10},{6,14},... | collective-permute-start | bytes 491528 | tf_op jit(solution)/shard_map/ppermute | solution.py:233
  62.9 9.7 %collective-permute-start.25 = (f32[48,768]{1,0:T(8,128)S(1)}, f32[48,768]{1,0:T(8,128)S(1)}, u32[]{:S(2)}, u32[]{:S(2)}) collective-permute-start(f32[48,768]{1,0:T(8,128)S(1)} %project_zero_2.1), channel_id=1, source_target_pairs={{0,4},{4,0},{8,12},{12,8},{1,5},{5,1},{9,13},{13,9},{2,6},{6,2},{1... | collective-permute-start | bytes 442376 | tf_op jit(solution)/shard_map/ppermute | solution.py:233
  64.4 10.5 %collective-permute-start.23 = (f32[40,768]{1,0:T(8,128)S(1)}, f32[40,768]{1,0:T(8,128)S(1)}, u32[]{:S(2)}, u32[]{:S(2)}) collective-permute-start(f32[40,768]{1,0:T(8,128)S(1)} %add.43), channel_id=1, source_target_pairs={{0,8},{4,12},{8,0},{12,4},{1,9},{5,13},{9,1},{13,5},{2,10},{6,14},... | collective-permute-start | bytes 368648 | tf_op jit(solution)/shard_map/ppermute | solution.py:233
  68.9 10.5 %collective-permute-start.18 = (f32[64,640]{1,0:T(8,128)S(1)}, f32[64,640]{1,0:T(8,128)S(1)}, u32[]{:S(2)}, u32[]{:S(2)}) collective-permute-start(f32[64,640]{1,0:T(8,128)S(1)} %add.41.refs_3_.refs_4_), channel_id=1, source_target_pairs={{0,4},{4,0},{8,12},{12,8},{1,5},{5,1},{9,13},{13,9},{2,6},{6,2},{1... | collective-permute-start | bytes 491528 | tf_op jit(solution)/shard_map/ppermute | solution.py:233
  72.6 11.5 %collective-permute-start.26 = (f32[48,768]{1,0:T(8,128)S(1)}, f32[48,768]{1,0:T(8,128)S(1)}, u32[]{:S(2)}, u32[]{:S(2)}) collective-permute-start(f32[48,768]{1,0:T(8,128)S(1)} %add.45.refs_10_), channel_id=1, source_target_pairs={{0,8},{4,12},{8,0},{12,4},{1,9},{5,13},{9,1},{13,5},{2,10},{6,14},... | collective-permute-start | bytes 442376 | tf_op jit(solution)/shard_map/ppermute | solution.py:233
  74.8 9.3 %collective-permute-start.21 = (f32[64,512]{1,0:T(8,128)S(1)}, f32[64,512]{1,0:T(8,128)S(1)}, u32[]{:S(2)}, u32[]{:S(2)}) collective-permute-start(f32[64,512]{1,0:T(8,128)S(1)} %add.42.refs_6_), channel_id=1, source_target_pairs={{0,4},{4,0},{8,12},{12,8},{1,5},{5,1},{9,13},{13,9},{2,6},{6,2},{1... | collective-permute-start | bytes 393224 | tf_op jit(solution)/shard_map/ppermute | solution.py:233
  74.9 9.1 %collective-permute-start.24 = (f32[40,768]{1,0:T(8,128)S(1)}, f32[40,768]{1,0:T(8,128)S(1)}, u32[]{:S(2)}, u32[]{:S(2)}) collective-permute-start(f32[40,768]{1,0:T(8,128)S(1)} %add.44.refs_8_), channel_id=1, source_target_pairs={{0,4},{4,0},{8,12},{12,8},{1,5},{5,1},{9,13},{13,9},{2,6},{6,2},{1... | collective-permute-start | bytes 368648 | tf_op jit(solution)/shard_map/ppermute | solution.py:233

commit v7 on v6

--- a/solution.py
+++ b/solution.py
@@ -7,7 +7,7 @@
 
 F32, BF16 = jnp.float32, jnp.bfloat16
 PIECES = ((1, 0, 64, True), (0, 0, 40, True), (0, 40, 64, False))
-SWAP_ROWS = (16, 16, 32)
+SWAP_ROWS = (16, 16, 8)
 NN = (((1,), (0,)), ((), ()))
 NT = (((1,), (1,)), ((), ()))
 TN = (((0,), (0,)), ((), ()))
@@ -301,7 +301,7 @@
         front = (*front, t0)
         last = len(far) - 1
         for n, (step, (block, first, final), value) in enumerate(far):
-            waits = list(running) if last != 2 else (("own1", "own0"), ("own1", 0, "own0"), ("own1",))[n]
+            waits = list(running) if last != 2 else (("own1", "own0"), ("own1", 0, "own0"), ())[n]
             value = after(value, *front, *arrived(*waits))
             start(*waits if last != 2 else (("own1", "own0"), ("own1",), ())[n])
             split_rows = halves[block, first, final]
@@ -309,12 +309,13 @@
             for at in range(0, final - first, swap_rows[block, first, final]):
                 upto = min(at + swap_rows[block, first, final], final - first)
                 pair.append((core_swap(value[at:upto]), upto - at, 0))
+            ready = after(high, *arrived("own1")) if n == 2 and last == 2 else high
             if block == 1:
                 all_ones += pair
                 front = project(f"project_one_{n}", pair, own[0], high, low, bit if split_rows else None)
             else:
                 all_zeros += pair
-                front = project(f"project_zero_{n}", pair, all_ones, high, low, bit if split_rows else None)
+                front = project(f"project_zero_{n}", pair, all_ones, ready, low, bit if split_rows else None)
             running[n] = sums(*front)
             start(n)
             if n == 1 and last == 2:

time: 90.3 us -> 90.1 us (level)
    ppermute x10 -> x12, starting transfers between devices: 2.32 us -> 3.12 us  [core_swap(): return lax.ppermute(value, 'col', [(i, i ^ 1) for i in range(cols)])]
    ppermute x10 -> x12, waiting for transfers between devices: 1.85 us -> 1.74 us  [core_swap(): return lax.ppermute(value, 'col', [(i, i ^ 1) for i in range(cols)])]
  transfers between devices with their start and end apart: 27 -> 29, of which waited for: 12 -> 11; matrix products, arithmetic and copies ran while one was open for 0% -> 0% of each run, Pallas kernels for 28% -> 28%
where the time goes in v7:
time: 90.1 us; the launch traced here: 89.9 us
  Pallas kernels  31.9 us (35%)
  waiting for transfers between devices  28.6 us (32%)
  starting transfers between devices  27.1 us (30%)
  local copies, waits for them, and re-layouts  1.82 us (2%)
    pallas_call x11, Pallas kernels, call(): pl.pallas_call(body, in_specs=specs, out_specs=out_specs, out_shape=outs,...  31.9 us
    ppermute x14, starting transfers between devices, row_swap(): return lax.ppermute(value, 'row', [(i, i ^ step) for i in range(rows)])  19.4 us
    ppermute x14, waiting for transfers between devices, row_swap(): return lax.ppermute(value, 'row', [(i, i ^ step) for i in range(rows)])  15 us
    ppermute x3, waiting for transfers between devices, from_chip(): lax.ppermute(value, 'col', [((i + 2 * step) % cols, i) for i in range(col...  11.9 us
    ppermute x3, starting transfers between devices, from_chip(): lax.ppermute(value, 'col', [((i + 2 * step) % cols, i) for i in range(col...  4.58 us
    ppermute x12, starting transfers between devices, core_swap(): return lax.ppermute(value, 'col', [(i, i ^ 1) for i in range(cols)])  3.12 us
  transfers between devices with their start and end apart: 29, of which 11 were waited for; matrix products, arithmetic and copies ran while one was open for 0% of the time, Pallas kernels for 28%

profile of v7, /device:TPU:0, one launch (start us, length us, event | category | flops | bytes accessed | tf_op | source)
XLA Modules:
  0.0 89.9 jit_solution(16619991245356453321)
XLA Ops:
  0.1 1.6 %copy-done = f32[2,64,4096]{2,1,0:T(8,128)S(1)} copy-done((f32[2,64,4096]{2,1,0:T(8,128)S(1)}, f32[2,64,4096]{2,1,0:T(8,128)}, u32[]{:S(2)}) %copy-start) | copy-done | bytes 2097176
  1.7 0.8 cut.1
  3.1 2.9 %collective-permute-start.5 = (f32[64,4096]{1,0:T(8,128)S(1)}, f32[64,4096]{1,0:T(8,128)S(1)}, u32[]{:S(2)}, u32[]{:S(2)}) collective-permute-start(f32[64,4096]{1,0:T(8,128)S(1)} %get-tuple-element.34.refs_1_.refs_5_.refs_6_.refs_4_), channel_id=1, source_target_pairs={{2,0},{3,1},{0,2},{1,3},{6,4},{7,5},{4,6},{5,7},{10,8},{11,9},{8,1... | collective-permute-start | bytes 3145736 | tf_op jit(solution)/shard_map/ppermute | solution.py:230
  6.0 3.6 %load.1 = (bf16[4096,512]{1,0:T(8,128)(2,1)S(1)}, bf16[4096,512]{1,0:T(8,128)(2,1)S(1)}) custom-call(f32[4096,512]{1,0:T(8,128)} %in_ref.2), custom_call_target="tpu_custom_call" | custom-call | flops 1 | bytes 1 | tf_op jit(solution)/shard_map/load/pallas_call | solution.py:20
  9.7 3.2 %project_own1.1 = (f32[64,640]{1,0:T(8,128)S(1)}, f32[64,640]{1,0:T(8,128)S(1)}) custom-call(s32[6]{0:T(128)S(1)} %stack.23.where_ref.refs_0_, f32[64,4096]{1,0:T(8,128)S(1)} %get-tuple-element.34.refs_1_.refs_5_.refs_6_.refs_4_, f32[64,4096]{1,0:T(8,128)S(1)} %collective-permute-done.refs_2_.refs_6_.refs_7_.refs_5_, ...), custom_call_target="tpu_custom_call" | custom-call | flops 1 | bytes 1 | tf_op jit(solution)/shard_map/project_own1/pallas_call | solution.py:20
  12.9 1.6 %collective-permute-start.2 = (f32[64,640]{1,0:T(8,128)S(1)}, f32[64,640]{1,0:T(8,128)S(1)}, u32[]{:S(2)}, u32[]{:S(2)}) collective-permute-start(f32[64,640]{1,0:T(8,128)S(1)} %get-tuple-element.40), channel_id=1, source_target_pairs={{0,4},{4,0},{8,12},{12,8},{1,5},{5,1},{9,13},{13,9},{2,6},{6,2},{1... | collective-permute-start | bytes 491528 | tf_op jit(solution)/shard_map/ppermute | solution.py:233
  14.5 2.3 %project_own0.1 = (f32[64,512]{1,0:T(8,128)S(1)}, f32[64,512]{1,0:T(8,128)S(1)}) custom-call(s32[6]{0:T(128)S(1)} %stack.23.where_ref.refs_0_, f32[64,4096]{1,0:T(8,128)S(1)} %get-tuple-element.49.refs_3_.refs_1_.refs_6_.in_ref.refs_13_, f32[64,4096]{1,0:T(8,128)S(1)} %collective-permute-done.1.refs_4_.refs_2_.refs_7_.refs_14_, ...), custom_call_target="tpu_custom_call" | custom-call | flops 1 | bytes 1 | tf_op jit(solution)/shard_map/project_own0/pallas_call | solution.py:20
  17.6 2.0 %reorder.1 = (f32[256,256]{1,0:T(8,128)S(1)}, f32[256,256]{1,0:T(8,128)S(1)}) custom-call(s32[6]{0:T(128)S(1)} %stack.23.where_ref.refs_0_, f32[2,256,256]{2,1,0:T(8,128)S(1)} %copy-done.1), custom_call_target="tpu_custom_call" | custom-call | flops 1 | bytes 1 | tf_op jit(solution)/shard_map/reorder/pallas_call | solution.py:20
  19.6 10.4 %collective-permute-done.5.refs_1_.refs_7_.refs_8_.refs_6_ = f32[64,4096]{1,0:T(8,128)S(1)} collective-permute-done((f32[64,4096]{1,0:T(8,128)S(1)}, f32[64,4096]{1,0:T(8,128)S(1)}, u32[]{:S(2)}, u32[]{:S(2)}) %collective-permute-start.5) | collective-permute-done | bytes 1048608 | tf_op jit(solution)/shard_map/ppermute | solution.py:230
  31.7 3.2 %collective-permute-start.3 = (f32[64,640]{1,0:T(8,128)S(1)}, f32[64,640]{1,0:T(8,128)S(1)}, u32[]{:S(2)}, u32[]{:S(2)}) collective-permute-start(f32[64,640]{1,0:T(8,128)S(1)} %add.37), channel_id=1, source_target_pairs={{0,8},{4,12},{8,0},{12,4},{1,9},{5,13},{9,1},{13,5},{2,10},{6,14},... | collective-permute-start | bytes 491528 | tf_op jit(solution)/shard_map/ppermute | solution.py:233
  34.8 3.2 %project_one_0.1 = (f32[64,640]{1,0:T(8,128)S(1)}, f32[64,640]{1,0:T(8,128)S(1)}) custom-call(s32[6]{0:T(128)S(1)} %stack.23.where_ref.refs_0_, f32[64,4096]{1,0:T(8,128)S(1)} %collective-permute-done.5.refs_1_.refs_7_.refs_8_.refs_6_, f32[16,4096]{1,0:T(8,128)S(1)} %collective-permute-done.7.refs_2_.refs_8_.refs_9_.refs_7_, ...), custom_call_target="tpu_custom_call" | custom-call | flops 1 | bytes 1 | tf_op jit(solution)/shard_map/project_one_0/pallas_call | solution.py:20
  38.0 1.6 %collective-permute-start.11 = (f32[64,640]{1,0:T(8,128)S(1)}, f32[64,640]{1,0:T(8,128)S(1)}, u32[]{:S(2)}, u32[]{:S(2)}) collective-permute-start(f32[64,640]{1,0:T(8,128)S(1)} %get-tuple-element.48), channel_id=1, source_target_pairs={{0,4},{4,0},{8,12},{12,8},{1,5},{5,1},{9,13},{13,9},{2,6},{6,2},{1... | collective-permute-start | bytes 491528 | tf_op jit(solution)/shard_map/ppermute | solution.py:233
  39.7 1.2 %collective-permute-start.13 = (f32[64,512]{1,0:T(8,128)S(1)}, f32[64,512]{1,0:T(8,128)S(1)}, u32[]{:S(2)}, u32[]{:S(2)}) collective-permute-start(f32[64,512]{1,0:T(8,128)S(1)} %add.39), channel_id=1, source_target_pairs={{0,8},{4,12},{8,0},{12,4},{1,9},{5,13},{9,1},{13,5},{2,10},{6,14},... | collective-permute-start | bytes 393224 | tf_op jit(solution)/shard_map/ppermute | solution.py:233
  40.9 1.5 %collective-permute-start.19 = (f32[24,4096]{1,0:T(8,128)S(1)}, f32[24,4096]{1,0:T(8,128)S(1)}, u32[]{:S(2)}, u32[]{:S(2)}) collective-permute-start(f32[24,4096]{1,0:T(8,128)S(1)} %get-tuple-element.57), channel_id=1, source_target_pairs={{2,0},{3,1},{0,2},{1,3},{6,4},{7,5},{4,6},{5,7},{10,8},{11,9},{8,1... | collective-permute-start | bytes 1179656 | tf_op jit(solution)/shard_map/ppermute | solution.py:230
  42.4 1.5 %collective-permute-done.12.refs_1_.refs_15_ = f32[40,4096]{1,0:T(8,128)S(1)} collective-permute-done((f32[40,4096]{1,0:T(8,128)S(1)}, f32[40,4096]{1,0:T(8,128)S(1)}, u32[]{:S(2)}, u32[]{:S(2)}) %collective-permute-start.12) | collective-permute-done | bytes 655392 | tf_op jit(solution)/shard_map/ppermute | solution.py:230
  43.8 4.8 %collective-permute-done.13 = f32[64,512]{1,0:T(8,128)S(1)} collective-permute-done((f32[64,512]{1,0:T(8,128)S(1)}, f32[64,512]{1,0:T(8,128)S(1)}, u32[]{:S(2)}, u32[]{:S(2)}) %collective-permute-start.13) | collective-permute-done | bytes 131104 | tf_op jit(solution)/shard_map/ppermute | solution.py:233
  48.6 0.6 collective-permute-done.11
  50.1 1.2 %collective-permute-done.16.refs_4_.refs_18_ = f32[8,4096]{1,0:T(8,128)S(1)} collective-permute-done((f32[8,4096]{1,0:T(8,128)S(1)}, f32[8,4096]{1,0:T(8,128)S(1)}, u32[]{:S(2)}, u32[]{:S(2)}) %collective-permute-start.16) | collective-permute-done | bytes 131104 | tf_op jit(solution)/shard_map/ppermute | solution.py:227
  51.4 3.5 %project_zero_1.1 = (f32[40,768]{1,0:T(8,128)S(1)}, f32[40,768]{1,0:T(8,128)S(1)}) custom-call(s32[6]{0:T(128)S(1)} %stack.23.where_ref.refs_0_, f32[40,4096]{1,0:T(8,128)S(1)} %collective-permute-done.12.refs_1_.refs_15_, f32[16,4096]{1,0:T(8,128)S(1)} %collective-permute-done.14.refs_2_.refs_16_, f32[16,4096]{1,0:T(8,128)S(1)} %collective-permute-done.15.refs_3_.refs_17_, ...), custom_call_target="tpu_custom_call" | custom-call | flops 1 | bytes 1 | tf_op jit(solution)/shard_map/project_zero_1/pallas_call | solution.py:20
  55.6 0.7 collective-permute-start.24
  56.6 3.3 %collective-permute-start.17 = (f32[64,640]{1,0:T(8,128)S(1)}, f32[64,640]{1,0:T(8,128)S(1)}, u32[]{:S(2)}, u32[]{:S(2)}) collective-permute-start(f32[64,640]{1,0:T(8,128)S(1)} %add.40), channel_id=1, source_target_pairs={{0,8},{4,12},{8,0},{12,4},{1,9},{5,13},{9,1},{13,5},{2,10},{6,14},... | collective-permute-start | bytes 491528 | tf_op jit(solution)/shard_map/ppermute | solution.py:233
  59.8 2.7 %project_zero_2.1 = f32[48,768]{1,0:T(8,128)S(1)} custom-call(f32[24,4096]{1,0:T(8,128)S(1)} %collective-permute-done.19.refs_0_.refs_19_, f32[8,4096]{1,0:T(8,128)S(1)} %collective-permute-done.20.refs_1_.refs_20_, f32[8,4096]{1,0:T(8,128)S(1)} %collective-permute-done.21.refs_2_.refs_21_, f32[8,4096]{1,0:T(8,128)S(1)} %collective-permute-done.22.refs_3_.refs_22_, ...), custom_call_target="tpu_custom_call" | custom-call | flops 1 | bytes 1 | tf_op jit(solution)/shard_map/project_zero_2/pallas_call | solution.py:20
  62.6 0.9 %collective-permute-start.27 = (f32[48,768]{1,0:T(8,128)S(1)}, f32[48,768]{1,0:T(8,128)S(1)}, u32[]{:S(2)}, u32[]{:S(2)}) collective-permute-start(f32[48,768]{1,0:T(8,128)S(1)} %project_zero_2.1), channel_id=1, source_target_pairs={{0,4},{4,0},{8,12},{12,8},{1,5},{5,1},{9,13},{13,9},{2,6},{6,2},{1... | collective-permute-start | bytes 442376 | tf_op jit(solution)/shard_map/ppermute | solution.py:233
  63.7 0.9 %collective-permute-start.25 = (f32[40,768]{1,0:T(8,128)S(1)}, f32[40,768]{1,0:T(8,128)S(1)}, u32[]{:S(2)}, u32[]{:S(2)}) collective-permute-start(f32[40,768]{1,0:T(8,128)S(1)} %add.43), channel_id=1, source_target_pairs={{0,8},{4,12},{8,0},{12,4},{1,9},{5,13},{9,1},{13,5},{2,10},{6,14},... | collective-permute-start | bytes 368648 | tf_op jit(solution)/shard_map/ppermute | solution.py:233
  64.6 3.9 %collective-permute-done.17 = f32[64,640]{1,0:T(8,128)S(1)} collective-permute-done((f32[64,640]{1,0:T(8,128)S(1)}, f32[64,640]{1,0:T(8,128)S(1)}, u32[]{:S(2)}, u32[]{:S(2)}) %collective-permute-start.17) | collective-permute-done | bytes 163872 | tf_op jit(solution)/shard_map/ppermute | solution.py:233
  68.5 1.1 %collective-permute-start.18 = (f32[64,640]{1,0:T(8,128)S(1)}, f32[64,640]{1,0:T(8,128)S(1)}, u32[]{:S(2)}, u32[]{:S(2)}) collective-permute-start(f32[64,640]{1,0:T(8,128)S(1)} %add.41.refs_3_.refs_4_), channel_id=1, source_target_pairs={{0,4},{4,0},{8,12},{12,8},{1,5},{5,1},{9,13},{13,9},{2,6},{6,2},{1... | collective-permute-start | bytes 491528 | tf_op jit(solution)/shard_map/ppermute | solution.py:233
  69.6 2.6 %collective-permute-done.27 = f32[48,768]{1,0:T(8,128)S(1)} collective-permute-done((f32[48,768]{1,0:T(8,128)S(1)}, f32[48,768]{1,0:T(8,128)S(1)}, u32[]{:S(2)}, u32[]{:S(2)}) %collective-permute-start.27) | collective-permute-done | bytes 147488 | tf_op jit(solution)/shard_map/ppermute | solution.py:233
  72.3 2.0 %collective-permute-start.28 = (f32[48,768]{1,0:T(8,128)S(1)}, f32[48,768]{1,0:T(8,128)S(1)}, u32[]{:S(2)}, u32[]{:S(2)}) collective-permute-start(f32[48,768]{1,0:T(8,128)S(1)} %add.45.refs_10_), channel_id=1, source_target_pairs={{0,8},{4,12},{8,0},{12,4},{1,9},{5,13},{9,1},{13,5},{2,10},{6,14},... | collective-permute-start | bytes 442376 | tf_op jit(solution)/shard_map/ppermute | solution.py:233
  74.4 2.1 %collective-permute-start.26 = (f32[40,768]{1,0:T(8,128)S(1)}, f32[40,768]{1,0:T(8,128)S(1)}, u32[]{:S(2)}, u32[]{:S(2)}) collective-permute-start(f32[40,768]{1,0:T(8,128)S(1)} %add.44.refs_8_), channel_id=1, source_target_pairs={{0,4},{4,0},{8,12},{12,8},{1,5},{5,1},{9,13},{13,9},{2,6},{6,2},{1... | collective-permute-start | bytes 368648 | tf_op jit(solution)/shard_map/ppermute | solution.py:233
  76.4 2.7 %collective-permute-done.18.refs_4_.refs_5_ = f32[64,640]{1,0:T(8,128)S(1)} collective-permute-done((f32[64,640]{1,0:T(8,128)S(1)}, f32[64,640]{1,0:T(8,128)S(1)}, u32[]{:S(2)}, u32[]{:S(2)}) %collective-permute-start.18) | collective-permute-done | bytes 163872 | tf_op jit(solution)/shard_map/ppermute | solution.py:233
  79.2 4.6 %update_one.1 = (f32[4096,512]{1,0:T(8,128)S(1)}, f32[256,512]{1,0:T(8,128)S(1)}) custom-call(s32[6]{0:T(128)S(1)} %stack.23.where_ref.refs_0_, f32[64,640]{1,0:T(8,128)S(1)} %add.38.refs_1_.refs_2_, f32[64,640]{1,0:T(8,128)S(1)} %collective-permute-done.4.refs_2_.refs_3_, f32[64,640]{1,0:T(8,128)S(1)} %add.41.refs_3_.refs_4_, ...), custom_call_target="tpu_custom_call" | custom-call | flops 1 | bytes 1 | tf_op jit(solution)/shard_map/update_one/pallas_call | solution.py:20
  83.8 6.0 %update_zero.1 = f32[4096,512]{1,0:T(8,128)} custom-call(s32[6]{0:T(128)S(1)} %stack.23.where_ref.refs_0_, f32[256,512]{1,0:T(8,128)S(1)} %get-tuple-element.56.refs_1_, f32[64,640]{1,0:T(8,128)S(1)} %add.38.refs_1_.refs_2_, f32[64,640]{1,0:T(8,128)S(1)} %collective-permute-done.4.refs_2_.refs_3_, f32[64,640]{1,0:T(8,128)S(1)} %add.41.refs_3_.refs_4_, ...), custom_call_target="tpu_custom_call" | custom-call | flops 1 | bytes 1 | tf_op jit(solution)/shard_map/update_zero/pallas_call | solution.py:20
  (55 shorter events, 5.5 us)
Async XLA Ops:
  0.1 1.6 %copy-start = (f32[2,64,4096]{2,1,0:T(8,128)S(1)}, f32[2,64,4096]{2,1,0:T(8,128)}, u32[]{:S(2)}) copy-start(f32[2,64,4096]{2,1,0:T(8,128)} %in_ref.1) | copy-start | bytes 6291460
  2.5 7.1 %collective-permute-start = (f32[64,4096]{1,0:T(8,128)S(1)}, f32[64,4096]{1,0:T(8,128)S(1)}, u32[]{:S(2)}, u32[]{:S(2)}) collective-permute-start(f32[64,4096]{1,0:T(8,128)S(1)} %get-tuple-element.34.refs_1_.refs_5_.refs_6_.refs_4_), channel_id=1, source_target_pairs={{0,1},{1,0},{2,3},{3,2},{4,5},{5,4},{6,7},{7,6},{8,9},{9,8},{10,11... | collective-permute-start | bytes 3145736 | tf_op jit(solution)/shard_map/ppermute | solution.py:227
  3.0 6.6 %collective-permute-start.1 = (f32[64,4096]{1,0:T(8,128)S(1)}, f32[64,4096]{1,0:T(8,128)S(1)}, u32[]{:S(2)}, u32[]{:S(2)}) collective-permute-start(f32[64,4096]{1,0:T(8,128)S(1)} %get-tuple-element.49.refs_3_.refs_1_.refs_6_.in_ref.refs_13_), channel_id=1, source_target_pairs={{0,1},{1,0},{2,3},{3,2},{4,5},{5,4},{6,7},{7,6},{8,9},{9,8},{10,11... | collective-permute-start | bytes 3145736 | tf_op jit(solution)/shard_map/ppermute | solution.py:227
  3.1 26.9 %collective-permute-start.5 = (f32[64,4096]{1,0:T(8,128)S(1)}, f32[64,4096]{1,0:T(8,128)S(1)}, u32[]{:S(2)}, u32[]{:S(2)}) collective-permute-start(f32[64,4096]{1,0:T(8,128)S(1)} %get-tuple-element.34.refs_1_.refs_5_.refs_6_.refs_4_), channel_id=1, source_target_pairs={{2,0},{3,1},{0,2},{1,3},{6,4},{7,5},{4,6},{5,7},{10,8},{11,9},{8,1... | collective-permute-start | bytes 3145736 | tf_op jit(solution)/shard_map/ppermute | solution.py:230
  12.8 4.7 %copy-start.1 = (f32[2,256,256]{2,1,0:T(8,128)S(1)}, f32[2,256,256]{2,1,0:T(8,128)}, u32[]{:S(2)}) copy-start(f32[2,256,256]{2,1,0:T(8,128)} %in_ref.3) | copy-start | bytes 1572868
  12.9 17.1 %collective-permute-start.2 = (f32[64,640]{1,0:T(8,128)S(1)}, f32[64,640]{1,0:T(8,128)S(1)}, u32[]{:S(2)}, u32[]{:S(2)}) collective-permute-start(f32[64,640]{1,0:T(8,128)S(1)} %get-tuple-element.40), channel_id=1, source_target_pairs={{0,4},{4,0},{8,12},{12,8},{1,5},{5,1},{9,13},{13,9},{2,6},{6,2},{1... | collective-permute-start | bytes 491528 | tf_op jit(solution)/shard_map/ppermute | solution.py:233
  16.8 13.2 %collective-permute-start.6 = (f32[64,512]{1,0:T(8,128)S(1)}, f32[64,512]{1,0:T(8,128)S(1)}, u32[]{:S(2)}, u32[]{:S(2)}) collective-permute-start(f32[64,512]{1,0:T(8,128)S(1)} %get-tuple-element.43), channel_id=1, source_target_pairs={{0,4},{4,0},{8,12},{12,8},{1,5},{5,1},{9,13},{13,9},{2,6},{6,2},{1... | collective-permute-start | bytes 393224 | tf_op jit(solution)/shard_map/ppermute | solution.py:233
  17.4 26.4 %collective-permute-start.12 = (f32[40,4096]{1,0:T(8,128)S(1)}, f32[40,4096]{1,0:T(8,128)S(1)}, u32[]{:S(2)}, u32[]{:S(2)}) collective-permute-start(f32[40,4096]{1,0:T(8,128)S(1)} %get-tuple-element.50), channel_id=1, source_target_pairs={{2,0},{3,1},{0,2},{1,3},{6,4},{7,5},{4,6},{5,7},{10,8},{11,9},{8,1... | collective-permute-start | bytes 1966088 | tf_op jit(solution)/shard_map/ppermute | solution.py:230
  30.1 1.6 %collective-permute-start.7 = (f32[16,4096]{1,0:T(8,128)S(1)}, f32[16,4096]{1,0:T(8,128)S(1)}, u32[]{:S(2)}, u32[]{:S(2)}) collective-permute-start(f32[16,4096]{1,0:T(8,128)S(1)} %get-tuple-element.66), channel_id=1, source_target_pairs={{0,1},{1,0},{2,3},{3,2},{4,5},{5,4},{6,7},{7,6},{8,9},{9,8},{10,11... | collective-permute-start | bytes 786440 | tf_op jit(solution)/shard_map/ppermute | solution.py:227
  30.1 4.7 %collective-permute-start.8 = (f32[16,4096]{1,0:T(8,128)S(1)}, f32[16,4096]{1,0:T(8,128)S(1)}, u32[]{:S(2)}, u32[]{:S(2)}) collective-permute-start(f32[16,4096]{1,0:T(8,128)S(1)} %get-tuple-element.65), channel_id=1, source_target_pairs={{0,1},{1,0},{2,3},{3,2},{4,5},{5,4},{6,7},{7,6},{8,9},{9,8},{10,11... | collective-permute-start | bytes 786440 | tf_op jit(solution)/shard_map/ppermute | solution.py:227
  30.6 4.2 %collective-permute-start.9 = (f32[16,4096]{1,0:T(8,128)S(1)}, f32[16,4096]{1,0:T(8,128)S(1)}, u32[]{:S(2)}, u32[]{:S(2)}) collective-permute-start(f32[16,4096]{1,0:T(8,128)S(1)} %get-tuple-element.64), channel_id=1, source_target_pairs={{0,1},{1,0},{2,3},{3,2},{4,5},{5,4},{6,7},{7,6},{8,9},{9,8},{10,11... | collective-permute-start | bytes 786440 | tf_op jit(solution)/shard_map/ppermute | solution.py:227
  30.7 4.1 %collective-permute-start.10 = (f32[16,4096]{1,0:T(8,128)S(1)}, f32[16,4096]{1,0:T(8,128)S(1)}, u32[]{:S(2)}, u32[]{:S(2)}) collective-permute-start(f32[16,4096]{1,0:T(8,128)S(1)} %get-tuple-element.63), channel_id=1, source_target_pairs={{0,1},{1,0},{2,3},{3,2},{4,5},{5,4},{6,7},{7,6},{8,9},{9,8},{10,11... | collective-permute-start | bytes 786440 | tf_op jit(solution)/shard_map/ppermute | solution.py:227
  31.7 16.9 %collective-permute-start.3 = (f32[64,640]{1,0:T(8,128)S(1)}, f32[64,640]{1,0:T(8,128)S(1)}, u32[]{:S(2)}, u32[]{:S(2)}) collective-permute-start(f32[64,640]{1,0:T(8,128)S(1)} %add.37), channel_id=1, source_target_pairs={{0,8},{4,12},{8,0},{12,4},{1,9},{5,13},{9,1},{13,5},{2,10},{6,14},... | collective-permute-start | bytes 491528 | tf_op jit(solution)/shard_map/ppermute | solution.py:233
  38.0 11.1 %collective-permute-start.11 = (f32[64,640]{1,0:T(8,128)S(1)}, f32[64,640]{1,0:T(8,128)S(1)}, u32[]{:S(2)}, u32[]{:S(2)}) collective-permute-start(f32[64,640]{1,0:T(8,128)S(1)} %get-tuple-element.48), channel_id=1, source_target_pairs={{0,4},{4,0},{8,12},{12,8},{1,5},{5,1},{9,13},{13,9},{2,6},{6,2},{1... | collective-permute-start | bytes 491528 | tf_op jit(solution)/shard_map/ppermute | solution.py:233
  39.7 8.9 %collective-permute-start.13 = (f32[64,512]{1,0:T(8,128)S(1)}, f32[64,512]{1,0:T(8,128)S(1)}, u32[]{:S(2)}, u32[]{:S(2)}) collective-permute-start(f32[64,512]{1,0:T(8,128)S(1)} %add.39), channel_id=1, source_target_pairs={{0,8},{4,12},{8,0},{12,4},{1,9},{5,13},{9,1},{13,5},{2,10},{6,14},... | collective-permute-start | bytes 393224 | tf_op jit(solution)/shard_map/ppermute | solution.py:233
  40.9 14.0 %collective-permute-start.19 = (f32[24,4096]{1,0:T(8,128)S(1)}, f32[24,4096]{1,0:T(8,128)S(1)}, u32[]{:S(2)}, u32[]{:S(2)}) collective-permute-start(f32[24,4096]{1,0:T(8,128)S(1)} %get-tuple-element.57), channel_id=1, source_target_pairs={{2,0},{3,1},{0,2},{1,3},{6,4},{7,5},{4,6},{5,7},{10,8},{11,9},{8,1... | collective-permute-start | bytes 1179656 | tf_op jit(solution)/shard_map/ppermute | solution.py:230
  49.2 2.2 %collective-permute-start.14 = (f32[16,4096]{1,0:T(8,128)S(1)}, f32[16,4096]{1,0:T(8,128)S(1)}, u32[]{:S(2)}, u32[]{:S(2)}) collective-permute-start(f32[16,4096]{1,0:T(8,128)S(1)} %get-tuple-element.68), channel_id=1, source_target_pairs={{0,1},{1,0},{2,3},{3,2},{4,5},{5,4},{6,7},{7,6},{8,9},{9,8},{10,11... | collective-permute-start | bytes 786440 | tf_op jit(solution)/shard_map/ppermute | solution.py:227
  49.3 2.1 %collective-permute-start.15 = (f32[16,4096]{1,0:T(8,128)S(1)}, f32[16,4096]{1,0:T(8,128)S(1)}, u32[]{:S(2)}, u32[]{:S(2)}) collective-permute-start(f32[16,4096]{1,0:T(8,128)S(1)} %get-tuple-element.67), channel_id=1, source_target_pairs={{0,1},{1,0},{2,3},{3,2},{4,5},{5,4},{6,7},{7,6},{8,9},{9,8},{10,11... | collective-permute-start | bytes 786440 | tf_op jit(solution)/shard_map/ppermute | solution.py:227
  49.8 1.6 %collective-permute-start.16 = (f32[8,4096]{1,0:T(8,128)S(1)}, f32[8,4096]{1,0:T(8,128)S(1)}, u32[]{:S(2)}, u32[]{:S(2)}) collective-permute-start(f32[8,4096]{1,0:T(8,128)S(1)} %slice.36), channel_id=1, source_target_pairs={{0,1},{1,0},{2,3},{3,2},{4,5},{5,4},{6,7},{7,6},{8,9},{9,8},{10,11... | collective-permute-start | bytes 393224 | tf_op jit(solution)/shard_map/ppermute | solution.py:227
  49.9 6.6 %collective-permute-start.4 = (f32[64,640]{1,0:T(8,128)S(1)}, f32[64,640]{1,0:T(8,128)S(1)}, u32[]{:S(2)}, u32[]{:S(2)}) collective-permute-start(f32[64,640]{1,0:T(8,128)S(1)} %add.38.refs_1_.refs_2_), channel_id=1, source_target_pairs={{0,4},{4,0},{8,12},{12,8},{1,5},{5,1},{9,13},{13,9},{2,6},{6,2},{1... | collective-permute-start | bytes 491528 | tf_op jit(solution)/shard_map/ppermute | solution.py:233
  54.9 4.9 %collective-permute-start.20 = (f32[8,4096]{1,0:T(8,128)S(1)}, f32[8,4096]{1,0:T(8,128)S(1)}, u32[]{:S(2)}, u32[]{:S(2)}) collective-permute-start(f32[8,4096]{1,0:T(8,128)S(1)} %get-tuple-element.71), channel_id=1, source_target_pairs={{0,1},{1,0},{2,3},{3,2},{4,5},{5,4},{6,7},{7,6},{8,9},{9,8},{10,11... | collective-permute-start | bytes 393224 | tf_op jit(solution)/shard_map/ppermute | solution.py:227
  55.1 4.7 %collective-permute-start.21 = (f32[8,4096]{1,0:T(8,128)S(1)}, f32[8,4096]{1,0:T(8,128)S(1)}, u32[]{:S(2)}, u32[]{:S(2)}) collective-permute-start(f32[8,4096]{1,0:T(8,128)S(1)} %get-tuple-element.70), channel_id=1, source_target_pairs={{0,1},{1,0},{2,3},{3,2},{4,5},{5,4},{6,7},{7,6},{8,9},{9,8},{10,11... | collective-permute-start | bytes 393224 | tf_op jit(solution)/shard_map/ppermute | solution.py:227
  55.5 4.4 %collective-permute-start.22 = (f32[8,4096]{1,0:T(8,128)S(1)}, f32[8,4096]{1,0:T(8,128)S(1)}, u32[]{:S(2)}, u32[]{:S(2)}) collective-permute-start(f32[8,4096]{1,0:T(8,128)S(1)} %get-tuple-element.69), channel_id=1, source_target_pairs={{0,1},{1,0},{2,3},{3,2},{4,5},{5,4},{6,7},{7,6},{8,9},{9,8},{10,11... | collective-permute-start | bytes 393224 | tf_op jit(solution)/shard_map/ppermute | solution.py:227
  55.6 8.1 %collective-permute-start.24 = (f32[40,768]{1,0:T(8,128)S(1)}, f32[40,768]{1,0:T(8,128)S(1)}, u32[]{:S(2)}, u32[]{:S(2)}) collective-permute-start(f32[40,768]{1,0:T(8,128)S(1)} %get-tuple-element.53), channel_id=1, source_target_pairs={{0,4},{4,0},{8,12},{12,8},{1,5},{5,1},{9,13},{13,9},{2,6},{6,2},{1... | collective-permute-start | bytes 368648 | tf_op jit(solution)/shard_map/ppermute | solution.py:233
  56.6 11.9 %collective-permute-start.17 = (f32[64,640]{1,0:T(8,128)S(1)}, f32[64,640]{1,0:T(8,128)S(1)}, u32[]{:S(2)}, u32[]{:S(2)}) collective-permute-start(f32[64,640]{1,0:T(8,128)S(1)} %add.40), channel_id=1, source_target_pairs={{0,8},{4,12},{8,0},{12,4},{1,9},{5,13},{9,1},{13,5},{2,10},{6,14},... | collective-permute-start | bytes 491528 | tf_op jit(solution)/shard_map/ppermute | solution.py:233
  62.6 9.7 %collective-permute-start.27 = (f32[48,768]{1,0:T(8,128)S(1)}, f32[48,768]{1,0:T(8,128)S(1)}, u32[]{:S(2)}, u32[]{:S(2)}) collective-permute-start(f32[48,768]{1,0:T(8,128)S(1)} %project_zero_2.1), channel_id=1, source_target_pairs={{0,4},{4,0},{8,12},{12,8},{1,5},{5,1},{9,13},{13,9},{2,6},{6,2},{1... | collective-permute-start | bytes 442376 | tf_op jit(solution)/shard_map/ppermute | solution.py:233
  63.7 10.7 %collective-permute-start.25 = (f32[40,768]{1,0:T(8,128)S(1)}, f32[40,768]{1,0:T(8,128)S(1)}, u32[]{:S(2)}, u32[]{:S(2)}) collective-permute-start(f32[40,768]{1,0:T(8,128)S(1)} %add.43), channel_id=1, source_target_pairs={{0,8},{4,12},{8,0},{12,4},{1,9},{5,13},{9,1},{13,5},{2,10},{6,14},... | collective-permute-start | bytes 368648 | tf_op jit(solution)/shard_map/ppermute | solution.py:233
  68.5 10.7 %collective-permute-start.18 = (f32[64,640]{1,0:T(8,128)S(1)}, f32[64,640]{1,0:T(8,128)S(1)}, u32[]{:S(2)}, u32[]{:S(2)}) collective-permute-start(f32[64,640]{1,0:T(8,128)S(1)} %add.41.refs_3_.refs_4_), channel_id=1, source_target_pairs={{0,4},{4,0},{8,12},{12,8},{1,5},{5,1},{9,13},{13,9},{2,6},{6,2},{1... | collective-permute-start | bytes 491528 | tf_op jit(solution)/shard_map/ppermute | solution.py:233
  72.3 11.5 %collective-permute-start.28 = (f32[48,768]{1,0:T(8,128)S(1)}, f32[48,768]{1,0:T(8,128)S(1)}, u32[]{:S(2)}, u32[]{:S(2)}) collective-permute-start(f32[48,768]{1,0:T(8,128)S(1)} %add.45.refs_10_), channel_id=1, source_target_pairs={{0,8},{4,12},{8,0},{12,4},{1,9},{5,13},{9,1},{13,5},{2,10},{6,14},... | collective-permute-start | bytes 442376 | tf_op jit(solution)/shard_map/ppermute | solution.py:233
  74.3 9.5 %collective-permute-start.23 = (f32[64,512]{1,0:T(8,128)S(1)}, f32[64,512]{1,0:T(8,128)S(1)}, u32[]{:S(2)}, u32[]{:S(2)}) collective-permute-start(f32[64,512]{1,0:T(8,128)S(1)} %add.42.refs_6_), channel_id=1, source_target_pairs={{0,4},{4,0},{8,12},{12,8},{1,5},{5,1},{9,13},{13,9},{2,6},{6,2},{1... | collective-permute-start | bytes 393224 | tf_op jit(solution)/shard_map/ppermute | solution.py:233
  74.4 9.4 %collective-permute-start.26 = (f32[40,768]{1,0:T(8,128)S(1)}, f32[40,768]{1,0:T(8,128)S(1)}, u32[]{:S(2)}, u32[]{:S(2)}) collective-permute-start(f32[40,768]{1,0:T(8,128)S(1)} %add.44.refs_8_), channel_id=1, source_target_pairs={{0,4},{4,0},{8,12},{12,8},{1,5},{5,1},{9,13},{13,9},{2,6},{6,2},{1... | collective-permute-start | bytes 368648 | tf_op jit(solution)/shard_map/ppermute | solution.py:233

commit v8 on v7

--- a/solution.py
+++ b/solution.py
@@ -183,7 +183,7 @@
 def update(name, make, ins, factor, pieces, current, last):
     here, nc = current[0].shape
     width = factor.shape[0]
-    steps = steps_of(here, 256)
+    steps = steps_of(here, 512)
 
     def body(*refs):
         in_refs, refs = refs[: len(ins)], refs[len(ins) :]

time: 90.1 us -> 89.9 us (level)
  transfers between devices with their start and end apart: 29 -> 29, of which waited for: 11 -> 12; matrix products, arithmetic and copies ran while one was open for 0% -> 0% of each run, Pallas kernels for 28% -> 28%
where the time goes in v8:
time: 89.9 us; the launch traced here: 89.7 us
  Pallas kernels  31.7 us (35%)
  waiting for transfers between devices  28.7 us (32%)
  starting transfers between devices  27.1 us (30%)
  local copies, waits for them, and re-layouts  1.82 us (2%)
    pallas_call x11, Pallas kernels, call(): pl.pallas_call(body, in_specs=specs, out_specs=out_specs, out_shape=outs,...  31.7 us
    ppermute x14, starting transfers between devices, row_swap(): return lax.ppermute(value, 'row', [(i, i ^ step) for i in range(rows)])  19.4 us
    ppermute x14, waiting for transfers between devices, row_swap(): return lax.ppermute(value, 'row', [(i, i ^ step) for i in range(rows)])  15.1 us
    ppermute x3, waiting for transfers between devices, from_chip(): lax.ppermute(value, 'col', [((i + 2 * step) % cols, i) for i in range(col...  11.9 us
    ppermute x3, starting transfers between devices, from_chip(): lax.ppermute(value, 'col', [((i + 2 * step) % cols, i) for i in range(col...  4.58 us
    ppermute x12, starting transfers between devices, core_swap(): return lax.ppermute(value, 'col', [(i, i ^ 1) for i in range(cols)])  3.12 us
  transfers between devices with their start and end apart: 29, of which 12 were waited for; matrix products, arithmetic and copies ran while one was open for 0% of the time, Pallas kernels for 28%

profile of v8, /device:TPU:0, one launch (start us, length us, event | category | flops | bytes accessed | tf_op | source)
XLA Modules:
  0.0 89.7 jit_solution(9675410519827885654)
XLA Ops:
  0.1 1.6 %copy-done = f32[2,64,4096]{2,1,0:T(8,128)S(1)} copy-done((f32[2,64,4096]{2,1,0:T(8,128)S(1)}, f32[2,64,4096]{2,1,0:T(8,128)}, u32[]{:S(2)}) %copy-start) | copy-done | bytes 2097176
  1.7 0.8 cut.1
  3.1 2.9 %collective-permute-start.5 = (f32[64,4096]{1,0:T(8,128)S(1)}, f32[64,4096]{1,0:T(8,128)S(1)}, u32[]{:S(2)}, u32[]{:S(2)}) collective-permute-start(f32[64,4096]{1,0:T(8,128)S(1)} %get-tuple-element.34.refs_1_.refs_5_.refs_6_.refs_4_), channel_id=1, source_target_pairs={{2,0},{3,1},{0,2},{1,3},{6,4},{7,5},{4,6},{5,7},{10,8},{11,9},{8,1... | collective-permute-start | bytes 3145736 | tf_op jit(solution)/shard_map/ppermute | solution.py:230
  6.0 3.6 %load.1 = (bf16[4096,512]{1,0:T(8,128)(2,1)S(1)}, bf16[4096,512]{1,0:T(8,128)(2,1)S(1)}) custom-call(f32[4096,512]{1,0:T(8,128)} %in_ref.2), custom_call_target="tpu_custom_call" | custom-call | flops 1 | bytes 1 | tf_op jit(solution)/shard_map/load/pallas_call | solution.py:20
  9.7 3.2 %project_own1.1 = (f32[64,640]{1,0:T(8,128)S(1)}, f32[64,640]{1,0:T(8,128)S(1)}) custom-call(s32[6]{0:T(128)S(1)} %stack.23.where_ref.refs_0_, f32[64,4096]{1,0:T(8,128)S(1)} %get-tuple-element.34.refs_1_.refs_5_.refs_6_.refs_4_, f32[64,4096]{1,0:T(8,128)S(1)} %collective-permute-done.refs_2_.refs_6_.refs_7_.refs_5_, ...), custom_call_target="tpu_custom_call" | custom-call | flops 1 | bytes 1 | tf_op jit(solution)/shard_map/project_own1/pallas_call | solution.py:20
  12.9 1.6 %collective-permute-start.2 = (f32[64,640]{1,0:T(8,128)S(1)}, f32[64,640]{1,0:T(8,128)S(1)}, u32[]{:S(2)}, u32[]{:S(2)}) collective-permute-start(f32[64,640]{1,0:T(8,128)S(1)} %get-tuple-element.40), channel_id=1, source_target_pairs={{0,4},{4,0},{8,12},{12,8},{1,5},{5,1},{9,13},{13,9},{2,6},{6,2},{1... | collective-permute-start | bytes 491528 | tf_op jit(solution)/shard_map/ppermute | solution.py:233
  14.5 2.3 %project_own0.1 = (f32[64,512]{1,0:T(8,128)S(1)}, f32[64,512]{1,0:T(8,128)S(1)}) custom-call(s32[6]{0:T(128)S(1)} %stack.23.where_ref.refs_0_, f32[64,4096]{1,0:T(8,128)S(1)} %get-tuple-element.49.refs_3_.refs_1_.refs_6_.in_ref.refs_13_, f32[64,4096]{1,0:T(8,128)S(1)} %collective-permute-done.1.refs_4_.refs_2_.refs_7_.refs_14_, ...), custom_call_target="tpu_custom_call" | custom-call | flops 1 | bytes 1 | tf_op jit(solution)/shard_map/project_own0/pallas_call | solution.py:20
  17.6 2.0 %reorder.1 = (f32[256,256]{1,0:T(8,128)S(1)}, f32[256,256]{1,0:T(8,128)S(1)}) custom-call(s32[6]{0:T(128)S(1)} %stack.23.where_ref.refs_0_, f32[2,256,256]{2,1,0:T(8,128)S(1)} %copy-done.1), custom_call_target="tpu_custom_call" | custom-call | flops 1 | bytes 1 | tf_op jit(solution)/shard_map/reorder/pallas_call | solution.py:20
  19.6 10.4 %collective-permute-done.5.refs_1_.refs_7_.refs_8_.refs_6_ = f32[64,4096]{1,0:T(8,128)S(1)} collective-permute-done((f32[64,4096]{1,0:T(8,128)S(1)}, f32[64,4096]{1,0:T(8,128)S(1)}, u32[]{:S(2)}, u32[]{:S(2)}) %collective-permute-start.5) | collective-permute-done | bytes 1048608 | tf_op jit(solution)/shard_map/ppermute | solution.py:230
  31.7 3.2 %collective-permute-start.3 = (f32[64,640]{1,0:T(8,128)S(1)}, f32[64,640]{1,0:T(8,128)S(1)}, u32[]{:S(2)}, u32[]{:S(2)}) collective-permute-start(f32[64,640]{1,0:T(8,128)S(1)} %add.37), channel_id=1, source_target_pairs={{0,8},{4,12},{8,0},{12,4},{1,9},{5,13},{9,1},{13,5},{2,10},{6,14},... | collective-permute-start | bytes 491528 | tf_op jit(solution)/shard_map/ppermute | solution.py:233
  34.8 3.2 %project_one_0.1 = (f32[64,640]{1,0:T(8,128)S(1)}, f32[64,640]{1,0:T(8,128)S(1)}) custom-call(s32[6]{0:T(128)S(1)} %stack.23.where_ref.refs_0_, f32[64,4096]{1,0:T(8,128)S(1)} %collective-permute-done.5.refs_1_.refs_7_.refs_8_.refs_6_, f32[16,4096]{1,0:T(8,128)S(1)} %collective-permute-done.7.refs_2_.refs_8_.refs_9_.refs_7_, ...), custom_call_target="tpu_custom_call" | custom-call | flops 1 | bytes 1 | tf_op jit(solution)/shard_map/project_one_0/pallas_call | solution.py:20
  38.0 1.6 %collective-permute-start.11 = (f32[64,640]{1,0:T(8,128)S(1)}, f32[64,640]{1,0:T(8,128)S(1)}, u32[]{:S(2)}, u32[]{:S(2)}) collective-permute-start(f32[64,640]{1,0:T(8,128)S(1)} %get-tuple-element.48), channel_id=1, source_target_pairs={{0,4},{4,0},{8,12},{12,8},{1,5},{5,1},{9,13},{13,9},{2,6},{6,2},{1... | collective-permute-start | bytes 491528 | tf_op jit(solution)/shard_map/ppermute | solution.py:233
  39.7 1.2 %collective-permute-start.13 = (f32[64,512]{1,0:T(8,128)S(1)}, f32[64,512]{1,0:T(8,128)S(1)}, u32[]{:S(2)}, u32[]{:S(2)}) collective-permute-start(f32[64,512]{1,0:T(8,128)S(1)} %add.39), channel_id=1, source_target_pairs={{0,8},{4,12},{8,0},{12,4},{1,9},{5,13},{9,1},{13,5},{2,10},{6,14},... | collective-permute-start | bytes 393224 | tf_op jit(solution)/shard_map/ppermute | solution.py:233
  40.9 1.5 %collective-permute-start.19 = (f32[24,4096]{1,0:T(8,128)S(1)}, f32[24,4096]{1,0:T(8,128)S(1)}, u32[]{:S(2)}, u32[]{:S(2)}) collective-permute-start(f32[24,4096]{1,0:T(8,128)S(1)} %get-tuple-element.57), channel_id=1, source_target_pairs={{2,0},{3,1},{0,2},{1,3},{6,4},{7,5},{4,6},{5,7},{10,8},{11,9},{8,1... | collective-permute-start | bytes 1179656 | tf_op jit(solution)/shard_map/ppermute | solution.py:230
  42.4 1.5 %collective-permute-done.12.refs_1_.refs_15_ = f32[40,4096]{1,0:T(8,128)S(1)} collective-permute-done((f32[40,4096]{1,0:T(8,128)S(1)}, f32[40,4096]{1,0:T(8,128)S(1)}, u32[]{:S(2)}, u32[]{:S(2)}) %collective-permute-start.12) | collective-permute-done | bytes 655392 | tf_op jit(solution)/shard_map/ppermute | solution.py:230
  43.8 4.8 %collective-permute-done.13 = f32[64,512]{1,0:T(8,128)S(1)} collective-permute-done((f32[64,512]{1,0:T(8,128)S(1)}, f32[64,512]{1,0:T(8,128)S(1)}, u32[]{:S(2)}, u32[]{:S(2)}) %collective-permute-start.13) | collective-permute-done | bytes 131104 | tf_op jit(solution)/shard_map/ppermute | solution.py:233
  48.6 0.6 collective-permute-done.11
  50.1 1.2 %collective-permute-done.16.refs_4_.refs_18_ = f32[8,4096]{1,0:T(8,128)S(1)} collective-permute-done((f32[8,4096]{1,0:T(8,128)S(1)}, f32[8,4096]{1,0:T(8,128)S(1)}, u32[]{:S(2)}, u32[]{:S(2)}) %collective-permute-start.16) | collective-permute-done | bytes 131104 | tf_op jit(solution)/shard_map/ppermute | solution.py:227
  51.4 3.5 %project_zero_1.1 = (f32[40,768]{1,0:T(8,128)S(1)}, f32[40,768]{1,0:T(8,128)S(1)}) custom-call(s32[6]{0:T(128)S(1)} %stack.23.where_ref.refs_0_, f32[40,4096]{1,0:T(8,128)S(1)} %collective-permute-done.12.refs_1_.refs_15_, f32[16,4096]{1,0:T(8,128)S(1)} %collective-permute-done.14.refs_2_.refs_16_, f32[16,4096]{1,0:T(8,128)S(1)} %collective-permute-done.15.refs_3_.refs_17_, ...), custom_call_target="tpu_custom_call" | custom-call | flops 1 | bytes 1 | tf_op jit(solution)/shard_map/project_zero_1/pallas_call | solution.py:20
  55.6 0.7 collective-permute-start.24
  56.6 3.3 %collective-permute-start.17 = (f32[64,640]{1,0:T(8,128)S(1)}, f32[64,640]{1,0:T(8,128)S(1)}, u32[]{:S(2)}, u32[]{:S(2)}) collective-permute-start(f32[64,640]{1,0:T(8,128)S(1)} %add.40), channel_id=1, source_target_pairs={{0,8},{4,12},{8,0},{12,4},{1,9},{5,13},{9,1},{13,5},{2,10},{6,14},... | collective-permute-start | bytes 491528 | tf_op jit(solution)/shard_map/ppermute | solution.py:233
  59.8 2.7 %project_zero_2.1 = f32[48,768]{1,0:T(8,128)S(1)} custom-call(f32[24,4096]{1,0:T(8,128)S(1)} %collective-permute-done.19.refs_0_.refs_19_, f32[8,4096]{1,0:T(8,128)S(1)} %collective-permute-done.20.refs_1_.refs_20_, f32[8,4096]{1,0:T(8,128)S(1)} %collective-permute-done.21.refs_2_.refs_21_, f32[8,4096]{1,0:T(8,128)S(1)} %collective-permute-done.22.refs_3_.refs_22_, ...), custom_call_target="tpu_custom_call" | custom-call | flops 1 | bytes 1 | tf_op jit(solution)/shard_map/project_zero_2/pallas_call | solution.py:20
  62.6 0.9 %collective-permute-start.27 = (f32[48,768]{1,0:T(8,128)S(1)}, f32[48,768]{1,0:T(8,128)S(1)}, u32[]{:S(2)}, u32[]{:S(2)}) collective-permute-start(f32[48,768]{1,0:T(8,128)S(1)} %project_zero_2.1), channel_id=1, source_target_pairs={{0,4},{4,0},{8,12},{12,8},{1,5},{5,1},{9,13},{13,9},{2,6},{6,2},{1... | collective-permute-start | bytes 442376 | tf_op jit(solution)/shard_map/ppermute | solution.py:233
  63.7 0.9 %collective-permute-start.25 = (f32[40,768]{1,0:T(8,128)S(1)}, f32[40,768]{1,0:T(8,128)S(1)}, u32[]{:S(2)}, u32[]{:S(2)}) collective-permute-start(f32[40,768]{1,0:T(8,128)S(1)} %add.43), channel_id=1, source_target_pairs={{0,8},{4,12},{8,0},{12,4},{1,9},{5,13},{9,1},{13,5},{2,10},{6,14},... | collective-permute-start | bytes 368648 | tf_op jit(solution)/shard_map/ppermute | solution.py:233
  64.6 3.9 %collective-permute-done.17 = f32[64,640]{1,0:T(8,128)S(1)} collective-permute-done((f32[64,640]{1,0:T(8,128)S(1)}, f32[64,640]{1,0:T(8,128)S(1)}, u32[]{:S(2)}, u32[]{:S(2)}) %collective-permute-start.17) | collective-permute-done | bytes 163872 | tf_op jit(solution)/shard_map/ppermute | solution.py:233
  68.5 1.1 %collective-permute-start.18 = (f32[64,640]{1,0:T(8,128)S(1)}, f32[64,640]{1,0:T(8,128)S(1)}, u32[]{:S(2)}, u32[]{:S(2)}) collective-permute-start(f32[64,640]{1,0:T(8,128)S(1)} %add.41.refs_3_.refs_4_), channel_id=1, source_target_pairs={{0,4},{4,0},{8,12},{12,8},{1,5},{5,1},{9,13},{13,9},{2,6},{6,2},{1... | collective-permute-start | bytes 491528 | tf_op jit(solution)/shard_map/ppermute | solution.py:233
  69.6 2.6 %collective-permute-done.27 = f32[48,768]{1,0:T(8,128)S(1)} collective-permute-done((f32[48,768]{1,0:T(8,128)S(1)}, f32[48,768]{1,0:T(8,128)S(1)}, u32[]{:S(2)}, u32[]{:S(2)}) %collective-permute-start.27) | collective-permute-done | bytes 147488 | tf_op jit(solution)/shard_map/ppermute | solution.py:233
  72.3 2.0 %collective-permute-start.28 = (f32[48,768]{1,0:T(8,128)S(1)}, f32[48,768]{1,0:T(8,128)S(1)}, u32[]{:S(2)}, u32[]{:S(2)}) collective-permute-start(f32[48,768]{1,0:T(8,128)S(1)} %add.45.refs_10_), channel_id=1, source_target_pairs={{0,8},{4,12},{8,0},{12,4},{1,9},{5,13},{9,1},{13,5},{2,10},{6,14},... | collective-permute-start | bytes 442376 | tf_op jit(solution)/shard_map/ppermute | solution.py:233
  74.4 2.1 %collective-permute-start.26 = (f32[40,768]{1,0:T(8,128)S(1)}, f32[40,768]{1,0:T(8,128)S(1)}, u32[]{:S(2)}, u32[]{:S(2)}) collective-permute-start(f32[40,768]{1,0:T(8,128)S(1)} %add.44.refs_8_), channel_id=1, source_target_pairs={{0,4},{4,0},{8,12},{12,8},{1,5},{5,1},{9,13},{13,9},{2,6},{6,2},{1... | collective-permute-start | bytes 368648 | tf_op jit(solution)/shard_map/ppermute | solution.py:233
  76.4 2.7 %collective-permute-done.18.refs_4_.refs_5_ = f32[64,640]{1,0:T(8,128)S(1)} collective-permute-done((f32[64,640]{1,0:T(8,128)S(1)}, f32[64,640]{1,0:T(8,128)S(1)}, u32[]{:S(2)}, u32[]{:S(2)}) %collective-permute-start.18) | collective-permute-done | bytes 163872 | tf_op jit(solution)/shard_map/ppermute | solution.py:233
  79.2 4.4 %update_one.1 = (f32[4096,512]{1,0:T(8,128)S(1)}, f32[256,512]{1,0:T(8,128)S(1)}) custom-call(s32[6]{0:T(128)S(1)} %stack.23.where_ref.refs_0_, f32[64,640]{1,0:T(8,128)S(1)} %add.38.refs_1_.refs_2_, f32[64,640]{1,0:T(8,128)S(1)} %collective-permute-done.4.refs_2_.refs_3_, f32[64,640]{1,0:T(8,128)S(1)} %add.41.refs_3_.refs_4_, ...), custom_call_target="tpu_custom_call" | custom-call | flops 1 | bytes 1 | tf_op jit(solution)/shard_map/update_one/pallas_call | solution.py:20
  83.7 5.9 %update_zero.1 = f32[4096,512]{1,0:T(8,128)} custom-call(s32[6]{0:T(128)S(1)} %stack.23.where_ref.refs_0_, f32[256,512]{1,0:T(8,128)S(1)} %get-tuple-element.56.refs_1_, f32[64,640]{1,0:T(8,128)S(1)} %add.38.refs_1_.refs_2_, f32[64,640]{1,0:T(8,128)S(1)} %collective-permute-done.4.refs_2_.refs_3_, f32[64,640]{1,0:T(8,128)S(1)} %add.41.refs_3_.refs_4_, ...), custom_call_target="tpu_custom_call" | custom-call | flops 1 | bytes 1 | tf_op jit(solution)/shard_map/update_zero/pallas_call | solution.py:20
  (55 shorter events, 5.6 us)
Async XLA Ops:
  0.1 1.6 %copy-start = (f32[2,64,4096]{2,1,0:T(8,128)S(1)}, f32[2,64,4096]{2,1,0:T(8,128)}, u32[]{:S(2)}) copy-start(f32[2,64,4096]{2,1,0:T(8,128)} %in_ref.1) | copy-start | bytes 6291460
  2.5 7.1 %collective-permute-start = (f32[64,4096]{1,0:T(8,128)S(1)}, f32[64,4096]{1,0:T(8,128)S(1)}, u32[]{:S(2)}, u32[]{:S(2)}) collective-permute-start(f32[64,4096]{1,0:T(8,128)S(1)} %get-tuple-element.34.refs_1_.refs_5_.refs_6_.refs_4_), channel_id=1, source_target_pairs={{0,1},{1,0},{2,3},{3,2},{4,5},{5,4},{6,7},{7,6},{8,9},{9,8},{10,11... | collective-permute-start | bytes 3145736 | tf_op jit(solution)/shard_map/ppermute | solution.py:227
  3.0 6.6 %collective-permute-start.1 = (f32[64,4096]{1,0:T(8,128)S(1)}, f32[64,4096]{1,0:T(8,128)S(1)}, u32[]{:S(2)}, u32[]{:S(2)}) collective-permute-start(f32[64,4096]{1,0:T(8,128)S(1)} %get-tuple-element.49.refs_3_.refs_1_.refs_6_.in_ref.refs_13_), channel_id=1, source_target_pairs={{0,1},{1,0},{2,3},{3,2},{4,5},{5,4},{6,7},{7,6},{8,9},{9,8},{10,11... | collective-permute-start | bytes 3145736 | tf_op jit(solution)/shard_map/ppermute | solution.py:227
  3.1 26.9 %collective-permute-start.5 = (f32[64,4096]{1,0:T(8,128)S(1)}, f32[64,4096]{1,0:T(8,128)S(1)}, u32[]{:S(2)}, u32[]{:S(2)}) collective-permute-start(f32[64,4096]{1,0:T(8,128)S(1)} %get-tuple-element.34.refs_1_.refs_5_.refs_6_.refs_4_), channel_id=1, source_target_pairs={{2,0},{3,1},{0,2},{1,3},{6,4},{7,5},{4,6},{5,7},{10,8},{11,9},{8,1... | collective-permute-start | bytes 3145736 | tf_op jit(solution)/shard_map/ppermute | solution.py:230
  12.8 4.7 %copy-start.1 = (f32[2,256,256]{2,1,0:T(8,128)S(1)}, f32[2,256,256]{2,1,0:T(8,128)}, u32[]{:S(2)}) copy-start(f32[2,256,256]{2,1,0:T(8,128)} %in_ref.3) | copy-start | bytes 1572868
  12.9 17.1 %collective-permute-start.2 = (f32[64,640]{1,0:T(8,128)S(1)}, f32[64,640]{1,0:T(8,128)S(1)}, u32[]{:S(2)}, u32[]{:S(2)}) collective-permute-start(f32[64,640]{1,0:T(8,128)S(1)} %get-tuple-element.40), channel_id=1, source_target_pairs={{0,4},{4,0},{8,12},{12,8},{1,5},{5,1},{9,13},{13,9},{2,6},{6,2},{1... | collective-permute-start | bytes 491528 | tf_op jit(solution)/shard_map/ppermute | solution.py:233
  16.8 13.2 %collective-permute-start.6 = (f32[64,512]{1,0:T(8,128)S(1)}, f32[64,512]{1,0:T(8,128)S(1)}, u32[]{:S(2)}, u32[]{:S(2)}) collective-permute-start(f32[64,512]{1,0:T(8,128)S(1)} %get-tuple-element.43), channel_id=1, source_target_pairs={{0,4},{4,0},{8,12},{12,8},{1,5},{5,1},{9,13},{13,9},{2,6},{6,2},{1... | collective-permute-start | bytes 393224 | tf_op jit(solution)/shard_map/ppermute | solution.py:233
  17.4 26.4 %collective-permute-start.12 = (f32[40,4096]{1,0:T(8,128)S(1)}, f32[40,4096]{1,0:T(8,128)S(1)}, u32[]{:S(2)}, u32[]{:S(2)}) collective-permute-start(f32[40,4096]{1,0:T(8,128)S(1)} %get-tuple-element.50), channel_id=1, source_target_pairs={{2,0},{3,1},{0,2},{1,3},{6,4},{7,5},{4,6},{5,7},{10,8},{11,9},{8,1... | collective-permute-start | bytes 1966088 | tf_op jit(solution)/shard_map/ppermute | solution.py:230
  30.1 1.6 %collective-permute-start.7 = (f32[16,4096]{1,0:T(8,128)S(1)}, f32[16,4096]{1,0:T(8,128)S(1)}, u32[]{:S(2)}, u32[]{:S(2)}) collective-permute-start(f32[16,4096]{1,0:T(8,128)S(1)} %get-tuple-element.66), channel_id=1, source_target_pairs={{0,1},{1,0},{2,3},{3,2},{4,5},{5,4},{6,7},{7,6},{8,9},{9,8},{10,11... | collective-permute-start | bytes 786440 | tf_op jit(solution)/shard_map/ppermute | solution.py:227
  30.1 4.7 %collective-permute-start.8 = (f32[16,4096]{1,0:T(8,128)S(1)}, f32[16,4096]{1,0:T(8,128)S(1)}, u32[]{:S(2)}, u32[]{:S(2)}) collective-permute-start(f32[16,4096]{1,0:T(8,128)S(1)} %get-tuple-element.65), channel_id=1, source_target_pairs={{0,1},{1,0},{2,3},{3,2},{4,5},{5,4},{6,7},{7,6},{8,9},{9,8},{10,11... | collective-permute-start | bytes 786440 | tf_op jit(solution)/shard_map/ppermute | solution.py:227
  30.6 4.2 %collective-permute-start.9 = (f32[16,4096]{1,0:T(8,128)S(1)}, f32[16,4096]{1,0:T(8,128)S(1)}, u32[]{:S(2)}, u32[]{:S(2)}) collective-permute-start(f32[16,4096]{1,0:T(8,128)S(1)} %get-tuple-element.64), channel_id=1, source_target_pairs={{0,1},{1,0},{2,3},{3,2},{4,5},{5,4},{6,7},{7,6},{8,9},{9,8},{10,11... | collective-permute-start | bytes 786440 | tf_op jit(solution)/shard_map/ppermute | solution.py:227
  30.7 4.1 %collective-permute-start.10 = (f32[16,4096]{1,0:T(8,128)S(1)}, f32[16,4096]{1,0:T(8,128)S(1)}, u32[]{:S(2)}, u32[]{:S(2)}) collective-permute-start(f32[16,4096]{1,0:T(8,128)S(1)} %get-tuple-element.63), channel_id=1, source_target_pairs={{0,1},{1,0},{2,3},{3,2},{4,5},{5,4},{6,7},{7,6},{8,9},{9,8},{10,11... | collective-permute-start | bytes 786440 | tf_op jit(solution)/shard_map/ppermute | solution.py:227
  31.7 16.9 %collective-permute-start.3 = (f32[64,640]{1,0:T(8,128)S(1)}, f32[64,640]{1,0:T(8,128)S(1)}, u32[]{:S(2)}, u32[]{:S(2)}) collective-permute-start(f32[64,640]{1,0:T(8,128)S(1)} %add.37), channel_id=1, source_target_pairs={{0,8},{4,12},{8,0},{12,4},{1,9},{5,13},{9,1},{13,5},{2,10},{6,14},... | collective-permute-start | bytes 491528 | tf_op jit(solution)/shard_map/ppermute | solution.py:233
  38.0 11.1 %collective-permute-start.11 = (f32[64,640]{1,0:T(8,128)S(1)}, f32[64,640]{1,0:T(8,128)S(1)}, u32[]{:S(2)}, u32[]{:S(2)}) collective-permute-start(f32[64,640]{1,0:T(8,128)S(1)} %get-tuple-element.48), channel_id=1, source_target_pairs={{0,4},{4,0},{8,12},{12,8},{1,5},{5,1},{9,13},{13,9},{2,6},{6,2},{1... | collective-permute-start | bytes 491528 | tf_op jit(solution)/shard_map/ppermute | solution.py:233
  39.7 8.9 %collective-permute-start.13 = (f32[64,512]{1,0:T(8,128)S(1)}, f32[64,512]{1,0:T(8,128)S(1)}, u32[]{:S(2)}, u32[]{:S(2)}) collective-permute-start(f32[64,512]{1,0:T(8,128)S(1)} %add.39), channel_id=1, source_target_pairs={{0,8},{4,12},{8,0},{12,4},{1,9},{5,13},{9,1},{13,5},{2,10},{6,14},... | collective-permute-start | bytes 393224 | tf_op jit(solution)/shard_map/ppermute | solution.py:233
  40.9 14.0 %collective-permute-start.19 = (f32[24,4096]{1,0:T(8,128)S(1)}, f32[24,4096]{1,0:T(8,128)S(1)}, u32[]{:S(2)}, u32[]{:S(2)}) collective-permute-start(f32[24,4096]{1,0:T(8,128)S(1)} %get-tuple-element.57), channel_id=1, source_target_pairs={{2,0},{3,1},{0,2},{1,3},{6,4},{7,5},{4,6},{5,7},{10,8},{11,9},{8,1... | collective-permute-start | bytes 1179656 | tf_op jit(solution)/shard_map/ppermute | solution.py:230
  49.2 2.2 %collective-permute-start.14 = (f32[16,4096]{1,0:T(8,128)S(1)}, f32[16,4096]{1,0:T(8,128)S(1)}, u32[]{:S(2)}, u32[]{:S(2)}) collective-permute-start(f32[16,4096]{1,0:T(8,128)S(1)} %get-tuple-element.68), channel_id=1, source_target_pairs={{0,1},{1,0},{2,3},{3,2},{4,5},{5,4},{6,7},{7,6},{8,9},{9,8},{10,11... | collective-permute-start | bytes 786440 | tf_op jit(solution)/shard_map/ppermute | solution.py:227
  49.3 2.1 %collective-permute-start.15 = (f32[16,4096]{1,0:T(8,128)S(1)}, f32[16,4096]{1,0:T(8,128)S(1)}, u32[]{:S(2)}, u32[]{:S(2)}) collective-permute-start(f32[16,4096]{1,0:T(8,128)S(1)} %get-tuple-element.67), channel_id=1, source_target_pairs={{0,1},{1,0},{2,3},{3,2},{4,5},{5,4},{6,7},{7,6},{8,9},{9,8},{10,11... | collective-permute-start | bytes 786440 | tf_op jit(solution)/shard_map/ppermute | solution.py:227
  49.8 1.6 %collective-permute-start.16 = (f32[8,4096]{1,0:T(8,128)S(1)}, f32[8,4096]{1,0:T(8,128)S(1)}, u32[]{:S(2)}, u32[]{:S(2)}) collective-permute-start(f32[8,4096]{1,0:T(8,128)S(1)} %slice.36), channel_id=1, source_target_pairs={{0,1},{1,0},{2,3},{3,2},{4,5},{5,4},{6,7},{7,6},{8,9},{9,8},{10,11... | collective-permute-start | bytes 393224 | tf_op jit(solution)/shard_map/ppermute | solution.py:227
  49.9 6.6 %collective-permute-start.4 = (f32[64,640]{1,0:T(8,128)S(1)}, f32[64,640]{1,0:T(8,128)S(1)}, u32[]{:S(2)}, u32[]{:S(2)}) collective-permute-start(f32[64,640]{1,0:T(8,128)S(1)} %add.38.refs_1_.refs_2_), channel_id=1, source_target_pairs={{0,4},{4,0},{8,12},{12,8},{1,5},{5,1},{9,13},{13,9},{2,6},{6,2},{1... | collective-permute-start | bytes 491528 | tf_op jit(solution)/shard_map/ppermute | solution.py:233
  54.9 4.9 %collective-permute-start.20 = (f32[8,4096]{1,0:T(8,128)S(1)}, f32[8,4096]{1,0:T(8,128)S(1)}, u32[]{:S(2)}, u32[]{:S(2)}) collective-permute-start(f32[8,4096]{1,0:T(8,128)S(1)} %get-tuple-element.71), channel_id=1, source_target_pairs={{0,1},{1,0},{2,3},{3,2},{4,5},{5,4},{6,7},{7,6},{8,9},{9,8},{10,11... | collective-permute-start | bytes 393224 | tf_op jit(solution)/shard_map/ppermute | solution.py:227
  55.1 4.7 %collective-permute-start.21 = (f32[8,4096]{1,0:T(8,128)S(1)}, f32[8,4096]{1,0:T(8,128)S(1)}, u32[]{:S(2)}, u32[]{:S(2)}) collective-permute-start(f32[8,4096]{1,0:T(8,128)S(1)} %get-tuple-element.70), channel_id=1, source_target_pairs={{0,1},{1,0},{2,3},{3,2},{4,5},{5,4},{6,7},{7,6},{8,9},{9,8},{10,11... | collective-permute-start | bytes 393224 | tf_op jit(solution)/shard_map/ppermute | solution.py:227
  55.5 4.4 %collective-permute-start.22 = (f32[8,4096]{1,0:T(8,128)S(1)}, f32[8,4096]{1,0:T(8,128)S(1)}, u32[]{:S(2)}, u32[]{:S(2)}) collective-permute-start(f32[8,4096]{1,0:T(8,128)S(1)} %get-tuple-element.69), channel_id=1, source_target_pairs={{0,1},{1,0},{2,3},{3,2},{4,5},{5,4},{6,7},{7,6},{8,9},{9,8},{10,11... | collective-permute-start | bytes 393224 | tf_op jit(solution)/shard_map/ppermute | solution.py:227
  55.6 8.1 %collective-permute-start.24 = (f32[40,768]{1,0:T(8,128)S(1)}, f32[40,768]{1,0:T(8,128)S(1)}, u32[]{:S(2)}, u32[]{:S(2)}) collective-permute-start(f32[40,768]{1,0:T(8,128)S(1)} %get-tuple-element.53), channel_id=1, source_target_pairs={{0,4},{4,0},{8,12},{12,8},{1,5},{5,1},{9,13},{13,9},{2,6},{6,2},{1... | collective-permute-start | bytes 368648 | tf_op jit(solution)/shard_map/ppermute | solution.py:233
  56.6 11.9 %collective-permute-start.17 = (f32[64,640]{1,0:T(8,128)S(1)}, f32[64,640]{1,0:T(8,128)S(1)}, u32[]{:S(2)}, u32[]{:S(2)}) collective-permute-start(f32[64,640]{1,0:T(8,128)S(1)} %add.40), channel_id=1, source_target_pairs={{0,8},{4,12},{8,0},{12,4},{1,9},{5,13},{9,1},{13,5},{2,10},{6,14},... | collective-permute-start | bytes 491528 | tf_op jit(solution)/shard_map/ppermute | solution.py:233
  62.6 9.7 %collective-permute-start.27 = (f32[48,768]{1,0:T(8,128)S(1)}, f32[48,768]{1,0:T(8,128)S(1)}, u32[]{:S(2)}, u32[]{:S(2)}) collective-permute-start(f32[48,768]{1,0:T(8,128)S(1)} %project_zero_2.1), channel_id=1, source_target_pairs={{0,4},{4,0},{8,12},{12,8},{1,5},{5,1},{9,13},{13,9},{2,6},{6,2},{1... | collective-permute-start | bytes 442376 | tf_op jit(solution)/shard_map/ppermute | solution.py:233
  63.7 10.7 %collective-permute-start.25 = (f32[40,768]{1,0:T(8,128)S(1)}, f32[40,768]{1,0:T(8,128)S(1)}, u32[]{:S(2)}, u32[]{:S(2)}) collective-permute-start(f32[40,768]{1,0:T(8,128)S(1)} %add.43), channel_id=1, source_target_pairs={{0,8},{4,12},{8,0},{12,4},{1,9},{5,13},{9,1},{13,5},{2,10},{6,14},... | collective-permute-start | bytes 368648 | tf_op jit(solution)/shard_map/ppermute | solution.py:233
  68.5 10.7 %collective-permute-start.18 = (f32[64,640]{1,0:T(8,128)S(1)}, f32[64,640]{1,0:T(8,128)S(1)}, u32[]{:S(2)}, u32[]{:S(2)}) collective-permute-start(f32[64,640]{1,0:T(8,128)S(1)} %add.41.refs_3_.refs_4_), channel_id=1, source_target_pairs={{0,4},{4,0},{8,12},{12,8},{1,5},{5,1},{9,13},{13,9},{2,6},{6,2},{1... | collective-permute-start | bytes 491528 | tf_op jit(solution)/shard_map/ppermute | solution.py:233
  72.3 11.4 %collective-permute-start.28 = (f32[48,768]{1,0:T(8,128)S(1)}, f32[48,768]{1,0:T(8,128)S(1)}, u32[]{:S(2)}, u32[]{:S(2)}) collective-permute-start(f32[48,768]{1,0:T(8,128)S(1)} %add.45.refs_10_), channel_id=1, source_target_pairs={{0,8},{4,12},{8,0},{12,4},{1,9},{5,13},{9,1},{13,5},{2,10},{6,14},... | collective-permute-start | bytes 442376 | tf_op jit(solution)/shard_map/ppermute | solution.py:233
  74.3 9.4 %collective-permute-start.23 = (f32[64,512]{1,0:T(8,128)S(1)}, f32[64,512]{1,0:T(8,128)S(1)}, u32[]{:S(2)}, u32[]{:S(2)}) collective-permute-start(f32[64,512]{1,0:T(8,128)S(1)} %add.42.refs_6_), channel_id=1, source_target_pairs={{0,4},{4,0},{8,12},{12,8},{1,5},{5,1},{9,13},{13,9},{2,6},{6,2},{1... | collective-permute-start | bytes 393224 | tf_op jit(solution)/shard_map/ppermute | solution.py:233
  74.4 9.3 %collective-permute-start.26 = (f32[40,768]{1,0:T(8,128)S(1)}, f32[40,768]{1,0:T(8,128)S(1)}, u32[]{:S(2)}, u32[]{:S(2)}) collective-permute-start(f32[40,768]{1,0:T(8,128)S(1)} %add.44.refs_8_), channel_id=1, source_target_pairs={{0,4},{4,0},{8,12},{12,8},{1,5},{5,1},{9,13},{13,9},{2,6},{6,2},{1... | collective-permute-start | bytes 368648 | tf_op jit(solution)/shard_map/ppermute | solution.py:233

commit v9 on v8

--- a/solution.py
+++ b/solution.py
@@ -121,7 +121,7 @@
     here, nc = high.shape
     height = sum(count for _, count, _ in rows)
     extra = sum(count for _, count, _ in partners)
-    steps = steps_of(here, 512)
+    steps = steps_of(here, 1024)
 
     def body(*refs):
         refs = list(refs)

time: 89.9 us -> 89.9 us (level)
  no operation moved by 1% of the time
where the time goes in v9:
time: 89.9 us; the launch traced here: 89.7 us
  Pallas kernels  31.6 us (35%)
  waiting for transfers between devices  28.6 us (32%)
  starting transfers between devices  27.1 us (30%)
  local copies, waits for them, and re-layouts  1.82 us (2%)
    pallas_call x11, Pallas kernels, call(): pl.pallas_call(body, in_specs=specs, out_specs=out_specs, out_shape=outs,...  31.6 us
    ppermute x14, starting transfers between devices, row_swap(): return lax.ppermute(value, 'row', [(i, i ^ step) for i in range(rows)])  19.4 us
    ppermute x14, waiting for transfers between devices, row_swap(): return lax.ppermute(value, 'row', [(i, i ^ step) for i in range(rows)])  15 us
    ppermute x3, waiting for transfers between devices, from_chip(): lax.ppermute(value, 'col', [((i + 2 * step) % cols, i) for i in range(col...  11.9 us
    ppermute x3, starting transfers between devices, from_chip(): lax.ppermute(value, 'col', [((i + 2 * step) % cols, i) for i in range(col...  4.57 us
    ppermute x12, starting transfers between devices, core_swap(): return lax.ppermute(value, 'col', [(i, i ^ 1) for i in range(cols)])  3.1 us
  transfers between devices with their start and end apart: 29, of which 12 were waited for; matrix products, arithmetic and copies ran while one was open for 0% of the time, Pallas kernels for 28%

profile of v9, /device:TPU:0, one launch (start us, length us, event | category | flops | bytes accessed | tf_op | source)
XLA Modules:
  0.0 89.7 jit_solution(10220396264215590321)
XLA Ops:
  0.1 1.6 %copy-done = f32[2,64,4096]{2,1,0:T(8,128)S(1)} copy-done((f32[2,64,4096]{2,1,0:T(8,128)S(1)}, f32[2,64,4096]{2,1,0:T(8,128)}, u32[]{:S(2)}) %copy-start) | copy-done | bytes 2097176
  1.7 0.8 cut.1
  3.1 2.9 %collective-permute-start.5 = (f32[64,4096]{1,0:T(8,128)S(1)}, f32[64,4096]{1,0:T(8,128)S(1)}, u32[]{:S(2)}, u32[]{:S(2)}) collective-permute-start(f32[64,4096]{1,0:T(8,128)S(1)} %get-tuple-element.34.refs_1_.refs_5_.refs_6_.refs_4_), channel_id=1, source_target_pairs={{2,0},{3,1},{0,2},{1,3},{6,4},{7,5},{4,6},{5,7},{10,8},{11,9},{8,1... | collective-permute-start | bytes 3145736 | tf_op jit(solution)/shard_map/ppermute | solution.py:230
  6.0 3.6 %load.1 = (bf16[4096,512]{1,0:T(8,128)(2,1)S(1)}, bf16[4096,512]{1,0:T(8,128)(2,1)S(1)}) custom-call(f32[4096,512]{1,0:T(8,128)} %in_ref.2), custom_call_target="tpu_custom_call" | custom-call | flops 1 | bytes 1 | tf_op jit(solution)/shard_map/load/pallas_call | solution.py:20
  9.7 3.2 %project_own1.1 = (f32[64,640]{1,0:T(8,128)S(1)}, f32[64,640]{1,0:T(8,128)S(1)}) custom-call(s32[6]{0:T(128)S(1)} %stack.23.where_ref.refs_0_, f32[64,4096]{1,0:T(8,128)S(1)} %get-tuple-element.34.refs_1_.refs_5_.refs_6_.refs_4_, f32[64,4096]{1,0:T(8,128)S(1)} %collective-permute-done.refs_2_.refs_6_.refs_7_.refs_5_, ...), custom_call_target="tpu_custom_call" | custom-call | flops 1 | bytes 1 | tf_op jit(solution)/shard_map/project_own1/pallas_call | solution.py:20
  12.8 1.6 %collective-permute-start.2 = (f32[64,640]{1,0:T(8,128)S(1)}, f32[64,640]{1,0:T(8,128)S(1)}, u32[]{:S(2)}, u32[]{:S(2)}) collective-permute-start(f32[64,640]{1,0:T(8,128)S(1)} %get-tuple-element.40), channel_id=1, source_target_pairs={{0,4},{4,0},{8,12},{12,8},{1,5},{5,1},{9,13},{13,9},{2,6},{6,2},{1... | collective-permute-start | bytes 491528 | tf_op jit(solution)/shard_map/ppermute | solution.py:233
  14.5 2.3 %project_own0.1 = (f32[64,512]{1,0:T(8,128)S(1)}, f32[64,512]{1,0:T(8,128)S(1)}) custom-call(s32[6]{0:T(128)S(1)} %stack.23.where_ref.refs_0_, f32[64,4096]{1,0:T(8,128)S(1)} %get-tuple-element.49.refs_3_.refs_1_.refs_6_.in_ref.refs_13_, f32[64,4096]{1,0:T(8,128)S(1)} %collective-permute-done.1.refs_4_.refs_2_.refs_7_.refs_14_, ...), custom_call_target="tpu_custom_call" | custom-call | flops 1 | bytes 1 | tf_op jit(solution)/shard_map/project_own0/pallas_call | solution.py:20
  17.6 2.0 %reorder.1 = (f32[256,256]{1,0:T(8,128)S(1)}, f32[256,256]{1,0:T(8,128)S(1)}) custom-call(s32[6]{0:T(128)S(1)} %stack.23.where_ref.refs_0_, f32[2,256,256]{2,1,0:T(8,128)S(1)} %copy-done.1), custom_call_target="tpu_custom_call" | custom-call | flops 1 | bytes 1 | tf_op jit(solution)/shard_map/reorder/pallas_call | solution.py:20
  19.6 10.4 %collective-permute-done.5.refs_1_.refs_7_.refs_8_.refs_6_ = f32[64,4096]{1,0:T(8,128)S(1)} collective-permute-done((f32[64,4096]{1,0:T(8,128)S(1)}, f32[64,4096]{1,0:T(8,128)S(1)}, u32[]{:S(2)}, u32[]{:S(2)}) %collective-permute-start.5) | collective-permute-done | bytes 1048608 | tf_op jit(solution)/shard_map/ppermute | solution.py:230
  31.7 3.2 %collective-permute-start.3 = (f32[64,640]{1,0:T(8,128)S(1)}, f32[64,640]{1,0:T(8,128)S(1)}, u32[]{:S(2)}, u32[]{:S(2)}) collective-permute-start(f32[64,640]{1,0:T(8,128)S(1)} %add.37), channel_id=1, source_target_pairs={{0,8},{4,12},{8,0},{12,4},{1,9},{5,13},{9,1},{13,5},{2,10},{6,14},... | collective-permute-start | bytes 491528 | tf_op jit(solution)/shard_map/ppermute | solution.py:233
  34.8 3.2 %project_one_0.1 = (f32[64,640]{1,0:T(8,128)S(1)}, f32[64,640]{1,0:T(8,128)S(1)}) custom-call(s32[6]{0:T(128)S(1)} %stack.23.where_ref.refs_0_, f32[64,4096]{1,0:T(8,128)S(1)} %collective-permute-done.5.refs_1_.refs_7_.refs_8_.refs_6_, f32[16,4096]{1,0:T(8,128)S(1)} %collective-permute-done.7.refs_2_.refs_8_.refs_9_.refs_7_, ...), custom_call_target="tpu_custom_call" | custom-call | flops 1 | bytes 1 | tf_op jit(solution)/shard_map/project_one_0/pallas_call | solution.py:20
  38.0 1.6 %collective-permute-start.11 = (f32[64,640]{1,0:T(8,128)S(1)}, f32[64,640]{1,0:T(8,128)S(1)}, u32[]{:S(2)}, u32[]{:S(2)}) collective-permute-start(f32[64,640]{1,0:T(8,128)S(1)} %get-tuple-element.48), channel_id=1, source_target_pairs={{0,4},{4,0},{8,12},{12,8},{1,5},{5,1},{9,13},{13,9},{2,6},{6,2},{1... | collective-permute-start | bytes 491528 | tf_op jit(solution)/shard_map/ppermute | solution.py:233
  39.7 1.2 %collective-permute-start.13 = (f32[64,512]{1,0:T(8,128)S(1)}, f32[64,512]{1,0:T(8,128)S(1)}, u32[]{:S(2)}, u32[]{:S(2)}) collective-permute-start(f32[64,512]{1,0:T(8,128)S(1)} %add.39), channel_id=1, source_target_pairs={{0,8},{4,12},{8,0},{12,4},{1,9},{5,13},{9,1},{13,5},{2,10},{6,14},... | collective-permute-start | bytes 393224 | tf_op jit(solution)/shard_map/ppermute | solution.py:233
  40.9 1.5 %collective-permute-start.19 = (f32[24,4096]{1,0:T(8,128)S(1)}, f32[24,4096]{1,0:T(8,128)S(1)}, u32[]{:S(2)}, u32[]{:S(2)}) collective-permute-start(f32[24,4096]{1,0:T(8,128)S(1)} %get-tuple-element.57), channel_id=1, source_target_pairs={{2,0},{3,1},{0,2},{1,3},{6,4},{7,5},{4,6},{5,7},{10,8},{11,9},{8,1... | collective-permute-start | bytes 1179656 | tf_op jit(solution)/shard_map/ppermute | solution.py:230
  42.4 1.5 %collective-permute-done.12.refs_1_.refs_15_ = f32[40,4096]{1,0:T(8,128)S(1)} collective-permute-done((f32[40,4096]{1,0:T(8,128)S(1)}, f32[40,4096]{1,0:T(8,128)S(1)}, u32[]{:S(2)}, u32[]{:S(2)}) %collective-permute-start.12) | collective-permute-done | bytes 655392 | tf_op jit(solution)/shard_map/ppermute | solution.py:230
  43.8 4.8 %collective-permute-done.13 = f32[64,512]{1,0:T(8,128)S(1)} collective-permute-done((f32[64,512]{1,0:T(8,128)S(1)}, f32[64,512]{1,0:T(8,128)S(1)}, u32[]{:S(2)}, u32[]{:S(2)}) %collective-permute-start.13) | collective-permute-done | bytes 131104 | tf_op jit(solution)/shard_map/ppermute | solution.py:233
  48.6 0.6 collective-permute-done.11
  50.1 1.2 %collective-permute-done.16.refs_4_.refs_18_ = f32[8,4096]{1,0:T(8,128)S(1)} collective-permute-done((f32[8,4096]{1,0:T(8,128)S(1)}, f32[8,4096]{1,0:T(8,128)S(1)}, u32[]{:S(2)}, u32[]{:S(2)}) %collective-permute-start.16) | collective-permute-done | bytes 131104 | tf_op jit(solution)/shard_map/ppermute | solution.py:227
  51.4 3.5 %project_zero_1.1 = (f32[40,768]{1,0:T(8,128)S(1)}, f32[40,768]{1,0:T(8,128)S(1)}) custom-call(s32[6]{0:T(128)S(1)} %stack.23.where_ref.refs_0_, f32[40,4096]{1,0:T(8,128)S(1)} %collective-permute-done.12.refs_1_.refs_15_, f32[16,4096]{1,0:T(8,128)S(1)} %collective-permute-done.14.refs_2_.refs_16_, f32[16,4096]{1,0:T(8,128)S(1)} %collective-permute-done.15.refs_3_.refs_17_, ...), custom_call_target="tpu_custom_call" | custom-call | flops 1 | bytes 1 | tf_op jit(solution)/shard_map/project_zero_1/pallas_call | solution.py:20
  55.6 0.7 collective-permute-start.24
  56.6 3.3 %collective-permute-start.17 = (f32[64,640]{1,0:T(8,128)S(1)}, f32[64,640]{1,0:T(8,128)S(1)}, u32[]{:S(2)}, u32[]{:S(2)}) collective-permute-start(f32[64,640]{1,0:T(8,128)S(1)} %add.40), channel_id=1, source_target_pairs={{0,8},{4,12},{8,0},{12,4},{1,9},{5,13},{9,1},{13,5},{2,10},{6,14},... | collective-permute-start | bytes 491528 | tf_op jit(solution)/shard_map/ppermute | solution.py:233
  59.9 2.7 %project_zero_2.1 = f32[48,768]{1,0:T(8,128)S(1)} custom-call(f32[24,4096]{1,0:T(8,128)S(1)} %collective-permute-done.19.refs_0_.refs_19_, f32[8,4096]{1,0:T(8,128)S(1)} %collective-permute-done.20.refs_1_.refs_20_, f32[8,4096]{1,0:T(8,128)S(1)} %collective-permute-done.21.refs_2_.refs_21_, f32[8,4096]{1,0:T(8,128)S(1)} %collective-permute-done.22.refs_3_.refs_22_, ...), custom_call_target="tpu_custom_call" | custom-call | flops 1 | bytes 1 | tf_op jit(solution)/shard_map/project_zero_2/pallas_call | solution.py:20
  62.5 0.9 collective-permute-start.27
  63.7 0.9 %collective-permute-start.25 = (f32[40,768]{1,0:T(8,128)S(1)}, f32[40,768]{1,0:T(8,128)S(1)}, u32[]{:S(2)}, u32[]{:S(2)}) collective-permute-start(f32[40,768]{1,0:T(8,128)S(1)} %add.43), channel_id=1, source_target_pairs={{0,8},{4,12},{8,0},{12,4},{1,9},{5,13},{9,1},{13,5},{2,10},{6,14},... | collective-permute-start | bytes 368648 | tf_op jit(solution)/shard_map/ppermute | solution.py:233
  64.6 3.8 %collective-permute-done.17 = f32[64,640]{1,0:T(8,128)S(1)} collective-permute-done((f32[64,640]{1,0:T(8,128)S(1)}, f32[64,640]{1,0:T(8,128)S(1)}, u32[]{:S(2)}, u32[]{:S(2)}) %collective-permute-start.17) | collective-permute-done | bytes 163872 | tf_op jit(solution)/shard_map/ppermute | solution.py:233
  68.5 1.1 %collective-permute-start.18 = (f32[64,640]{1,0:T(8,128)S(1)}, f32[64,640]{1,0:T(8,128)S(1)}, u32[]{:S(2)}, u32[]{:S(2)}) collective-permute-start(f32[64,640]{1,0:T(8,128)S(1)} %add.41.refs_3_.refs_4_), channel_id=1, source_target_pairs={{0,4},{4,0},{8,12},{12,8},{1,5},{5,1},{9,13},{13,9},{2,6},{6,2},{1... | collective-permute-start | bytes 491528 | tf_op jit(solution)/shard_map/ppermute | solution.py:233
  69.6 2.7 %collective-permute-done.27 = f32[48,768]{1,0:T(8,128)S(1)} collective-permute-done((f32[48,768]{1,0:T(8,128)S(1)}, f32[48,768]{1,0:T(8,128)S(1)}, u32[]{:S(2)}, u32[]{:S(2)}) %collective-permute-start.27) | collective-permute-done | bytes 147488 | tf_op jit(solution)/shard_map/ppermute | solution.py:233
  72.2 2.1 %collective-permute-start.28 = (f32[48,768]{1,0:T(8,128)S(1)}, f32[48,768]{1,0:T(8,128)S(1)}, u32[]{:S(2)}, u32[]{:S(2)}) collective-permute-start(f32[48,768]{1,0:T(8,128)S(1)} %add.45.refs_10_), channel_id=1, source_target_pairs={{0,8},{4,12},{8,0},{12,4},{1,9},{5,13},{9,1},{13,5},{2,10},{6,14},... | collective-permute-start | bytes 442376 | tf_op jit(solution)/shard_map/ppermute | solution.py:233
  74.5 2.1 %collective-permute-start.26 = (f32[40,768]{1,0:T(8,128)S(1)}, f32[40,768]{1,0:T(8,128)S(1)}, u32[]{:S(2)}, u32[]{:S(2)}) collective-permute-start(f32[40,768]{1,0:T(8,128)S(1)} %add.44.refs_8_), channel_id=1, source_target_pairs={{0,4},{4,0},{8,12},{12,8},{1,5},{5,1},{9,13},{13,9},{2,6},{6,2},{1... | collective-permute-start | bytes 368648 | tf_op jit(solution)/shard_map/ppermute | solution.py:233
  76.5 2.6 %collective-permute-done.18.refs_4_.refs_5_ = f32[64,640]{1,0:T(8,128)S(1)} collective-permute-done((f32[64,640]{1,0:T(8,128)S(1)}, f32[64,640]{1,0:T(8,128)S(1)}, u32[]{:S(2)}, u32[]{:S(2)}) %collective-permute-start.18) | collective-permute-done | bytes 163872 | tf_op jit(solution)/shard_map/ppermute | solution.py:233
  79.2 4.4 %update_one.1 = (f32[4096,512]{1,0:T(8,128)S(1)}, f32[256,512]{1,0:T(8,128)S(1)}) custom-call(s32[6]{0:T(128)S(1)} %stack.23.where_ref.refs_0_, f32[64,640]{1,0:T(8,128)S(1)} %add.38.refs_1_.refs_2_, f32[64,640]{1,0:T(8,128)S(1)} %collective-permute-done.4.refs_2_.refs_3_, f32[64,640]{1,0:T(8,128)S(1)} %add.41.refs_3_.refs_4_, ...), custom_call_target="tpu_custom_call" | custom-call | flops 1 | bytes 1 | tf_op jit(solution)/shard_map/update_one/pallas_call | solution.py:20
  83.7 5.9 %update_zero.1 = f32[4096,512]{1,0:T(8,128)} custom-call(s32[6]{0:T(128)S(1)} %stack.23.where_ref.refs_0_, f32[256,512]{1,0:T(8,128)S(1)} %get-tuple-element.56.refs_1_, f32[64,640]{1,0:T(8,128)S(1)} %add.38.refs_1_.refs_2_, f32[64,640]{1,0:T(8,128)S(1)} %collective-permute-done.4.refs_2_.refs_3_, f32[64,640]{1,0:T(8,128)S(1)} %add.41.refs_3_.refs_4_, ...), custom_call_target="tpu_custom_call" | custom-call | flops 1 | bytes 1 | tf_op jit(solution)/shard_map/update_zero/pallas_call | solution.py:20
  (55 shorter events, 5.6 us)
Async XLA Ops:
  0.1 1.6 %copy-start = (f32[2,64,4096]{2,1,0:T(8,128)S(1)}, f32[2,64,4096]{2,1,0:T(8,128)}, u32[]{:S(2)}) copy-start(f32[2,64,4096]{2,1,0:T(8,128)} %in_ref.1) | copy-start | bytes 6291460
  2.5 7.1 %collective-permute-start = (f32[64,4096]{1,0:T(8,128)S(1)}, f32[64,4096]{1,0:T(8,128)S(1)}, u32[]{:S(2)}, u32[]{:S(2)}) collective-permute-start(f32[64,4096]{1,0:T(8,128)S(1)} %get-tuple-element.34.refs_1_.refs_5_.refs_6_.refs_4_), channel_id=1, source_target_pairs={{0,1},{1,0},{2,3},{3,2},{4,5},{5,4},{6,7},{7,6},{8,9},{9,8},{10,11... | collective-permute-start | bytes 3145736 | tf_op jit(solution)/shard_map/ppermute | solution.py:227
  3.0 6.6 %collective-permute-start.1 = (f32[64,4096]{1,0:T(8,128)S(1)}, f32[64,4096]{1,0:T(8,128)S(1)}, u32[]{:S(2)}, u32[]{:S(2)}) collective-permute-start(f32[64,4096]{1,0:T(8,128)S(1)} %get-tuple-element.49.refs_3_.refs_1_.refs_6_.in_ref.refs_13_), channel_id=1, source_target_pairs={{0,1},{1,0},{2,3},{3,2},{4,5},{5,4},{6,7},{7,6},{8,9},{9,8},{10,11... | collective-permute-start | bytes 3145736 | tf_op jit(solution)/shard_map/ppermute | solution.py:227
  3.1 26.9 %collective-permute-start.5 = (f32[64,4096]{1,0:T(8,128)S(1)}, f32[64,4096]{1,0:T(8,128)S(1)}, u32[]{:S(2)}, u32[]{:S(2)}) collective-permute-start(f32[64,4096]{1,0:T(8,128)S(1)} %get-tuple-element.34.refs_1_.refs_5_.refs_6_.refs_4_), channel_id=1, source_target_pairs={{2,0},{3,1},{0,2},{1,3},{6,4},{7,5},{4,6},{5,7},{10,8},{11,9},{8,1... | collective-permute-start | bytes 3145736 | tf_op jit(solution)/shard_map/ppermute | solution.py:230
  12.8 4.7 %copy-start.1 = (f32[2,256,256]{2,1,0:T(8,128)S(1)}, f32[2,256,256]{2,1,0:T(8,128)}, u32[]{:S(2)}) copy-start(f32[2,256,256]{2,1,0:T(8,128)} %in_ref.3) | copy-start | bytes 1572868
  12.8 17.1 %collective-permute-start.2 = (f32[64,640]{1,0:T(8,128)S(1)}, f32[64,640]{1,0:T(8,128)S(1)}, u32[]{:S(2)}, u32[]{:S(2)}) collective-permute-start(f32[64,640]{1,0:T(8,128)S(1)} %get-tuple-element.40), channel_id=1, source_target_pairs={{0,4},{4,0},{8,12},{12,8},{1,5},{5,1},{9,13},{13,9},{2,6},{6,2},{1... | collective-permute-start | bytes 491528 | tf_op jit(solution)/shard_map/ppermute | solution.py:233
  16.8 13.2 %collective-permute-start.6 = (f32[64,512]{1,0:T(8,128)S(1)}, f32[64,512]{1,0:T(8,128)S(1)}, u32[]{:S(2)}, u32[]{:S(2)}) collective-permute-start(f32[64,512]{1,0:T(8,128)S(1)} %get-tuple-element.43), channel_id=1, source_target_pairs={{0,4},{4,0},{8,12},{12,8},{1,5},{5,1},{9,13},{13,9},{2,6},{6,2},{1... | collective-permute-start | bytes 393224 | tf_op jit(solution)/shard_map/ppermute | solution.py:233
  17.4 26.4 %collective-permute-start.12 = (f32[40,4096]{1,0:T(8,128)S(1)}, f32[40,4096]{1,0:T(8,128)S(1)}, u32[]{:S(2)}, u32[]{:S(2)}) collective-permute-start(f32[40,4096]{1,0:T(8,128)S(1)} %get-tuple-element.50), channel_id=1, source_target_pairs={{2,0},{3,1},{0,2},{1,3},{6,4},{7,5},{4,6},{5,7},{10,8},{11,9},{8,1... | collective-permute-start | bytes 1966088 | tf_op jit(solution)/shard_map/ppermute | solution.py:230
  30.1 1.6 %collective-permute-start.7 = (f32[16,4096]{1,0:T(8,128)S(1)}, f32[16,4096]{1,0:T(8,128)S(1)}, u32[]{:S(2)}, u32[]{:S(2)}) collective-permute-start(f32[16,4096]{1,0:T(8,128)S(1)} %get-tuple-element.66), channel_id=1, source_target_pairs={{0,1},{1,0},{2,3},{3,2},{4,5},{5,4},{6,7},{7,6},{8,9},{9,8},{10,11... | collective-permute-start | bytes 786440 | tf_op jit(solution)/shard_map/ppermute | solution.py:227
  30.1 4.7 %collective-permute-start.8 = (f32[16,4096]{1,0:T(8,128)S(1)}, f32[16,4096]{1,0:T(8,128)S(1)}, u32[]{:S(2)}, u32[]{:S(2)}) collective-permute-start(f32[16,4096]{1,0:T(8,128)S(1)} %get-tuple-element.65), channel_id=1, source_target_pairs={{0,1},{1,0},{2,3},{3,2},{4,5},{5,4},{6,7},{7,6},{8,9},{9,8},{10,11... | collective-permute-start | bytes 786440 | tf_op jit(solution)/shard_map/ppermute | solution.py:227
  30.6 4.2 %collective-permute-start.9 = (f32[16,4096]{1,0:T(8,128)S(1)}, f32[16,4096]{1,0:T(8,128)S(1)}, u32[]{:S(2)}, u32[]{:S(2)}) collective-permute-start(f32[16,4096]{1,0:T(8,128)S(1)} %get-tuple-element.64), channel_id=1, source_target_pairs={{0,1},{1,0},{2,3},{3,2},{4,5},{5,4},{6,7},{7,6},{8,9},{9,8},{10,11... | collective-permute-start | bytes 786440 | tf_op jit(solution)/shard_map/ppermute | solution.py:227
  30.7 4.1 %collective-permute-start.10 = (f32[16,4096]{1,0:T(8,128)S(1)}, f32[16,4096]{1,0:T(8,128)S(1)}, u32[]{:S(2)}, u32[]{:S(2)}) collective-permute-start(f32[16,4096]{1,0:T(8,128)S(1)} %get-tuple-element.63), channel_id=1, source_target_pairs={{0,1},{1,0},{2,3},{3,2},{4,5},{5,4},{6,7},{7,6},{8,9},{9,8},{10,11... | collective-permute-start | bytes 786440 | tf_op jit(solution)/shard_map/ppermute | solution.py:227
  31.7 16.9 %collective-permute-start.3 = (f32[64,640]{1,0:T(8,128)S(1)}, f32[64,640]{1,0:T(8,128)S(1)}, u32[]{:S(2)}, u32[]{:S(2)}) collective-permute-start(f32[64,640]{1,0:T(8,128)S(1)} %add.37), channel_id=1, source_target_pairs={{0,8},{4,12},{8,0},{12,4},{1,9},{5,13},{9,1},{13,5},{2,10},{6,14},... | collective-permute-start | bytes 491528 | tf_op jit(solution)/shard_map/ppermute | solution.py:233
  38.0 11.1 %collective-permute-start.11 = (f32[64,640]{1,0:T(8,128)S(1)}, f32[64,640]{1,0:T(8,128)S(1)}, u32[]{:S(2)}, u32[]{:S(2)}) collective-permute-start(f32[64,640]{1,0:T(8,128)S(1)} %get-tuple-element.48), channel_id=1, source_target_pairs={{0,4},{4,0},{8,12},{12,8},{1,5},{5,1},{9,13},{13,9},{2,6},{6,2},{1... | collective-permute-start | bytes 491528 | tf_op jit(solution)/shard_map/ppermute | solution.py:233
  39.7 8.9 %collective-permute-start.13 = (f32[64,512]{1,0:T(8,128)S(1)}, f32[64,512]{1,0:T(8,128)S(1)}, u32[]{:S(2)}, u32[]{:S(2)}) collective-permute-start(f32[64,512]{1,0:T(8,128)S(1)} %add.39), channel_id=1, source_target_pairs={{0,8},{4,12},{8,0},{12,4},{1,9},{5,13},{9,1},{13,5},{2,10},{6,14},... | collective-permute-start | bytes 393224 | tf_op jit(solution)/shard_map/ppermute | solution.py:233
  40.9 14.0 %collective-permute-start.19 = (f32[24,4096]{1,0:T(8,128)S(1)}, f32[24,4096]{1,0:T(8,128)S(1)}, u32[]{:S(2)}, u32[]{:S(2)}) collective-permute-start(f32[24,4096]{1,0:T(8,128)S(1)} %get-tuple-element.57), channel_id=1, source_target_pairs={{2,0},{3,1},{0,2},{1,3},{6,4},{7,5},{4,6},{5,7},{10,8},{11,9},{8,1... | collective-permute-start | bytes 1179656 | tf_op jit(solution)/shard_map/ppermute | solution.py:230
  49.2 2.2 %collective-permute-start.14 = (f32[16,4096]{1,0:T(8,128)S(1)}, f32[16,4096]{1,0:T(8,128)S(1)}, u32[]{:S(2)}, u32[]{:S(2)}) collective-permute-start(f32[16,4096]{1,0:T(8,128)S(1)} %get-tuple-element.68), channel_id=1, source_target_pairs={{0,1},{1,0},{2,3},{3,2},{4,5},{5,4},{6,7},{7,6},{8,9},{9,8},{10,11... | collective-permute-start | bytes 786440 | tf_op jit(solution)/shard_map/ppermute | solution.py:227
  49.3 2.1 %collective-permute-start.15 = (f32[16,4096]{1,0:T(8,128)S(1)}, f32[16,4096]{1,0:T(8,128)S(1)}, u32[]{:S(2)}, u32[]{:S(2)}) collective-permute-start(f32[16,4096]{1,0:T(8,128)S(1)} %get-tuple-element.67), channel_id=1, source_target_pairs={{0,1},{1,0},{2,3},{3,2},{4,5},{5,4},{6,7},{7,6},{8,9},{9,8},{10,11... | collective-permute-start | bytes 786440 | tf_op jit(solution)/shard_map/ppermute | solution.py:227
  49.8 1.6 %collective-permute-start.16 = (f32[8,4096]{1,0:T(8,128)S(1)}, f32[8,4096]{1,0:T(8,128)S(1)}, u32[]{:S(2)}, u32[]{:S(2)}) collective-permute-start(f32[8,4096]{1,0:T(8,128)S(1)} %slice.36), channel_id=1, source_target_pairs={{0,1},{1,0},{2,3},{3,2},{4,5},{5,4},{6,7},{7,6},{8,9},{9,8},{10,11... | collective-permute-start | bytes 393224 | tf_op jit(solution)/shard_map/ppermute | solution.py:227
  49.9 6.6 %collective-permute-start.4 = (f32[64,640]{1,0:T(8,128)S(1)}, f32[64,640]{1,0:T(8,128)S(1)}, u32[]{:S(2)}, u32[]{:S(2)}) collective-permute-start(f32[64,640]{1,0:T(8,128)S(1)} %add.38.refs_1_.refs_2_), channel_id=1, source_target_pairs={{0,4},{4,0},{8,12},{12,8},{1,5},{5,1},{9,13},{13,9},{2,6},{6,2},{1... | collective-permute-start | bytes 491528 | tf_op jit(solution)/shard_map/ppermute | solution.py:233
  54.9 4.9 %collective-permute-start.20 = (f32[8,4096]{1,0:T(8,128)S(1)}, f32[8,4096]{1,0:T(8,128)S(1)}, u32[]{:S(2)}, u32[]{:S(2)}) collective-permute-start(f32[8,4096]{1,0:T(8,128)S(1)} %get-tuple-element.71), channel_id=1, source_target_pairs={{0,1},{1,0},{2,3},{3,2},{4,5},{5,4},{6,7},{7,6},{8,9},{9,8},{10,11... | collective-permute-start | bytes 393224 | tf_op jit(solution)/shard_map/ppermute | solution.py:227
  55.1 4.7 %collective-permute-start.21 = (f32[8,4096]{1,0:T(8,128)S(1)}, f32[8,4096]{1,0:T(8,128)S(1)}, u32[]{:S(2)}, u32[]{:S(2)}) collective-permute-start(f32[8,4096]{1,0:T(8,128)S(1)} %get-tuple-element.70), channel_id=1, source_target_pairs={{0,1},{1,0},{2,3},{3,2},{4,5},{5,4},{6,7},{7,6},{8,9},{9,8},{10,11... | collective-permute-start | bytes 393224 | tf_op jit(solution)/shard_map/ppermute | solution.py:227
  55.5 4.4 %collective-permute-start.22 = (f32[8,4096]{1,0:T(8,128)S(1)}, f32[8,4096]{1,0:T(8,128)S(1)}, u32[]{:S(2)}, u32[]{:S(2)}) collective-permute-start(f32[8,4096]{1,0:T(8,128)S(1)} %get-tuple-element.69), channel_id=1, source_target_pairs={{0,1},{1,0},{2,3},{3,2},{4,5},{5,4},{6,7},{7,6},{8,9},{9,8},{10,11... | collective-permute-start | bytes 393224 | tf_op jit(solution)/shard_map/ppermute | solution.py:227
  55.6 8.1 %collective-permute-start.24 = (f32[40,768]{1,0:T(8,128)S(1)}, f32[40,768]{1,0:T(8,128)S(1)}, u32[]{:S(2)}, u32[]{:S(2)}) collective-permute-start(f32[40,768]{1,0:T(8,128)S(1)} %get-tuple-element.53), channel_id=1, source_target_pairs={{0,4},{4,0},{8,12},{12,8},{1,5},{5,1},{9,13},{13,9},{2,6},{6,2},{1... | collective-permute-start | bytes 368648 | tf_op jit(solution)/shard_map/ppermute | solution.py:233
  56.6 11.9 %collective-permute-start.17 = (f32[64,640]{1,0:T(8,128)S(1)}, f32[64,640]{1,0:T(8,128)S(1)}, u32[]{:S(2)}, u32[]{:S(2)}) collective-permute-start(f32[64,640]{1,0:T(8,128)S(1)} %add.40), channel_id=1, source_target_pairs={{0,8},{4,12},{8,0},{12,4},{1,9},{5,13},{9,1},{13,5},{2,10},{6,14},... | collective-permute-start | bytes 491528 | tf_op jit(solution)/shard_map/ppermute | solution.py:233
  62.5 9.7 %collective-permute-start.27 = (f32[48,768]{1,0:T(8,128)S(1)}, f32[48,768]{1,0:T(8,128)S(1)}, u32[]{:S(2)}, u32[]{:S(2)}) collective-permute-start(f32[48,768]{1,0:T(8,128)S(1)} %project_zero_2.1), channel_id=1, source_target_pairs={{0,4},{4,0},{8,12},{12,8},{1,5},{5,1},{9,13},{13,9},{2,6},{6,2},{1... | collective-permute-start | bytes 442376 | tf_op jit(solution)/shard_map/ppermute | solution.py:233
  63.7 10.7 %collective-permute-start.25 = (f32[40,768]{1,0:T(8,128)S(1)}, f32[40,768]{1,0:T(8,128)S(1)}, u32[]{:S(2)}, u32[]{:S(2)}) collective-permute-start(f32[40,768]{1,0:T(8,128)S(1)} %add.43), channel_id=1, source_target_pairs={{0,8},{4,12},{8,0},{12,4},{1,9},{5,13},{9,1},{13,5},{2,10},{6,14},... | collective-permute-start | bytes 368648 | tf_op jit(solution)/shard_map/ppermute | solution.py:233
  68.5 10.7 %collective-permute-start.18 = (f32[64,640]{1,0:T(8,128)S(1)}, f32[64,640]{1,0:T(8,128)S(1)}, u32[]{:S(2)}, u32[]{:S(2)}) collective-permute-start(f32[64,640]{1,0:T(8,128)S(1)} %add.41.refs_3_.refs_4_), channel_id=1, source_target_pairs={{0,4},{4,0},{8,12},{12,8},{1,5},{5,1},{9,13},{13,9},{2,6},{6,2},{1... | collective-permute-start | bytes 491528 | tf_op jit(solution)/shard_map/ppermute | solution.py:233
  72.2 11.5 %collective-permute-start.28 = (f32[48,768]{1,0:T(8,128)S(1)}, f32[48,768]{1,0:T(8,128)S(1)}, u32[]{:S(2)}, u32[]{:S(2)}) collective-permute-start(f32[48,768]{1,0:T(8,128)S(1)} %add.45.refs_10_), channel_id=1, source_target_pairs={{0,8},{4,12},{8,0},{12,4},{1,9},{5,13},{9,1},{13,5},{2,10},{6,14},... | collective-permute-start | bytes 442376 | tf_op jit(solution)/shard_map/ppermute | solution.py:233
  74.4 9.3 %collective-permute-start.23 = (f32[64,512]{1,0:T(8,128)S(1)}, f32[64,512]{1,0:T(8,128)S(1)}, u32[]{:S(2)}, u32[]{:S(2)}) collective-permute-start(f32[64,512]{1,0:T(8,128)S(1)} %add.42.refs_6_), channel_id=1, source_target_pairs={{0,4},{4,0},{8,12},{12,8},{1,5},{5,1},{9,13},{13,9},{2,6},{6,2},{1... | collective-permute-start | bytes 393224 | tf_op jit(solution)/shard_map/ppermute | solution.py:233
  74.5 9.2 %collective-permute-start.26 = (f32[40,768]{1,0:T(8,128)S(1)}, f32[40,768]{1,0:T(8,128)S(1)}, u32[]{:S(2)}, u32[]{:S(2)}) collective-permute-start(f32[40,768]{1,0:T(8,128)S(1)} %add.44.refs_8_), channel_id=1, source_target_pairs={{0,4},{4,0},{8,12},{12,8},{1,5},{5,1},{9,13},{13,9},{2,6},{6,2},{1... | collective-permute-start | bytes 368648 | tf_op jit(solution)/shard_map/ppermute | solution.py:233
